TPU v7x, 32 devices: a whole 2x2x4 slice. The times are simulated.
32 devices in a mesh: fsdp: 4 (over x, core), ctx: 8 (over z, y).
Axes of the slice: x: 2, y: 2, z: 4, core: 2. Of those that a mesh axis runs over, the one named last changes fastest.
Arguments:
- layer_in: bfloat16 [8, 1024, 768], P('fsdp', 'ctx'), may hold values from -6 to 6
- encoded: bfloat16 [8, 1024, 768], P('fsdp', 'ctx'), may hold values from -6 to 6
- pairing: int32 [8, 2], replicated, may hold values from 0 to 15, as said below
- attn_weight: bfloat16 [6, 768, 768], P(None, 'fsdp'), may hold values from -1 to 1
- out_weight: bfloat16 [2, 768, 768], P(None, 'fsdp'), may hold values from -1.75 to 1.75
- up_weight: bfloat16 [768, 3072], P('fsdp'), may hold values from -0.21875 to 0.21875
- down_weight: bfloat16 [3072, 768], P('fsdp'), may hold values from -0.109375 to 0.109375
- norm_gains: bfloat16 [3, 768], P(None, 'fsdp'), may hold values from 0.5 to 1.5
- bias_rows: bfloat16 [9, 768], P(None, 'fsdp'), may hold values from -2.5 to 2.5
- up_bias: bfloat16 [3072], P('fsdp'), may hold values from -2.5 to 2.5
- down_bias: bfloat16 [768], P('fsdp'), may hold values from -2.5 to 2.5
- out_cotangent: bfloat16 [8, 1024, 768], P('fsdp', 'ctx'), may hold values from -6 to 6
Outputs:
- layer_out: bfloat16 [8, 1024, 768], P('fsdp', 'ctx')
- grad_layer_in: float32 [8, 1024, 768], P('fsdp', 'ctx')
- grad_encoded: float32 [8, 1024, 768], P('fsdp', 'ctx')
- grad_attn_weight: float32 [6, 768, 768], P(None, 'fsdp')
- grad_out_weight: float32 [2, 768, 768], P(None, 'fsdp')
- grad_up_weight: float32 [768, 3072], P('fsdp')
- grad_down_weight: float32 [3072, 768], P('fsdp')
- grad_norm_gains: float32 [3, 768], P(None, 'fsdp')
- grad_bias_rows: float32 [9, 768], P(None, 'fsdp')
- grad_up_bias: float32 [3072], P('fsdp')
- grad_down_bias: float32 [768], P('fsdp')
Inputs may be any that keep to these rules, and one draw needn't show every extreme that they name: `pairing`: row r lists two spans c and 15 - c; every span of 0 to 15 appears exactly once in the table.
All inputs are finite; a program needn't handle non-finite values.
Results may differ from a plain program's by a relative error of at most 0.02.
Values may be sent and summed in bfloat16 or wider, within the bound.
No kernel may reach another device: no remote copies, remote signals or barrier semaphores. Data moves between devices by JAX's collectives and lax.ppermute only.
A program may use at most 384 MiB of HBM per device.

v0:
```python
import jax
import jax.numpy as jnp
from jax import lax
from jax.sharding import PartitionSpec as P

H = 12
HD = 64


SCORE_SCALE = 0.125
MASK_FILL = -1e30
NORM_EPSILON = 1e-05


def layer_norm(values, gain, shift):
    center = values - jnp.mean(values, axis=-1, keepdims=True)
    spread = jnp.mean(center * center, axis=-1, keepdims=True)
    return center * lax.rsqrt(spread + NORM_EPSILON) * gain + shift


def gelu_exact(values):
    return jax.nn.gelu(values, approximate=False)


def matmul(left, right):
    return jnp.dot(left, right, preferred_element_type=jnp.float32)


def contract_rows(left, right):
    return lax.dot_general(
        left, right, (((0,), (0,)), ((), ())), preferred_element_type=jnp.float32
    )


def contract_cols(left, right):
    return lax.dot_general(
        left, right, (((1,), (1,)), ((), ())), preferred_element_type=jnp.float32
    )


def column_sum(values):
    return jnp.sum(values.astype(jnp.float32), axis=0)


def token_places(pairing, half_len):
    offsets = jnp.arange(half_len, dtype=jnp.int32)
    places = pairing[:, :, None] * half_len + offsets[None, None, :]
    return places.reshape(-1)


def head_scores(query_heads, key_heads, query_places, key_places, masked):
    scores = (
        jnp.einsum("qhd,khd->hqk", query_heads, key_heads, preferred_element_type=jnp.float32)
        * SCORE_SCALE
    )
    if masked:
        allowed = key_places[None, None, :] <= query_places[None, :, None]
        scores = jnp.where(allowed, scores, MASK_FILL)
    return scores


def row_delta(dout_bf, mixed):
    query_count = mixed.shape[0]
    dout_heads = dout_bf.reshape(query_count, H, HD).astype(jnp.float32)
    return jnp.einsum("qhd,qhd->hq", dout_heads, mixed.reshape(query_count, H, HD))


def attention_forward(query_bf, key_all, value_all, query_places, key_places, masked):
    query_count = query_bf.shape[0]
    key_count = key_all.shape[0]
    block_size = min(1024, key_count)
    block_count = key_count // block_size
    query_heads = query_bf.reshape(query_count, H, HD)
    key_blocks = key_all.reshape(block_count, block_size, H, HD)
    value_blocks = value_all.reshape(block_count, block_size, H, HD)
    place_blocks = key_places.reshape(block_count, block_size)

    def max_step(running, block_item):
        running_max, row_mass = running
        key_heads, places = block_item
        scores = head_scores(query_heads, key_heads, query_places, places, masked)
        new_max = jnp.maximum(running_max, jnp.max(scores, axis=-1))
        row_mass = row_mass * jnp.exp(running_max - new_max) + jnp.sum(
            jnp.exp(scores - new_max[:, :, None]), axis=-1
        )
        return ((new_max, row_mass), None)

    start = (
        jnp.full((H, query_count), MASK_FILL, jnp.float32),
        jnp.zeros((H, query_count), jnp.float32),
    )
    (running_max, row_mass), unused = lax.scan(max_step, start, (key_blocks, place_blocks))
    log_mass = running_max + jnp.log(row_mass)

    def out_step(accum, block_item):
        key_heads, value_heads, places = block_item
        scores = head_scores(query_heads, key_heads, query_places, places, masked)
        weights = jnp.exp(scores - log_mass[:, :, None]).astype(jnp.bfloat16)
        accum = accum + jnp.einsum(
            "hqk,khd->qhd", weights, value_heads, preferred_element_type=jnp.float32
        )
        return (accum, None)

    mixed, unused = lax.scan(
        out_step,
        jnp.zeros((query_count, H, HD), jnp.float32),
        (key_blocks, value_blocks, place_blocks),
    )
    return (log_mass, mixed.reshape(query_count, H * HD))


def block_grads(
    query_heads,
    dout_heads,
    log_mass,
    delta,
    query_places,
    key_heads,
    value_heads,
    key_places,
    masked,
):
    scores = head_scores(query_heads, key_heads, query_places, key_places, masked)
    probs = jnp.exp(scores - log_mass[:, :, None])
    dprobs = jnp.einsum("qhd,khd->hqk", dout_heads, value_heads, preferred_element_type=jnp.float32)
    dscores = (probs * (dprobs - delta[:, :, None])).astype(jnp.bfloat16)
    dquery = jnp.einsum("hqk,khd->qhd", dscores, key_heads, preferred_element_type=jnp.float32)
    dkeys = (
        jnp.einsum("hqk,qhd->khd", dscores, query_heads, preferred_element_type=jnp.float32)
        * SCORE_SCALE
    )
    dvalues = jnp.einsum(
        "hqk,qhd->khd", probs.astype(jnp.bfloat16), dout_heads, preferred_element_type=jnp.float32
    )
    return (dquery, dkeys, dvalues)


def grads_by_keys(
    query_bf, dout_bf, log_mass, delta, key_all, value_all, query_places, key_places, masked
):
    query_count = query_bf.shape[0]
    key_count = key_all.shape[0]
    block_size = min(1024, key_count)
    block_count = key_count // block_size
    query_heads = query_bf.reshape(query_count, H, HD)
    dout_heads = dout_bf.reshape(query_count, H, HD)
    key_blocks = key_all.reshape(block_count, block_size, H, HD)
    value_blocks = value_all.reshape(block_count, block_size, H, HD)
    place_blocks = key_places.reshape(block_count, block_size)

    def back_step(accum, block_item):
        key_heads, value_heads, places = block_item
        dquery, dkeys, dvalues = block_grads(
            query_heads,
            dout_heads,
            log_mass,
            delta,
            query_places,
            key_heads,
            value_heads,
            places,
            masked,
        )
        return (accum + dquery, (dkeys, dvalues))

    accum, (dkeys, dvalues) = lax.scan(
        back_step,
        jnp.zeros((query_count, H, HD), jnp.float32),
        (key_blocks, value_blocks, place_blocks),
    )
    dquery_all = accum.reshape(query_count, H * HD) * SCORE_SCALE
    return (dquery_all, dkeys.reshape(key_count, H * HD), dvalues.reshape(key_count, H * HD))


def sequence_step(layer_row, encoded_row, cotangent, weights, query_places, all_places):
    attn_weight, out_weight, up_weight, down_weight, norm_gains, bias_rows, up_bias, down_bias = (
        weights
    )
    gain_float = norm_gains.astype(jnp.float32)
    bias_float = bias_rows.astype(jnp.float32)
    up_float = up_bias.astype(jnp.float32)
    down_float = down_bias.astype(jnp.float32)
    layer_float = layer_row.astype(jnp.float32)
    normed_one = layer_norm(layer_float, gain_float[0], bias_float[6]).astype(jnp.bfloat16)
    query_self = (matmul(normed_one, attn_weight[0]) + bias_float[0]).astype(jnp.bfloat16)
    key_self = matmul(normed_one, attn_weight[1]).astype(jnp.bfloat16)
    value_self = (matmul(normed_one, attn_weight[2]) + bias_float[1]).astype(jnp.bfloat16)
    key_all, value_all = (
        lax.all_gather(key_self, "ctx", axis=0, tiled=True),
        lax.all_gather(value_self, "ctx", axis=0, tiled=True),
    )
    mass_self, mixed_self = attention_forward(
        query_self, key_all, value_all, query_places, all_places, True
    )
    mixed_self_bf = mixed_self.astype(jnp.bfloat16)
    first_res = layer_float + matmul(mixed_self_bf, out_weight[0]) + bias_float[2]
    normed_two = layer_norm(first_res, gain_float[1], bias_float[7]).astype(jnp.bfloat16)
    query_cross = (matmul(normed_two, attn_weight[3]) + bias_float[3]).astype(jnp.bfloat16)
    local_keys = matmul(encoded_row, attn_weight[4]).astype(jnp.bfloat16)
    local_values = (matmul(encoded_row, attn_weight[5]) + bias_float[4]).astype(jnp.bfloat16)
    cross_keys, cross_values = (
        lax.all_gather(local_keys, "ctx", axis=0, tiled=True),
        lax.all_gather(local_values, "ctx", axis=0, tiled=True),
    )
    cross_places = jnp.zeros((cross_keys.shape[0],), jnp.int32)
    mass_cross, mixed_cross = attention_forward(
        query_cross, cross_keys, cross_values, query_places, cross_places, False
    )
    mixed_cross_bf = mixed_cross.astype(jnp.bfloat16)
    second_res = first_res + matmul(mixed_cross_bf, out_weight[1]) + bias_float[5]
    normed_three = layer_norm(second_res, gain_float[2], bias_float[8]).astype(jnp.bfloat16)
    hidden_pre = matmul(normed_three, up_weight) + up_float
    hidden_act, gelu_back = jax.vjp(gelu_exact, hidden_pre)
    hidden_bf = hidden_act.astype(jnp.bfloat16)
    layer_out = (second_res + matmul(hidden_bf, down_weight) + down_float).astype(jnp.bfloat16)
    cot_float = cotangent.astype(jnp.float32)
    grad_down = contract_rows(hidden_bf, cotangent)
    grad_hidden = contract_cols(cotangent, down_weight)
    grad_pre = gelu_back(grad_hidden)[0].astype(jnp.bfloat16)
    grad_up = contract_rows(normed_three, grad_pre)
    grad_normed_three = contract_cols(grad_pre, up_weight)
    back_three = jax.vjp(layer_norm, second_res, gain_float[2], bias_float[8])[1](grad_normed_three)
    grad_second = cot_float + back_three[0]
    branch_cross = grad_second.astype(jnp.bfloat16)
    grad_out_cross = contract_rows(mixed_cross_bf, branch_cross)
    dout_cross = contract_cols(branch_cross, out_weight[1]).astype(jnp.bfloat16)
    delta_cross = row_delta(dout_cross, mixed_cross)
    dquery_cross, dkey_cross, dvalue_cross = grads_by_keys(
        query_cross,
        dout_cross,
        mass_cross,
        delta_cross,
        cross_keys,
        cross_values,
        query_places,
        cross_places,
        False,
    )
    dkey_enc, dvalue_enc = (
        lax.psum_scatter(dkey_cross, "ctx", scatter_dimension=0, tiled=True),
        lax.psum_scatter(dvalue_cross, "ctx", scatter_dimension=0, tiled=True),
    )
    dkey_enc_bf = dkey_enc.astype(jnp.bfloat16)
    dvalue_enc_bf = dvalue_enc.astype(jnp.bfloat16)
    dquery_cross_bf = dquery_cross.astype(jnp.bfloat16)
    grad_encoded = contract_cols(dkey_enc_bf, attn_weight[4]) + contract_cols(
        dvalue_enc_bf, attn_weight[5]
    )
    grad_attn_three = contract_rows(normed_two, dquery_cross_bf)
    grad_attn_four = contract_rows(encoded_row, dkey_enc_bf)
    grad_attn_five = contract_rows(encoded_row, dvalue_enc_bf)
    grad_normed_two = contract_cols(dquery_cross_bf, attn_weight[3])
    back_two = jax.vjp(layer_norm, first_res, gain_float[1], bias_float[7])[1](grad_normed_two)
    grad_first = grad_second + back_two[0]
    branch_self = grad_first.astype(jnp.bfloat16)
    grad_out_self = contract_rows(mixed_self_bf, branch_self)
    dout_self = contract_cols(branch_self, out_weight[0]).astype(jnp.bfloat16)
    delta_self = row_delta(dout_self, mixed_self)
    dquery_own, dkey_part, dvalue_part = grads_by_keys(
        query_self,
        dout_self,
        mass_self,
        delta_self,
        key_all,
        value_all,
        query_places,
        all_places,
        True,
    )
    dkey_own, dvalue_own = (
        lax.psum_scatter(dkey_part, "ctx", scatter_dimension=0, tiled=True),
        lax.psum_scatter(dvalue_part, "ctx", scatter_dimension=0, tiled=True),
    )
    dquery_bf = dquery_own.astype(jnp.bfloat16)
    dkey_bf = dkey_own.astype(jnp.bfloat16)
    dvalue_bf = dvalue_own.astype(jnp.bfloat16)
    grad_attn_zero = contract_rows(normed_one, dquery_bf)
    grad_attn_one = contract_rows(normed_one, dkey_bf)
    grad_attn_two = contract_rows(normed_one, dvalue_bf)
    grad_normed_one = (
        contract_cols(dquery_bf, attn_weight[0])
        + contract_cols(dkey_bf, attn_weight[1])
        + contract_cols(dvalue_bf, attn_weight[2])
    )
    back_one = jax.vjp(layer_norm, layer_float, gain_float[0], bias_float[6])[1](grad_normed_one)
    grad_layer = grad_first + back_one[0]
    grad_attn = jnp.stack(
        [
            grad_attn_zero,
            grad_attn_one,
            grad_attn_two,
            grad_attn_three,
            grad_attn_four,
            grad_attn_five,
        ]
    )
    grad_outs = jnp.stack([grad_out_self, grad_out_cross])
    grad_gain = jnp.stack([back_one[1], back_two[1], back_three[1]])
    grad_bias = jnp.stack(
        [
            column_sum(dquery_bf),
            column_sum(dvalue_bf),
            column_sum(branch_self),
            column_sum(dquery_cross_bf),
            column_sum(dvalue_enc_bf),
            column_sum(branch_cross),
            back_one[2],
            back_two[2],
            back_three[2],
        ]
    )
    grads = (
        grad_attn,
        grad_outs,
        grad_up,
        grad_down,
        grad_gain,
        grad_bias,
        column_sum(grad_pre),
        column_sum(cotangent),
    )
    return (layer_out, grad_layer, grad_encoded, grads)


def per_device(
    layer_in,
    encoded,
    pairing,
    attn_weight,
    out_weight,
    up_weight,
    down_weight,
    norm_gains,
    bias_rows,
    up_bias,
    down_bias,
    out_cotangent,
):
    micro_count = layer_in.shape[0]
    local_rows = layer_in.shape[1]
    all_places = token_places(pairing, local_rows // 2)
    query_places = lax.dynamic_slice_in_dim(
        all_places, lax.axis_index("ctx") * local_rows, local_rows
    )
    outputs_list = []
    grad_in_list = []
    grad_enc_list = []
    totals = None
    for micro_index in range(micro_count):
        weights = (
            lax.all_gather(attn_weight, "fsdp", axis=1, tiled=True),
            lax.all_gather(out_weight, "fsdp", axis=1, tiled=True),
            lax.all_gather(up_weight, "fsdp", axis=0, tiled=True),
            lax.all_gather(down_weight, "fsdp", axis=0, tiled=True),
            lax.all_gather(norm_gains, "fsdp", axis=1, tiled=True),
            lax.all_gather(bias_rows, "fsdp", axis=1, tiled=True),
            lax.all_gather(up_bias, "fsdp", axis=0, tiled=True),
            lax.all_gather(down_bias, "fsdp", axis=0, tiled=True),
        )
        layer_out, grad_layer, grad_encoded, grads = sequence_step(
            layer_in[micro_index],
            encoded[micro_index],
            out_cotangent[micro_index],
            weights,
            query_places,
            all_places,
        )
        outputs_list.append(layer_out)
        grad_in_list.append(grad_layer)
        grad_enc_list.append(grad_encoded)
        if totals is None:
            totals = grads
        else:
            totals = tuple((earlier + later for earlier, later in zip(totals, grads)))
    reduced = (
        lax.psum_scatter(
            totals[0].astype(jnp.bfloat16), "fsdp", scatter_dimension=1, tiled=True
        ).astype(jnp.float32),
        lax.psum_scatter(
            totals[1].astype(jnp.bfloat16), "fsdp", scatter_dimension=1, tiled=True
        ).astype(jnp.float32),
        lax.psum_scatter(
            totals[2].astype(jnp.bfloat16), "fsdp", scatter_dimension=0, tiled=True
        ).astype(jnp.float32),
        lax.psum_scatter(
            totals[3].astype(jnp.bfloat16), "fsdp", scatter_dimension=0, tiled=True
        ).astype(jnp.float32),
        lax.psum_scatter(
            totals[4].astype(jnp.bfloat16), "fsdp", scatter_dimension=1, tiled=True
        ).astype(jnp.float32),
        lax.psum_scatter(
            totals[5].astype(jnp.bfloat16), "fsdp", scatter_dimension=1, tiled=True
        ).astype(jnp.float32),
        lax.psum_scatter(
            totals[6].astype(jnp.bfloat16), "fsdp", scatter_dimension=0, tiled=True
        ).astype(jnp.float32),
        lax.psum_scatter(
            totals[7].astype(jnp.bfloat16), "fsdp", scatter_dimension=0, tiled=True
        ).astype(jnp.float32),
    )
    summed = lax.psum(
        (
            reduced[0],
            reduced[1],
            reduced[2],
            reduced[3],
            reduced[4],
            reduced[5],
            reduced[6],
            reduced[7],
        ),
        "ctx",
    )
    return (
        jnp.stack(outputs_list),
        jnp.stack(grad_in_list),
        jnp.stack(grad_enc_list),
        summed[0],
        summed[1],
        summed[2],
        summed[3],
        summed[4],
        summed[5],
        summed[6],
        summed[7],
    )


def solution(mesh):
    return jax.shard_map(
        per_device,
        mesh=mesh,
        in_specs=(
            P("fsdp", "ctx", None),
            P("fsdp", "ctx", None),
            P(),
            P(None, "fsdp", None),
            P(None, "fsdp", None),
            P("fsdp", None),
            P("fsdp", None),
            P(None, "fsdp"),
            P(None, "fsdp"),
            P("fsdp"),
            P("fsdp"),
            P("fsdp", "ctx", None),
        ),
        out_specs=(
            P("fsdp", "ctx", None),
            P("fsdp", "ctx", None),
            P("fsdp", "ctx", None),
            P(None, "fsdp", None),
            P(None, "fsdp", None),
            P("fsdp", None),
            P("fsdp", None),
            P(None, "fsdp"),
            P(None, "fsdp"),
            P("fsdp"),
            P("fsdp"),
        ),
        check_vma=False,
    )
```

profile of v0, /device:TPU:0, one launch (start us, length us, event | category | flops | bytes accessed | tf_op | source)
XLA Modules:
  0.0 1796.4 jit_solution(9854066395887659069)
XLA Ops:
  8.0 6.3 all-gather
  14.3 5.6 all-gather.1
  21.2 42.0 %all-gather.16.cloned.1.call-done = bf16[6,768,768]{2,1,0:T(8,128)(2,1)} async-done(((bf16[6,192,768]{2,1,0:T(8,128)(2,1)}), bf16[6,768,768]{2,1,0:T(8,128)(2,1)}) %all-gather.16.cloned.1.call-update) | async-done | bytes 7077904 | tf_op jit(solution)/shard_map/all_gather | solution.py:351
  84.4 5.2 all-gather.2
  94.2 15.9 all-gather.20.cloned.1.call-done
  112.3 3.9 fusion.5
  116.2 39.7 %all-gather.34.cloned.1.call-done = bf16[1024,768]{1,0:T(8,128)(2,1)} async-done(((bf16[128,768]{1,0:T(8,128)(2,1)}), bf16[1024,768]{1,0:T(8,128)(2,1)}) %all-gather.34.cloned.1.call-update) | async-done | bytes 1572880 | tf_op jit(solution)/shard_map/all_gather | solution.py:189
  157.7 5.5 exponential_reduce_fusion.3
  166.0 35.4 %all-gather.32.cloned.1.call-done = bf16[1024,768]{1,0:T(8,128)(2,1)} async-done(((bf16[128,768]{1,0:T(8,128)(2,1)}), bf16[1024,768]{1,0:T(8,128)(2,1)}) %all-gather.32.cloned.1.call-update) | async-done | bytes 1572880 | tf_op jit(solution)/shard_map/all_gather | solution.py:190
  203.1 5.7 bitcast_convert_fusion.1
  208.8 16.8 all-gather.22.cloned.1.call-done
  230.6 41.9 %all-gather.18.cloned.1.call-done = bf16[1024,768]{1,0:T(8,128)(2,1)} async-done(((bf16[128,768]{1,0:T(8,128)(2,1)}), bf16[1024,768]{1,0:T(8,128)(2,1)}) %all-gather.18.cloned.1.call-update) | async-done | bytes 1572880 | tf_op jit(solution)/shard_map/all_gather | solution.py:190
  275.2 5.8 bitcast_convert_fusion.3
  285.2 32.6 %all-gather.26.cloned.1.call-done = bf16[1024,768]{1,0:T(8,128)(2,1)} async-done(((bf16[128,768]{1,0:T(8,128)(2,1)}), bf16[1024,768]{1,0:T(8,128)(2,1)}) %all-gather.26.cloned.1.call-update) | async-done | bytes 1572880 | tf_op jit(solution)/shard_map/all_gather | solution.py:202
  317.7 2.6 copy.114
  320.4 5.0 multiply_reduce_fusion.1
  325.4 38.1 %all-gather.36.cloned.1.call-done = bf16[1024,768]{1,0:T(8,128)(2,1)} async-done(((bf16[128,768]{1,0:T(8,128)(2,1)}), bf16[1024,768]{1,0:T(8,128)(2,1)}) %all-gather.36.cloned.1.call-update) | async-done | bytes 1572880 | tf_op jit(solution)/shard_map/all_gather | solution.py:203
  366.1 43.2 %all-gather.24.cloned.1.call-done = bf16[1024,768]{1,0:T(8,128)(2,1)} async-done(((bf16[128,768]{1,0:T(8,128)(2,1)}), bf16[1024,768]{1,0:T(8,128)(2,1)}) %all-gather.24.cloned.1.call-update) | async-done | bytes 1572880 | tf_op jit(solution)/shard_map/all_gather | solution.py:203
  411.9 43.0 %all-gather.38.cloned.1.call-done = bf16[1024,768]{1,0:T(8,128)(2,1)} async-done(((bf16[128,768]{1,0:T(8,128)(2,1)}), bf16[1024,768]{1,0:T(8,128)(2,1)}) %all-gather.38.cloned.1.call-update) | async-done | bytes 1572880 | tf_op jit(solution)/shard_map/all_gather | solution.py:202
  455.0 2.7 copy.120
  457.7 4.2 exponential_reduce_fusion.2
  462.7 3.7 bitcast_convert_fusion.2
  476.4 16.4 all-gather.28.cloned.1.call-done
  492.8 8.7 multiply_convert_fusion.5
  501.5 6.6 multiply_convert_fusion.4
  508.1 23.6 %all-gather.30.cloned.1.call-done = bf16[3072,768]{1,0:T(8,128)(2,1)} async-done(((bf16[768,768]{1,0:T(8,128)(2,1)}), bf16[3072,768]{1,0:T(8,128)(2,1)}) %all-gather.30.cloned.1.call-update) | async-done | bytes 4718608 | tf_op jit(solution)/shard_map/all_gather | solution.py:354
  531.7 5.9 convert_reduce_fusion
  548.6 5.9 fusion.59
  555.3 5.9 fusion.63
  562.5 5.5 multiply_convert_fusion.1
  576.8 2.8 multiply_reduce_fusion.5
  585.4 6.3 fusion.136
  591.7 2.6 convolution_convert_fusion.2
  596.1 6.3 fusion.140
  603.6 5.9 multiply_convert_fusion
  609.5 2.8 convolution_multiply_fusion.2
  613.6 5.8 multiply_convert_fusion.2
  619.5 2.8 convolution_multiply_fusion.3
  622.3 4.3 convolution_multiply_fusion.1
  626.7 3.2 convolution_multiply_fusion
  643.9 4.5 convert_reduce_fusion.11
  649.8 3.2 convert_reduce_fusion.17
  657.5 5.2 fusion.181
  664.4 42.9 %reduce-scatter.29.cloned.1.call-done = f32[128,768]{0,1:T(8,128)} async-done(((f32[1024,768]{0,1:T(8,128)}), f32[128,768]{0,1:T(8,128)}) %reduce-scatter.29.cloned.1.call-update) | async-done | bytes 393232 | tf_op jit(solution)/shard_map/reduce_scatter | solution.py:241
  709.0 76.0 %reduce-scatter.25.cloned.1.call-done = f32[128,768]{0,1:T(8,128)} async-done(((f32[1024,768]{0,1:T(8,128)}), f32[128,768]{0,1:T(8,128)}) %reduce-scatter.25.cloned.1.call-update) | async-done | bytes 393232 | tf_op jit(solution)/shard_map/reduce_scatter | solution.py:272
  786.9 75.7 %reduce-scatter.21.cloned.1.call-done = f32[128,768]{0,1:T(8,128)} async-done(((f32[1024,768]{0,1:T(8,128)}), f32[128,768]{0,1:T(8,128)}) %reduce-scatter.21.cloned.1.call-update) | async-done | bytes 393232 | tf_op jit(solution)/shard_map/reduce_scatter | solution.py:272
  864.3 75.9 %reduce-scatter.23.cloned.1.call-done = f32[128,768]{0,1:T(8,128)} async-done(((f32[1024,768]{0,1:T(8,128)}), f32[128,768]{0,1:T(8,128)}) %reduce-scatter.23.cloned.1.call-update) | async-done | bytes 393232 | tf_op jit(solution)/shard_map/reduce_scatter | solution.py:271
  944.1 74.0 %reduce-scatter.19.cloned.1.call-done = f32[128,768]{0,1:T(8,128)} async-done(((f32[1024,768]{0,1:T(8,128)}), f32[128,768]{0,1:T(8,128)}) %reduce-scatter.19.cloned.1.call-update) | async-done | bytes 393232 | tf_op jit(solution)/shard_map/reduce_scatter | solution.py:271
  1028.9 7.3 add_convert_fusion.2
  1038.8 3.6 add_convert_fusion.1
  1053.3 42.6 %reduce-scatter.27.cloned.1.call-done = f32[128,768]{0,1:T(8,128)} async-done(((f32[1024,768]{0,1:T(8,128)}), f32[128,768]{0,1:T(8,128)}) %reduce-scatter.27.cloned.1.call-update) | async-done | bytes 393232 | tf_op jit(solution)/shard_map/reduce_scatter | solution.py:240
  1095.9 3.1 bitcast_dynamic-update-slice_fusion.3
  1107.1 66.4 %reduce-scatter.31.cloned.1.call-done = f32[128,768]{0,1:T(8,128)} async-done(((f32[1024,768]{0,1:T(8,128)}), f32[128,768]{0,1:T(8,128)}) %reduce-scatter.31.cloned.1.call-update) | async-done | bytes 393232 | tf_op jit(solution)/shard_map/reduce_scatter | solution.py:240
  1173.5 2.9 bitcast_dynamic-update-slice_fusion.1
  1178.3 13.8 add_convert_fusion
  1195.6 11.2 all-reduce.4
  1206.9 3.4 fusion.41
  1210.3 3.2 fusion.42
  1224.1 7.9 reduce-scatter.43.cloned.1.call-done
  1232.9 21.5 %reduce-scatter.45.cloned.1.call-done = bf16[192,9]{1,0:T(8,128)(2,1)} async-done(((bf16[768,9]{1,0:T(8,128)(2,1)}), bf16[192,9]{1,0:T(8,128)(2,1)}) %reduce-scatter.45.cloned.1.call-update) | async-done | bytes 3472
  1255.2 49.5 %reduce-scatter.39.cloned.1.call-done = bf16[192,3072]{1,0:T(8,128)(2,1)} async-done(((bf16[768,3072]{1,0:T(8,128)(2,1)}), bf16[192,3072]{1,0:T(8,128)(2,1)}) %reduce-scatter.39.cloned.1.call-update) | async-done | bytes 1179664 | tf_op jit(solution)/shard_map/reduce_scatter | solution.py:382
  1304.8 50.4 %reduce-scatter.41.cloned.1.call-done = bf16[768,768]{1,0:T(8,128)(2,1)} async-done(((bf16[3072,768]{1,0:T(8,128)(2,1)}), bf16[768,768]{1,0:T(8,128)(2,1)}) %reduce-scatter.41.cloned.1.call-update) | async-done | bytes 1179664 | tf_op jit(solution)/shard_map/reduce_scatter | solution.py:385
  1355.2 66.2 %reduce-scatter.35.cloned.1.call-done = bf16[6,192,768]{2,1,0:T(8,128)(2,1)} async-done(((bf16[6,768,768]{2,1,0:T(8,128)(2,1)}), bf16[6,192,768]{2,1,0:T(8,128)(2,1)}) %reduce-scatter.35.cloned.1.call-update) | async-done | bytes 1769488 | tf_op jit(solution)/shard_map/reduce_scatter | solution.py:376
  1421.4 368.3 %all-reduce.6 = (f32[6,192,768]{2,1,0:T(8,128)}, f32[2,192,768]{2,1,0:T(8,128)}, f32[192,3072]{1,0:T(8,128)}, f32[768,768]{1,0:T(8,128)}, f32[3,192]{1,0:T(4,128...) all-reduce(bf16[6,192,768]{2,1,0:T(8,128)(2,1)} %reduce-scatter.35., ...), channel_id=1, replica_groups=mesh['fsdp'=4,'ctx'=8] {'ctx'}, use_global_device_ids=true, to_apply=%region_41.42 | all-reduce | flops 2362560 | bytes 14177280 | tf_op jit(solution)/shard_map/psum | solution.py:401
  (650 shorter events, 172.8 us)
Async XLA Ops:
  7.2 13.5 copy-start.4
  7.2 56.0 %all-gather.16.cloned.1.call-start = ((), (), s32[]{:S(2)}) async-start(), calls=%async_computation.14 | async-start | bytes 8847360 | tf_op jit(solution)/shard_map/all_gather | solution.py:351
  7.9 102.2 %all-gather.20.cloned.1.call-start = ((), (), s32[]{:S(2)}) async-start(), calls=%async_computation.16 | async-start | bytes 1769472 | tf_op jit(solution)/shard_map/all_gather | solution.py:189
  20.7 71.6 %copy-start.95 = (f32[768]{0:T(1024)}, f32[768]{0:T(1024)S(1)}, u32[]{:S(2)}) copy-start(f32[768]{0:T(1024)S(1)} %get-tuple-element.287) | copy-start | bytes 9220
  20.7 205.0 %copy-start.106 = (f32[768]{0:T(1024)}, f32[768]{0:T(1024)S(1)}, u32[]{:S(2)}) copy-start(f32[768]{0:T(1024)S(1)} %get-tuple-element.284) | copy-start | bytes 9220
  20.7 207.0 %copy-start.102 = (f32[768]{0:T(1024)}, f32[768]{0:T(1024)S(1)}, u32[]{:S(2)}) copy-start(f32[768]{0:T(1024)S(1)} %get-tuple-element.276) | copy-start | bytes 9220
  20.7 207.0 %copy-start.171 = (f32[768]{0:T(1024)}, f32[768]{0:T(1024)S(1)}, u32[]{:S(2)}) copy-start(f32[768]{0:T(1024)S(1)} %get-tuple-element.275) | copy-start | bytes 9220
  20.8 69.6 %copy-start.112 = (f32[128]{0:T(128)}, f32[128]{0:T(128)S(1)}, u32[]{:S(2)}) copy-start(f32[128]{0:T(128)S(1)} %get-tuple-element.432) | copy-start | bytes 1540
  20.9 71.5 %copy-start.117 = (f32[128]{0:T(128)}, f32[128]{0:T(128)S(1)}, u32[]{:S(2)}) copy-start(f32[128]{0:T(128)S(1)} %get-tuple-element.433) | copy-start | bytes 1540
  21.1 46.8 %copy-start.190 = (f32[128]{0:T(128)}, f32[128]{0:T(128)S(1)}, u32[]{:S(2)}) copy-start(f32[128]{0:T(128)S(1)} %get-tuple-element.263) | copy-start | bytes 1540
  21.1 46.8 %copy-start.192 = (f32[128]{0:T(128)}, f32[128]{0:T(128)S(1)}, u32[]{:S(2)}) copy-start(f32[128]{0:T(128)S(1)} %get-tuple-element.262) | copy-start | bytes 1540
  21.1 71.2 %copy-start.135 = (f32[128]{0:T(128)}, f32[128]{0:T(128)S(1)}, u32[]{:S(2)}) copy-start(f32[128]{0:T(128)S(1)} %fusion.145) | copy-start | bytes 1540
  65.5 90.5 %all-gather.34.cloned.1.call-start = ((), (), s32[]{:S(2)}) async-start(), calls=%async_computation.23 | async-start | bytes 1769472 | tf_op jit(solution)/shard_map/all_gather | solution.py:189
  65.6 24.9 %copy-start.140 = (f32[128]{0:T(128)}, f32[128]{0:T(128)S(1)}, u32[]{:S(2)}) copy-start(f32[128]{0:T(128)S(1)} %fusion.148) | copy-start | bytes 1540
  67.9 133.4 %all-gather.32.cloned.1.call-start = ((), (), s32[]{:S(2)}) async-start(), calls=%async_computation.22 | async-start | bytes 1769472 | tf_op jit(solution)/shard_map/all_gather | solution.py:190
  70.4 155.3 %all-gather.22.cloned.1.call-start = ((), (), s32[]{:S(2)}) async-start(), calls=%async_computation.17 | async-start | bytes 2949120 | tf_op jit(solution)/shard_map/all_gather | solution.py:352
  71.0 201.5 %all-gather.18.cloned.1.call-start = ((), (), s32[]{:S(2)}) async-start(), calls=%async_computation.15 | async-start | bytes 1769472 | tf_op jit(solution)/shard_map/all_gather | solution.py:190
  73.4 244.4 %all-gather.26.cloned.1.call-start = ((), (), s32[]{:S(2)}) async-start(), calls=%async_computation.19 | async-start | bytes 1769472 | tf_op jit(solution)/shard_map/all_gather | solution.py:202
  75.7 287.8 %all-gather.36.cloned.1.call-start = ((), (), s32[]{:S(2)}) async-start(), calls=%async_computation.24 | async-start | bytes 1769472 | tf_op jit(solution)/shard_map/all_gather | solution.py:203
  78.1 331.2 %all-gather.24.cloned.1.call-start = ((), (), s32[]{:S(2)}) async-start(), calls=%async_computation.18 | async-start | bytes 1769472 | tf_op jit(solution)/shard_map/all_gather | solution.py:203
  80.4 374.5 %all-gather.38.cloned.1.call-start = ((), (), s32[]{:S(2)}) async-start(), calls=%async_computation.25 | async-start | bytes 1769472 | tf_op jit(solution)/shard_map/all_gather | solution.py:202
  82.8 410.0 %all-gather.28.cloned.1.call-start = ((), (), s32[]{:S(2)}) async-start(), calls=%async_computation.20 | async-start | bytes 5898240 | tf_op jit(solution)/shard_map/all_gather | solution.py:353
  83.5 448.2 %all-gather.30.cloned.1.call-start = ((), (), s32[]{:S(2)}) async-start(), calls=%async_computation.21 | async-start | bytes 5898240 | tf_op jit(solution)/shard_map/all_gather | solution.py:354
  84.1 578.5 %reduce-scatter.33.cloned.1.call-start = ((), (), s32[]{:S(2)}) async-start(), calls=%async_computation.33 | async-start | bytes 3538944 | tf_op jit(solution)/shard_map/reduce_scatter | solution.py:241
  90.4 184.7 %copy-start.48 = (pred[128,1024]{1,0:T(8,128)(4,1)}, pred[128,1024]{1,0:T(8,128)(4,1)S(1)}, u32[]{:S(2)}) copy-start(pred[128,1024]{1,0:T(8,128)(4,1)S(1)} %broadcast_compare_fusion) | copy-start | bytes 393220
  92.3 65.4 %copy-start.82 = (bf16[128,768]{0,1:T(8,128)(2,1)}, bf16[128,768]{0,1:T(8,128)(2,1)S(1)}, u32[]{:S(2)}) copy-start(bf16[128,768]{0,1:T(8,128)(2,1)S(1)} %copy.116) | copy-start | bytes 589828
  94.2 22.0 %copy-start.60 = (bf16[128,768]{0,1:T(8,128)(2,1)}, bf16[128,768]{0,1:T(8,128)(2,1)S(1)}, u32[]{:S(2)}) copy-start(bf16[128,768]{0,1:T(8,128)(2,1)S(1)} %copy.110) | copy-start | bytes 589828
  163.3 111.9 %copy-start.110 = (f32[12,128]{1,0:T(8,128)}, f32[12,128]{1,0:T(8,128)S(1)}, u32[]{:S(2)}) copy-start(f32[12,128]{1,0:T(8,128)S(1)} %log_add_fusion.3) | copy-start | bytes 18436
  165.9 42.9 %copy-start.111 = (f32[12,128]{1,0:T(8,128)}, f32[12,128]{1,0:T(8,128)S(1)}, u32[]{:S(2)}) copy-start(f32[12,128]{1,0:T(8,128)S(1)} %log_add_fusion.1) | copy-start | bytes 18436
  208.8 21.8 %copy-start.86 = (bf16[128,12,64]{0,2,1:T(8,128)(2,1)}, bf16[128,12,64]{0,2,1:T(8,128)(2,1)S(1)}, u32[]{:S(2)}) copy-start(bf16[128,12,64]{0,2,1:T(8,128)(2,1)S(1)} %get-tuple-element.395) | copy-start | bytes 589828
  227.4 47.7 %copy-start.161 = (f32[128]{0:T(128)}, f32[128]{0:T(128)S(1)}, u32[]{:S(2)}) copy-start(f32[128]{0:T(128)S(1)} %broadcast_multiply_fusion.2) | copy-start | bytes 1540
  227.6 47.5 %copy-start.196 = (f32[128]{0:T(128)}, f32[128]{0:T(128)S(1)}, u32[]{:S(2)}) copy-start(f32[128]{0:T(128)S(1)} %multiply_reduce_fusion.11) | copy-start | bytes 1540
  227.6 47.5 %copy-start.179 = (f32[128]{0:T(128)}, f32[128]{0:T(128)S(1)}, u32[]{:S(2)}) copy-start(f32[128]{0:T(128)S(1)} %fusion.149) | copy-start | bytes 1540
  281.5 184.9 %copy-start.27 = (f32[128,768]{1,0:T(8,128)}, f32[128,768]{1,0:T(8,128)S(1)}, u32[]{:S(2)}) copy-start(f32[128,768]{1,0:T(8,128)S(1)} %get-tuple-element.409) | copy-start | bytes 1179652
  281.5 38.9 %copy-start.164 = (f32[128]{0:T(128)}, f32[128]{0:T(128)S(1)}, u32[]{:S(2)}) copy-start(f32[128]{0:T(128)S(1)} %broadcast_multiply_fusion.5) | copy-start | bytes 1540
  281.7 38.7 %copy-start.198 = (f32[128]{0:T(128)}, f32[128]{0:T(128)S(1)}, u32[]{:S(2)}) copy-start(f32[128]{0:T(128)S(1)} %multiply_reduce_fusion.13) | copy-start | bytes 1540
  281.7 38.6 %copy-start.182 = (f32[128]{0:T(128)}, f32[128]{0:T(128)S(1)}, u32[]{:S(2)}) copy-start(f32[128]{0:T(128)S(1)} %fusion.146) | copy-start | bytes 1540
  285.2 40.2 %copy-start.63 = (bf16[128,768]{0,1:T(8,128)(2,1)}, bf16[128,768]{0,1:T(8,128)(2,1)S(1)}, u32[]{:S(2)}) copy-start(bf16[128,768]{0,1:T(8,128)(2,1)S(1)} %copy.113) | copy-start | bytes 589828
  466.8 78.4 %copy-start.10 = (f32[128,768]{1,0:T(8,128)}, f32[128,768]{1,0:T(8,128)S(1)}, u32[]{:S(2)}) copy-start(f32[128,768]{1,0:T(8,128)S(1)} %get-tuple-element.415) | copy-start | bytes 1179652
  474.5 70.7 %copy-start.19 = (f32[128,768]{1,0:T(8,128)}, f32[128,768]{1,0:T(8,128)S(1)}, u32[]{:S(2)}) copy-start(f32[128,768]{1,0:T(8,128)S(1)} %get-tuple-element.404) | copy-start | bytes 1179652
  548.5 13.8 copy-start.53
  554.5 152.8 %reduce-scatter.29.cloned.1.call-start = ((), (), s32[]{:S(2)}) async-start(), calls=%async_computation.31 | async-start | bytes 3538944 | tf_op jit(solution)/shard_map/reduce_scatter | solution.py:241
  561.2 223.8 %reduce-scatter.25.cloned.1.call-start = ((), (), s32[]{:S(2)}) async-start(), calls=%async_computation.29 | async-start | bytes 3538944 | tf_op jit(solution)/shard_map/reduce_scatter | solution.py:272
  562.4 10.0 slice-start
  562.5 9.9 slice-start.1
  591.7 270.9 %reduce-scatter.21.cloned.1.call-start = ((), (), s32[]{:S(2)}) async-start(), calls=%async_computation.27 | async-start | bytes 3538944 | tf_op jit(solution)/shard_map/reduce_scatter | solution.py:272
  602.5 337.8 %reduce-scatter.23.cloned.1.call-start = ((), (), s32[]{:S(2)}) async-start(), calls=%async_computation.28 | async-start | bytes 3538944 | tf_op jit(solution)/shard_map/reduce_scatter | solution.py:271
  612.3 405.8 %reduce-scatter.19.cloned.1.call-start = ((), (), s32[]{:S(2)}) async-start(), calls=%async_computation.26 | async-start | bytes 3538944 | tf_op jit(solution)/shard_map/reduce_scatter | solution.py:271
  622.2 473.7 %reduce-scatter.27.cloned.1.call-start = ((), (), s32[]{:S(2)}) async-start(), calls=%async_computation.30 | async-start | bytes 3538944 | tf_op jit(solution)/shard_map/reduce_scatter | solution.py:240
  626.7 546.8 %reduce-scatter.31.cloned.1.call-start = ((), (), s32[]{:S(2)}) async-start(), calls=%async_computation.32 | async-start | bytes 3538944 | tf_op jit(solution)/shard_map/reduce_scatter | solution.py:240
  629.9 584.4 %reduce-scatter.37.cloned.1.call-start = ((), (), s32[]{:S(2)}) async-start(), calls=%async_computation.35 | async-start | bytes 2949120 | tf_op jit(solution)/shard_map/reduce_scatter | solution.py:379
  634.9 9.0 copy-start.31
  634.9 597.1 %reduce-scatter.43.cloned.1.call-start = ((), (), s32[]{:S(2)}) async-start(), calls=%async_computation.38 | async-start | bytes 245760
  785.0 157.2 %copy-start.44 = (f32[128,768]{0,1:T(8,128)S(1)}, f32[128,768]{0,1:T(8,128)}, u32[]{:S(2)}) copy-start(f32[128,768]{0,1:T(8,128)} %reduce-scatter.25.cloned.1.call-done) | copy-start | bytes 1179652
  942.2 77.9 %copy-start.76 = (f32[128,768]{0,1:T(8,128)S(1)}, f32[128,768]{0,1:T(8,128)}, u32[]{:S(2)}) copy-start(f32[128,768]{0,1:T(8,128)} %reduce-scatter.21.cloned.1.call-done) | copy-start | bytes 1179652
  1024.9 229.4 %reduce-scatter.45.cloned.1.call-start = ((), (), s32[]{:S(2)}) async-start(), calls=%async_computation.39 | async-start | bytes 245760
  1028.8 276.0 %reduce-scatter.39.cloned.1.call-start = ((), (), s32[]{:S(2)}) async-start(), calls=%async_computation.36 | async-start | bytes 5898240 | tf_op jit(solution)/shard_map/reduce_scatter | solution.py:382
  1036.2 319.0 %reduce-scatter.41.cloned.1.call-start = ((), (), s32[]{:S(2)}) async-start(), calls=%async_computation.37 | async-start | bytes 5898240 | tf_op jit(solution)/shard_map/reduce_scatter | solution.py:385
  1042.4 378.9 %reduce-scatter.35.cloned.1.call-start = ((), (), s32[]{:S(2)}) async-start(), calls=%async_computation.34 | async-start | bytes 8847360 | tf_op jit(solution)/shard_map/reduce_scatter | solution.py:376
  1051.2 47.8 %copy-start.43 = (f32[128,768]{0,1:T(8,128)S(1)}, f32[128,768]{0,1:T(8,128)}, u32[]{:S(2)}) copy-start(f32[128,768]{0,1:T(8,128)} %reduce-scatter.29.cloned.1.call-done) | copy-start | bytes 1179652
  1053.3 45.7 %copy-start.71 = (bf16[2,128,768]{2,1,0:T(8,128)(2,1)S(1)}, bf16[2,128,768]{2,1,0:T(8,128)(2,1)}, u32[]{:S(2)}) copy-start(bf16[2,128,768]{2,1,0:T(8,128)(2,1)} %param.13) | copy-start | bytes 1179652
  1105.0 71.4 %copy-start.42 = (f32[128,768]{0,1:T(8,128)S(1)}, f32[128,768]{0,1:T(8,128)}, u32[]{:S(2)}) copy-start(f32[128,768]{0,1:T(8,128)} %reduce-scatter.33.cloned.1.call-done) | copy-start | bytes 1179652
  1107.1 69.3 %copy-start.72 = (bf16[2,128,768]{2,1,0:T(8,128)(2,1)S(1)}, bf16[2,128,768]{2,1,0:T(8,128)(2,1)}, u32[]{:S(2)}) copy-start(bf16[2,128,768]{2,1,0:T(8,128)(2,1)} %param.13) | copy-start | bytes 1179652
  1222.7 198.7 %copy-start.94 = (bf16[2,192,768]{2,1,0:T(8,128)(2,1)S(1)}, bf16[2,192,768]{2,1,0:T(8,128)(2,1)}, u32[]{:S(2)}) copy-start(bf16[2,192,768]{2,1,0:T(8,128)(2,1)} %reduce-scatter.37.cloned.1.call-done) | copy-start | bytes 1769476
  (171 other events, 611.8 us)
Sparse Core Ops, SparseCore 0:
  9.6 53.5 all-gather.15
  65.9 44.2 all-gather.19
  112.9 42.9 all-gather.33
  158.6 42.7 all-gather.31
  202.8 22.8 all-gather.21
  228.3 44.1 all-gather.17
  274.7 42.9 all-gather.25
  320.5 42.9 all-gather.35
  366.3 42.9 all-gather.23
  411.9 42.9 all-gather.37
  456.5 36.2 all-gather.27
  494.2 37.4 all-gather.29
  554.6 75.1 reduce-scatter.32
  633.3 73.9 reduce-scatter.28
  710.7 74.2 reduce-scatter.24
  788.5 74.0 reduce-scatter.20
  866.0 74.1 reduce-scatter.22
  943.7 74.3 reduce-scatter.18
  1021.7 74.1 reduce-scatter.26
  1099.4 74.0 reduce-scatter.30
  1176.6 32.4 reduce-scatter.36
  1212.2 19.7 reduce-scatter.42
  1234.6 19.7 reduce-scatter.44
  1256.9 47.7 reduce-scatter.38
  1307.3 47.8 reduce-scatter.40
  1357.7 63.5 reduce-scatter.34
where the time goes:
time: 1800 us
  waiting for transfers between devices  1040 us (58%)
  blocking collectives  396 us (22%)
  matrix products  238 us (13%)
  local copies, waits for them, and re-layouts  60.5 us (3%)
  other arithmetic  40.4 us (2%)
  between operations  18.8 us (1%)
    psum x1, blocking collectives, per_device(): lax.psum((reduced[0], reduced[1], reduced[2], reduced[3], reduced[4], red...  368 us
    reduce_scatter x2, waiting for transfers between devices, sequence_step(): lax.psum_scatter(dvalue_part, 'ctx', scatter_dimension=0, tiled=True)  152 us
    reduce_scatter x2, waiting for transfers between devices, sequence_step(): lax.psum_scatter(dkey_part, 'ctx', scatter_dimension=0, tiled=True)  150 us
    reduce_scatter x2, waiting for transfers between devices, sequence_step(): lax.psum_scatter(dkey_cross, 'ctx', scatter_dimension=0, tiled=True)  109 us
    all_gather x2, waiting for transfers between devices, sequence_step(): lax.all_gather(local_values, 'ctx', axis=0, tiled=True)  81.3 us
    all_gather x2, waiting for transfers between devices, sequence_step(): lax.all_gather(value_self, 'ctx', axis=0, tiled=True)  77.3 us
    all_gather x2, waiting for transfers between devices, sequence_step(): lax.all_gather(local_keys, 'ctx', axis=0, tiled=True)  75.6 us
    reduce_scatter x1, waiting for transfers between devices, per_device(): lax.psum_scatter(totals[0].astype(jnp.bfloat16), 'fsdp', scatter_dimensio...  66.2 us
  transfers between devices with their start and end apart: 26, of which 24 were waited for; matrix products, arithmetic and copies ran while one was open for 17% of the time, Pallas kernels for 0%

commit v1 on v0

v1 whole, which is shorter than its diff:
```python
import functools
import math

import jax
import jax.numpy as jnp
from jax import lax
from jax.experimental import pallas as pl
from jax.experimental.pallas import tpu as pltpu
from jax.sharding import Mesh
from jax.sharding import PartitionSpec as P

HEADS = 12
HD = 64
PAIR = 2 * HD
SCORE_SCALE = 0.125
MASK_FILL = -1e30
NORM_EPSILON = 1e-05
LINE = 4
SWAP = [(0, 1), (1, 0)]
BF = jnp.bfloat16
F32 = jnp.float32
VMEM_LIMIT = 48 * 1024 * 1024


def dot(left, right):
    return jnp.dot(left, right, preferred_element_type=F32)


def dot_t(left, right):
    return lax.dot_general(left, right, (((1,), (1,)), ((), ())), preferred_element_type=F32)


def t_dot(left, right):
    return lax.dot_general(left, right, (((0,), (0,)), ((), ())), preferred_element_type=F32)


def split_heads(block):
    lane = lax.broadcasted_iota(jnp.int32, block.shape, 1)
    zero = jnp.zeros_like(block)
    return jnp.concatenate([jnp.where(lane < HD, block, zero), jnp.where(lane < HD, zero, block)], axis=0)


def join_heads(columns):
    rows = columns.shape[1] // 2
    return jnp.concatenate([columns[:HD, :rows], columns[HD:, rows:]], axis=0).T


def forward_kernel(masked, pieces, *refs):
    if masked:
        key_place_ref, query_place_ref, refs = refs[0], refs[1], refs[2:]
    query_ref, kv_refs = refs[0], refs[1 : 1 + pieces]
    out_ref, mass_ref, scores_ref = refs[1 + pieces :]
    query = split_heads(query_ref[...] * jnp.asarray(SCORE_SCALE, BF))
    piece = kv_refs[0].shape[1]
    if masked:
        query_place = query_place_ref[...]
        query_place = jnp.concatenate([query_place, query_place], axis=1)
    top = None
    for i in range(pieces):
        scores = dot_t(kv_refs[i][0], query)
        if masked:
            scores = jnp.where(key_place_ref[pl.ds(i * piece, piece), :] <= query_place, scores, MASK_FILL)
        scores_ref[pl.ds(i * piece, piece), :] = scores
        high = jnp.max(scores, axis=0, keepdims=True)
        top = high if top is None else jnp.maximum(top, high)
    mass = jnp.zeros_like(top)
    mixed = None
    for i in range(pieces):
        probs = jnp.exp(scores_ref[pl.ds(i * piece, piece), :] - top)
        mass = mass + jnp.sum(probs, axis=0, keepdims=True)
        part = t_dot(kv_refs[i][1], probs.astype(BF))
        mixed = part if mixed is None else mixed + part
    out_ref[...] = join_heads(mixed * (1.0 / mass)).astype(BF)
    mass_ref[0] = top + jnp.log(mass)


def backward_kernel(masked, pieces, *refs):
    if masked:
        key_place_ref, query_place_ref, refs = refs[0], refs[1], refs[2:]
    query_ref, dout_ref, out_ref, mass_ref = refs[:4]
    kv_refs = refs[4 : 4 + pieces]
    dquery_ref = refs[4 + pieces]
    dkv_refs = refs[5 + pieces :]
    query = split_heads(query_ref[...] * jnp.asarray(SCORE_SCALE, BF))
    dout = dout_ref[...]
    prod = (dout.astype(F32) * out_ref[...].astype(F32)).T
    delta = jnp.concatenate(
        [jnp.sum(prod[:HD], axis=0, keepdims=True), jnp.sum(prod[HD:], axis=0, keepdims=True)], axis=1
    )
    dout = split_heads(dout)
    log_mass = mass_ref[0]
    piece = kv_refs[0].shape[1]
    if masked:
        query_place = query_place_ref[...]
        query_place = jnp.concatenate([query_place, query_place], axis=1)
    dquery = None
    for i in range(pieces):
        keys = kv_refs[i][0]
        scores = dot_t(keys, query)
        if masked:
            scores = jnp.where(key_place_ref[pl.ds(i * piece, piece), :] <= query_place, scores, MASK_FILL)
        probs = jnp.exp(scores - log_mass)
        dprobs = dot_t(kv_refs[i][1], dout)
        dscores = (probs * (dprobs - delta)).astype(BF)
        dkv_refs[i][0] = dot(dscores, query).astype(BF)
        dkv_refs[i][1] = dot(probs.astype(BF), dout).astype(BF)
        part = t_dot(keys, dscores)
        dquery = part if dquery is None else dquery + part
    dquery_ref[...] = (join_heads(dquery) * SCORE_SCALE).astype(BF)


def place_specs(masked, places):
    if not masked:
        return [], []
    key_places, query_places = places
    return [key_places, query_places], [
        pl.BlockSpec(key_places.shape, lambda h: (0, 0)),
        pl.BlockSpec(query_places.shape, lambda h: (0, 0)),
    ]


def attention(query, kv, places):
    masked = places is not None
    rows, width = query.shape
    piece = kv[0].shape[1]
    extra, extra_specs = place_specs(masked, places)
    keys = piece * len(kv)
    return pl.pallas_call(
        functools.partial(forward_kernel, masked, len(kv)),
        grid=(width // PAIR,),
        in_specs=extra_specs
        + [pl.BlockSpec((rows, PAIR), lambda h: (0, h))]
        + [pl.BlockSpec((2, piece, PAIR), lambda h: (0, 0, h))] * len(kv),
        out_specs=[
            pl.BlockSpec((rows, PAIR), lambda h: (0, h)),
            pl.BlockSpec((1, 1, 2 * rows), lambda h: (h, 0, 0)),
        ],
        out_shape=[
            jax.ShapeDtypeStruct((rows, width), BF),
            jax.ShapeDtypeStruct((width // PAIR, 1, 2 * rows), F32),
        ],
        scratch_shapes=[pltpu.VMEM((keys, 2 * rows), F32)],
        compiler_params=pltpu.CompilerParams(vmem_limit_bytes=VMEM_LIMIT),
        cost_estimate=pl.CostEstimate(
            flops=4 * rows * keys * width * 2,
            bytes_accessed=4 * keys * width,
            transcendentals=rows * keys * HEADS,
        ),
    )(*extra, query, *kv)


def attention_back(query, dout, out, mass, kv, places):
    masked = places is not None
    rows, width = query.shape
    piece = kv[0].shape[1]
    extra, extra_specs = place_specs(masked, places)
    keys = piece * len(kv)
    column = pl.BlockSpec((rows, PAIR), lambda h: (0, h))
    pair = pl.BlockSpec((2, piece, PAIR), lambda h: (0, 0, h))
    res = pl.pallas_call(
        functools.partial(backward_kernel, masked, len(kv)),
        grid=(width // PAIR,),
        in_specs=extra_specs
        + [column, column, column, pl.BlockSpec((1, 1, 2 * rows), lambda h: (h, 0, 0))]
        + [pair] * len(kv),
        out_specs=[column] + [pair] * len(kv),
        out_shape=[jax.ShapeDtypeStruct((rows, width), BF)]
        + [jax.ShapeDtypeStruct((2, piece, width), BF)] * len(kv),
        compiler_params=pltpu.CompilerParams(vmem_limit_bytes=VMEM_LIMIT),
        cost_estimate=pl.CostEstimate(
            flops=10 * rows * keys * width * 2,
            bytes_accessed=8 * keys * width,
            transcendentals=rows * keys * HEADS,
        ),
    )(*extra, query, dout, out, mass, *kv)
    return res[0], list(res[1:])


def deal_perms():
    perms = []
    for r in range(LINE):
        perm = []
        for c in range(2):
            for z in range(LINE):
                k = (r - z) % LINE
                perm.append((c * LINE + z, (k % 2) * LINE + 2 * c + k // 2))
        perms.append(perm)
    return perms


DEAL = deal_perms()


def deal(array):
    rows = array.shape[1]
    chunks = array.reshape(LINE, rows // 2, array.shape[2])
    z = lax.axis_index("z")
    got = []
    for r in range(LINE):
        chunk = lax.dynamic_index_in_dim(chunks, lax.rem(r - z + LINE, LINE), keepdims=False)
        got.append(lax.ppermute(chunk, ("core", "z"), DEAL[r]))
    return jnp.concatenate(got, axis=0)


def undeal(array):
    half = array.shape[0] // LINE
    got = []
    for r in range(LINE):
        got.append(
            lax.ppermute(array[r * half : (r + 1) * half], ("core", "z"), [(b, a) for a, b in DEAL[r]])
        )
    both = jnp.stack(got + got)
    mine = lax.dynamic_slice_in_dim(both, lax.axis_index("z"), LINE, axis=0)
    return mine.reshape(2, 2 * half, array.shape[1])


def group_perm(groups, step):
    return [(i, (i + step) % groups) for i in range(groups)]


def spread(own, groups):
    got = []
    for step in range(groups):
        block = own if step == 0 else lax.ppermute(own, ("o", "y"), group_perm(groups, step))
        got.append(block)
    pieces = []
    for block in got:
        pieces.append(block)
        pieces.append(lax.ppermute(block, "core", SWAP))
    return pieces


def collect(pieces, groups):
    sums = []
    for step in range(groups):
        other = lax.ppermute(pieces[2 * step + 1], "core", SWAP)
        sums.append(pieces[2 * step].astype(F32) + other.astype(F32))
    total = sums[0]
    for step in range(1, groups):
        back = [(b, a) for a, b in group_perm(groups, step)]
        total = total + lax.ppermute(sums[step].astype(BF), ("o", "y"), back).astype(F32)
    return total


def assemble(own, other, axis):
    near = lax.ppermute(own, "core", SWAP)
    far = lax.ppermute(other, "core", SWAP)
    fx, core = lax.axis_index("fx"), lax.axis_index("core")
    shape = list(own.shape)
    step = shape[axis]
    shape[axis] *= 4
    full = jnp.zeros(shape, own.dtype)
    for block, place in (
        (own, 2 * fx + core),
        (near, 2 * fx + 1 - core),
        (other, 2 - 2 * fx + core),
        (far, 3 - 2 * fx - core),
    ):
        full = lax.dynamic_update_slice_in_dim(full, block, place * step, axis)
    return full


def after(value, earlier):
    return lax.optimization_barrier((value, earlier))[0]


def reduce_units(units):
    n, rows, width = units.shape
    shard = rows // 4
    fx, core = lax.axis_index("fx"), lax.axis_index("core")
    y = lax.axis_index("y")
    split = units.reshape(n, 2, 2, shard, width)
    theirs = lax.dynamic_index_in_dim(split, 1 - core, axis=2, keepdims=False)
    mine = lax.dynamic_index_in_dim(split, core, axis=2, keepdims=False)
    mine = (mine.astype(F32) + lax.ppermute(theirs, "core", SWAP).astype(F32)).astype(BF)
    theirs = lax.dynamic_index_in_dim(mine, 1 - fx, axis=1, keepdims=False)
    mine = lax.dynamic_index_in_dim(mine, fx, axis=1, keepdims=False)
    mine = (mine.astype(F32) + lax.ppermute(theirs, "fx", SWAP).astype(F32)).astype(BF)
    if lax.axis_size("o") > 1:
        return lax.psum(mine, ("o", "z", "y")).astype(F32)
    lines = mine.reshape(2, LINE, n * shard // (2 * LINE), width)
    theirs = lax.dynamic_index_in_dim(lines, 1 - y, axis=0, keepdims=False)
    mine = lax.dynamic_index_in_dim(lines, y, axis=0, keepdims=False)
    mine = (mine.astype(F32) + lax.ppermute(theirs, "y", SWAP).astype(F32)).astype(BF)
    parts = lax.all_to_all(mine, "z", 0, 0, tiled=True)
    total = jnp.sum(parts.astype(F32), axis=0, keepdims=True).astype(BF)
    line = lax.all_to_all(jnp.broadcast_to(total, (LINE,) + total.shape[1:]), "z", 0, 0, tiled=True)
    other = lax.ppermute(line, "y", SWAP)
    low = jnp.where(y == 0, line, other)
    high = jnp.where(y == 0, other, line)
    return jnp.concatenate([low, high], axis=0).astype(F32).reshape(n, shard, width)


def standard(values):
    center = values - jnp.mean(values, axis=-1, keepdims=True)
    inverse = lax.rsqrt(jnp.mean(center * center, axis=-1, keepdims=True) + NORM_EPSILON)
    return center * inverse, inverse


def norm_back(dnormed, values, gain):
    z, inverse = standard(values)
    a = dnormed * gain
    dvalues = (
        a - jnp.mean(a, axis=-1, keepdims=True) - z * jnp.mean(a * z, axis=-1, keepdims=True)
    ) * inverse
    return dvalues, jnp.sum(dnormed * z, axis=0), jnp.sum(dnormed, axis=0)


def column_sum(values):
    return jnp.sum(values.astype(F32), axis=0)


def gelu_exact(values):
    return jax.nn.gelu(values, approximate=False)


def per_device(
    layer_in,
    encoded,
    pairing,
    attn_weight,
    out_weight,
    up_weight,
    down_weight,
    norm_gains,
    bias_rows,
    up_bias,
    down_bias,
    out_cotangent,
):
    seqs, local_rows, width = layer_in.shape
    outer = lax.axis_size("o")
    groups = outer * 2
    half = local_rows // 2
    shard = attn_weight.shape[1]
    hidden = up_weight.shape[1]
    blocks = hidden // width

    vectors = jnp.concatenate(
        [norm_gains, bias_rows, up_bias.reshape(blocks, shard), down_bias.reshape(1, shard)], axis=0
    )
    x_bf = deal(layer_in)
    vec_other = lax.ppermute(vectors, "fx", SWAP)
    qkv_shard = attn_weight[:3]
    qkv_other = lax.ppermute(after(qkv_shard, vec_other), "fx", SWAP)
    enc_bf = deal(encoded)
    mid_shard = jnp.concatenate([attn_weight[3:], out_weight], axis=0)
    mid_other = lax.ppermute(after(mid_shard, qkv_other), "fx", SWAP)
    up_other = lax.ppermute(after(up_weight, mid_other), "fx", SWAP)
    down_other = lax.ppermute(after(down_weight, up_other), "fx", SWAP)
    cot = deal(out_cotangent)

    vec = assemble(vectors[None], vec_other[None], 0).astype(F32)
    flat = vec[:, : 3 + 9].transpose(1, 0, 2).reshape(12, width)
    gain, bias = flat[:3], flat[3:]
    up_b = vec[:, 12 : 12 + blocks].reshape(1, hidden)
    down_b = vec[:, 12 + blocks].reshape(1, width)

    z, y, o, core = (lax.axis_index(a) for a in ("z", "y", "o", "core"))
    group = o * 2 + y
    spots = []
    for step in range(groups):
        source = lax.rem(group - step + groups, groups)
        for flip in range(2):
            c = core if flip == 0 else 1 - core
            k = 2 * lax.rem(z, 2) + c
            for r in range(LINE):
                line = lax.rem(r - k + LINE, LINE)
                spots.append((((source // 2) * LINE + line) * 2 + lax.rem(source, 2)) * 2 + c)
    spans = jnp.take(pairing.reshape(-1), jnp.stack(spots), axis=0)
    key_places = (spans[:, None] * half + jnp.arange(half, dtype=jnp.int32)[None, :]).reshape(-1, 1)
    query_places = key_places[: LINE * half].reshape(1, -1)
    places = (key_places, query_places)

    x = x_bf.astype(F32)
    n1 = (standard(x)[0] * gain[0] + bias[6]).astype(BF)
    w_qkv = assemble(qkv_shard, qkv_other, 1)
    key = dot(n1, w_qkv[1]).astype(BF)
    value = (dot(n1, w_qkv[2]) + bias[1]).astype(BF)
    kv_self = spread(jnp.stack([key, value]), groups)
    query = (dot(n1, w_qkv[0]) + bias[0]).astype(BF)

    w_mid = assemble(mid_shard, mid_other, 1)
    ckey = dot(enc_bf, w_mid[1]).astype(BF)
    cvalue = (dot(enc_bf, w_mid[2]) + bias[4]).astype(BF)
    kv_cross = spread(jnp.stack([ckey, cvalue]), groups)

    mixed, mass = attention(query, kv_self, places)
    r1 = x + dot(mixed, w_mid[3]) + bias[2]
    n2 = (standard(r1)[0] * gain[1] + bias[7]).astype(BF)
    cquery = (dot(n2, w_mid[0]) + bias[3]).astype(BF)
    cmixed, cmass = attention(cquery, kv_cross, None)
    r2 = r1 + dot(cmixed, w_mid[4]) + bias[5]
    n3 = (standard(r2)[0] * gain[2] + bias[8]).astype(BF)

    w_up = assemble(up_weight, up_other, 0)
    w_down = assemble(down_weight, down_other, 0)
    pre = dot(n3, w_up) + up_b
    act, gelu_back = jax.vjp(gelu_exact, pre)
    act = act.astype(BF)
    layer_out = undeal((r2 + dot(act, w_down) + down_b).astype(BF))
    dact = dot_t(cot, w_down)
    dpre = gelu_back(dact)[0].astype(BF)
    g_down = t_dot(act, cot).astype(BF)
    g_up = [t_dot(n3, dpre[:, b * width : (b + 1) * width]).astype(BF) for b in range(blocks)]
    g_down = g_down.reshape(4, blocks, shard, width).transpose(1, 0, 2, 3).reshape(blocks, width, width)
    ffn = reduce_units(jnp.concatenate([jnp.stack(g_up), g_down], axis=0))
    dn3 = dot_t(dpre, w_up)
    back3, dgain3, dshift3 = norm_back(dn3, r2, gain[2])
    dr2 = cot.astype(F32) + back3

    gc = dr2.astype(BF)
    doc = dot_t(gc, w_mid[4]).astype(BF)
    dcq, dckv = attention_back(cquery, doc, cmixed, cmass, kv_cross, None)
    dckv = collect(dckv, groups).astype(BF)
    dn2 = dot_t(dcq, w_mid[0])
    back2, dgain2, dshift2 = norm_back(dn2, r1, gain[1])
    dr1 = dr2 + back2
    gs = dr1.astype(BF)
    dos = dot_t(gs, w_mid[3]).astype(BF)
    dq, dkv = attention_back(query, dos, mixed, mass, kv_self, places)
    grad_encoded = undeal((dot_t(dckv[0], w_mid[1]) + dot_t(dckv[1], w_mid[2])).astype(BF))
    cross = reduce_units(
        jnp.stack(
            [
                t_dot(n2, dcq).astype(BF),
                t_dot(enc_bf, dckv[0]).astype(BF),
                t_dot(enc_bf, dckv[1]).astype(BF),
                t_dot(cmixed, gc).astype(BF),
            ]
        )
    )
    dkv = collect(dkv, groups).astype(BF)
    own = reduce_units(
        jnp.stack(
            [
                t_dot(n1, dq).astype(BF),
                t_dot(n1, dkv[0]).astype(BF),
                t_dot(n1, dkv[1]).astype(BF),
                t_dot(mixed, gs).astype(BF),
            ]
        )
    )
    dn1 = dot_t(dq, w_qkv[0]) + dot_t(dkv[0], w_qkv[1]) + dot_t(dkv[1], w_qkv[2])
    back1, dgain1, dshift1 = norm_back(dn1, x, gain[0])
    grad_layer = undeal((dr1 + back1).astype(BF))

    rows = jnp.concatenate(
        [
            jnp.stack(
                [
                    dgain1,
                    dgain2,
                    dgain3,
                    column_sum(dq),
                    column_sum(dkv[1]),
                    column_sum(gs),
                    column_sum(dcq),
                    column_sum(dckv[1]),
                    column_sum(gc),
                    dshift1,
                    dshift2,
                    dshift3,
                ]
            ),
            column_sum(dpre).reshape(blocks, width),
            column_sum(cot).reshape(1, width),
        ],
        axis=0,
    )
    rows = lax.psum(rows, ("fx", "core", "o", "z", "y"))
    me = 2 * lax.axis_index("fx") + core
    by_shard = rows.reshape(rows.shape[0], 4, shard)
    mine = lax.dynamic_index_in_dim(by_shard, me, axis=1, keepdims=False)
    grad_up_bias = lax.dynamic_index_in_dim(
        rows[12 : 12 + blocks].reshape(4, hidden // 4), me, axis=0, keepdims=False
    )
    return (
        layer_out,
        grad_layer.astype(F32),
        grad_encoded.astype(F32),
        jnp.concatenate([own[:3], cross[:3]], axis=0),
        jnp.concatenate([own[3:], cross[3:]], axis=0),
        jnp.concatenate([ffn[b] for b in range(blocks)], axis=1),
        ffn[blocks:].reshape(blocks * shard, width),
        mine[:3],
        mine[3:12],
        grad_up_bias,
        mine[12 + blocks],
    )


def solution(mesh):
    ctx = mesh.shape["ctx"]
    grid = Mesh(mesh.devices.reshape(2, 2, ctx // (2 * LINE), LINE, 2), ("fx", "core", "o", "z", "y"))
    fsdp = ("fx", "core")
    rows = P(fsdp, ("o", "z", "y"), None)
    weights = (
        P(None, fsdp, None),
        P(None, fsdp, None),
        P(fsdp, None),
        P(fsdp, None),
        P(None, fsdp),
        P(None, fsdp),
        P(fsdp),
        P(fsdp),
    )
    return jax.shard_map(
        per_device,
        mesh=grid,
        in_specs=(rows, rows, P()) + weights + (rows,),
        out_specs=(rows, rows, rows) + weights,
        check_vma=False,
    )
```

time: 1800 us -> 667 us (0.37)
  waiting for transfers between devices: 1040 us -> 166 us
  blocking collectives: 396 us -> 124 us
  matrix products: 238 us -> 70.1 us
  starting transfers between devices: 1.64 us -> 114 us
  Pallas kernels: 0 us -> 42.1 us
  local copies, waits for them, and re-layouts: 60.5 us -> 98.2 us
    reduce_scatter x12 -> x0, waiting for transfers between devices: 620 us -> none  [the longest x2 152 us: sequence_step(): lax.psum_scatter(dvalue_part, 'ctx', scatter_dimension=0, tiled=True)]
    all_gather x12 -> x0, waiting for transfers between devices: 389 us -> none  [the longest x2 81.3 us: sequence_step(): lax.all_gather(local_values, 'ctx', axis=0, tiled=True)]
    psum x1, blocking collectives: 368 us -> 124 us  [per_device(): rows = lax.psum(rows, ('fx', 'core', 'o', 'z', 'y'))]
    dot_general x84 -> x33, matrix products: 238 us -> 70.1 us  [the longest x10 32.9 us: dot_t(): lax.dot_general(left, right, (((1,), (1,)), ((), ())), preferred_element_...]
    ppermute x0 -> x63, waiting for transfers between devices: none -> 128 us  [the longest x3 31.8 us: reduce_units(): other = lax.ppermute(line, 'y', SWAP)]
    ppermute x0 -> x63, starting transfers between devices: none -> 90.8 us  [the longest x12 31.4 us: undeal(): lax.ppermute(array[r * half:(r + 1) * half], ('core', 'z'), [(b, a) for a...]
    pallas_call x0 -> x4, Pallas kernels: none -> 42.1 us  [the longest x2 26.2 us: attention_back(): pl.pallas_call(functools.partial(backward_kernel, masked, len(kv)), grid=...]
    all_to_all x0 -> x6, waiting for transfers between devices: none -> 38.5 us  [the longest x3 20.7 us: reduce_units(): parts = lax.all_to_all(mine, 'z', 0, 0, tiled=True)]
  transfers between devices with their start and end apart: 26 -> 69, of which waited for: 24 -> 19; matrix products, arithmetic and copies ran while one was open for 17% -> 22% of each run, Pallas kernels for 0% -> 4%
where the time goes in v1:
time: 667 us; the launch traced here: 657 us
  waiting for transfers between devices  166 us (25%)
  blocking collectives  124 us (19%)
  starting transfers between devices  114 us (17%)
  local copies, waits for them, and re-layouts  98.2 us (15%)
  matrix products  70.1 us (11%)
  Pallas kernels  42.1 us (6%)
  other arithmetic  40.5 us (6%)
    psum x1, blocking collectives, per_device(): rows = lax.psum(rows, ('fx', 'core', 'o', 'z', 'y'))  124 us
    unnamed x184, local copies, waits for them, and re-layouts  35.7 us
    dot_general x10, matrix products, dot_t(): lax.dot_general(left, right, (((1,), (1,)), ((), ())), preferred_element_...  32.9 us
    ppermute x3, waiting for transfers between devices, reduce_units(): other = lax.ppermute(line, 'y', SWAP)  31.8 us
    ppermute x12, starting transfers between devices, undeal(): lax.ppermute(array[r * half:(r + 1) * half], ('core', 'z'), [(b, a) for a...  31.4 us
    ppermute x12, starting transfers between devices, deal(): got.append(lax.ppermute(chunk, ('core', 'z'), DEAL[r]))  28.4 us
    ppermute x2, waiting for transfers between devices, collect(): lax.ppermute(sums[step].astype(BF), ('o', 'y'), back).astype(F32)  28.4 us
    pallas_call x2, Pallas kernels, attention_back(): pl.pallas_call(functools.partial(backward_kernel, masked, len(kv)), grid=...  26.2 us
  transfers between devices with their start and end apart: 69, of which 19 were waited for; matrix products, arithmetic and copies ran while one was open for 22% of the time, Pallas kernels for 4%

profile of v1, /device:TPU:0, one launch (start us, length us, event | category | flops | bytes accessed | tf_op | source)
XLA Modules:
  0.0 657.4 jit_solution(1632315139455275605)
XLA Ops:
  3.5 2.9 collective-permute-start.5
  9.8 6.3 collective-permute-start.3
  16.1 2.0 broadcast_in_dim.25
  23.2 2.7 broadcast_in_dim.28
  25.9 2.7 constant_dynamic-update-slice_fusion.16
  28.6 2.9 broadcast_in_dim.26
  36.4 2.1 collective-permute-start.16
  42.4 3.3 collective-permute-start.1
  51.1 3.3 collective-permute-start.17
  54.4 2.6 collective-permute-done.8
  57.5 2.6 collective-permute-start.36
  61.1 2.3 constant_dynamic-update-slice_fusion.26
  64.8 2.0 collective-permute-start.35
  68.7 3.5 collective-permute-start.23
  75.2 2.8 collective-permute-done.34
  81.5 16.4 %collective-permute-done.14 = bf16[5,192,768]{2,1,0:T(8,128)(2,1)S(1)} collective-permute-done((bf16[5,192,768]{2,1,0:T(8,128)(2,1)}, bf16[5,192,768]{2,1,0:T(8,128)(2,1)S(1)}, u32[]{:S(2)}, u32[]{:S(2)}) %collective-permute-start.14) | collective-permute-done | bytes 1474592 | tf_op jit(solution)/shard_map/ppermute | solution.py:348
  105.5 8.2 %shard_map.203 = (bf16[256,768]{1,0:T(8,128)(2,1)S(1)}, f32[6,1,512]{2,1,0:T(1,128)S(1)}) custom-call(s32[1024,1]{1,0:T(8,128)S(1)} %add.768.refs_0_, s32[1,256]{1,0:T(1,128)S(1)} %reshape.1180.refs_1_, bf16[256,768]{1,0:T(8,128)(2,1)S(1)} %fusion.18.refs_2_, bf16[2,256,768]{2,1,0:T(8,128)(2,1)S(1)} %pad_maximum_fusion.7.refs_3_.refs_6_, ...), custom_call_target="tpu_custom_call" | custom-call | flops 1610612736 | bytes 3145728 | tf_op jit(solution)/shard_map/pallas_call | solution.py:128
  113.8 12.5 %collective-permute-done.24 = bf16[192,3072]{1,0:T(8,128)(2,1)S(1)} collective-permute-done((bf16[192,3072]{1,0:T(8,128)(2,1)S(1)}, bf16[192,3072]{1,0:T(8,128)(2,1)S(1)}, u32[]{:S(2)}, u32[]{:S(2)}) %collective-permute-start.24) | collective-permute-done | bytes 1179680 | tf_op jit(solution)/shard_map/ppermute | solution.py:349
  127.1 2.6 constant_dynamic-update-slice_fusion.21
  137.2 16.1 %collective-permute-done.21.refs_3_.refs_6_ = bf16[2,256,768]{2,1,0:T(8,128)(2,1)S(1)} collective-permute-done((bf16[2,256,768]{2,1,0:T(8,128)(2,1)S(1)}, bf16[2,256,768]{2,1,0:T(8,128)(2,1)S(1)}, u32[]{:S(2)}, u32[]{:S(2)}) %collective-permute-start.21) | collective-permute-done | bytes 786464 | tf_op jit(solution)/shard_map/ppermute | solution.py:224
  153.4 2.1 fusion.20.refs_0_
  157.1 7.7 %shard_map.204 = (bf16[256,768]{1,0:T(8,128)(2,1)S(1)}, f32[6,1,512]{2,1,0:T(1,128)S(1)}) custom-call(bf16[256,768]{1,0:T(8,128)(2,1)S(1)} %fusion.20.refs_0_, bf16[2,256,768]{2,1,0:T(8,128)(2,1)S(1)} %pad_maximum_fusion.8.refs_1_.refs_4_, bf16[2,256,768]{2,1,0:T(8,128)(2,1)S(1)} %collective-permute-done.20.refs_2_.refs_5_, ...), custom_call_target="tpu_custom_call" | custom-call | flops 1610612736 | bytes 3145728 | tf_op jit(solution)/shard_map/pallas_call | solution.py:128
  169.7 11.5 %convert_reduce_fusion = (f32[3072]{0:T(1024)S(1)}, bf16[256,3072]{1,0:T(8,128)(2,1)S(1)}, f32[256,3072]{1,0:T(8,128)}) fusion(f32[256,3072]{1,0:T(8,128)S(1)} %convolution_add_fusion, bf16[256,768]{1,0:T(8,128)(2,1)S(1)} %constant_dynamic-update-slice_fusion.4, bf16[3072,768]{1,0:T(8,128)(2,1)} %constant_dynamic-update-slice_fusion.13), kind=kOutput, calls=%fused_computation.17 | convolution fusion | flops 1266152448 | bytes 12988416 | tf_op jit(solution)/shard_map/dot_general | solution.py:30
  181.2 2.2 multiply_reduce_fusion
  187.1 13.0 %shard_map.205 = (bf16[256,768]{1,0:T(8,128)(2,1)S(1)}, bf16[2,256,768]{2,1,0:T(8,128)(2,1)S(1)}, bf16[2,256,768]{2,1,0:T(8,128)(2,1)S(1)}, bf16[2,256,768]{2,1,0:T(8,128)(2,1)S(1)}, bf16[2,256,768]{2,1,0:T(8,128)(2,1)S(1)}) custom-call(bf16[256,768]{1,0:T(8,128)(2,1)S(1)} %fusion.20.refs_0_, bf16[256,768]{1,0:T(8,128)(2,1)S(1)} %convolution_convert_fusion.14.refs_1_, ...), custom_call_target="tpu_custom_call" | custom-call | flops 4026531840 | bytes 6291456 | tf_op jit(solution)/shard_map/pallas_call | solution.py:160
  200.3 3.1 multiply_reduce_fusion.1
  203.7 2.8 convolution_convert_fusion.13.refs_3_
  215.3 3.6 convolution_convert_fusion
  218.9 4.5 fusion.17
  225.9 3.9 collective-permute-start.32
  229.7 2.3 collective-permute-start.31
  239.0 13.2 %shard_map.206 = (bf16[256,768]{1,0:T(8,128)(2,1)S(1)}, bf16[2,256,768]{2,1,0:T(8,128)(2,1)S(1)}, bf16[2,256,768]{2,1,0:T(8,128)(2,1)S(1)}, bf16[2,256,768]{2,1,0:T(8,128)(2,1)S(1)}, bf16[2,256,768]{2,1,0:T(8,128)(2,1)S(1)}) custom-call(s32[1024,1]{1,0:T(8,128)S(1)} %add.768.refs_0_, s32[1,256]{1,0:T(1,128)S(1)} %reshape.1180.refs_1_, ...), custom_call_target="tpu_custom_call" | custom-call | flops 4026531840 | bytes 6291456 | tf_op jit(solution)/shard_map/pallas_call | solution.py:160
  258.0 2.5 dynamic-slice_bitcast_fusion
  269.7 14.7 %collective-permute-done.39 = bf16[2,256,768]{2,1,0:T(8,128)(2,1)S(1)} collective-permute-done((bf16[2,256,768]{2,1,0:T(8,128)(2,1)S(1)}, bf16[2,256,768]{2,1,0:T(8,128)(2,1)S(1)}, u32[]{:S(2)}, u32[]{:S(2)}) %collective-permute-start.39) | collective-permute-done | bytes 786464 | tf_op jit(solution)/shard_map/ppermute | solution.py:241
  287.1 13.7 %collective-permute-done.46 = bf16[2,256,768]{2,1,0:T(8,128)(2,1)S(1)} collective-permute-done((bf16[2,256,768]{2,1,0:T(8,128)(2,1)S(1)}, bf16[2,256,768]{2,1,0:T(8,128)(2,1)S(1)}, u32[]{:S(2)}, u32[]{:S(2)}) %collective-permute-start.46) | collective-permute-done | bytes 786464 | tf_op jit(solution)/shard_map/ppermute | solution.py:241
  311.2 3.4 fusion.47
  320.1 3.8 fusion
  323.8 2.2 copy-done.16
  329.1 123.5 %psum.7 = f32[17,768]{1,0:T(8,128)S(1)} all-reduce(f32[17,768]{1,0:T(8,128)S(1)} %concatenate.97), channel_id=1, replica_groups=mesh['fx'=2,'core'=2,'o'=1,'z'=4,'y'=2] {'fx','core','o','z','y'}, use_global_device_ids=true, to_apply=%region_29.30 | all-reduce | flops 13056 | bytes 104448 | tf_op jit(solution)/shard_map/psum | solution.py:471
  454.8 2.3 collective-permute-start.53
  457.1 2.7 fusion.33
  462.5 8.9 %collective-permute-done.53 = bf16[4,96,768]{2,1,0:T(8,128)(2,1)S(1)} collective-permute-done((bf16[4,96,768]{2,1,0:T(8,128)(2,1)S(1)}, bf16[4,96,768]{2,1,0:T(8,128)(2,1)S(1)}, u32[]{:S(2)}, u32[]{:S(2)}) %collective-permute-start.53) | collective-permute-done | bytes 589856 | tf_op jit(solution)/shard_map/ppermute | solution.py:284
  472.3 3.5 all-to-all-start
  478.6 5.7 collective-permute-start.50
  486.3 2.1 collective-permute-start.48
  489.0 2.1 collective-permute-start.47
  491.1 2.0 fusion.28
  494.0 4.2 all-to-all-start.2
  498.3 2.9 fusion.1
  507.3 6.9 %all-to-all-done.2 = bf16[4,96,768]{2,1,0:T(8,128)(2,1)} async-done(((bf16[4,96,768]{2,1,0:T(8,128)(2,1)}), bf16[4,96,768]{2,1,0:T(8,128)(2,1)}, u32[]{:S(2)}, u32[]{:S(2)}) %all-to-all-start.2) | async-done | bytes 589856 | tf_op jit(solution)/shard_map/all_to_all | solution.py:285
  516.0 4.2 all-to-all-start.1
  523.6 6.8 %collective-permute-done.61 = bf16[4,192,768]{2,1,0:T(8,128)(2,1)} collective-permute-done((bf16[4,192,768]{2,1,0:T(8,128)(2,1)}, bf16[4,192,768]{2,1,0:T(8,128)(2,1)}, u32[]{:S(2)}, u32[]{:S(2)}) %collective-permute-start.61) | collective-permute-done | bytes 1179680 | tf_op jit(solution)/shard_map/ppermute | solution.py:284
  530.5 5.4 collective-permute-start.43
  535.8 2.6 fusion.10
  540.3 3.9 all-to-all-start.4
  545.8 2.0 collective-permute-start.41
  561.3 12.9 %all-to-all-done.4 = bf16[4,192,768]{2,1,0:T(8,128)(2,1)S(1)} async-done(((bf16[4,192,768]{2,1,0:T(8,128)(2,1)}), bf16[4,192,768]{2,1,0:T(8,128)(2,1)S(1)}, u32[]{:S(2)}, u32[]{:S(2)}) %all-to-all-start.4) | async-done | bytes 1179680 | tf_op jit(solution)/shard_map/all_to_all | solution.py:285
  575.0 3.8 all-to-all-start.3
  581.7 11.4 %all-to-all-done.3 = bf16[4,96,768]{2,1,0:T(8,128)(2,1)S(1)} async-done(((bf16[4,96,768]{2,1,0:T(8,128)(2,1)}), bf16[4,96,768]{2,1,0:T(8,128)(2,1)S(1)}, u32[]{:S(2)}, u32[]{:S(2)}) %all-to-all-start.3) | async-done | bytes 589856 | tf_op jit(solution)/shard_map/all_to_all | solution.py:287
  594.1 3.5 all-to-all-start.5
  606.2 11.6 %collective-permute-done.54 = bf16[4,96,768]{2,1,0:T(8,128)(2,1)S(1)} collective-permute-done((bf16[4,96,768]{2,1,0:T(8,128)(2,1)}, bf16[4,96,768]{2,1,0:T(8,128)(2,1)S(1)}, u32[]{:S(2)}, u32[]{:S(2)}) %collective-permute-start.54) | collective-permute-done | bytes 589856 | tf_op jit(solution)/shard_map/ppermute | solution.py:288
  618.9 6.3 all-to-all-done.5
  632.8 2.2 pad_maximum_fusion.2
  635.0 18.3 %collective-permute-done.62 = bf16[4,192,768]{2,1,0:T(8,128)(2,1)S(1)} collective-permute-done((bf16[4,192,768]{2,1,0:T(8,128)(2,1)S(1)}, bf16[4,192,768]{2,1,0:T(8,128)(2,1)S(1)}, u32[]{:S(2)}, u32[]{:S(2)}) %collective-permute-start.62) | collective-permute-done | bytes 1179680 | tf_op jit(solution)/shard_map/ppermute | solution.py:288
  (465 shorter events, 183.0 us)
Async XLA Ops:
  3.5 31.1 %collective-permute-start.5 = (bf16[17,192]{1,0:T(8,128)(2,1)}, bf16[17,192]{1,0:T(8,128)(2,1)S(1)}, u32[]{:S(2)}, u32[]{:S(2)}) collective-permute-start(bf16[17,192]{1,0:T(8,128)(2,1)} %get-tuple-element.79), channel_id=1, source_target_pairs={{0,16},{16,0},{1,17},{17,1},{2,18},{18,2},{3,19},{19,3},{4,20},{20... | collective-permute-start | bytes 19592 | tf_op jit(solution)/shard_map/ppermute | solution.py:343
  6.5 28.6 %collective-permute-start.4 = (bf16[1,17,192]{2,1,0:T(8,128)(2,1)}, bf16[1,17,192]{2,1,0:T(8,128)(2,1)}, u32[]{:S(2)}, u32[]{:S(2)}) collective-permute-start(bf16[1,17,192]{2,1,0:T(8,128)(2,1)} %bitcast.38), channel_id=1, source_target_pairs={{0,8},{8,0},{1,9},{9,1},{2,10},{10,2},{3,11},{11,3},{4,12},{12,4},... | collective-permute-start | bytes 19592 | tf_op jit(solution)/shard_map/ppermute | solution.py:246
  8.3 32.2 %collective-permute-start = (bf16[64,768]{1,0:T(8,128)(2,1)}, bf16[64,768]{1,0:T(8,128)(2,1)S(1)}, u32[]{:S(2)}, u32[]{:S(2)}) collective-permute-start(bf16[64,768]{1,0:T(8,128)(2,1)} %get-tuple-element.116), channel_id=1, source_target_pairs={{0,0},{2,10},{4,2},{6,8},{8,4},{10,14},{12,6},{14,12},{1,1},{3,11}... | collective-permute-start | bytes 294920 | tf_op jit(solution)/shard_map/ppermute | solution.py:201
  9.8 36.8 %collective-permute-start.3 = (bf16[64,768]{1,0:T(8,128)(2,1)}, bf16[64,768]{1,0:T(8,128)(2,1)S(1)}, u32[]{:S(2)}, u32[]{:S(2)}) collective-permute-start(bf16[64,768]{1,0:T(8,128)(2,1)} %get-tuple-element.117), channel_id=1, source_target_pairs={{0,10},{2,2},{4,8},{6,0},{8,14},{10,6},{12,12},{14,4},{1,11},{3,3}... | collective-permute-start | bytes 294920 | tf_op jit(solution)/shard_map/ppermute | solution.py:201
  19.5 38.0 %collective-permute-start.7 = (bf16[3,192,768]{2,1,0:T(8,128)(2,1)}, bf16[3,192,768]{2,1,0:T(8,128)(2,1)S(1)}, u32[]{:S(2)}, u32[]{:S(2)}) collective-permute-start(bf16[3,192,768]{2,1,0:T(8,128)(2,1)} %get-tuple-element.29), channel_id=1, source_target_pairs={{0,8},{8,0},{1,9},{9,1},{2,10},{10,2},{3,11},{11,3},{4,12},{12,4},... | collective-permute-start | bytes 2654216 | tf_op jit(solution)/shard_map/ppermute | solution.py:246
  35.1 22.0 %collective-permute-start.8 = (bf16[3,192,768]{2,1,0:T(8,128)(2,1)}, bf16[3,192,768]{2,1,0:T(8,128)(2,1)}, u32[]{:S(2)}, u32[]{:S(2)}) collective-permute-start(bf16[3,192,768]{2,1,0:T(8,128)(2,1)} %get-tuple-element.29), channel_id=1, source_target_pairs={{0,16},{16,0},{1,17},{17,1},{2,18},{18,2},{3,19},{19,3},{4,20},{20... | collective-permute-start | bytes 2654216 | tf_op jit(solution)/shard_map/ppermute | solution.py:345
  40.4 8.8 %collective-permute-start.2 = (bf16[64,768]{1,0:T(8,128)(2,1)}, bf16[64,768]{1,0:T(8,128)(2,1)S(1)}, u32[]{:S(2)}, u32[]{:S(2)}) collective-permute-start(bf16[64,768]{1,0:T(8,128)(2,1)} %get-tuple-element.118), channel_id=1, source_target_pairs={{0,2},{2,8},{4,0},{6,10},{8,6},{10,12},{12,4},{14,14},{1,3},{3,9},... | collective-permute-start | bytes 294920 | tf_op jit(solution)/shard_map/ppermute | solution.py:201
  42.4 8.7 %collective-permute-start.1 = (bf16[64,768]{1,0:T(8,128)(2,1)S(1)}, bf16[64,768]{1,0:T(8,128)(2,1)S(1)}, u32[]{:S(2)}, u32[]{:S(2)}) collective-permute-start(bf16[64,768]{1,0:T(8,128)(2,1)S(1)} %copy-done.58), channel_id=1, source_target_pairs={{0,8},{2,0},{4,10},{6,2},{8,12},{10,4},{12,14},{14,6},{1,9},{3,1},... | collective-permute-start | bytes 294920 | tf_op jit(solution)/shard_map/ppermute | solution.py:201
  46.6 18.2 %collective-permute-start.19 = (bf16[64,768]{1,0:T(8,128)(2,1)}, bf16[64,768]{1,0:T(8,128)(2,1)S(1)}, u32[]{:S(2)}, u32[]{:S(2)}) collective-permute-start(bf16[64,768]{1,0:T(8,128)(2,1)} %get-tuple-element.112), channel_id=1, source_target_pairs={{0,10},{2,2},{4,8},{6,0},{8,14},{10,6},{12,12},{14,4},{1,11},{3,3}... | collective-permute-start | bytes 294920 | tf_op jit(solution)/shard_map/ppermute | solution.py:201
  49.2 19.4 %collective-permute-start.18 = (bf16[64,768]{1,0:T(8,128)(2,1)}, bf16[64,768]{1,0:T(8,128)(2,1)S(1)}, u32[]{:S(2)}, u32[]{:S(2)}) collective-permute-start(bf16[64,768]{1,0:T(8,128)(2,1)} %get-tuple-element.113), channel_id=1, source_target_pairs={{0,2},{2,8},{4,0},{6,10},{8,6},{10,12},{12,4},{14,14},{1,3},{3,9},... | collective-permute-start | bytes 294920 | tf_op jit(solution)/shard_map/ppermute | solution.py:201
  51.1 21.0 %collective-permute-start.17 = (bf16[64,768]{1,0:T(8,128)(2,1)}, bf16[64,768]{1,0:T(8,128)(2,1)S(1)}, u32[]{:S(2)}, u32[]{:S(2)}) collective-permute-start(bf16[64,768]{1,0:T(8,128)(2,1)} %get-tuple-element.114), channel_id=1, source_target_pairs={{0,8},{2,0},{4,10},{6,2},{8,12},{10,4},{12,14},{14,6},{1,9},{3,1},... | collective-permute-start | bytes 294920 | tf_op jit(solution)/shard_map/ppermute | solution.py:201
  57.1 6.3 collective-permute-start.9
  57.5 14.7 %collective-permute-start.36 = (bf16[64,768]{1,0:T(8,128)(2,1)S(1)}, bf16[64,768]{1,0:T(8,128)(2,1)S(1)}, u32[]{:S(2)}, u32[]{:S(2)}) collective-permute-start(bf16[64,768]{1,0:T(8,128)(2,1)S(1)} %get-tuple-element.108), channel_id=1, source_target_pairs={{0,10},{2,2},{4,8},{6,0},{8,14},{10,6},{12,12},{14,4},{1,11},{3,3}... | collective-permute-start | bytes 294920 | tf_op jit(solution)/shard_map/ppermute | solution.py:201
  63.4 34.5 %collective-permute-start.14 = (bf16[5,192,768]{2,1,0:T(8,128)(2,1)}, bf16[5,192,768]{2,1,0:T(8,128)(2,1)S(1)}, u32[]{:S(2)}, u32[]{:S(2)}) collective-permute-start(bf16[5,192,768]{2,1,0:T(8,128)(2,1)} %get-tuple-element.31), channel_id=1, source_target_pairs={{0,16},{16,0},{1,17},{17,1},{2,18},{18,2},{3,19},{19,3},{4,20},{20... | collective-permute-start | bytes 4423688 | tf_op jit(solution)/shard_map/ppermute | solution.py:348
  64.8 8.6 %collective-permute-start.35 = (bf16[64,768]{1,0:T(8,128)(2,1)S(1)}, bf16[64,768]{1,0:T(8,128)(2,1)S(1)}, u32[]{:S(2)}, u32[]{:S(2)}) collective-permute-start(bf16[64,768]{1,0:T(8,128)(2,1)S(1)} %get-tuple-element.109), channel_id=1, source_target_pairs={{0,2},{2,8},{4,0},{6,10},{8,6},{10,12},{12,4},{14,14},{1,3},{3,9},... | collective-permute-start | bytes 294920 | tf_op jit(solution)/shard_map/ppermute | solution.py:201
  68.7 29.2 %collective-permute-start.23 = (bf16[192,3072]{1,0:T(8,128)(2,1)S(1)}, bf16[192,3072]{1,0:T(8,128)(2,1)S(1)}, u32[]{:S(2)}, u32[]{:S(2)}) collective-permute-start(bf16[192,3072]{1,0:T(8,128)(2,1)S(1)} %copy-done.47), channel_id=1, source_target_pairs={{0,8},{8,0},{1,9},{9,1},{2,10},{10,2},{3,11},{11,3},{4,12},{12,4},... | collective-permute-start | bytes 3538952 | tf_op jit(solution)/shard_map/ppermute | solution.py:246
  72.1 26.4 %collective-permute-start.26 = (bf16[768,768]{1,0:T(8,128)(2,1)}, bf16[768,768]{1,0:T(8,128)(2,1)S(1)}, u32[]{:S(2)}, u32[]{:S(2)}) collective-permute-start(bf16[768,768]{1,0:T(8,128)(2,1)} %param.18), channel_id=1, source_target_pairs={{0,8},{8,0},{1,9},{9,1},{2,10},{10,2},{3,11},{11,3},{4,12},{12,4},... | collective-permute-start | bytes 3538952 | tf_op jit(solution)/shard_map/ppermute | solution.py:246
  72.2 28.9 %collective-permute-start.13 = (bf16[5,192,768]{2,1,0:T(8,128)(2,1)}, bf16[5,192,768]{2,1,0:T(8,128)(2,1)S(1)}, u32[]{:S(2)}, u32[]{:S(2)}) collective-permute-start(bf16[5,192,768]{2,1,0:T(8,128)(2,1)} %get-tuple-element.31), channel_id=1, source_target_pairs={{0,8},{8,0},{1,9},{9,1},{2,10},{10,2},{3,11},{11,3},{4,12},{12,4},... | collective-permute-start | bytes 4423688 | tf_op jit(solution)/shard_map/ppermute | solution.py:246
  79.6 19.2 %collective-permute-start.11 = (bf16[2,256,768]{2,1,0:T(8,128)(2,1)S(1)}, bf16[2,256,768]{2,1,0:T(8,128)(2,1)S(1)}, u32[]{:S(2)}, u32[]{:S(2)}) collective-permute-start(bf16[2,256,768]{2,1,0:T(8,128)(2,1)S(1)} %pad_maximum_fusion.7.refs_3_.refs_6_), channel_id=1, source_target_pairs={{0,1},{1,0},{2,3},{3,2},{4,5},{5,4},{6,7},{7,6},{8,9},{9,8},{10,11... | collective-permute-start | bytes 2359304 | tf_op jit(solution)/shard_map/ppermute | solution.py:224
  97.9 7.6 %collective-permute-start.10 = (bf16[2,256,768]{2,1,0:T(8,128)(2,1)S(1)}, bf16[2,256,768]{2,1,0:T(8,128)(2,1)S(1)}, u32[]{:S(2)}, u32[]{:S(2)}) collective-permute-start(bf16[2,256,768]{2,1,0:T(8,128)(2,1)S(1)} %pad_maximum_fusion.7.refs_3_.refs_6_), channel_id=1, source_target_pairs={{0,8},{8,0},{1,9},{9,1},{2,10},{10,2},{3,11},{11,3},{4,12},{12,4},... | collective-permute-start | bytes 2359304 | tf_op jit(solution)/shard_map/ppermute | solution.py:229
  97.9 28.4 %collective-permute-start.24 = (bf16[192,3072]{1,0:T(8,128)(2,1)S(1)}, bf16[192,3072]{1,0:T(8,128)(2,1)S(1)}, u32[]{:S(2)}, u32[]{:S(2)}) collective-permute-start(bf16[192,3072]{1,0:T(8,128)(2,1)S(1)} %copy-done.47), channel_id=1, source_target_pairs={{0,16},{16,0},{1,17},{17,1},{2,18},{18,2},{3,19},{19,3},{4,20},{20... | collective-permute-start | bytes 3538952 | tf_op jit(solution)/shard_map/ppermute | solution.py:349
  98.5 28.5 %collective-permute-start.15 = (bf16[5,192,768]{2,1,0:T(8,128)(2,1)S(1)}, bf16[5,192,768]{2,1,0:T(8,128)(2,1)}, u32[]{:S(2)}, u32[]{:S(2)}) collective-permute-start(bf16[5,192,768]{2,1,0:T(8,128)(2,1)S(1)} %collective-permute-done.14), channel_id=1, source_target_pairs={{0,8},{8,0},{1,9},{9,1},{2,10},{10,2},{3,11},{11,3},{4,12},{12,4},... | collective-permute-start | bytes 4423688 | tf_op jit(solution)/shard_map/ppermute | solution.py:247
  98.8 6.7 %collective-permute-start.12 = (bf16[2,256,768]{2,1,0:T(8,128)(2,1)S(1)}, bf16[2,256,768]{2,1,0:T(8,128)(2,1)S(1)}, u32[]{:S(2)}, u32[]{:S(2)}) collective-permute-start(bf16[2,256,768]{2,1,0:T(8,128)(2,1)S(1)} %collective-permute-done.11.refs_5_.refs_8_), channel_id=1, source_target_pairs={{0,8},{8,0},{1,9},{9,1},{2,10},{10,2},{3,11},{11,3},{4,12},{12,4},... | collective-permute-start | bytes 2359304 | tf_op jit(solution)/shard_map/ppermute | solution.py:229
  126.3 29.2 %collective-permute-start.27 = (bf16[768,768]{1,0:T(8,128)(2,1)}, bf16[768,768]{1,0:T(8,128)(2,1)S(1)}, u32[]{:S(2)}, u32[]{:S(2)}) collective-permute-start(bf16[768,768]{1,0:T(8,128)(2,1)} %param.18), channel_id=1, source_target_pairs={{0,16},{16,0},{1,17},{17,1},{2,18},{18,2},{3,19},{19,3},{4,20},{20... | collective-permute-start | bytes 3538952 | tf_op jit(solution)/shard_map/ppermute | solution.py:350
  126.9 30.0 %collective-permute-start.25 = (bf16[192,3072]{1,0:T(8,128)(2,1)S(1)}, bf16[192,3072]{1,0:T(8,128)(2,1)S(1)}, u32[]{:S(2)}, u32[]{:S(2)}) collective-permute-start(bf16[192,3072]{1,0:T(8,128)(2,1)S(1)} %collective-permute-done.24), channel_id=1, source_target_pairs={{0,8},{8,0},{1,9},{9,1},{2,10},{10,2},{3,11},{11,3},{4,12},{12,4},... | collective-permute-start | bytes 3538952 | tf_op jit(solution)/shard_map/ppermute | solution.py:247
  133.3 20.0 %collective-permute-start.21 = (bf16[2,256,768]{2,1,0:T(8,128)(2,1)S(1)}, bf16[2,256,768]{2,1,0:T(8,128)(2,1)S(1)}, u32[]{:S(2)}, u32[]{:S(2)}) collective-permute-start(bf16[2,256,768]{2,1,0:T(8,128)(2,1)S(1)} %pad_maximum_fusion.8.refs_1_.refs_4_), channel_id=1, source_target_pairs={{0,1},{1,0},{2,3},{3,2},{4,5},{5,4},{6,7},{7,6},{8,9},{9,8},{10,11... | collective-permute-start | bytes 2359304 | tf_op jit(solution)/shard_map/ppermute | solution.py:224
  134.9 22.2 %collective-permute-start.20 = (bf16[2,256,768]{2,1,0:T(8,128)(2,1)S(1)}, bf16[2,256,768]{2,1,0:T(8,128)(2,1)S(1)}, u32[]{:S(2)}, u32[]{:S(2)}) collective-permute-start(bf16[2,256,768]{2,1,0:T(8,128)(2,1)S(1)} %pad_maximum_fusion.8.refs_1_.refs_4_), channel_id=1, source_target_pairs={{0,8},{8,0},{1,9},{9,1},{2,10},{10,2},{3,11},{11,3},{4,12},{12,4},... | collective-permute-start | bytes 2359304 | tf_op jit(solution)/shard_map/ppermute | solution.py:229
  155.5 13.1 %collective-permute-start.28 = (bf16[768,768]{1,0:T(8,128)(2,1)S(1)}, bf16[768,768]{1,0:T(8,128)(2,1)S(1)}, u32[]{:S(2)}, u32[]{:S(2)}) collective-permute-start(bf16[768,768]{1,0:T(8,128)(2,1)S(1)} %collective-permute-done.27), channel_id=1, source_target_pairs={{0,8},{8,0},{1,9},{9,1},{2,10},{10,2},{3,11},{11,3},{4,12},{12,4},... | collective-permute-start | bytes 3538952 | tf_op jit(solution)/shard_map/ppermute | solution.py:247
  225.9 41.8 %collective-permute-start.32 = (bf16[64,768]{1,0:T(8,128)(2,1)}, bf16[64,768]{1,0:T(8,128)(2,1)}, u32[]{:S(2)}, u32[]{:S(2)}) collective-permute-start(bf16[64,768]{1,0:T(8,128)(2,1)} %get-tuple-element.104), channel_id=1, source_target_pairs={{10,0},{2,2},{8,4},{0,6},{14,8},{6,10},{12,12},{4,14},{11,1},{3,3}... | collective-permute-start | bytes 294920 | tf_op jit(solution)/shard_map/ppermute | solution.py:210
  229.7 36.7 %collective-permute-start.31 = (bf16[64,768]{1,0:T(8,128)(2,1)}, bf16[64,768]{1,0:T(8,128)(2,1)}, u32[]{:S(2)}, u32[]{:S(2)}) collective-permute-start(bf16[64,768]{1,0:T(8,128)(2,1)} %get-tuple-element.105), channel_id=1, source_target_pairs={{2,0},{8,2},{0,4},{10,6},{6,8},{12,10},{4,12},{14,14},{3,1},{9,3},... | collective-permute-start | bytes 294920 | tf_op jit(solution)/shard_map/ppermute | solution.py:210
  232.0 32.0 %collective-permute-start.30 = (bf16[64,768]{1,0:T(8,128)(2,1)}, bf16[64,768]{1,0:T(8,128)(2,1)}, u32[]{:S(2)}, u32[]{:S(2)}) collective-permute-start(bf16[64,768]{1,0:T(8,128)(2,1)} %get-tuple-element.106), channel_id=1, source_target_pairs={{8,0},{0,2},{10,4},{2,6},{12,8},{4,10},{14,12},{6,14},{9,1},{1,3},... | collective-permute-start | bytes 294920 | tf_op jit(solution)/shard_map/ppermute | solution.py:210
  233.7 28.9 %collective-permute-start.29 = (bf16[64,768]{1,0:T(8,128)(2,1)S(1)}, bf16[64,768]{1,0:T(8,128)(2,1)S(1)}, u32[]{:S(2)}, u32[]{:S(2)}) collective-permute-start(bf16[64,768]{1,0:T(8,128)(2,1)S(1)} %get-tuple-element.107), channel_id=1, source_target_pairs={{0,0},{10,2},{2,4},{8,6},{4,8},{14,10},{6,12},{12,14},{1,1},{11,3}... | collective-permute-start | bytes 294920 | tf_op jit(solution)/shard_map/ppermute | solution.py:210
  252.3 11.4 %collective-permute-start.38 = (bf16[2,256,768]{2,1,0:T(8,128)(2,1)S(1)}, bf16[2,256,768]{2,1,0:T(8,128)(2,1)S(1)}, u32[]{:S(2)}, u32[]{:S(2)}) collective-permute-start(bf16[2,256,768]{2,1,0:T(8,128)(2,1)S(1)} %get-tuple-element.42), channel_id=1, source_target_pairs={{0,8},{8,0},{1,9},{9,1},{2,10},{10,2},{3,11},{11,3},{4,12},{12,4},... | collective-permute-start | bytes 2359304 | tf_op jit(solution)/shard_map/ppermute | solution.py:236
  262.7 6.3 collective-permute-start.45
  263.7 6.0 collective-permute-start.37
  264.0 20.4 %collective-permute-start.39 = (bf16[2,256,768]{2,1,0:T(8,128)(2,1)S(1)}, bf16[2,256,768]{2,1,0:T(8,128)(2,1)S(1)}, u32[]{:S(2)}, u32[]{:S(2)}) collective-permute-start(bf16[2,256,768]{2,1,0:T(8,128)(2,1)S(1)} %add_convert_fusion.4), channel_id=1, source_target_pairs={{1,0},{0,1},{3,2},{2,3},{5,4},{4,5},{7,6},{6,7},{9,8},{8,9},{11,10... | collective-permute-start | bytes 2359304 | tf_op jit(solution)/shard_map/ppermute | solution.py:241
  266.5 20.6 %collective-permute-start.44 = (bf16[2,256,768]{2,1,0:T(8,128)(2,1)S(1)}, bf16[2,256,768]{2,1,0:T(8,128)(2,1)S(1)}, u32[]{:S(2)}, u32[]{:S(2)}) collective-permute-start(bf16[2,256,768]{2,1,0:T(8,128)(2,1)S(1)} %copy-done.7), channel_id=1, source_target_pairs={{0,8},{8,0},{1,9},{9,1},{2,10},{10,2},{3,11},{11,3},{4,12},{12,4},... | collective-permute-start | bytes 2359304 | tf_op jit(solution)/shard_map/ppermute | solution.py:236
  267.7 52.3 %collective-permute-start.59 = (bf16[8,2,192,768]{3,2,0,1:T(8,128)(2,1)}, bf16[8,2,192,768]{3,2,0,1:T(8,128)(2,1)}, u32[]{:S(2)}, u32[]{:S(2)}) collective-permute-start(bf16[8,2,192,768]{3,2,0,1:T(8,128)(2,1)} %dynamic-slice_bitcast_fusion), channel_id=1, source_target_pairs={{0,8},{8,0},{1,9},{9,1},{2,10},{10,2},{3,11},{11,3},{4,12},{12,4},... | collective-permute-start | bytes 14155784 | tf_op jit(solution)/shard_map/ppermute | solution.py:275
  269.1 31.7 %collective-permute-start.46 = (bf16[2,256,768]{2,1,0:T(8,128)(2,1)S(1)}, bf16[2,256,768]{2,1,0:T(8,128)(2,1)S(1)}, u32[]{:S(2)}, u32[]{:S(2)}) collective-permute-start(bf16[2,256,768]{2,1,0:T(8,128)(2,1)S(1)} %add_convert_fusion.2), channel_id=1, source_target_pairs={{1,0},{0,1},{3,2},{2,3},{5,4},{4,5},{7,6},{6,7},{9,8},{8,9},{11,10... | collective-permute-start | bytes 2359304 | tf_op jit(solution)/shard_map/ppermute | solution.py:241
  287.1 27.5 %collective-permute-start.51 = (bf16[4,2,192,768]{3,2,1,0:T(8,128)(2,1)S(1)}, bf16[4,2,192,768]{3,2,1,0:T(8,128)(2,1)S(1)}, u32[]{:S(2)}, u32[]{:S(2)}) collective-permute-start(bf16[4,2,192,768]{3,2,1,0:T(8,128)(2,1)S(1)} %dynamic-slice_bitcast_fusion.3), channel_id=1, source_target_pairs={{0,8},{8,0},{1,9},{9,1},{2,10},{10,2},{3,11},{11,3},{4,12},{12,4},... | collective-permute-start | bytes 7077896 | tf_op jit(solution)/shard_map/ppermute | solution.py:275
  303.3 14.3 %collective-permute-start.55 = (bf16[4,2,192,768]{3,2,1,0:T(8,128)(2,1)S(1)}, bf16[4,2,192,768]{3,2,1,0:T(8,128)(2,1)S(1)}, u32[]{:S(2)}, u32[]{:S(2)}) collective-permute-start(bf16[4,2,192,768]{3,2,1,0:T(8,128)(2,1)S(1)} %dynamic-slice_bitcast_fusion.2), channel_id=1, source_target_pairs={{0,8},{8,0},{1,9},{9,1},{2,10},{10,2},{3,11},{11,3},{4,12},{12,4},... | collective-permute-start | bytes 7077896 | tf_op jit(solution)/shard_map/ppermute | solution.py:275
  316.3 136.5 %collective-permute-start.52 = (bf16[4,192,768]{2,1,0:T(8,128)(2,1)}, bf16[4,192,768]{2,1,0:T(8,128)(2,1)}, u32[]{:S(2)}, u32[]{:S(2)}) collective-permute-start(bf16[4,192,768]{2,1,0:T(8,128)(2,1)} %dynamic-slice_bitcast_fusion.6), channel_id=1, source_target_pairs={{0,16},{16,0},{1,17},{17,1},{2,18},{18,2},{3,19},{19,3},{4,20},{20... | collective-permute-start | bytes 3538952 | tf_op jit(solution)/shard_map/ppermute | solution.py:278
  319.3 140.5 %collective-permute-start.56 = (bf16[4,192,768]{2,1,0:T(8,128)(2,1)}, bf16[4,192,768]{2,1,0:T(8,128)(2,1)}, u32[]{:S(2)}, u32[]{:S(2)}) collective-permute-start(bf16[4,192,768]{2,1,0:T(8,128)(2,1)} %dynamic-slice_bitcast_fusion.5), channel_id=1, source_target_pairs={{0,16},{16,0},{1,17},{17,1},{2,18},{18,2},{3,19},{19,3},{4,20},{20... | collective-permute-start | bytes 3538952 | tf_op jit(solution)/shard_map/ppermute | solution.py:278
  327.6 170.7 %collective-permute-start.60 = (bf16[8,192,768]{2,1,0:T(8,128)(2,1)}, bf16[8,192,768]{2,1,0:T(8,128)(2,1)}, u32[]{:S(2)}, u32[]{:S(2)}) collective-permute-start(bf16[8,192,768]{2,1,0:T(8,128)(2,1)} %dynamic-slice_bitcast_fusion.1), channel_id=1, source_target_pairs={{0,16},{16,0},{1,17},{17,1},{2,18},{18,2},{3,19},{19,3},{4,20},{20... | collective-permute-start | bytes 7077896 | tf_op jit(solution)/shard_map/ppermute | solution.py:278
  454.8 16.6 %collective-permute-start.53 = (bf16[4,96,768]{2,1,0:T(8,128)(2,1)S(1)}, bf16[4,96,768]{2,1,0:T(8,128)(2,1)S(1)}, u32[]{:S(2)}, u32[]{:S(2)}) collective-permute-start(bf16[4,96,768]{2,1,0:T(8,128)(2,1)S(1)} %dynamic-slice_bitcast_fusion.8), channel_id=1, source_target_pairs={{0,1},{1,0},{2,3},{3,2},{4,5},{5,4},{6,7},{7,6},{8,9},{9,8},{10,11... | collective-permute-start | bytes 1769480 | tf_op jit(solution)/shard_map/ppermute | solution.py:284
  462.4 26.6 %collective-permute-start.57 = (bf16[4,96,768]{2,1,0:T(8,128)(2,1)S(1)}, bf16[4,96,768]{2,1,0:T(8,128)(2,1)}, u32[]{:S(2)}, u32[]{:S(2)}) collective-permute-start(bf16[4,96,768]{2,1,0:T(8,128)(2,1)S(1)} %dynamic-slice_bitcast_fusion.7), channel_id=1, source_target_pairs={{0,1},{1,0},{2,3},{3,2},{4,5},{5,4},{6,7},{7,6},{8,9},{9,8},{10,11... | collective-permute-start | bytes 1769480 | tf_op jit(solution)/shard_map/ppermute | solution.py:284
  472.3 21.7 %all-to-all-start = ((bf16[4,96,768]{2,1,0:T(8,128)(2,1)}), bf16[4,96,768]{2,1,0:T(8,128)(2,1)S(1)}, u32[]{:S(2)}, u32[]{:S(2)}) async-start(bf16[4,96,768]{2,1,0:T(8,128)(2,1)} %fusion.29), calls=%async_computation | async-start | bytes 1179648 | tf_op jit(solution)/shard_map/all_to_all | solution.py:285
  478.6 73.8 %collective-permute-start.50 = (bf16[64,768]{1,0:T(8,128)(2,1)}, bf16[64,768]{1,0:T(8,128)(2,1)}, u32[]{:S(2)}, u32[]{:S(2)}) collective-permute-start(bf16[64,768]{1,0:T(8,128)(2,1)} %get-tuple-element.96), channel_id=1, source_target_pairs={{10,0},{2,2},{8,4},{0,6},{14,8},{6,10},{12,12},{4,14},{11,1},{3,3}... | collective-permute-start | bytes 294920 | tf_op jit(solution)/shard_map/ppermute | solution.py:210
  484.4 65.0 %collective-permute-start.49 = (bf16[64,768]{1,0:T(8,128)(2,1)}, bf16[64,768]{1,0:T(8,128)(2,1)}, u32[]{:S(2)}, u32[]{:S(2)}) collective-permute-start(bf16[64,768]{1,0:T(8,128)(2,1)} %get-tuple-element.97), channel_id=1, source_target_pairs={{2,0},{8,2},{0,4},{10,6},{6,8},{12,10},{4,12},{14,14},{3,1},{9,3},... | collective-permute-start | bytes 294920 | tf_op jit(solution)/shard_map/ppermute | solution.py:210
  486.3 59.5 %collective-permute-start.48 = (bf16[64,768]{1,0:T(8,128)(2,1)}, bf16[64,768]{1,0:T(8,128)(2,1)}, u32[]{:S(2)}, u32[]{:S(2)}) collective-permute-start(bf16[64,768]{1,0:T(8,128)(2,1)} %get-tuple-element.98), channel_id=1, source_target_pairs={{8,0},{0,2},{10,4},{2,6},{12,8},{4,10},{14,12},{6,14},{9,1},{1,3},... | collective-permute-start | bytes 294920 | tf_op jit(solution)/shard_map/ppermute | solution.py:210
  489.0 49.4 %collective-permute-start.47 = (bf16[64,768]{1,0:T(8,128)(2,1)}, bf16[64,768]{1,0:T(8,128)(2,1)}, u32[]{:S(2)}, u32[]{:S(2)}) collective-permute-start(bf16[64,768]{1,0:T(8,128)(2,1)} %get-tuple-element.99), channel_id=1, source_target_pairs={{0,0},{10,2},{2,4},{8,6},{4,8},{14,10},{6,12},{12,14},{1,1},{11,3}... | collective-permute-start | bytes 294920 | tf_op jit(solution)/shard_map/ppermute | solution.py:210
  494.0 20.2 %all-to-all-start.2 = ((bf16[4,96,768]{2,1,0:T(8,128)(2,1)}), bf16[4,96,768]{2,1,0:T(8,128)(2,1)}, u32[]{:S(2)}, u32[]{:S(2)}) async-start(bf16[4,96,768]{2,1,0:T(8,128)(2,1)} %fusion.28), calls=%async_computation.2 | async-start | bytes 1179648 | tf_op jit(solution)/shard_map/all_to_all | solution.py:285
  502.3 28.1 %collective-permute-start.61 = (bf16[4,192,768]{2,1,0:T(8,128)(2,1)}, bf16[4,192,768]{2,1,0:T(8,128)(2,1)}, u32[]{:S(2)}, u32[]{:S(2)}) collective-permute-start(bf16[4,192,768]{2,1,0:T(8,128)(2,1)} %dynamic-slice_bitcast_fusion.4), channel_id=1, source_target_pairs={{0,1},{1,0},{2,3},{3,2},{4,5},{5,4},{6,7},{7,6},{8,9},{9,8},{10,11... | collective-permute-start | bytes 3538952 | tf_op jit(solution)/shard_map/ppermute | solution.py:284
  516.0 24.3 %all-to-all-start.1 = ((bf16[4,96,768]{2,1,0:T(8,128)(2,1)}), bf16[4,96,768]{2,1,0:T(8,128)(2,1)}, u32[]{:S(2)}, u32[]{:S(2)}) async-start(bf16[4,96,768]{2,1,0:T(8,128)(2,1)} %broadcast_in_dim.29), calls=%async_computation.1 | async-start | bytes 1179648 | tf_op jit(solution)/shard_map/all_to_all | solution.py:287
  530.5 50.3 %collective-permute-start.43 = (bf16[64,768]{1,0:T(8,128)(2,1)S(1)}, bf16[64,768]{1,0:T(8,128)(2,1)S(1)}, u32[]{:S(2)}, u32[]{:S(2)}) collective-permute-start(bf16[64,768]{1,0:T(8,128)(2,1)S(1)} %get-tuple-element.100), channel_id=1, source_target_pairs={{10,0},{2,2},{8,4},{0,6},{14,8},{6,10},{12,12},{4,14},{11,1},{3,3}... | collective-permute-start | bytes 294920 | tf_op jit(solution)/shard_map/ppermute | solution.py:210
  538.4 41.7 %collective-permute-start.42 = (bf16[64,768]{1,0:T(8,128)(2,1)S(1)}, bf16[64,768]{1,0:T(8,128)(2,1)S(1)}, u32[]{:S(2)}, u32[]{:S(2)}) collective-permute-start(bf16[64,768]{1,0:T(8,128)(2,1)S(1)} %get-tuple-element.101), channel_id=1, source_target_pairs={{2,0},{8,2},{0,4},{10,6},{6,8},{12,10},{4,12},{14,14},{3,1},{9,3},... | collective-permute-start | bytes 294920 | tf_op jit(solution)/shard_map/ppermute | solution.py:210
  540.3 33.8 %all-to-all-start.4 = ((bf16[4,192,768]{2,1,0:T(8,128)(2,1)}), bf16[4,192,768]{2,1,0:T(8,128)(2,1)S(1)}, u32[]{:S(2)}, u32[]{:S(2)}) async-start(bf16[4,192,768]{2,1,0:T(8,128)(2,1)} %fusion.10), calls=%async_computation.4 | async-start | bytes 2359296 | tf_op jit(solution)/shard_map/all_to_all | solution.py:285
  545.8 33.7 %collective-permute-start.41 = (bf16[64,768]{1,0:T(8,128)(2,1)}, bf16[64,768]{1,0:T(8,128)(2,1)S(1)}, u32[]{:S(2)}, u32[]{:S(2)}) collective-permute-start(bf16[64,768]{1,0:T(8,128)(2,1)} %get-tuple-element.102), channel_id=1, source_target_pairs={{8,0},{0,2},{10,4},{2,6},{12,8},{4,10},{14,12},{6,14},{9,1},{1,3},... | collective-permute-start | bytes 294920 | tf_op jit(solution)/shard_map/ppermute | solution.py:210
  549.3 29.4 %collective-permute-start.40 = (bf16[64,768]{1,0:T(8,128)(2,1)}, bf16[64,768]{1,0:T(8,128)(2,1)S(1)}, u32[]{:S(2)}, u32[]{:S(2)}) collective-permute-start(bf16[64,768]{1,0:T(8,128)(2,1)} %get-tuple-element.103), channel_id=1, source_target_pairs={{0,0},{10,2},{2,4},{8,6},{4,8},{14,10},{6,12},{12,14},{1,1},{11,3}... | collective-permute-start | bytes 294920 | tf_op jit(solution)/shard_map/ppermute | solution.py:210
  575.0 18.1 %all-to-all-start.3 = ((bf16[4,96,768]{2,1,0:T(8,128)(2,1)}), bf16[4,96,768]{2,1,0:T(8,128)(2,1)S(1)}, u32[]{:S(2)}, u32[]{:S(2)}) async-start(bf16[4,96,768]{2,1,0:T(8,128)(2,1)} %broadcast_in_dim.30), calls=%async_computation.3 | async-start | bytes 1179648 | tf_op jit(solution)/shard_map/all_to_all | solution.py:287
  594.1 31.1 %all-to-all-start.5 = ((bf16[4,192,768]{2,1,0:T(8,128)(2,1)}), bf16[4,192,768]{2,1,0:T(8,128)(2,1)S(1)}, u32[]{:S(2)}, u32[]{:S(2)}) async-start(bf16[4,192,768]{2,1,0:T(8,128)(2,1)} %broadcast_in_dim.31), calls=%async_computation.5 | async-start | bytes 2359296 | tf_op jit(solution)/shard_map/all_to_all | solution.py:287
  601.3 16.5 %collective-permute-start.54 = (bf16[4,96,768]{2,1,0:T(8,128)(2,1)}, bf16[4,96,768]{2,1,0:T(8,128)(2,1)S(1)}, u32[]{:S(2)}, u32[]{:S(2)}) collective-permute-start(bf16[4,96,768]{2,1,0:T(8,128)(2,1)} %all-to-all-done.1), channel_id=1, source_target_pairs={{0,1},{1,0},{2,3},{3,2},{4,5},{5,4},{6,7},{7,6},{8,9},{9,8},{10,11... | collective-permute-start | bytes 1769480 | tf_op jit(solution)/shard_map/ppermute | solution.py:288
  605.0 24.1 %collective-permute-start.58 = (bf16[4,96,768]{2,1,0:T(8,128)(2,1)S(1)}, bf16[4,96,768]{2,1,0:T(8,128)(2,1)S(1)}, u32[]{:S(2)}, u32[]{:S(2)}) collective-permute-start(bf16[4,96,768]{2,1,0:T(8,128)(2,1)S(1)} %all-to-all-done.3), channel_id=1, source_target_pairs={{0,1},{1,0},{2,3},{3,2},{4,5},{5,4},{6,7},{7,6},{8,9},{9,8},{10,11... | collective-permute-start | bytes 1769480 | tf_op jit(solution)/shard_map/ppermute | solution.py:288
  625.3 28.0 %collective-permute-start.62 = (bf16[4,192,768]{2,1,0:T(8,128)(2,1)S(1)}, bf16[4,192,768]{2,1,0:T(8,128)(2,1)S(1)}, u32[]{:S(2)}, u32[]{:S(2)}) collective-permute-start(bf16[4,192,768]{2,1,0:T(8,128)(2,1)S(1)} %all-to-all-done.5), channel_id=1, source_target_pairs={{0,1},{1,0},{2,3},{3,2},{4,5},{5,4},{6,7},{7,6},{8,9},{9,8},{10,11... | collective-permute-start | bytes 3538952 | tf_op jit(solution)/shard_map/ppermute | solution.py:288
  (82 other events, 1191.7 us)

commit v2 on v1

--- a/solution.py
+++ b/solution.py
@@ -79,8 +79,7 @@
         key_place_ref, query_place_ref, refs = refs[0], refs[1], refs[2:]
     query_ref, dout_ref, out_ref, mass_ref = refs[:4]
     kv_refs = refs[4 : 4 + pieces]
-    dquery_ref = refs[4 + pieces]
-    dkv_refs = refs[5 + pieces :]
+    dquery_ref, mine_ref, theirs_ref = refs[4 + pieces :]
     query = split_heads(query_ref[...] * jnp.asarray(SCORE_SCALE, BF))
     dout = dout_ref[...]
     prod = (dout.astype(F32) * out_ref[...].astype(F32)).T
@@ -102,8 +101,9 @@
         probs = jnp.exp(scores - log_mass)
         dprobs = dot_t(kv_refs[i][1], dout)
         dscores = (probs * (dprobs - delta)).astype(BF)
-        dkv_refs[i][0] = dot(dscores, query).astype(BF)
-        dkv_refs[i][1] = dot(probs.astype(BF), dout).astype(BF)
+        dkv_ref = theirs_ref if i % 2 else mine_ref
+        dkv_ref[i // 2, 0] = dot(dscores, query).astype(BF)
+        dkv_ref[i // 2, 1] = dot(probs.astype(BF), dout).astype(BF)
         part = t_dot(keys, dscores)
         dquery = part if dquery is None else dquery + part
     dquery_ref[...] = (join_heads(dquery) * SCORE_SCALE).astype(BF)
@@ -157,15 +157,17 @@
     keys = piece * len(kv)
     column = pl.BlockSpec((rows, PAIR), lambda h: (0, h))
     pair = pl.BlockSpec((2, piece, PAIR), lambda h: (0, 0, h))
-    res = pl.pallas_call(
+    groups = len(kv) // 2
+    blocks = pl.BlockSpec((groups, 2, piece, PAIR), lambda h: (0, 0, 0, h))
+    return pl.pallas_call(
         functools.partial(backward_kernel, masked, len(kv)),
         grid=(width // PAIR,),
         in_specs=extra_specs
         + [column, column, column, pl.BlockSpec((1, 1, 2 * rows), lambda h: (h, 0, 0))]
         + [pair] * len(kv),
-        out_specs=[column] + [pair] * len(kv),
+        out_specs=[column, blocks, blocks],
         out_shape=[jax.ShapeDtypeStruct((rows, width), BF)]
-        + [jax.ShapeDtypeStruct((2, piece, width), BF)] * len(kv),
+        + [jax.ShapeDtypeStruct((groups, 2, piece, width), BF)] * 2,
         compiler_params=pltpu.CompilerParams(vmem_limit_bytes=VMEM_LIMIT),
         cost_estimate=pl.CostEstimate(
             flops=10 * rows * keys * width * 2,
@@ -173,45 +175,36 @@
             transcendentals=rows * keys * HEADS,
         ),
     )(*extra, query, dout, out, mass, *kv)
-    return res[0], list(res[1:])
-
-
-def deal_perms():
-    perms = []
-    for r in range(LINE):
-        perm = []
-        for c in range(2):
-            for z in range(LINE):
-                k = (r - z) % LINE
-                perm.append((c * LINE + z, (k % 2) * LINE + 2 * c + k // 2))
-        perms.append(perm)
-    return perms
-
-
-DEAL = deal_perms()
 
 
 def deal(array):
-    rows = array.shape[1]
-    chunks = array.reshape(LINE, rows // 2, array.shape[2])
-    z = lax.axis_index("z")
-    got = []
-    for r in range(LINE):
-        chunk = lax.dynamic_index_in_dim(chunks, lax.rem(r - z + LINE, LINE), keepdims=False)
-        got.append(lax.ppermute(chunk, ("core", "z"), DEAL[r]))
-    return jnp.concatenate(got, axis=0)
+    lead = array.shape[:-3]
+    _, rows, width = array.shape[-3:]
+    core = lax.axis_index("core")
+    parts = array.reshape(lead + (2, 2, rows // 2, width))
+    axis = len(lead) + 1
+    mine = lax.dynamic_index_in_dim(parts, core, axis, keepdims=False)
+    theirs = lax.dynamic_index_in_dim(parts, 1 - core, axis, keepdims=False)
+    got = lax.ppermute(theirs, "core", SWAP)
+    low, high = jnp.where(core == 0, mine, got), jnp.where(core == 0, got, mine)
+    chunks = jnp.concatenate([low, high], axis=len(lead))
+    out = lax.all_to_all(chunks, "z", len(lead), len(lead), tiled=True)
+    return out.reshape(lead + (2 * rows, width))
 
 
 def undeal(array):
-    half = array.shape[0] // LINE
-    got = []
-    for r in range(LINE):
-        got.append(
-            lax.ppermute(array[r * half : (r + 1) * half], ("core", "z"), [(b, a) for a, b in DEAL[r]])
-        )
-    both = jnp.stack(got + got)
-    mine = lax.dynamic_slice_in_dim(both, lax.axis_index("z"), LINE, axis=0)
-    return mine.reshape(2, 2 * half, array.shape[1])
+    lead = array.shape[:-2]
+    rows, width = array.shape[-2] // 2, array.shape[-1]
+    core = lax.axis_index("core")
+    axis = len(lead)
+    chunks = lax.all_to_all(
+        array.reshape(lead + (LINE, rows // 2, width)), "z", axis, axis, tiled=True
+    ).reshape(lead + (2, 2, rows // 2, width))
+    mine = lax.dynamic_index_in_dim(chunks, core, axis, keepdims=False)
+    theirs = lax.dynamic_index_in_dim(chunks, 1 - core, axis, keepdims=False)
+    got = lax.ppermute(theirs, "core", SWAP)
+    low, high = jnp.where(core == 0, mine, got), jnp.where(core == 0, got, mine)
+    return jnp.stack([low, high], axis=axis + 1).reshape(lead + (2, rows, width))
 
 
 def group_perm(groups, step):
@@ -230,11 +223,9 @@
     return pieces
 
 
-def collect(pieces, groups):
-    sums = []
-    for step in range(groups):
-        other = lax.ppermute(pieces[2 * step + 1], "core", SWAP)
-        sums.append(pieces[2 * step].astype(F32) + other.astype(F32))
+def collect(mine, theirs, groups):
+    got = lax.ppermute(theirs, "core", SWAP)
+    sums = mine.astype(F32) + got.astype(F32)
     total = sums[0]
     for step in range(1, groups):
         back = [(b, a) for a, b in group_perm(groups, step)]
@@ -264,31 +255,66 @@
     return lax.optimization_barrier((value, earlier))[0]
 
 
-def reduce_units(units):
+def both(mine, theirs, axis):
+    return (mine.astype(F32) + lax.ppermute(theirs, axis, SWAP).astype(F32)).astype(BF)
+
+
+def split_of(array, axis, name):
+    i = lax.axis_index(name)
+    mine = lax.dynamic_index_in_dim(array, i, axis=axis, keepdims=False)
+    theirs = lax.dynamic_index_in_dim(array, 1 - i, axis=axis, keepdims=False)
+    return mine, theirs
+
+
+def over_cores(units):
     n, rows, width = units.shape
-    shard = rows // 4
-    fx, core = lax.axis_index("fx"), lax.axis_index("core")
+    return both(*split_of(units.reshape(n, 2, 2, rows // 4, width), 2, "core"), "core")
+
+
+def over_x(sums):
+    return both(*split_of(sums, 1, "fx"), "fx")
+
+
+def over_y(sums):
+    n, shard, width = sums.shape
+    return both(*split_of(sums.reshape(2, LINE, n * shard // (2 * LINE), width), 0, "y"), "y")
+
+
+def over_z(sums):
+    parts = lax.all_to_all(sums, "z", 0, 0, tiled=True)
+    return jnp.sum(parts.astype(F32), axis=0, keepdims=True).astype(BF)
+
+
+def back_z(total):
+    return lax.all_to_all(jnp.broadcast_to(total, (LINE,) + total.shape[1:]), "z", 0, 0, tiled=True)
+
+
+def back_y(line, shape):
+    other = lax.ppermute(line, "y", SWAP)
     y = lax.axis_index("y")
-    split = units.reshape(n, 2, 2, shard, width)
-    theirs = lax.dynamic_index_in_dim(split, 1 - core, axis=2, keepdims=False)
-    mine = lax.dynamic_index_in_dim(split, core, axis=2, keepdims=False)
-    mine = (mine.astype(F32) + lax.ppermute(theirs, "core", SWAP).astype(F32)).astype(BF)
-    theirs = lax.dynamic_index_in_dim(mine, 1 - fx, axis=1, keepdims=False)
-    mine = lax.dynamic_index_in_dim(mine, fx, axis=1, keepdims=False)
-    mine = (mine.astype(F32) + lax.ppermute(theirs, "fx", SWAP).astype(F32)).astype(BF)
-    if lax.axis_size("o") > 1:
-        return lax.psum(mine, ("o", "z", "y")).astype(F32)
-    lines = mine.reshape(2, LINE, n * shard // (2 * LINE), width)
-    theirs = lax.dynamic_index_in_dim(lines, 1 - y, axis=0, keepdims=False)
-    mine = lax.dynamic_index_in_dim(lines, y, axis=0, keepdims=False)
-    mine = (mine.astype(F32) + lax.ppermute(theirs, "y", SWAP).astype(F32)).astype(BF)
-    parts = lax.all_to_all(mine, "z", 0, 0, tiled=True)
-    total = jnp.sum(parts.astype(F32), axis=0, keepdims=True).astype(BF)
-    line = lax.all_to_all(jnp.broadcast_to(total, (LINE,) + total.shape[1:]), "z", 0, 0, tiled=True)
-    other = lax.ppermute(line, "y", SWAP)
     low = jnp.where(y == 0, line, other)
     high = jnp.where(y == 0, other, line)
-    return jnp.concatenate([low, high], axis=0).astype(F32).reshape(n, shard, width)
+    return jnp.concatenate([low, high], axis=0).astype(F32).reshape(shape)
+
+
+def over_ctx(sums):
+    if lax.axis_size("o") > 1:
+        return lax.psum(sums, ("o", "z", "y")).astype(F32)
+    return back_y(back_z(over_z(over_y(sums))), sums.shape)
+
+
+def sum_vectors(rows):
+    count, width = rows.shape
+    n_ctx = lax.axis_size("o") * 2 * LINE
+    shard = width // 4
+    size = count * shard
+    lines = -(-size // (16 * 128)) * 16
+    cut = rows.reshape(count, 4, shard).transpose(1, 0, 2).reshape(4, size)
+    cut = jnp.pad(cut, ((0, 0), (0, lines * 128 - size))).reshape(4, 1, lines, 128).astype(BF)
+    cut = jnp.broadcast_to(cut, (4, n_ctx, lines, 128)).reshape(4 * n_ctx, lines, 128)
+    got = lax.all_to_all(cut, ("fx", "core", "o", "z", "y"), 0, 0, tiled=True)
+    total = jnp.sum(got.astype(F32), axis=0)
+    return total.reshape(-1)[:size].reshape(count, shard)
 
 
 def standard(values):
@@ -340,32 +366,30 @@
         [norm_gains, bias_rows, up_bias.reshape(blocks, shard), down_bias.reshape(1, shard)], axis=0
     )
     x_bf = deal(layer_in)
-    vec_other = lax.ppermute(vectors, "fx", SWAP)
+    vec = lax.all_to_all(jnp.stack([vectors] * 4), ("fx", "core"), 0, 0, tiled=True).astype(F32)
     qkv_shard = attn_weight[:3]
-    qkv_other = lax.ppermute(after(qkv_shard, vec_other), "fx", SWAP)
-    enc_bf = deal(encoded)
+    qkv_other = lax.ppermute(qkv_shard, "fx", SWAP)
     mid_shard = jnp.concatenate([attn_weight[3:], out_weight], axis=0)
     mid_other = lax.ppermute(after(mid_shard, qkv_other), "fx", SWAP)
     up_other = lax.ppermute(after(up_weight, mid_other), "fx", SWAP)
     down_other = lax.ppermute(after(down_weight, up_other), "fx", SWAP)
-    cot = deal(out_cotangent)
-
-    vec = assemble(vectors[None], vec_other[None], 0).astype(F32)
+    enc_cot = deal(after(jnp.stack([encoded, out_cotangent]), x_bf)) if encoded.shape == layer_in.shape else None
+    enc_bf = deal(encoded) if enc_cot is None else enc_cot[0]
+    cot = deal(out_cotangent) if enc_cot is None else enc_cot[1]
+
     flat = vec[:, : 3 + 9].transpose(1, 0, 2).reshape(12, width)
     gain, bias = flat[:3], flat[3:]
     up_b = vec[:, 12 : 12 + blocks].reshape(1, hidden)
     down_b = vec[:, 12 + blocks].reshape(1, width)
 
-    z, y, o, core = (lax.axis_index(a) for a in ("z", "y", "o", "core"))
+    y, o, core = (lax.axis_index(a) for a in ("y", "o", "core"))
     group = o * 2 + y
     spots = []
     for step in range(groups):
         source = lax.rem(group - step + groups, groups)
         for flip in range(2):
             c = core if flip == 0 else 1 - core
-            k = 2 * lax.rem(z, 2) + c
-            for r in range(LINE):
-                line = lax.rem(r - k + LINE, LINE)
+            for line in range(LINE):
                 spots.append((((source // 2) * LINE + line) * 2 + lax.rem(source, 2)) * 2 + c)
     spans = jnp.take(pairing.reshape(-1), jnp.stack(spots), axis=0)
     key_places = (spans[:, None] * half + jnp.arange(half, dtype=jnp.int32)[None, :]).reshape(-1, 1)
@@ -398,29 +422,33 @@
     pre = dot(n3, w_up) + up_b
     act, gelu_back = jax.vjp(gelu_exact, pre)
     act = act.astype(BF)
-    layer_out = undeal((r2 + dot(act, w_down) + down_b).astype(BF))
+    layer_out = (r2 + dot(act, w_down) + down_b).astype(BF)
     dact = dot_t(cot, w_down)
     dpre = gelu_back(dact)[0].astype(BF)
     g_down = t_dot(act, cot).astype(BF)
     g_up = [t_dot(n3, dpre[:, b * width : (b + 1) * width]).astype(BF) for b in range(blocks)]
     g_down = g_down.reshape(4, blocks, shard, width).transpose(1, 0, 2, 3).reshape(blocks, width, width)
-    ffn = reduce_units(jnp.concatenate([jnp.stack(g_up), g_down], axis=0))
     dn3 = dot_t(dpre, w_up)
     back3, dgain3, dshift3 = norm_back(dn3, r2, gain[2])
     dr2 = cot.astype(F32) + back3
+    ffn_a = over_cores(g_down)
+    ffn_b = over_cores(jnp.stack(g_up))
 
     gc = dr2.astype(BF)
     doc = dot_t(gc, w_mid[4]).astype(BF)
-    dcq, dckv = attention_back(cquery, doc, cmixed, cmass, kv_cross, None)
-    dckv = collect(dckv, groups).astype(BF)
+    dcq, cmine, ctheirs = attention_back(cquery, doc, cmixed, cmass, kv_cross, None)
+    dcq, ffn_a, ffn_b = lax.optimization_barrier((dcq, ffn_a, ffn_b))
+    ffn_a = over_x(ffn_a)
+    dckv = collect(cmine, ctheirs, groups).astype(BF)
     dn2 = dot_t(dcq, w_mid[0])
     back2, dgain2, dshift2 = norm_back(dn2, r1, gain[1])
     dr1 = dr2 + back2
     gs = dr1.astype(BF)
     dos = dot_t(gs, w_mid[3]).astype(BF)
-    dq, dkv = attention_back(query, dos, mixed, mass, kv_self, places)
-    grad_encoded = undeal((dot_t(dckv[0], w_mid[1]) + dot_t(dckv[1], w_mid[2])).astype(BF))
-    cross = reduce_units(
+    dq, mine, theirs = attention_back(query, dos, mixed, mass, kv_self, places)
+    mine, theirs, dckv, ffn_a = lax.optimization_barrier((mine, theirs, dckv, ffn_a))
+    ffn_b = over_x(ffn_b)
+    cross = over_cores(
         jnp.stack(
             [
                 t_dot(n2, dcq).astype(BF),
@@ -430,8 +458,16 @@
             ]
         )
     )
-    dkv = collect(dkv, groups).astype(BF)
-    own = reduce_units(
+    grad_encoded = (dot_t(dckv[0], w_mid[1]) + dot_t(dckv[1], w_mid[2])).astype(BF)
+    if grad_encoded.shape == layer_out.shape:
+        layer_out, grad_encoded = undeal(jnp.stack([layer_out, grad_encoded]))
+    else:
+        layer_out, grad_encoded = undeal(layer_out), undeal(grad_encoded)
+    dkv = collect(mine, theirs, groups).astype(BF)
+    dkv, cross, ffn_b = lax.optimization_barrier((dkv, cross, ffn_b))
+    cross = over_x(cross)
+    ffn_a, ffn_b = over_ctx(ffn_a), over_ctx(ffn_b)
+    own = over_cores(
         jnp.stack(
             [
                 t_dot(n1, dq).astype(BF),
@@ -444,6 +480,8 @@
     dn1 = dot_t(dq, w_qkv[0]) + dot_t(dkv[0], w_qkv[1]) + dot_t(dkv[1], w_qkv[2])
     back1, dgain1, dshift1 = norm_back(dn1, x, gain[0])
     grad_layer = undeal((dr1 + back1).astype(BF))
+    own = over_ctx(over_x(own))
+    cross = over_ctx(cross)
 
     rows = jnp.concatenate(
         [
@@ -463,29 +501,23 @@
                     dshift3,
                 ]
             ),
-            column_sum(dpre).reshape(blocks, width),
+            column_sum(dpre).reshape(4, blocks, shard).transpose(1, 0, 2).reshape(blocks, width),
             column_sum(cot).reshape(1, width),
         ],
         axis=0,
     )
-    rows = lax.psum(rows, ("fx", "core", "o", "z", "y"))
-    me = 2 * lax.axis_index("fx") + core
-    by_shard = rows.reshape(rows.shape[0], 4, shard)
-    mine = lax.dynamic_index_in_dim(by_shard, me, axis=1, keepdims=False)
-    grad_up_bias = lax.dynamic_index_in_dim(
-        rows[12 : 12 + blocks].reshape(4, hidden // 4), me, axis=0, keepdims=False
-    )
+    mine = sum_vectors(rows)
     return (
         layer_out,
         grad_layer.astype(F32),
         grad_encoded.astype(F32),
         jnp.concatenate([own[:3], cross[:3]], axis=0),
         jnp.concatenate([own[3:], cross[3:]], axis=0),
-        jnp.concatenate([ffn[b] for b in range(blocks)], axis=1),
-        ffn[blocks:].reshape(blocks * shard, width),
+        jnp.concatenate([ffn_b[b] for b in range(blocks)], axis=1),
+        ffn_a.reshape(blocks * shard, width),
         mine[:3],
         mine[3:12],
-        grad_up_bias,
+        mine[12 : 12 + blocks].reshape(-1),
         mine[12 + blocks],
     )
 

time: 667 us -> 507 us (0.76)
  blocking collectives: 124 us -> 0 us
  starting transfers between devices: 114 us -> 85.3 us
  other arithmetic: 40.5 us -> 64.6 us
  waiting for transfers between devices: 166 us -> 145 us
  local copies, waits for them, and re-layouts: 98.2 us -> 87.7 us
    psum x1 -> x0, blocking collectives: 124 us -> none  [per_device(): rows = lax.psum(rows, ('fx', 'core', 'o', 'z', 'y'))]
    ppermute x42 -> x23, starting transfers between devices: 77.2 us -> 18.6 us  [the longest x12 9.15 us: both(): lax.ppermute(theirs, axis, SWAP).astype(F32)]
    all_to_all x6 -> x14, waiting for transfers between devices: 38.5 us -> 75.8 us  [the longest x4 34.8 us: back_z(): lax.all_to_all(jnp.broadcast_to(total, (LINE,) + total.shape[1:]), 'z', 0...]
    all_to_all x6 -> x14, starting transfers between devices: 23.1 us -> 54.5 us  [the longest x4 15.4 us: back_z(): lax.all_to_all(jnp.broadcast_to(total, (LINE,) + total.shape[1:]), 'z', 0...]
    ppermute x2, waiting for transfers between devices: 28.4 us -> 4.09 us  [collect(): lax.ppermute(sums[step].astype(BF), ('o', 'y'), back).astype(F32)]
    ppermute x42 -> x23, waiting for transfers between devices: 54.4 us -> 32.1 us  [the longest x12 24 us: both(): lax.ppermute(theirs, axis, SWAP).astype(F32)]
    unnamed x184 -> x126, local copies, waits for them, and re-layouts: 35.7 us -> 15 us
    convert_element_type x17 -> x20, other arithmetic: 19.7 us -> 32.1 us  [the longest x12 26.6 us: both(): (mine.astype(F32) + lax.ppermute(theirs, axis, SWAP).astype(F32)).astype(BF)]
  transfers between devices with their start and end apart: 69 -> 56, of which waited for: 19 -> 21; matrix products, arithmetic and copies ran while one was open for 22% -> 36% of each run, Pallas kernels for 4% -> 6%
where the time goes in v2:
time: 507 us; the launch traced here: 497 us
  waiting for transfers between devices  145 us (29%)
  local copies, waits for them, and re-layouts  87.7 us (17%)
  starting transfers between devices  85.3 us (17%)
  matrix products  70 us (14%)
  other arithmetic  64.6 us (13%)
  Pallas kernels  42.3 us (8%)
    all_to_all x4, waiting for transfers between devices, back_z(): lax.all_to_all(jnp.broadcast_to(total, (LINE,) + total.shape[1:]), 'z', 0...  34.8 us
    dot_general x10, matrix products, dot_t(): lax.dot_general(left, right, (((1,), (1,)), ((), ())), preferred_element_...  33.6 us
    convert_element_type x12, other arithmetic, both(): (mine.astype(F32) + lax.ppermute(theirs, axis, SWAP).astype(F32)).astype(BF)  26.6 us
    pallas_call x2, Pallas kernels, attention_back(): pl.pallas_call(functools.partial(backward_kernel, masked, len(kv)), grid=...  26.3 us
    dynamic_update_slice x15, local copies, waits for them, and re-layouts, assemble(): full = lax.dynamic_update_slice_in_dim(full, block, place * step, axis)  26.1 us
    dot_general x10, matrix products, dot(): return jnp.dot(left, right, preferred_element_type=F32)  24.1 us
    ppermute x12, waiting for transfers between devices, both(): lax.ppermute(theirs, axis, SWAP).astype(F32)  24 us
    squeeze x12, local copies, waits for them, and re-layouts, split_of(): theirs = lax.dynamic_index_in_dim(array, 1 - i, axis=axis, keepdims=False)  16.8 us
  transfers between devices with their start and end apart: 56, of which 21 were waited for; matrix products, arithmetic and copies ran while one was open for 36% of the time, Pallas kernels for 6%

profile of v2, /device:TPU:0, one launch (start us, length us, event | category | flops | bytes accessed | tf_op | source)
XLA Modules:
  0.0 496.9 jit_solution(16107421402528201686)
XLA Ops:
  4.7 2.5 collective-permute-start.2
  7.9 3.3 all-to-all-start.1
  12.5 2.8 broadcast_in_dim.22
  17.3 2.9 broadcast_in_dim.21
  23.0 5.2 %all-to-all-done.1 = bf16[4,17,192]{2,1,0:T(8,128)(2,1)S(1)} async-done(((bf16[4,17,192]{2,1,0:T(8,128)(2,1)}), bf16[4,17,192]{2,1,0:T(8,128)(2,1)S(1)}, u32[]{:S(2)}, u32[]{:S(2)}) %all-to-all-start.1) | async-done | bytes 26144 | tf_op jit(solution)/shard_map/all_to_all | solution.py:369
  28.2 5.1 %all-to-all-start = ((bf16[4,64,768]{2,1,0:T(8,128)(2,1)}), bf16[4,64,768]{2,1,0:T(8,128)(2,1)S(1)}, u32[]{:S(2)}, u32[]{:S(2)}) async-start(bf16[4,64,768]{2,1,0:T(8,128)(2,1)} %pad_maximum_fusion.14), calls=%async_computation | async-start | bytes 786432 | tf_op jit(solution)/shard_map/all_to_all | solution.py:191
  35.5 9.7 %all-to-all-done = bf16[4,64,768]{2,1,0:T(8,128)(2,1)S(1)} async-done(((bf16[4,64,768]{2,1,0:T(8,128)(2,1)}), bf16[4,64,768]{2,1,0:T(8,128)(2,1)S(1)}, u32[]{:S(2)}, u32[]{:S(2)}) %all-to-all-start) | async-done | bytes 393248 | tf_op jit(solution)/shard_map/all_to_all | solution.py:191
  58.1 4.4 all-to-all-start.2
  62.5 2.4 broadcast_in_dim.23
  66.8 14.2 %collective-permute-done.8 = bf16[5,192,768]{2,1,0:T(8,128)(2,1)} collective-permute-done((bf16[5,192,768]{2,1,0:T(8,128)(2,1)}, bf16[5,192,768]{2,1,0:T(8,128)(2,1)}, u32[]{:S(2)}, u32[]{:S(2)}) %collective-permute-start.8) | collective-permute-done | bytes 1474592 | tf_op jit(solution)/shard_map/ppermute | solution.py:373
  82.5 2.5 constant_dynamic-update-slice_fusion.6
  85.0 2.4 constant_dynamic-update-slice_fusion.2
  87.9 2.6 constant_dynamic-update-slice_fusion.10
  90.4 2.5 fusion.23.refs_2_
  92.9 2.6 constant_dynamic-update-slice_fusion.9
  98.2 8.3 %shard_map.203 = (bf16[256,768]{1,0:T(8,128)(2,1)S(1)}, f32[6,1,512]{2,1,0:T(1,128)S(1)}) custom-call(s32[1024,1]{1,0:T(8,128)S(1)} %add.601.refs_0_, s32[1,256]{1,0:T(1,128)S(1)} %reshape.1416.refs_1_, bf16[256,768]{1,0:T(8,128)(2,1)S(1)} %copy-done.2, bf16[2,256,768]{2,1,0:T(8,128)(2,1)S(1)} %pad_maximum_fusion.8.refs_3_.refs_6_, ...), custom_call_target="tpu_custom_call" | custom-call | flops 1610612736 | bytes 3145728 | tf_op jit(solution)/shard_map/pallas_call | solution.py:128
  106.6 2.3 collective-permute-done.15
  110.4 2.4 constant_dynamic-update-slice_fusion.5
  112.8 2.6 constant_dynamic-update-slice_fusion.8
  123.0 16.1 %collective-permute-done.12.refs_3_.refs_6_ = bf16[2,256,768]{2,1,0:T(8,128)(2,1)S(1)} collective-permute-done((bf16[2,256,768]{2,1,0:T(8,128)(2,1)S(1)}, bf16[2,256,768]{2,1,0:T(8,128)(2,1)S(1)}, u32[]{:S(2)}, u32[]{:S(2)}) %collective-permute-start.12) | collective-permute-done | bytes 786464 | tf_op jit(solution)/shard_map/ppermute | solution.py:217
  143.7 7.7 %shard_map.204 = (bf16[256,768]{1,0:T(8,128)(2,1)S(1)}, f32[6,1,512]{2,1,0:T(1,128)S(1)}) custom-call(bf16[256,768]{1,0:T(8,128)(2,1)S(1)} %fusion.25.refs_0_, bf16[2,256,768]{2,1,0:T(8,128)(2,1)S(1)} %pad_maximum_fusion.11.refs_1_.refs_4_, bf16[2,256,768]{2,1,0:T(8,128)(2,1)S(1)} %collective-permute-done.11.refs_2_.refs_5_, ...), custom_call_target="tpu_custom_call" | custom-call | flops 1610612736 | bytes 3145728 | tf_op jit(solution)/shard_map/pallas_call | solution.py:128
  153.7 3.8 convolution_add_fusion
  158.6 10.4 %fusion.95 = (bf16[3072]{0:T(1024)(128)(2,1)S(1)}, bf16[256,3072]{1,0:T(8,128)(2,1)S(1)}, f32[256,3072]{1,0:T(8,128)S(1)}) fusion(f32[256,3072]{1,0:T(8,128)S(1)} %convolution_add_fusion, bf16[256,768]{1,0:T(8,128)(2,1)S(1)} %bitcast.351, bf16[3072,768]{1,0:T(8,128)(2,1)} %constant_dynamic-update-slice_fusion), kind=kOutput, calls=%fused_computation.293 | convolution fusion | flops 1265366016 | bytes 12982272 | tf_op jit(solution)/shard_map/dot_general | solution.py:30
  169.1 4.1 multiply_reduce_fusion
  178.4 12.7 %shard_map.205 = (bf16[256,768]{1,0:T(8,128)(2,1)S(1)}, bf16[2,2,256,768]{3,2,1,0:T(8,128)(2,1)}, bf16[2,2,256,768]{3,2,1,0:T(8,128)(2,1)}) custom-call(bf16[256,768]{1,0:T(8,128)(2,1)S(1)} %fusion.25.refs_0_, bf16[256,768]{1,0:T(8,128)(2,1)S(1)} %convolution_convert_fusion.14.refs_1_, bf16[256,768]{1,0:T(8,128)(2,1)S(1)} %get-tuple-element.38.refs_2_, ...), custom_call_target="tpu_custom_call" | custom-call | flops 4026531840 | bytes 6291456 | tf_op jit(solution)/shard_map/pallas_call | solution.py:162
  201.0 2.8 convolution_convert_fusion.5
  203.8 5.3 %fusion.22 = bf16[256,768]{1,0:T(8,128)(2,1)} fusion(f32[256,768]{1,0:T(8,128)} %copy-done.8, bf16[256,3072]{1,0:T(8,128)(2,1)} %copy-done.19, bf16[3072,768]{1,0:T(8,128)(2,1)} %constant_dynamic-update-slice_fusion, f32[768]{0:T(1024)S(1)} %add.571), kind=kOutput, calls=%fused_computation.81 | convolution fusion | flops 1208549376 | bytes 7474176 | tf_op jit(solution)/shard_map/dot_general | solution.py:26
  215.2 3.6 fusion.2
  221.2 2.8 multiply_reduce_fusion.1
  228.2 13.6 %shard_map.206 = (bf16[256,768]{1,0:T(8,128)(2,1)S(1)}, bf16[2,2,256,768]{3,2,1,0:T(8,128)(2,1)}, bf16[2,2,256,768]{3,2,1,0:T(8,128)(2,1)}) custom-call(s32[1024,1]{1,0:T(8,128)S(1)} %add.601.refs_0_, s32[1,256]{1,0:T(1,128)S(1)} %reshape.1416.refs_1_, bf16[256,768]{1,0:T(8,128)(2,1)S(1)} %copy-done.3, ...), custom_call_target="tpu_custom_call" | custom-call | flops 4026531840 | bytes 6291456 | tf_op jit(solution)/shard_map/pallas_call | solution.py:162
  242.4 2.5 dynamic-slice_bitcast_fusion.6
  250.0 6.8 %collective-permute-done.24 = bf16[4,192,768]{2,1,0:T(8,128)(2,1)} collective-permute-done((bf16[4,192,768]{2,1,0:T(8,128)(2,1)}, bf16[4,192,768]{2,1,0:T(8,128)(2,1)}, u32[]{:S(2)}, u32[]{:S(2)}) %collective-permute-start.24) | collective-permute-done | bytes 1179680 | tf_op jit(solution)/shard_map/ppermute | solution.py:259
  266.1 2.7 fusion.39
  268.7 3.5 collective-permute-done.40
  273.3 3.5 all-to-all-start.11
  285.5 2.6 fusion.12
  288.1 2.7 all-to-all-done.11
  290.8 4.2 all-to-all-start.3
  295.1 4.1 collective-permute-done.27
  300.9 4.4 fusion.1
  310.6 2.7 fusion.37
  314.5 4.3 all-to-all-start.12
  323.1 2.8 fusion.58
  326.5 9.0 %all-to-all-done.12 = bf16[4,96,768]{2,1,0:T(8,128)(2,1)} async-done(((bf16[4,96,768]{2,1,0:T(8,128)(2,1)}), bf16[4,96,768]{2,1,0:T(8,128)(2,1)}, u32[]{:S(2)}, u32[]{:S(2)}) %all-to-all-start.12) | async-done | bytes 589856 | tf_op jit(solution)/shard_map/all_to_all | solution.py:289
  336.2 2.6 all-to-all-start.13
  338.8 2.4 dynamic-slice_bitcast_fusion.4
  344.9 4.6 all-to-all-done.13
  349.5 3.5 all-to-all-start.9
  355.2 2.9 fusion
  361.2 7.9 %all-to-all-done.9 = bf16[4,96,768]{2,1,0:T(8,128)(2,1)S(1)} async-done(((bf16[4,96,768]{2,1,0:T(8,128)(2,1)}), bf16[4,96,768]{2,1,0:T(8,128)(2,1)S(1)}, u32[]{:S(2)}, u32[]{:S(2)}) %all-to-all-start.9) | async-done | bytes 589856 | tf_op jit(solution)/shard_map/all_to_all | solution.py:284
  369.0 4.1 all-to-all-start.4
  378.8 5.6 %all-to-all-done.4 = bf16[4,64,768]{2,1,0:T(8,128)(2,1)} async-done(((bf16[4,64,768]{2,1,0:T(8,128)(2,1)}), bf16[4,64,768]{2,1,0:T(8,128)(2,1)}, u32[]{:S(2)}, u32[]{:S(2)}) %all-to-all-start.4) | async-done | bytes 393248 | tf_op jit(solution)/shard_map/all_to_all | solution.py:200
  386.2 4.2 all-to-all-start.10
  392.4 3.7 collective-permute-done.32
  397.6 6.8 %all-to-all-done.10 = bf16[4,96,768]{2,1,0:T(8,128)(2,1)} async-done(((bf16[4,96,768]{2,1,0:T(8,128)(2,1)}), bf16[4,96,768]{2,1,0:T(8,128)(2,1)}, u32[]{:S(2)}, u32[]{:S(2)}) %all-to-all-start.10) | async-done | bytes 589856 | tf_op jit(solution)/shard_map/all_to_all | solution.py:289
  404.5 3.5 all-to-all-start.7
  411.5 9.9 %collective-permute-done.33 = bf16[4,96,768]{2,1,0:T(8,128)(2,1)S(1)} collective-permute-done((bf16[4,96,768]{2,1,0:T(8,128)(2,1)S(1)}, bf16[4,96,768]{2,1,0:T(8,128)(2,1)S(1)}, u32[]{:S(2)}, u32[]{:S(2)}) %collective-permute-start.33) | collective-permute-done | bytes 589856 | tf_op jit(solution)/shard_map/ppermute | solution.py:259
  422.3 5.0 %all-to-all-start.5 = ((bf16[4,96,768]{2,1,0:T(8,128)(2,1)}), bf16[4,96,768]{2,1,0:T(8,128)(2,1)S(1)}, u32[]{:S(2)}, u32[]{:S(2)}) async-start(bf16[4,96,768]{2,1,0:T(8,128)(2,1)} %fusion.35), calls=%async_computation.5 | async-start | bytes 1179648 | tf_op jit(solution)/shard_map/all_to_all | solution.py:284
  436.2 4.9 all-to-all-done.5
  441.9 3.5 all-to-all-start.8
  450.9 8.6 %all-to-all-done.8 = bf16[4,96,768]{2,1,0:T(8,128)(2,1)S(1)} async-done(((bf16[4,96,768]{2,1,0:T(8,128)(2,1)}), bf16[4,96,768]{2,1,0:T(8,128)(2,1)S(1)}, u32[]{:S(2)}, u32[]{:S(2)}) %all-to-all-start.8) | async-done | bytes 589856 | tf_op jit(solution)/shard_map/all_to_all | solution.py:289
  460.3 3.5 all-to-all-start.6
  467.8 10.5 %all-to-all-done.6 = bf16[4,96,768]{2,1,0:T(8,128)(2,1)S(1)} async-done(((bf16[4,96,768]{2,1,0:T(8,128)(2,1)}), bf16[4,96,768]{2,1,0:T(8,128)(2,1)S(1)}, u32[]{:S(2)}, u32[]{:S(2)}) %all-to-all-start.6) | async-done | bytes 589856 | tf_op jit(solution)/shard_map/all_to_all | solution.py:289
  484.1 8.2 %collective-permute-done.34 = bf16[4,96,768]{2,1,0:T(8,128)(2,1)S(1)} collective-permute-done((bf16[4,96,768]{2,1,0:T(8,128)(2,1)S(1)}, bf16[4,96,768]{2,1,0:T(8,128)(2,1)S(1)}, u32[]{:S(2)}, u32[]{:S(2)}) %collective-permute-start.34) | collective-permute-done | bytes 589856 | tf_op jit(solution)/shard_map/ppermute | solution.py:293
  (397 shorter events, 169.6 us)
Async XLA Ops:
  4.2 41.7 %collective-permute-start.1 = (bf16[3,192,768]{2,1,0:T(8,128)(2,1)}, bf16[3,192,768]{2,1,0:T(8,128)(2,1)S(1)}, u32[]{:S(2)}, u32[]{:S(2)}) collective-permute-start(bf16[3,192,768]{2,1,0:T(8,128)(2,1)} %get-tuple-element.96), channel_id=1, source_target_pairs={{0,8},{8,0},{1,9},{9,1},{2,10},{10,2},{3,11},{11,3},{4,12},{12,4},... | collective-permute-start | bytes 2654216 | tf_op jit(solution)/shard_map/ppermute | solution.py:237
  4.7 40.6 %collective-permute-start.2 = (bf16[3,192,768]{2,1,0:T(8,128)(2,1)}, bf16[3,192,768]{2,1,0:T(8,128)(2,1)}, u32[]{:S(2)}, u32[]{:S(2)}) collective-permute-start(bf16[3,192,768]{2,1,0:T(8,128)(2,1)} %get-tuple-element.96), channel_id=1, source_target_pairs={{0,16},{16,0},{1,17},{17,1},{2,18},{18,2},{3,19},{19,3},{4,20},{20... | collective-permute-start | bytes 2654216 | tf_op jit(solution)/shard_map/ppermute | solution.py:371
  7.9 20.3 %all-to-all-start.1 = ((bf16[4,17,192]{2,1,0:T(8,128)(2,1)}), bf16[4,17,192]{2,1,0:T(8,128)(2,1)S(1)}, u32[]{:S(2)}, u32[]{:S(2)}) async-start(bf16[4,17,192]{2,1,0:T(8,128)(2,1)} %stack.237), calls=%async_computation.1 | async-start | bytes 98304 | tf_op jit(solution)/shard_map/all_to_all | solution.py:369
  11.2 10.9 %collective-permute-start = (bf16[2,64,768]{2,1,0:T(8,128)(2,1)S(1)}, bf16[2,64,768]{2,1,0:T(8,128)(2,1)S(1)}, u32[]{:S(2)}, u32[]{:S(2)}) collective-permute-start(bf16[2,64,768]{2,1,0:T(8,128)(2,1)S(1)} %dynamic-slice_bitcast_fusion.14), channel_id=1, source_target_pairs={{0,8},{8,0},{1,9},{9,1},{2,10},{10,2},{3,11},{11,3},{4,12},{12,4},... | collective-permute-start | bytes 589832 | tf_op jit(solution)/shard_map/ppermute | solution.py:188
  11.7 70.8 %collective-permute-start.14 = (bf16[192,3072]{1,0:T(8,128)(2,1)}, bf16[192,3072]{1,0:T(8,128)(2,1)}, u32[]{:S(2)}, u32[]{:S(2)}) collective-permute-start(bf16[192,3072]{1,0:T(8,128)(2,1)} %param.17), channel_id=1, source_target_pairs={{0,8},{8,0},{1,9},{9,1},{2,10},{10,2},{3,11},{11,3},{4,12},{12,4},... | collective-permute-start | bytes 3538952 | tf_op jit(solution)/shard_map/ppermute | solution.py:237
  11.8 73.2 %collective-permute-start.17 = (bf16[768,768]{1,0:T(8,128)(2,1)}, bf16[768,768]{1,0:T(8,128)(2,1)}, u32[]{:S(2)}, u32[]{:S(2)}) collective-permute-start(bf16[768,768]{1,0:T(8,128)(2,1)} %param.18), channel_id=1, source_target_pairs={{0,8},{8,0},{1,9},{9,1},{2,10},{10,2},{3,11},{11,3},{4,12},{12,4},... | collective-permute-start | bytes 3538952 | tf_op jit(solution)/shard_map/ppermute | solution.py:237
  22.1 65.8 %collective-permute-start.7 = (bf16[5,192,768]{2,1,0:T(8,128)(2,1)}, bf16[5,192,768]{2,1,0:T(8,128)(2,1)}, u32[]{:S(2)}, u32[]{:S(2)}) collective-permute-start(bf16[5,192,768]{2,1,0:T(8,128)(2,1)} %get-tuple-element.36), channel_id=1, source_target_pairs={{0,8},{8,0},{1,9},{9,1},{2,10},{10,2},{3,11},{11,3},{4,12},{12,4},... | collective-permute-start | bytes 4423688 | tf_op jit(solution)/shard_map/ppermute | solution.py:237
  28.2 16.9 %all-to-all-start = ((bf16[4,64,768]{2,1,0:T(8,128)(2,1)}), bf16[4,64,768]{2,1,0:T(8,128)(2,1)S(1)}, u32[]{:S(2)}, u32[]{:S(2)}) async-start(bf16[4,64,768]{2,1,0:T(8,128)(2,1)} %pad_maximum_fusion.14), calls=%async_computation | async-start | bytes 786432 | tf_op jit(solution)/shard_map/all_to_all | solution.py:191
  45.3 5.3 %collective-permute-start.3 = (bf16[3,192,768]{2,1,0:T(8,128)(2,1)}, bf16[3,192,768]{2,1,0:T(8,128)(2,1)S(1)}, u32[]{:S(2)}, u32[]{:S(2)}) collective-permute-start(bf16[3,192,768]{2,1,0:T(8,128)(2,1)} %collective-permute-done.2), channel_id=1, source_target_pairs={{0,8},{8,0},{1,9},{9,1},{2,10},{10,2},{3,11},{11,3},{4,12},{12,4},... | collective-permute-start | bytes 2654216 | tf_op jit(solution)/shard_map/ppermute | solution.py:238
  45.9 44.5 %copy-start.33 = (bf16[4,64,768]{2,1,0:T(8,128)(2,1)}, bf16[4,64,768]{2,1,0:T(8,128)(2,1)S(1)}, u32[]{:S(2)}) copy-start(bf16[4,64,768]{2,1,0:T(8,128)(2,1)S(1)} %fusion.45) | copy-start | bytes 1179652
  45.9 35.1 %collective-permute-start.8 = (bf16[5,192,768]{2,1,0:T(8,128)(2,1)}, bf16[5,192,768]{2,1,0:T(8,128)(2,1)}, u32[]{:S(2)}, u32[]{:S(2)}) collective-permute-start(bf16[5,192,768]{2,1,0:T(8,128)(2,1)} %get-tuple-element.36), channel_id=1, source_target_pairs={{0,16},{16,0},{1,17},{17,1},{2,18},{18,2},{3,19},{19,3},{4,20},{20... | collective-permute-start | bytes 4423688 | tf_op jit(solution)/shard_map/ppermute | solution.py:373
  50.6 4.8 collective-permute-start.10
  55.4 32.4 %collective-permute-start.5 = (bf16[2,256,768]{2,1,0:T(8,128)(2,1)S(1)}, bf16[2,256,768]{2,1,0:T(8,128)(2,1)S(1)}, u32[]{:S(2)}, u32[]{:S(2)}) collective-permute-start(bf16[2,256,768]{2,1,0:T(8,128)(2,1)S(1)} %pad_maximum_fusion.8.refs_3_.refs_6_), channel_id=1, source_target_pairs={{0,1},{1,0},{2,3},{3,2},{4,5},{5,4},{6,7},{7,6},{8,9},{9,8},{10,11... | collective-permute-start | bytes 2359304 | tf_op jit(solution)/shard_map/ppermute | solution.py:217
  58.1 37.5 %all-to-all-start.2 = ((bf16[2,4,64,768]{3,2,0,1:T(8,128)(2,1)}), bf16[2,4,64,768]{3,2,0,1:T(8,128)(2,1)}, u32[]{:S(2)}, u32[]{:S(2)}) async-start(bf16[2,4,64,768]{3,2,0,1:T(8,128)(2,1)} %copy.115), calls=%async_computation.2 | async-start | bytes 1572864 | tf_op jit(solution)/shard_map/all_to_all | solution.py:191
  81.0 27.9 %collective-permute-start.15 = (bf16[192,3072]{1,0:T(8,128)(2,1)}, bf16[192,3072]{1,0:T(8,128)(2,1)}, u32[]{:S(2)}, u32[]{:S(2)}) collective-permute-start(bf16[192,3072]{1,0:T(8,128)(2,1)} %param.17), channel_id=1, source_target_pairs={{0,16},{16,0},{1,17},{17,1},{2,18},{18,2},{3,19},{19,3},{4,20},{20... | collective-permute-start | bytes 3538952 | tf_op jit(solution)/shard_map/ppermute | solution.py:374
  85.0 27.9 %collective-permute-start.9 = (bf16[5,192,768]{2,1,0:T(8,128)(2,1)}, bf16[5,192,768]{2,1,0:T(8,128)(2,1)}, u32[]{:S(2)}, u32[]{:S(2)}) collective-permute-start(bf16[5,192,768]{2,1,0:T(8,128)(2,1)} %collective-permute-done.8), channel_id=1, source_target_pairs={{0,8},{8,0},{1,9},{9,1},{2,10},{10,2},{3,11},{11,3},{4,12},{12,4},... | collective-permute-start | bytes 4423688 | tf_op jit(solution)/shard_map/ppermute | solution.py:238
  87.4 9.6 %collective-permute-start.4 = (bf16[2,256,768]{2,1,0:T(8,128)(2,1)S(1)}, bf16[2,256,768]{2,1,0:T(8,128)(2,1)S(1)}, u32[]{:S(2)}, u32[]{:S(2)}) collective-permute-start(bf16[2,256,768]{2,1,0:T(8,128)(2,1)S(1)} %pad_maximum_fusion.8.refs_3_.refs_6_), channel_id=1, source_target_pairs={{0,8},{8,0},{1,9},{9,1},{2,10},{10,2},{3,11},{11,3},{4,12},{12,4},... | collective-permute-start | bytes 2359304 | tf_op jit(solution)/shard_map/ppermute | solution.py:222
  87.8 9.1 %collective-permute-start.6 = (bf16[2,256,768]{2,1,0:T(8,128)(2,1)S(1)}, bf16[2,256,768]{2,1,0:T(8,128)(2,1)}, u32[]{:S(2)}, u32[]{:S(2)}) collective-permute-start(bf16[2,256,768]{2,1,0:T(8,128)(2,1)S(1)} %collective-permute-done.5.refs_5_.refs_8_), channel_id=1, source_target_pairs={{0,8},{8,0},{1,9},{9,1},{2,10},{10,2},{3,11},{11,3},{4,12},{12,4},... | collective-permute-start | bytes 2359304 | tf_op jit(solution)/shard_map/ppermute | solution.py:222
  96.9 20.3 %copy-start.35 = (bf16[1,4,64,768]{3,2,0,1:T(8,128)(2,1)}, bf16[1,4,64,768]{3,2,0,1:T(8,128)(2,1)S(1)}, u32[]{:S(2)}) copy-start(bf16[1,4,64,768]{3,2,0,1:T(8,128)(2,1)S(1)} %get-tuple-element.111) | copy-start | bytes 1179652
  108.9 32.0 %collective-permute-start.18 = (bf16[768,768]{1,0:T(8,128)(2,1)S(1)}, bf16[768,768]{1,0:T(8,128)(2,1)S(1)}, u32[]{:S(2)}, u32[]{:S(2)}) collective-permute-start(bf16[768,768]{1,0:T(8,128)(2,1)S(1)} %copy-done.43), channel_id=1, source_target_pairs={{0,16},{16,0},{1,17},{17,1},{2,18},{18,2},{3,19},{19,3},{4,20},{20... | collective-permute-start | bytes 3538952 | tf_op jit(solution)/shard_map/ppermute | solution.py:375
  110.4 32.2 %collective-permute-start.16 = (bf16[192,3072]{1,0:T(8,128)(2,1)}, bf16[192,3072]{1,0:T(8,128)(2,1)S(1)}, u32[]{:S(2)}, u32[]{:S(2)}) collective-permute-start(bf16[192,3072]{1,0:T(8,128)(2,1)} %collective-permute-done.15), channel_id=1, source_target_pairs={{0,8},{8,0},{1,9},{9,1},{2,10},{10,2},{3,11},{11,3},{4,12},{12,4},... | collective-permute-start | bytes 3538952 | tf_op jit(solution)/shard_map/ppermute | solution.py:238
  119.1 20.0 %collective-permute-start.12 = (bf16[2,256,768]{2,1,0:T(8,128)(2,1)S(1)}, bf16[2,256,768]{2,1,0:T(8,128)(2,1)S(1)}, u32[]{:S(2)}, u32[]{:S(2)}) collective-permute-start(bf16[2,256,768]{2,1,0:T(8,128)(2,1)S(1)} %pad_maximum_fusion.11.refs_1_.refs_4_), channel_id=1, source_target_pairs={{0,1},{1,0},{2,3},{3,2},{4,5},{5,4},{6,7},{7,6},{8,9},{9,8},{10,11... | collective-permute-start | bytes 2359304 | tf_op jit(solution)/shard_map/ppermute | solution.py:217
  120.7 23.1 %collective-permute-start.11 = (bf16[2,256,768]{2,1,0:T(8,128)(2,1)S(1)}, bf16[2,256,768]{2,1,0:T(8,128)(2,1)S(1)}, u32[]{:S(2)}, u32[]{:S(2)}) collective-permute-start(bf16[2,256,768]{2,1,0:T(8,128)(2,1)S(1)} %pad_maximum_fusion.11.refs_1_.refs_4_), channel_id=1, source_target_pairs={{0,8},{8,0},{1,9},{9,1},{2,10},{10,2},{3,11},{11,3},{4,12},{12,4},... | collective-permute-start | bytes 2359304 | tf_op jit(solution)/shard_map/ppermute | solution.py:222
  122.7 28.7 %copy-start.9 = (f32[256,768]{1,0:T(8,128)}, f32[256,768]{1,0:T(8,128)S(1)}, u32[]{:S(2)}) copy-start(f32[256,768]{1,0:T(8,128)S(1)} %get-tuple-element.123) | copy-start | bytes 2359300
  139.1 4.6 collective-permute-start.13
  141.0 16.5 %collective-permute-start.19 = (bf16[768,768]{1,0:T(8,128)(2,1)S(1)}, bf16[768,768]{1,0:T(8,128)(2,1)S(1)}, u32[]{:S(2)}, u32[]{:S(2)}) collective-permute-start(bf16[768,768]{1,0:T(8,128)(2,1)S(1)} %collective-permute-done.18), channel_id=1, source_target_pairs={{0,8},{8,0},{1,9},{9,1},{2,10},{10,2},{3,11},{11,3},{4,12},{12,4},... | collective-permute-start | bytes 3538952 | tf_op jit(solution)/shard_map/ppermute | solution.py:238
  153.2 22.6 %copy-start.8 = (f32[256,768]{1,0:T(8,128)}, f32[256,768]{1,0:T(8,128)S(1)}, u32[]{:S(2)}) copy-start(f32[256,768]{1,0:T(8,128)S(1)} %get-tuple-element.125) | copy-start | bytes 2359300
  175.8 19.9 %copy-start.19 = (bf16[256,3072]{1,0:T(8,128)(2,1)}, bf16[256,3072]{1,0:T(8,128)(2,1)S(1)}, u32[]{:S(2)}) copy-start(bf16[256,3072]{1,0:T(8,128)(2,1)S(1)} %multiply_convert_fusion) | copy-start | bytes 4718596
  176.2 14.9 %copy-start.14 = (f32[256,768]{1,0:T(8,128)}, f32[256,768]{1,0:T(8,128)S(1)}, u32[]{:S(2)}) copy-start(f32[256,768]{1,0:T(8,128)S(1)} %get-tuple-element.87) | copy-start | bytes 2359300
  191.1 18.0 %collective-permute-start.22 = (bf16[2,2,256,768]{3,2,1,0:T(8,128)(2,1)}, bf16[2,2,256,768]{3,2,1,0:T(8,128)(2,1)}, u32[]{:S(2)}, u32[]{:S(2)}) collective-permute-start(bf16[2,2,256,768]{3,2,1,0:T(8,128)(2,1)} %get-tuple-element.48), channel_id=1, source_target_pairs={{0,8},{8,0},{1,9},{9,1},{2,10},{10,2},{3,11},{11,3},{4,12},{12,4},... | collective-permute-start | bytes 4718600 | tf_op jit(solution)/shard_map/ppermute | solution.py:227
  195.3 19.9 %collective-permute-start.21 = (bf16[4,2,192,768]{3,2,1,0:T(8,128)(2,1)}, bf16[4,2,192,768]{3,2,1,0:T(8,128)(2,1)}, u32[]{:S(2)}, u32[]{:S(2)}) collective-permute-start(bf16[4,2,192,768]{3,2,1,0:T(8,128)(2,1)} %dynamic-slice_bitcast_fusion.2), channel_id=1, source_target_pairs={{0,8},{8,0},{1,9},{9,1},{2,10},{10,2},{3,11},{11,3},{4,12},{12,4},... | collective-permute-start | bytes 7077896 | tf_op jit(solution)/shard_map/ppermute | solution.py:259
  200.2 18.6 %collective-permute-start.20 = (bf16[4,2,192,768]{3,2,0,1:T(8,128)(2,1)}, bf16[4,2,192,768]{3,2,0,1:T(8,128)(2,1)}, u32[]{:S(2)}, u32[]{:S(2)}) collective-permute-start(bf16[4,2,192,768]{3,2,0,1:T(8,128)(2,1)} %dynamic-slice_bitcast_fusion.3), channel_id=1, source_target_pairs={{0,8},{8,0},{1,9},{9,1},{2,10},{10,2},{3,11},{11,3},{4,12},{12,4},... | collective-permute-start | bytes 7077896 | tf_op jit(solution)/shard_map/ppermute | solution.py:259
  213.6 34.9 %collective-permute-start.23 = (bf16[2,256,768]{2,1,0:T(8,128)(2,1)}, bf16[2,256,768]{2,1,0:T(8,128)(2,1)}, u32[]{:S(2)}, u32[]{:S(2)}) collective-permute-start(bf16[2,256,768]{2,1,0:T(8,128)(2,1)} %fusion.59), channel_id=1, source_target_pairs={{1,0},{0,1},{3,2},{2,3},{5,4},{4,5},{7,6},{6,7},{9,8},{8,9},{11,10... | collective-permute-start | bytes 2359304 | tf_op jit(solution)/shard_map/ppermute | solution.py:232
  227.7 29.1 %collective-permute-start.24 = (bf16[4,192,768]{2,1,0:T(8,128)(2,1)}, bf16[4,192,768]{2,1,0:T(8,128)(2,1)}, u32[]{:S(2)}, u32[]{:S(2)}) collective-permute-start(bf16[4,192,768]{2,1,0:T(8,128)(2,1)} %dynamic-slice_bitcast_fusion.7), channel_id=1, source_target_pairs={{0,16},{16,0},{1,17},{17,1},{2,18},{18,2},{3,19},{19,3},{4,20},{20... | collective-permute-start | bytes 3538952 | tf_op jit(solution)/shard_map/ppermute | solution.py:259
  244.9 40.6 %collective-permute-start.29 = (bf16[4,192,768]{2,1,0:T(8,128)(2,1)}, bf16[4,192,768]{2,1,0:T(8,128)(2,1)}, u32[]{:S(2)}, u32[]{:S(2)}) collective-permute-start(bf16[4,192,768]{2,1,0:T(8,128)(2,1)} %dynamic-slice_bitcast_fusion.6), channel_id=1, source_target_pairs={{0,16},{16,0},{1,17},{17,1},{2,18},{18,2},{3,19},{19,3},{4,20},{20... | collective-permute-start | bytes 3538952 | tf_op jit(solution)/shard_map/ppermute | solution.py:259
  258.4 13.8 %collective-permute-start.40 = (bf16[4,96,768]{2,1,0:T(8,128)(2,1)S(1)}, bf16[4,96,768]{2,1,0:T(8,128)(2,1)S(1)}, u32[]{:S(2)}, u32[]{:S(2)}) collective-permute-start(bf16[4,96,768]{2,1,0:T(8,128)(2,1)S(1)} %dynamic-slice_bitcast_fusion.8), channel_id=1, source_target_pairs={{0,1},{1,0},{2,3},{3,2},{4,5},{5,4},{6,7},{7,6},{8,9},{9,8},{10,11... | collective-permute-start | bytes 1769480 | tf_op jit(solution)/shard_map/ppermute | solution.py:259
  259.5 17.2 %collective-permute-start.26 = (bf16[2,2,256,768]{3,2,1,0:T(8,128)(2,1)}, bf16[2,2,256,768]{3,2,1,0:T(8,128)(2,1)}, u32[]{:S(2)}, u32[]{:S(2)}) collective-permute-start(bf16[2,2,256,768]{3,2,1,0:T(8,128)(2,1)} %get-tuple-element.53), channel_id=1, source_target_pairs={{0,8},{8,0},{1,9},{9,1},{2,10},{10,2},{3,11},{11,3},{4,12},{12,4},... | collective-permute-start | bytes 4718600 | tf_op jit(solution)/shard_map/ppermute | solution.py:227
  263.9 37.0 %collective-permute-start.28 = (bf16[4,2,192,768]{3,2,1,0:T(8,128)(2,1)}, bf16[4,2,192,768]{3,2,1,0:T(8,128)(2,1)}, u32[]{:S(2)}, u32[]{:S(2)}) collective-permute-start(bf16[4,2,192,768]{3,2,1,0:T(8,128)(2,1)} %dynamic-slice_bitcast_fusion.1), channel_id=1, source_target_pairs={{0,8},{8,0},{1,9},{9,1},{2,10},{10,2},{3,11},{11,3},{4,12},{12,4},... | collective-permute-start | bytes 7077896 | tf_op jit(solution)/shard_map/ppermute | solution.py:259
  273.3 17.5 %all-to-all-start.11 = ((bf16[4,96,768]{2,1,0:T(8,128)(2,1)}), bf16[4,96,768]{2,1,0:T(8,128)(2,1)S(1)}, u32[]{:S(2)}, u32[]{:S(2)}) async-start(bf16[4,96,768]{2,1,0:T(8,128)(2,1)} %fusion.32), calls=%async_computation.11 | async-start | bytes 1179648 | tf_op jit(solution)/shard_map/all_to_all | solution.py:284
  281.7 17.5 %collective-permute-start.27 = (bf16[2,256,768]{2,1,0:T(8,128)(2,1)}, bf16[2,256,768]{2,1,0:T(8,128)(2,1)}, u32[]{:S(2)}, u32[]{:S(2)}) collective-permute-start(bf16[2,256,768]{2,1,0:T(8,128)(2,1)} %fusion.60), channel_id=1, source_target_pairs={{1,0},{0,1},{3,2},{2,3},{5,4},{4,5},{7,6},{6,7},{9,8},{8,9},{11,10... | collective-permute-start | bytes 2359304 | tf_op jit(solution)/shard_map/ppermute | solution.py:232
  290.8 22.9 %all-to-all-start.3 = ((bf16[2,4,64,768]{3,2,0,1:T(8,128)(2,1)}), bf16[2,4,64,768]{3,2,0,1:T(8,128)(2,1)}, u32[]{:S(2)}, u32[]{:S(2)}) async-start(bf16[2,4,64,768]{3,2,0,1:T(8,128)(2,1)} %pad_maximum_fusion.12), calls=%async_computation.3 | async-start | bytes 1572864 | tf_op jit(solution)/shard_map/all_to_all | solution.py:200
  310.6 44.6 %collective-permute-start.31 = (bf16[4,2,192,768]{3,2,1,0:T(8,128)(2,1)}, bf16[4,2,192,768]{3,2,1,0:T(8,128)(2,1)}, u32[]{:S(2)}, u32[]{:S(2)}) collective-permute-start(bf16[4,2,192,768]{3,2,1,0:T(8,128)(2,1)} %dynamic-slice_bitcast_fusion), channel_id=1, source_target_pairs={{0,8},{8,0},{1,9},{9,1},{2,10},{10,2},{3,11},{11,3},{4,12},{12,4},... | collective-permute-start | bytes 7077896 | tf_op jit(solution)/shard_map/ppermute | solution.py:259
  314.5 21.0 %all-to-all-start.12 = ((bf16[4,96,768]{2,1,0:T(8,128)(2,1)}), bf16[4,96,768]{2,1,0:T(8,128)(2,1)}, u32[]{:S(2)}, u32[]{:S(2)}) async-start(bf16[4,96,768]{2,1,0:T(8,128)(2,1)} %broadcast_in_dim.27), calls=%async_computation.12 | async-start | bytes 1179648 | tf_op jit(solution)/shard_map/all_to_all | solution.py:289
  320.8 22.0 %collective-permute-start.38 = (bf16[4,96,768]{2,1,0:T(8,128)(2,1)}, bf16[4,96,768]{2,1,0:T(8,128)(2,1)}, u32[]{:S(2)}, u32[]{:S(2)}) collective-permute-start(bf16[4,96,768]{2,1,0:T(8,128)(2,1)} %dynamic-slice_bitcast_fusion.9), channel_id=1, source_target_pairs={{0,1},{1,0},{2,3},{3,2},{4,5},{5,4},{6,7},{7,6},{8,9},{9,8},{10,11... | collective-permute-start | bytes 1769480 | tf_op jit(solution)/shard_map/ppermute | solution.py:259
  325.9 16.9 %copy-start.32 = (bf16[4,192,768]{2,1,0:T(8,128)(2,1)S(1)}, bf16[4,192,768]{2,1,0:T(8,128)(2,1)}, u32[]{:S(2)}) copy-start(bf16[4,192,768]{2,1,0:T(8,128)(2,1)} %fusion.12) | copy-start | bytes 3538948
  336.2 13.2 %all-to-all-start.13 = ((bf16[32,32,128]{2,1,0:T(8,128)(2,1)}), bf16[32,32,128]{2,1,0:T(8,128)(2,1)S(1)}, u32[]{:S(2)}, u32[]{:S(2)}) async-start(bf16[32,32,128]{2,1,0:T(8,128)(2,1)} %bitcast.141), calls=%async_computation.13 | async-start | bytes 524288 | tf_op jit(solution)/shard_map/all_to_all | solution.py:315
  341.2 32.0 %collective-permute-start.35 = (bf16[4,192,768]{2,1,0:T(8,128)(2,1)}, bf16[4,192,768]{2,1,0:T(8,128)(2,1)}, u32[]{:S(2)}, u32[]{:S(2)}) collective-permute-start(bf16[4,192,768]{2,1,0:T(8,128)(2,1)} %dynamic-slice_bitcast_fusion.4), channel_id=1, source_target_pairs={{0,16},{16,0},{1,17},{17,1},{2,18},{18,2},{3,19},{19,3},{4,20},{20... | collective-permute-start | bytes 3538952 | tf_op jit(solution)/shard_map/ppermute | solution.py:259
  349.5 19.6 %all-to-all-start.9 = ((bf16[4,96,768]{2,1,0:T(8,128)(2,1)}), bf16[4,96,768]{2,1,0:T(8,128)(2,1)S(1)}, u32[]{:S(2)}, u32[]{:S(2)}) async-start(bf16[4,96,768]{2,1,0:T(8,128)(2,1)} %fusion.33), calls=%async_computation.9 | async-start | bytes 1179648 | tf_op jit(solution)/shard_map/all_to_all | solution.py:284
  360.6 35.5 %collective-permute-start.32 = (bf16[4,192,768]{2,1,0:T(8,128)(2,1)}, bf16[4,192,768]{2,1,0:T(8,128)(2,1)}, u32[]{:S(2)}, u32[]{:S(2)}) collective-permute-start(bf16[4,192,768]{2,1,0:T(8,128)(2,1)} %dynamic-slice_bitcast_fusion.5), channel_id=1, source_target_pairs={{0,16},{16,0},{1,17},{17,1},{2,18},{18,2},{3,19},{19,3},{4,20},{20... | collective-permute-start | bytes 3538952 | tf_op jit(solution)/shard_map/ppermute | solution.py:259
  369.0 15.4 %all-to-all-start.4 = ((bf16[4,64,768]{2,1,0:T(8,128)(2,1)}), bf16[4,64,768]{2,1,0:T(8,128)(2,1)}, u32[]{:S(2)}, u32[]{:S(2)}) async-start(bf16[4,64,768]{2,1,0:T(8,128)(2,1)} %bitcast.100), calls=%async_computation.4 | async-start | bytes 786432 | tf_op jit(solution)/shard_map/all_to_all | solution.py:200
  375.6 20.5 %copy-start.28 = (bf16[4,2,192,768]{3,2,1,0:T(8,128)(2,1)S(1)}, bf16[4,2,192,768]{3,2,1,0:T(8,128)(2,1)}, u32[]{:S(2)}) copy-start(bf16[4,2,192,768]{3,2,1,0:T(8,128)(2,1)} %copy-done.27) | copy-start | bytes 7077892
  375.6 14.7 %collective-permute-start.36 = (bf16[4,96,768]{2,1,0:T(8,128)(2,1)}, bf16[4,96,768]{2,1,0:T(8,128)(2,1)}, u32[]{:S(2)}, u32[]{:S(2)}) collective-permute-start(bf16[4,96,768]{2,1,0:T(8,128)(2,1)} %dynamic-slice_bitcast_fusion.10), channel_id=1, source_target_pairs={{0,1},{1,0},{2,3},{3,2},{4,5},{5,4},{6,7},{7,6},{8,9},{9,8},{10,11... | collective-permute-start | bytes 1769480 | tf_op jit(solution)/shard_map/ppermute | solution.py:259
  386.2 18.3 %all-to-all-start.10 = ((bf16[4,96,768]{2,1,0:T(8,128)(2,1)}), bf16[4,96,768]{2,1,0:T(8,128)(2,1)}, u32[]{:S(2)}, u32[]{:S(2)}) async-start(bf16[4,96,768]{2,1,0:T(8,128)(2,1)} %broadcast_in_dim.26), calls=%async_computation.10 | async-start | bytes 1179648 | tf_op jit(solution)/shard_map/all_to_all | solution.py:289
  404.5 17.9 %all-to-all-start.7 = ((bf16[4,96,768]{2,1,0:T(8,128)(2,1)}), bf16[4,96,768]{2,1,0:T(8,128)(2,1)S(1)}, u32[]{:S(2)}, u32[]{:S(2)}) async-start(bf16[4,96,768]{2,1,0:T(8,128)(2,1)} %fusion.34), calls=%async_computation.7 | async-start | bytes 1179648 | tf_op jit(solution)/shard_map/all_to_all | solution.py:284
  408.0 13.4 %collective-permute-start.33 = (bf16[4,96,768]{2,1,0:T(8,128)(2,1)S(1)}, bf16[4,96,768]{2,1,0:T(8,128)(2,1)S(1)}, u32[]{:S(2)}, u32[]{:S(2)}) collective-permute-start(bf16[4,96,768]{2,1,0:T(8,128)(2,1)S(1)} %dynamic-slice_bitcast_fusion.11), channel_id=1, source_target_pairs={{0,1},{1,0},{2,3},{3,2},{4,5},{5,4},{6,7},{7,6},{8,9},{9,8},{10,11... | collective-permute-start | bytes 1769480 | tf_op jit(solution)/shard_map/ppermute | solution.py:259
  411.5 15.9 %collective-permute-start.25 = (bf16[2,2,64,768]{3,2,1,0:T(8,128)(2,1)}, bf16[2,2,64,768]{3,2,1,0:T(8,128)(2,1)S(1)}, u32[]{:S(2)}, u32[]{:S(2)}) collective-permute-start(bf16[2,2,64,768]{3,2,1,0:T(8,128)(2,1)} %bitcast.320), channel_id=1, source_target_pairs={{0,8},{8,0},{1,9},{9,1},{2,10},{10,2},{3,11},{11,3},{4,12},{12,4},... | collective-permute-start | bytes 1179656 | tf_op jit(solution)/shard_map/ppermute | solution.py:205
  422.3 18.7 %all-to-all-start.5 = ((bf16[4,96,768]{2,1,0:T(8,128)(2,1)}), bf16[4,96,768]{2,1,0:T(8,128)(2,1)S(1)}, u32[]{:S(2)}, u32[]{:S(2)}) async-start(bf16[4,96,768]{2,1,0:T(8,128)(2,1)} %fusion.35), calls=%async_computation.5 | async-start | bytes 1179648 | tf_op jit(solution)/shard_map/all_to_all | solution.py:284
  429.1 16.2 %collective-permute-start.41 = (bf16[4,96,768]{2,1,0:T(8,128)(2,1)}, bf16[4,96,768]{2,1,0:T(8,128)(2,1)S(1)}, u32[]{:S(2)}, u32[]{:S(2)}) collective-permute-start(bf16[4,96,768]{2,1,0:T(8,128)(2,1)} %all-to-all-done.12), channel_id=1, source_target_pairs={{0,1},{1,0},{2,3},{3,2},{4,5},{5,4},{6,7},{7,6},{8,9},{9,8},{10,11... | collective-permute-start | bytes 1769480 | tf_op jit(solution)/shard_map/ppermute | solution.py:293
  436.0 13.8 %collective-permute-start.30 = (bf16[2,64,768]{2,1,0:T(8,128)(2,1)S(1)}, bf16[2,64,768]{2,1,0:T(8,128)(2,1)S(1)}, u32[]{:S(2)}, u32[]{:S(2)}) collective-permute-start(bf16[2,64,768]{2,1,0:T(8,128)(2,1)S(1)} %dynamic-slice_bitcast_fusion.13), channel_id=1, source_target_pairs={{0,8},{8,0},{1,9},{9,1},{2,10},{10,2},{3,11},{11,3},{4,12},{12,4},... | collective-permute-start | bytes 589832 | tf_op jit(solution)/shard_map/ppermute | solution.py:205
  441.9 17.6 %all-to-all-start.8 = ((bf16[4,96,768]{2,1,0:T(8,128)(2,1)}), bf16[4,96,768]{2,1,0:T(8,128)(2,1)S(1)}, u32[]{:S(2)}, u32[]{:S(2)}) async-start(bf16[4,96,768]{2,1,0:T(8,128)(2,1)} %broadcast_in_dim.25), calls=%async_computation.8 | async-start | bytes 1179648 | tf_op jit(solution)/shard_map/all_to_all | solution.py:289
  446.7 18.1 %collective-permute-start.39 = (bf16[4,96,768]{2,1,0:T(8,128)(2,1)}, bf16[4,96,768]{2,1,0:T(8,128)(2,1)S(1)}, u32[]{:S(2)}, u32[]{:S(2)}) collective-permute-start(bf16[4,96,768]{2,1,0:T(8,128)(2,1)} %all-to-all-done.10), channel_id=1, source_target_pairs={{0,1},{1,0},{2,3},{3,2},{4,5},{5,4},{6,7},{7,6},{8,9},{9,8},{10,11... | collective-permute-start | bytes 1769480 | tf_op jit(solution)/shard_map/ppermute | solution.py:293
  460.3 17.9 %all-to-all-start.6 = ((bf16[4,96,768]{2,1,0:T(8,128)(2,1)}), bf16[4,96,768]{2,1,0:T(8,128)(2,1)S(1)}, u32[]{:S(2)}, u32[]{:S(2)}) async-start(bf16[4,96,768]{2,1,0:T(8,128)(2,1)} %broadcast_in_dim.24), calls=%async_computation.6 | async-start | bytes 1179648 | tf_op jit(solution)/shard_map/all_to_all | solution.py:289
  466.1 15.3 %collective-permute-start.37 = (bf16[4,96,768]{2,1,0:T(8,128)(2,1)S(1)}, bf16[4,96,768]{2,1,0:T(8,128)(2,1)}, u32[]{:S(2)}, u32[]{:S(2)}) collective-permute-start(bf16[4,96,768]{2,1,0:T(8,128)(2,1)S(1)} %all-to-all-done.8), channel_id=1, source_target_pairs={{0,1},{1,0},{2,3},{3,2},{4,5},{5,4},{6,7},{7,6},{8,9},{9,8},{10,11... | collective-permute-start | bytes 1769480 | tf_op jit(solution)/shard_map/ppermute | solution.py:293
  478.2 14.0 %collective-permute-start.34 = (bf16[4,96,768]{2,1,0:T(8,128)(2,1)S(1)}, bf16[4,96,768]{2,1,0:T(8,128)(2,1)S(1)}, u32[]{:S(2)}, u32[]{:S(2)}) collective-permute-start(bf16[4,96,768]{2,1,0:T(8,128)(2,1)S(1)} %all-to-all-done.6), channel_id=1, source_target_pairs={{0,1},{1,0},{2,3},{3,2},{4,5},{5,4},{6,7},{7,6},{8,9},{9,8},{10,11... | collective-permute-start | bytes 1769480 | tf_op jit(solution)/shard_map/ppermute | solution.py:293
  (54 other events, 264.1 us)

commit v3 on v1

v3 whole, which is shorter than its diff:
```python
import functools
import math

import jax
import jax.numpy as jnp
from jax import lax
from jax.experimental import pallas as pl
from jax.experimental.pallas import tpu as pltpu
from jax.sharding import Mesh
from jax.sharding import PartitionSpec as P

HEADS = 12
HD = 64
PAIR = 2 * HD
SCORE_SCALE = 0.125
MASK_FILL = -1e30
NORM_EPSILON = 1e-05
LINE = 4
SWAP = [(0, 1), (1, 0)]
BF = jnp.bfloat16
F32 = jnp.float32
MIB = 1 << 20


def dot(left, right):
    return jnp.dot(left, right, preferred_element_type=F32)


def dot_t(left, right):
    return lax.dot_general(left, right, (((1,), (1,)), ((), ())), preferred_element_type=F32)


def t_dot(left, right):
    return lax.dot_general(left, right, (((0,), (0,)), ((), ())), preferred_element_type=F32)


def split_heads(block):
    lane = lax.broadcasted_iota(jnp.int32, block.shape, 1)
    zero = jnp.zeros_like(block)
    return jnp.concatenate([jnp.where(lane < HD, block, zero), jnp.where(lane < HD, zero, block)], axis=0)


def join_heads(columns):
    rows = columns.shape[1] // 2
    return jnp.concatenate([columns[:HD, :rows], columns[HD:, rows:]], axis=0).T


def forward_kernel(masked, pieces, *refs):
    if masked:
        key_place_ref, query_place_ref, refs = refs[0], refs[1], refs[2:]
    query_ref, kv_refs = refs[0], refs[1 : 1 + pieces]
    out_ref, mass_ref, scores_ref = refs[1 + pieces :]
    query = split_heads(query_ref[...] * jnp.asarray(SCORE_SCALE, BF))
    piece = kv_refs[0].shape[1]
    if masked:
        query_place = query_place_ref[...]
        query_place = jnp.concatenate([query_place, query_place], axis=1)
    top = None
    for i in range(pieces):
        scores = dot_t(kv_refs[i][0], query)
        if masked:
            scores = jnp.where(key_place_ref[pl.ds(i * piece, piece), :] <= query_place, scores, MASK_FILL)
        scores_ref[pl.ds(i * piece, piece), :] = scores
        high = jnp.max(scores, axis=0, keepdims=True)
        top = high if top is None else jnp.maximum(top, high)
    mass = jnp.zeros_like(top)
    mixed = None
    for i in range(pieces):
        probs = jnp.exp(scores_ref[pl.ds(i * piece, piece), :] - top)
        mass = mass + jnp.sum(probs, axis=0, keepdims=True)
        part = t_dot(kv_refs[i][1], probs.astype(BF))
        mixed = part if mixed is None else mixed + part
    out_ref[...] = join_heads(mixed * (1.0 / mass)).astype(BF)
    mass_ref[0] = top + jnp.log(mass)


def backward_kernel(masked, pieces, *refs):
    if masked:
        key_place_ref, query_place_ref, refs = refs[0], refs[1], refs[2:]
    query_ref, dout_ref, out_ref, mass_ref = refs[:4]
    kv_refs = refs[4 : 4 + pieces]
    dquery_ref, mine_ref, theirs_ref = refs[4 + pieces :]
    query = split_heads(query_ref[...] * jnp.asarray(SCORE_SCALE, BF))
    dout = dout_ref[...]
    prod = (dout.astype(F32) * out_ref[...].astype(F32)).T
    delta = jnp.concatenate(
        [jnp.sum(prod[:HD], axis=0, keepdims=True), jnp.sum(prod[HD:], axis=0, keepdims=True)], axis=1
    )
    dout = split_heads(dout)
    log_mass = mass_ref[0]
    piece = kv_refs[0].shape[1]
    if masked:
        query_place = query_place_ref[...]
        query_place = jnp.concatenate([query_place, query_place], axis=1)
    dquery = None
    for i in range(pieces):
        keys = kv_refs[i][0]
        scores = dot_t(keys, query)
        if masked:
            scores = jnp.where(key_place_ref[pl.ds(i * piece, piece), :] <= query_place, scores, MASK_FILL)
        probs = jnp.exp(scores - log_mass)
        dprobs = dot_t(kv_refs[i][1], dout)
        dscores = (probs * (dprobs - delta)).astype(BF)
        dkv_ref = theirs_ref if i % 2 else mine_ref
        dkv_ref[i // 2, 0] = dot(dscores, query).astype(BF)
        dkv_ref[i // 2, 1] = dot(probs.astype(BF), dout).astype(BF)
        part = t_dot(keys, dscores)
        dquery = part if dquery is None else dquery + part
    dquery_ref[...] = (join_heads(dquery) * SCORE_SCALE).astype(BF)


def place_specs(masked, places):
    if not masked:
        return [], []
    key_places, query_places = places
    return [key_places, query_places], [
        pl.BlockSpec(key_places.shape, lambda h: (0, 0)),
        pl.BlockSpec(query_places.shape, lambda h: (0, 0)),
    ]


def attention(query, kv, places):
    masked = places is not None
    rows, width = query.shape
    piece = kv[0].shape[1]
    extra, extra_specs = place_specs(masked, places)
    keys = piece * len(kv)
    return pl.pallas_call(
        functools.partial(forward_kernel, masked, len(kv)),
        grid=(width // PAIR,),
        in_specs=extra_specs
        + [pl.BlockSpec((rows, PAIR), lambda h: (0, h))]
        + [pl.BlockSpec((2, piece, PAIR), lambda h: (0, 0, h))] * len(kv),
        out_specs=[
            pl.BlockSpec((rows, PAIR), lambda h: (0, h)),
            pl.BlockSpec((1, 1, 2 * rows), lambda h: (h, 0, 0)),
        ],
        out_shape=[
            jax.ShapeDtypeStruct((rows, width), BF),
            jax.ShapeDtypeStruct((width // PAIR, 1, 2 * rows), F32),
        ],
        scratch_shapes=[pltpu.VMEM((keys, 2 * rows), F32)],
        compiler_params=pltpu.CompilerParams(vmem_limit_bytes=8 * MIB + 4096 * keys),
        cost_estimate=cost(8 * rows * keys / 2**18),
    )(*extra, query, *kv)


def attention_back(query, dout, out, mass, kv, places):
    masked = places is not None
    rows, width = query.shape
    piece = kv[0].shape[1]
    extra, extra_specs = place_specs(masked, places)
    keys = piece * len(kv)
    column = pl.BlockSpec((rows, PAIR), lambda h: (0, h))
    pair = pl.BlockSpec((2, piece, PAIR), lambda h: (0, 0, h))
    groups = len(kv) // 2
    blocks = pl.BlockSpec((groups, 2, piece, PAIR), lambda h: (0, 0, 0, h))
    return pl.pallas_call(
        functools.partial(backward_kernel, masked, len(kv)),
        grid=(width // PAIR,),
        in_specs=extra_specs
        + [column, column, column, pl.BlockSpec((1, 1, 2 * rows), lambda h: (h, 0, 0))]
        + [pair] * len(kv),
        out_specs=[column, blocks, blocks],
        out_shape=[jax.ShapeDtypeStruct((rows, width), BF)]
        + [jax.ShapeDtypeStruct((groups, 2, piece, width), BF)] * 2,
        compiler_params=pltpu.CompilerParams(vmem_limit_bytes=8 * MIB + 4096 * keys),
        cost_estimate=cost(13 * rows * keys / 2**18),
    )(*extra, query, dout, out, mass, *kv)


def deal_perms():
    perms = []
    for r in range(LINE):
        perm = []
        for c in range(2):
            for z in range(LINE):
                k = (r - z) % LINE
                perm.append((c * LINE + z, (k % 2) * LINE + 2 * c + k // 2))
        perms.append(perm)
    return perms


DEAL = deal_perms()


def deal(arrays):
    if len({array.shape for array in arrays}) > 1:
        return [deal([array])[0] for array in arrays]
    _, rows, width = arrays[0].shape
    chunks = [array.reshape(LINE, rows // 2, width) for array in arrays]
    z = lax.axis_index("z")
    got = []
    for r in range(LINE):
        k = lax.rem(r - z + LINE, LINE)
        chunk = jnp.stack([lax.dynamic_index_in_dim(c, k, keepdims=False) for c in chunks])
        got.append(lax.ppermute(chunk, ("core", "z"), DEAL[r]))
    return [jnp.concatenate([g[i] for g in got], axis=0) for i in range(len(arrays))]


def undeal(arrays, kind):
    count = len(arrays)
    half = arrays[0].shape[0] // LINE
    got = []
    for r in range(LINE):
        chunk = jnp.stack([array[r * half : (r + 1) * half] for array in arrays])
        got.append(lax.ppermute(chunk, ("core", "z"), [(b, a) for a, b in DEAL[r]]))
    z = lax.axis_index("z")
    outs = []
    for i in range(count):
        mine = lax.dynamic_slice_in_dim(jnp.stack([g[i] for g in got + got]), z, LINE, axis=0)
        outs.append(mine.reshape(2, 2 * half, arrays[0].shape[1]).astype(kind[i]))
    return outs


def group_perm(groups, step):
    return [(i, (i + step) % groups) for i in range(groups)]


def to_others(own, groups):
    return [own] + [lax.ppermute(own, ("o", "y"), group_perm(groups, step)) for step in range(1, groups)]


def with_cores(blocks):
    pieces = []
    for block in blocks:
        pieces += [block, lax.ppermute(block, "core", SWAP)]
    return pieces


def collect(mine, got, groups):
    terms = [mine, got]
    for step in range(1, groups):
        back = [(b, a) for a, b in group_perm(groups, step)]
        terms.append(lax.ppermute(add([mine[step], got[step]]), ("o", "y"), back))
    return terms


def between_cores(array):
    return lax.ppermute(array, "core", SWAP)


def gather(own, other):
    return own, lax.ppermute(own, "core", SWAP), other, lax.ppermute(other, "core", SWAP)


def after(value, earlier):
    return lax.optimization_barrier((value, earlier))[0]


def add(terms):
    total = terms[0].astype(F32)
    for term in terms[1:]:
        total = total + term.astype(F32)
    return total.astype(BF)


def over_cores(keep, send):
    return [keep, lax.ppermute(send, "core", SWAP)]


def over_x(terms):
    got = lax.ppermute(add([term[1] for term in terms]), "fx", SWAP)
    return [term[0] for term in terms] + [got]


HALVES = ("y", "z0", "z1")


def exchange(array, name):
    if name == "y":
        return lax.ppermute(array, "y", SWAP)
    flip = 1 if name == "z0" else 2
    return lax.ppermute(array, "z", [(i, i ^ flip) for i in range(LINE)])


def half_index(name):
    z = lax.axis_index("z")
    return lax.axis_index("y") if name == "y" else lax.rem(z, 2) if name == "z0" else lax.div(z, 2)


def cut_rows(terms, order):
    return [term.reshape(2, 2, 2, -1, term.shape[-1]) for term in terms]


def halve(terms, name):
    i = half_index(name)
    theirs = add([lax.dynamic_index_in_dim(term, 1 - i, 0, keepdims=False) for term in terms])
    got = exchange(theirs, name)
    return [lax.dynamic_index_in_dim(term, i, 0, keepdims=False) for term in terms] + [got]


def double(part, name):
    other = exchange(part, name)
    first = half_index(name) == 0
    return jnp.concatenate([jnp.where(first, part, other), jnp.where(first, other, part)], axis=0)


def sum_down(terms, order):
    terms = cut_rows(terms, order)
    for name in order:
        terms = halve(terms, name)
    return add(terms)


def send_back(part, order, shape):
    for name in reversed(order):
        part = double(part, name)
    return part.astype(F32).reshape(shape)


def over_ctx(terms, order, shape):
    if lax.axis_size("o") > 1:
        return lax.psum(add(terms), ("o", "z", "y")).astype(F32).reshape(shape)
    return send_back(sum_down(terms, order), order, shape)


def sum_vectors(cut):
    n_ctx = lax.axis_size("o") * 2 * LINE
    cut = jnp.broadcast_to(cut[:, None], (4, n_ctx) + cut.shape[1:]).reshape((4 * n_ctx,) + cut.shape[1:])
    got = lax.all_to_all(cut, ("fx", "core", "o", "z", "y"), 0, 0, tiled=True)
    return jnp.sum(got.astype(F32), axis=0)


def standard(values):
    center = values - jnp.mean(values, axis=-1, keepdims=True)
    inverse = lax.rsqrt(jnp.mean(center * center, axis=-1, keepdims=True) + NORM_EPSILON)
    return center * inverse, inverse


def norm_back(dnormed, values, gain):
    z, inverse = standard(values)
    a = dnormed * gain
    dvalues = (
        a - jnp.mean(a, axis=-1, keepdims=True) - z * jnp.mean(a * z, axis=-1, keepdims=True)
    ) * inverse
    return dvalues, jnp.sum(dnormed * z, axis=0, keepdims=True), jnp.sum(dnormed, axis=0, keepdims=True)


def column_sum(values):
    return jnp.sum(values.astype(F32), axis=0, keepdims=True)


GAIN, BIAS, UP, DOWN = 0, 3, 12, 13
TABLE = 24
PAIR_AT, REST_AT, LAST_AT = (0, 0, 0, 0), (2, 2, 0, 0), (4, 4, 2, 2)


def vector(vec_ref, row):
    return vec_ref[row : row + 1, :]


def start_packed(pieces, slot_ref, full_ref, sems):
    n, rows = full_ref.shape[0], full_ref.shape[1] // 4
    copies = []
    for j, piece in enumerate(pieces):
        place = pl.ds(pl.multiple_of(slot_ref[j] * rows, rows), rows)
        for i in range(n):
            copy = pltpu.make_async_copy(
                piece.at[pl.ds(i * rows, rows), :], full_ref.at[i, place, :], sems.at[j * n + i]
            )
            copy.start()
            copies.append(copy)
    return copies


def start_copies(pieces, firsts, slot_ref, full_ref, sems, base):
    copies = []
    for j, piece in enumerate(pieces):
        rows = piece.shape[-2]
        place = pl.ds(pl.multiple_of(slot_ref[j] * rows, rows), rows)
        if len(piece.shape) == 3:
            source, target = piece.at[pl.ds(firsts[j], full_ref.shape[0])], full_ref.at[:, place, :]
        else:
            source, target = piece, full_ref.at[place, :]
        copy = pltpu.make_async_copy(source, target, sems.at[base + j])
        copy.start()
        copies.append(copy)
    return copies


def wait_all(copies):
    for copy in copies:
        copy.wait()


def put_grad(unit, turned, right, slot_ref, keep_ref, send_ref):
    rows = turned.shape[0] // 4
    for j in range(4):
        place = pl.ds(pl.multiple_of(slot_ref[j] * rows, rows), rows)
        block = dot(turned[place, :], right).astype(BF)
        target = send_ref if j % 2 else keep_ref
        target[j // 2, unit] = block


def self_in_kernel(slot_ref, x_ref, *refs):
    pieces, (n_ref, query_ref, kv_ref, vec_ref, full_ref, parts_ref, sems) = refs[:4], refs[4:]
    weights, shard = full_ref.shape[0], full_ref.shape[1] // 4
    extra = parts_ref.shape[1]
    small = []
    for j, piece in enumerate(pieces):
        copy = pltpu.make_async_copy(
            piece.at[pl.ds(weights * shard, extra), :], parts_ref.at[j], sems.at[4 * weights + j]
        )
        copy.start()
        small.append(copy)
    copies = start_packed(pieces, slot_ref, full_ref, sems)
    z = standard(x_ref[...].astype(F32))[0]
    wait_all(small)
    parts = [parts_ref[lax.bitwise_xor(slot_ref[0], p)].astype(F32)[:, :shard] for p in range(4)]
    own = parts_ref[0].astype(F32)[:, :shard]
    table = jnp.concatenate(parts, axis=1)
    vec_ref[0:UP, :] = table[0:UP]
    vec_ref[UP:DOWN, :] = jnp.concatenate([own[UP + i : UP + i + 1] for i in range(4)], axis=1)
    vec_ref[DOWN : DOWN + 1, :] = table[UP + 4 : UP + 5]
    normed = (z * table[GAIN : GAIN + 1] + table[BIAS + 6 : BIAS + 7]).astype(BF)
    n_ref[...] = normed
    wait_all(copies)
    kv_ref[0] = dot(normed, full_ref[1]).astype(BF)
    kv_ref[1] = (dot(normed, full_ref[2]) + table[BIAS + 1 : BIAS + 2]).astype(BF)
    query_ref[...] = (dot(normed, full_ref[0]) + table[BIAS : BIAS + 1]).astype(BF)


def cross_in_kernel(slot_ref, vec_ref, enc_ref, *refs):
    pieces, (kv_ref, full_ref, sems) = refs[:4], refs[4:]
    copies = start_copies(pieces, PAIR_AT, slot_ref, full_ref, sems, 0)
    enc = enc_ref[...]
    wait_all(copies)
    kv_ref[0] = dot(enc, full_ref[0]).astype(BF)
    kv_ref[1] = (dot(enc, full_ref[1]) + vector(vec_ref, BIAS + 4)).astype(BF)


def middle_kernel(slot_ref, vec_ref, mixed_ref, x_ref, *refs):
    pieces, (res_ref, n_ref, query_ref, full_ref, sems) = refs[:4], refs[4:]
    copies = start_copies(pieces, REST_AT, slot_ref, full_ref, sems, 0)
    wait_all(copies)
    res = x_ref[...].astype(F32) + dot(mixed_ref[...], full_ref[1]) + vector(vec_ref, BIAS + 2)
    res_ref[...] = res
    normed = (standard(res)[0] * vector(vec_ref, GAIN + 1) + vector(vec_ref, BIAS + 7)).astype(BF)
    n_ref[...] = normed
    query_ref[...] = (dot(normed, full_ref[0]) + vector(vec_ref, BIAS + 3)).astype(BF)


def before_feed_kernel(slot_ref, vec_ref, mixed_ref, res_ref, *refs):
    pieces, (out_ref, n_ref, full_ref, sems) = refs[:4], refs[4:]
    wait_all(start_copies(pieces, LAST_AT, slot_ref, full_ref, sems, 0))
    res = res_ref[...] + dot(mixed_ref[...], full_ref[0]) + vector(vec_ref, BIAS + 5)
    out_ref[...] = res
    n_ref[...] = (standard(res)[0] * vector(vec_ref, GAIN + 2) + vector(vec_ref, BIAS + 8)).astype(BF)


def feed_kernel(vec_ref, up_ref, down_ref, *refs):
    normed_refs, cot_refs = refs[:4], refs[4:8]
    dn_keep, dn_send, out_keep, out_send, act_ref, dpre_ref, rows_ref = refs[8:]
    bias = vector(vec_ref, UP)
    total = None
    for j in (1, 3, 0, 2):
        pre = dot(normed_refs[j][...], up_ref[...]) + bias
        phi = 0.5 * (1.0 + lax.erf(pre * math.sqrt(0.5)))
        slope = phi + pre * (jnp.exp(-0.5 * pre * pre) * (1.0 / math.sqrt(2.0 * math.pi)))
        act = (pre * phi).astype(BF)
        dpre = (dot_t(cot_refs[j][...], down_ref[...]) * slope).astype(BF)
        out, dn = (out_send, dn_send) if j % 2 else (out_keep, dn_keep)
        dn[j // 2] = dot_t(dpre, up_ref[...]).astype(BF)
        out[j // 2] = dot(act, down_ref[...]).astype(BF)
        act_ref[j] = act
        dpre_ref[j] = dpre
        sums = column_sum(dpre)
        total = sums if total is None else total + sums
    rows_ref[0:1, :] = total


def feed_grad_kernel(act_ref, dpre_ref, *refs):
    normed_refs, cot_refs, (cut_ref,) = refs[:4], refs[4:8], refs[8:]
    quarter, half = cut_ref.shape[-2:]

    def put(grad, first):
        for p in range(4):
            for q in range(4):
                rows = grad[(4 * p + q) * quarter : (4 * p + q + 1) * quarter].astype(BF)
                cut_ref[q, 0, first + p] = rows[:, :half]
                cut_ref[q, 1, first + p] = rows[:, half:]

    total = None
    for j in range(4):
        part = t_dot(normed_refs[j][...], dpre_ref[j])
        total = part if total is None else total + part
    put(total, 0)
    total = None
    for j in range(4):
        part = t_dot(act_ref[j], cot_refs[j][...])
        total = part if total is None else total + part
    put(total, 4)


def after_feed_kernel(slot_ref, vec_ref, dn_ref, dn_near_ref, dn_far_ref, res_ref, cot_ref, *refs):
    pieces, (dres_ref, dout_ref, rows_ref, full_ref, sems) = refs[:4], refs[4:]
    copies = start_copies(pieces, LAST_AT, slot_ref, full_ref, sems, 0)
    dn = dn_ref[0].astype(F32) + dn_near_ref[0].astype(F32) + dn_far_ref[...].astype(F32)
    cot = cot_ref[...].astype(F32)
    dvalues, dgain, dshift = norm_back(dn, res_ref[...], vector(vec_ref, GAIN + 2))
    dres = cot + dvalues
    dres_ref[...] = dres
    branch = dres.astype(BF)
    wait_all(copies)
    dout_ref[...] = dot_t(branch, full_ref[0]).astype(BF)
    rows_ref[0:1, :] = dgain
    rows_ref[1:2, :] = dshift
    rows_ref[2:3, :] = column_sum(branch)
    rows_ref[3:4, :] = column_sum(cot)


def middle_back_kernel(slot_ref, vec_ref, dquery_ref, n_ref, res_ref, dres_ref, mixed_ref, cmixed_ref, *refs):
    pieces, (dout_res_ref, dout_ref, keep_ref, send_ref, rows_ref, full_ref, turned_ref, sems) = refs[:4], refs[4:]
    copies = start_copies(pieces, REST_AT, slot_ref, full_ref, sems, 0)
    turned_ref[...] = n_ref[...].T
    dquery = dquery_ref[...]
    put_grad(0, turned_ref, dquery, slot_ref, keep_ref, send_ref)
    wait_all(copies)
    dn = dot_t(dquery, full_ref[0])
    dvalues, dgain, dshift = norm_back(dn, res_ref[...], vector(vec_ref, GAIN + 1))
    turned_ref[...] = cmixed_ref[...].T
    put_grad(2, turned_ref, dres_ref[...].astype(BF), slot_ref, keep_ref, send_ref)
    dres = dres_ref[...] + dvalues
    dout_res_ref[...] = dres
    branch = dres.astype(BF)
    dout_ref[...] = dot_t(branch, full_ref[1]).astype(BF)
    turned_ref[...] = mixed_ref[...].T
    put_grad(1, turned_ref, branch, slot_ref, keep_ref, send_ref)
    rows_ref[0:1, :] = dgain
    rows_ref[1:2, :] = dshift
    rows_ref[2:3, :] = column_sum(dquery)
    rows_ref[3:4, :] = column_sum(branch)


def total_of(parts):
    total = parts[0][0].astype(F32) + parts[1][0].astype(F32)
    for part in parts[2:]:
        total = total + part[...].astype(F32)
    return total.astype(BF)


def cross_back_kernel(count, slot_ref, enc_ref, n_ref, dquery_ref, *refs):
    parts, pieces = refs[:count], refs[count : count + 4]
    denc_ref, keep_ref, send_ref, rows_ref, full_ref, turned_ref, turned_enc_ref, sems = refs[count + 4 :]
    copies = start_copies(pieces, PAIR_AT, slot_ref, full_ref, sems, 0)
    turned_ref[...] = n_ref[...].T
    put_grad(2, turned_ref, dquery_ref[...], slot_ref, keep_ref, send_ref)
    dkv = total_of(parts)
    turned_enc_ref[...] = enc_ref[...].T
    put_grad(0, turned_enc_ref, dkv[0], slot_ref, keep_ref, send_ref)
    put_grad(1, turned_enc_ref, dkv[1], slot_ref, keep_ref, send_ref)
    rows_ref[0:1, :] = column_sum(dkv[1])
    wait_all(copies)
    denc_ref[...] = (dot_t(dkv[0], full_ref[0]) + dot_t(dkv[1], full_ref[1])).astype(BF)


def self_back_kernel(count, slot_ref, vec_ref, x_ref, n_ref, dquery_ref, dres_ref, up_ref, ffn_ref, mid_ref, enc_ref, res_ref, out_ref, out_near_ref, out_far_ref, *refs):
    parts, pieces = refs[:count], refs[count : count + 4]
    dx_ref, layer_ref, keep_ref, send_ref, cut_ref, full_ref, turned_ref, sems = refs[count + 4 :]
    copies = start_packed(pieces, slot_ref, full_ref, sems)
    dkv = total_of(parts)
    dquery = dquery_ref[...]
    turned_ref[...] = n_ref[...].T
    put_grad(0, turned_ref, dkv[0], slot_ref, keep_ref, send_ref)
    put_grad(1, turned_ref, dkv[1], slot_ref, keep_ref, send_ref)
    out = out_ref[0].astype(F32) + out_near_ref[0].astype(F32) + out_far_ref[...].astype(F32)
    layer_ref[...] = (res_ref[...] + out + vector(vec_ref, DOWN)).astype(BF)
    wait_all(copies)
    dn = dot_t(dquery, full_ref[0]) + dot_t(dkv[0], full_ref[1]) + dot_t(dkv[1], full_ref[2])
    dvalues, dgain, dshift = norm_back(dn, x_ref[...].astype(F32), vector(vec_ref, GAIN))
    dx_ref[...] = (dres_ref[...] + dvalues).astype(BF)
    rows = [
        dgain,
        mid_ref[0:1, :],
        ffn_ref[0:1, :],
        column_sum(dquery),
        column_sum(dkv[1]),
        mid_ref[3:4, :],
        mid_ref[2:3, :],
        enc_ref[0:1, :],
        ffn_ref[2:3, :],
        dshift,
        mid_ref[1:2, :],
        ffn_ref[1:2, :],
    ]
    shard = dgain.shape[1] // 4
    common = jnp.concatenate(rows + [ffn_ref[3:4, :]], axis=0)
    pad = jnp.zeros((cut_ref.shape[1] - common.shape[0] - 4, shard), F32)
    for p in range(4):
        up = jnp.where(slot_ref[0] == p, up_ref[0:1, :], 0.0)
        ups = [up[:, i * shard : (i + 1) * shard] for i in range(4)]
        cut_ref[p] = jnp.concatenate([common[:, p * shard : (p + 1) * shard]] + ups + [pad], axis=0).astype(BF)


ROWS_CUT = 32
WHOLE = pl.BlockSpec(memory_space=pltpu.VMEM)
LEFT = pl.BlockSpec(memory_space=pl.ANY)
SCALARS = pl.BlockSpec(memory_space=pltpu.SMEM)


def cost(microseconds):
    return pl.CostEstimate(flops=0, bytes_accessed=int(microseconds * 3.5e6), transcendentals=0)


def dense(kernel, scalars, blocks, pieces, outs, scratch, microseconds, copies=None):
    copies = len(pieces) if copies is None else copies
    held = sum(math.prod(b.shape) * b.dtype.itemsize for b in blocks)
    held += sum(math.prod(shape) * jnp.dtype(kind).itemsize for shape, kind in outs)
    held += sum(math.prod(ref.shape) * jnp.dtype(ref.dtype).itemsize for ref in scratch)
    return pl.pallas_call(
        kernel,
        in_specs=[SCALARS] * len(scalars) + [WHOLE] * len(blocks) + [LEFT] * len(pieces),
        out_specs=[WHOLE] * len(outs),
        out_shape=[jax.ShapeDtypeStruct(shape, kind) for shape, kind in outs],
        scratch_shapes=scratch + ([pltpu.SemaphoreType.DMA((copies,))] if pieces else []),
        compiler_params=pltpu.CompilerParams(vmem_limit_bytes=8 * MIB + held),
        cost_estimate=cost(microseconds),
    )(*scalars, *blocks, *pieces)


def hold(*values):
    return lax.optimization_barrier(values)


def per_device(
    layer_in,
    encoded,
    pairing,
    attn_weight,
    out_weight,
    up_weight,
    down_weight,
    norm_gains,
    bias_rows,
    up_bias,
    down_bias,
    out_cotangent,
):
    seqs, local_rows, width = layer_in.shape
    outer = lax.axis_size("o")
    groups = outer * 2
    half = local_rows // 2
    shard = attn_weight.shape[1]
    hidden = up_weight.shape[1]
    blocks = hidden // width
    rows = LINE * half
    enc_rows = LINE * (encoded.shape[1] // 2)
    fx, y, z, o, core = (lax.axis_index(a) for a in ("fx", "y", "z", "o", "core"))

    vectors = jnp.concatenate(
        [norm_gains, bias_rows, up_bias.reshape(blocks, shard), down_bias.reshape(1, shard)], axis=0
    )
    vectors = jnp.pad(vectors, ((0, ROWS_CUT - vectors.shape[0]), (0, width - shard)))
    slots = jnp.stack([2 * fx + core, 2 * fx + 1 - core, 2 - 2 * fx + core, 3 - 2 * fx - core])
    qkv_shard = jnp.concatenate([attn_weight[:3].reshape(3 * shard, width), vectors], axis=0)
    qkv_other = lax.ppermute(qkv_shard, "fx", SWAP)
    qkv_near = between_cores(qkv_shard)
    x_bf, enc_bf, cot = deal([layer_in, encoded, out_cotangent])

    group = o * 2 + y
    spots = []
    for step in range(groups):
        source = lax.rem(group - step + groups, groups)
        for flip in range(2):
            c = core if flip == 0 else 1 - core
            k = 2 * lax.rem(z, 2) + c
            for r in range(LINE):
                line = lax.rem(r - k + LINE, LINE)
                spots.append((((source // 2) * LINE + line) * 2 + lax.rem(source, 2)) * 2 + c)
    spans = jnp.take(pairing.reshape(-1), jnp.stack(spots), axis=0)
    key_places = (spans[:, None] * half + jnp.arange(half, dtype=jnp.int32)[None, :]).reshape(-1, 1)
    query_places = key_places[:rows].reshape(1, -1)
    places = (key_places, query_places)

    product = 2 * rows * width * width
    square = (width, width)
    act, real = ((rows, width), BF), ((rows, width), F32)
    turned = pltpu.VMEM((width, rows), BF)

    def weights(n):
        return pltpu.VMEM((n,) + square, BF)

    def grads(n):
        return [((2, n, shard, width), BF)] * 2

    note = ((16, width), F32)

    mid_shard = jnp.concatenate([attn_weight[4:], attn_weight[3:4], out_weight], axis=0)
    x_bf, enc_bf, cot, qkv_other, qkv_near, mid_shard, pair_shard, rest_shard, up_weight = hold(
        x_bf, enc_bf, cot, qkv_other, qkv_near, mid_shard, attn_weight[4:], mid_shard[2:], up_weight
    )
    w_qkv = (qkv_shard, qkv_near, qkv_other, between_cores(qkv_other))
    pair_other = lax.ppermute(pair_shard, "fx", SWAP)
    mid_near = between_cores(mid_shard)
    extra = ROWS_CUT
    n1, query, kv, vec = dense(
        self_in_kernel,
        [slots],
        [x_bf],
        w_qkv,
        [act, act, ((2, rows, width), BF), ((TABLE, width), F32)],
        [weights(3), pltpu.VMEM((4, extra, width), BF)],
        4,
        copies=16,
    )
    n1, query, kv, vec = hold(n1, query, kv, vec)
    kv_self = to_others(kv, groups)
    near_self = between_cores(kv)
    pair_other, rest_shard, mid_near = hold(pair_other, rest_shard, mid_near)
    rest_other = lax.ppermute(rest_shard, "fx", SWAP)
    w_pair = (mid_shard, mid_near, pair_other, between_cores(pair_other))
    (kv,) = dense(
        cross_in_kernel, [slots], [vec, enc_bf], w_pair, [((2, enc_rows, width), BF)], [weights(2)], 3.5
    )
    kv_self, near_self, kv = hold(kv_self, near_self, kv)
    kv_cross = to_others(kv, groups)
    near_cross = between_cores(kv)
    kv_self = [kv_self[0], near_self] + with_cores(kv_self[1:])
    mixed, mass = attention(query, kv_self, places)
    up_cut = up_weight.reshape(shard, 4, width).transpose(1, 0, 2)
    mixed, mass, up_cut, rest_other, cot = hold(mixed, mass, up_cut, rest_other, cot)
    w_rest = (mid_shard, mid_near, rest_other, between_cores(rest_other))
    up_own = lax.all_to_all(up_cut, ("fx", "core"), 0, 0, tiled=True).reshape(width, width)
    cot_other = lax.ppermute(cot, "fx", SWAP)
    cot_near = between_cores(cot)
    r1, n2, cquery = dense(middle_kernel, [slots], [vec, mixed, x_bf], w_rest, [real, act, act], [weights(2)], 3.3)
    r1, n2, cquery, kv_cross, near_cross = hold(r1, n2, cquery, kv_cross, near_cross)
    kv_cross = [kv_cross[0], near_cross] + with_cores(kv_cross[1:])
    cmixed, cmass = attention(cquery, kv_cross, None)
    cmixed, cmass, cot_other, cot_near, up_own = hold(cmixed, cmass, cot_other, cot_near, up_own)
    r2, n3 = dense(before_feed_kernel, [slots], [vec, cmixed, r1], w_rest, [real, act], [weights(1)], 2.7)
    n3_other = lax.ppermute(n3, "fx", SWAP)
    cots = (cot, cot_near, cot_other, between_cores(cot_other))
    n3s = (n3, between_cores(n3), n3_other, between_cores(n3_other))
    pair = ((2, rows, width), BF)
    four = ((4, rows, width), BF)
    dn_keep, dn_send, out_keep, out_send, hidden_act, dpre, up_rows = dense(
        feed_kernel,
        [],
        [vec, up_own, down_weight] + list(n3s) + list(cots),
        [],
        [pair, pair, pair, pair, four, four, ((8, width), F32)],
        [],
        8,
    )

    order = ("y", "z0", "z1")
    single = outer == 1

    def step(terms, name):
        return halve(terms, name) if single else terms

    dn_got = between_cores(dn_send)
    dn_keep, dn_got, hidden_act, dpre = hold(dn_keep, dn_got, hidden_act, dpre)
    dn_far = lax.ppermute(add([dn_keep[1], dn_got[1]]), "fx", SWAP)
    (feed,) = dense(
        feed_grad_kernel,
        [],
        [hidden_act, dpre] + list(n3s) + list(cots),
        [],
        [((4, 2, 8, shard // 4, width // 2), BF)],
        [],
        6,
    )
    dn_far, feed, out_keep, out_send = hold(dn_far, feed, out_keep, out_send)
    feed = [feed.reshape((2, 2, 2) + feed.shape[2:])]
    feed = step(feed, "y")
    dr2, doc, ffn_rows = dense(
        after_feed_kernel, [slots], [vec, dn_keep, dn_got, dn_far, r2, cot], w_rest, [real, act, note], [weights(1)], 2.7
    )

    dcq, cmine, ctheirs = attention_back(cquery, doc, cmixed, cmass, kv_cross, None)
    dcq, cmine, ctheirs, feed, dr2, ffn_rows = hold(dcq, cmine, ctheirs, feed, dr2, ffn_rows)
    cgot = between_cores(ctheirs)
    feed = step(feed, "z0")
    dr1, dos, middle_keep, middle_send, mid_rows = dense(
        middle_back_kernel,
        [slots],
        [vec, dcq, n2, r1, dr2, mixed, cmixed],
        w_rest,
        [real, act] + grads(3) + [note],
        [weights(2), turned],
        6,
    )
    dr1, dos, middle_keep, middle_send, mid_rows, cgot, cmine = hold(
        dr1, dos, middle_keep, middle_send, mid_rows, cgot, cmine
    )
    dckv = collect(cmine, cgot, groups)
    middle_got = between_cores(middle_send)
    dq, mine, theirs = attention_back(query, dos, mixed, mass, kv_self, places)
    dq, mine, theirs, dckv, feed, middle_keep, middle_got = hold(dq, mine, theirs, dckv, feed, middle_keep, middle_got)
    got = between_cores(theirs)
    middle = over_x([middle_keep, middle_got])
    feed = step(feed, "z1")
    mine, got, out_keep, out_send = hold(mine, got, out_keep, out_send)
    dkv = collect(mine, got, groups)
    out_got = between_cores(out_send)
    grad_encoded, late_keep, late_send, enc_rows_sum = dense(
        functools.partial(cross_back_kernel, len(dckv)),
        [slots],
        [enc_bf, n1, dq] + dckv,
        w_pair,
        [((enc_rows, width), BF)] + grads(3) + [note],
        [weights(2), turned, pltpu.VMEM((width, enc_rows), BF)],
        6,
    )
    grad_encoded, late_keep, late_send, middle, feed, out_keep, out_got = hold(
        grad_encoded, late_keep, late_send, middle, feed, out_keep, out_got
    )
    out_far = lax.ppermute(add([out_keep[1], out_got[1]]), "fx", SWAP)
    (grad_encoded,) = undeal([grad_encoded], [F32])
    late_got = between_cores(late_send)
    middle = cut_rows(middle, order)
    middle = step(middle, "y")
    dkv, late_keep, late_got, out_far, feed, grad_encoded = hold(dkv, late_keep, late_got, out_far, feed, grad_encoded)
    late = over_x([late_keep, late_got])
    grad_layer, layer_out, keep, send, cut = dense(
        functools.partial(self_back_kernel, len(dkv)),
        [slots],
        [vec, x_bf, n1, dq, dr1, up_rows, ffn_rows, mid_rows, enc_rows_sum, r2, out_keep, out_got, out_far] + dkv,
        w_qkv,
        [act, act] + grads(2) + [((4, ROWS_CUT, shard), BF)],
        [weights(3), turned],
        7,
        copies=12,
    )
    if single:
        feed = add(feed)
        feed_up = lax.all_to_all(feed[:4], ("fx", "core"), 0, 0, tiled=True)
        feed = jnp.concatenate([feed_up, feed[4:]], axis=0)[None]
    grad_layer, layer_out, keep, send, cut, middle, feed, late = hold(
        grad_layer, layer_out, keep, send, cut, middle, feed, late
    )
    if single:
        got = between_cores(send)
        feed = double(feed, "z1")
        middle = halve(middle, "z0")
        late = halve(cut_rows(late, order), "y")
        keep, got, feed, middle, late, grad_layer, layer_out = hold(keep, got, feed, middle, late, grad_layer, layer_out)
        own = over_x([keep, got])
        feed = double(feed, "z0")
        middle = halve(middle, "z1")
        late = halve(late, "z0")
        own, feed, middle, late, grad_layer, layer_out = hold(own, feed, middle, late, grad_layer, layer_out)
        own = add(own).reshape(2 * LINE, -1, width)
        own = lax.all_to_all(own, ("z", "y"), 0, 0, tiled=True)
        feed = double(feed, "y")
        middle = double(add(middle), "z1")
        late = halve(late, "z1")
        own, feed, middle, late, grad_layer, layer_out = hold(own, feed, middle, late, grad_layer, layer_out)
        own = jnp.sum(own.astype(F32), axis=0, keepdims=True).astype(BF)
        own = lax.all_to_all(jnp.broadcast_to(own, (2 * LINE,) + own.shape[1:]), ("z", "y"), 0, 0, tiled=True)
        middle = double(middle, "z0")
        late = double(add(late), "z1")
        own, middle, late, grad_layer, layer_out, cut = hold(own, middle, late, grad_layer, layer_out, cut)
        total = sum_vectors(cut)
        middle = double(middle, "y")
        late = double(late, "z0")
        layer_out, grad_layer = undeal([layer_out, grad_layer], [BF, F32])
        middle, late = hold(middle, late)
        late = double(late, "y").astype(F32).reshape(3, shard, width)
        middle = middle.astype(F32).reshape(3, shard, width)
        own = own.astype(F32).reshape(2, shard, width)
        feed = feed.astype(F32).reshape(2, 2, 2, 8, shard // 4, width // 2)
    else:
        own = over_ctx(over_x(over_cores(keep, send)), (), (2, shard, width))
        total = sum_vectors(cut)
        layer_out, grad_layer = undeal([layer_out, grad_layer], [BF, F32])
        feed = lax.psum(feed[0], ("o", "z", "y"))
        feed_up = feed[:, :, :, :4].transpose(3, 0, 1, 2, 4, 5)
        feed_up = lax.all_to_all(feed_up, ("fx", "core"), 0, 0, tiled=True).transpose(1, 2, 3, 0, 4, 5)
        feed = jnp.concatenate([feed_up, feed[:, :, :, 4:]], axis=3).astype(F32)
        middle = over_ctx([t.reshape(3, shard, width) for t in middle], order, (3, shard, width))
        late = over_ctx(late, order, (3, shard, width))
    g_up = feed[:, :, :, :4].transpose(0, 1, 4, 3, 2, 5).reshape(shard, hidden)
    g_down = feed[:, :, :, 4:].transpose(3, 0, 1, 4, 2, 5).reshape(hidden // 4, width)
    return (
        layer_out,
        grad_layer,
        grad_encoded,
        jnp.concatenate([late[2:], own, middle[:1], late[:2]], axis=0),
        middle[1:],
        g_up,
        g_down,
        total[:3],
        total[3:12],
        total[13 : 13 + blocks].reshape(-1),
        total[12],
    )


def solution(mesh):
    ctx = mesh.shape["ctx"]
    grid = Mesh(mesh.devices.reshape(2, 2, ctx // (2 * LINE), LINE, 2), ("fx", "core", "o", "z", "y"))
    fsdp = ("fx", "core")
    rows = P(fsdp, ("o", "z", "y"), None)
    weights = (
        P(None, fsdp, None),
        P(None, fsdp, None),
        P(fsdp, None),
        P(fsdp, None),
        P(None, fsdp),
        P(None, fsdp),
        P(fsdp),
        P(fsdp),
    )
    return jax.shard_map(
        per_device,
        mesh=grid,
        in_specs=(rows, rows, P()) + weights + (rows,),
        out_specs=(rows, rows, rows) + weights,
        check_vma=False,
    )
```

time: 667 us -> 479 us (0.72)
  the two profiles are of different devices: /device:TPU:0 before, /device:TPU:11 now
where the time goes in v3:
time: 479 us; the launch traced here: 471 us
  waiting for transfers between devices  133 us (28%)
  starting transfers between devices  113 us (24%)
  local copies, waits for them, and re-layouts  97.1 us (20%)
  Pallas kernels  86.3 us (18%)
  other arithmetic  39.3 us (8%)
    unnamed x279, local copies, waits for them, and re-layouts  50.4 us
    pallas_call x10, Pallas kernels, dense(): pl.pallas_call(kernel, in_specs=[SCALARS] * len(scalars) + [WHOLE] * len(...  42.8 us
    ppermute x12, waiting for transfers between devices, exchange(): return lax.ppermute(array, 'z', [(i, i ^ flip) for i in range(LINE)])  34.2 us
    ppermute x8, starting transfers between devices, undeal(): got.append(lax.ppermute(chunk, ('core', 'z'), [(b, a) for a, b in DEAL[r]]))  31.7 us
    pallas_call x2, Pallas kernels, attention_back(): pl.pallas_call(functools.partial(backward_kernel, masked, len(kv)), grid=...  26.8 us
    ppermute x6, waiting for transfers between devices, exchange(): return lax.ppermute(array, 'y', SWAP)  20.4 us
    convert_element_type x17, other arithmetic, add(): return total.astype(BF)  18.5 us
    squeeze x29, local copies, waits for them, and re-layouts, halve(): lax.dynamic_index_in_dim(term, i, 0, keepdims=False)  18.4 us
  transfers between devices with their start and end apart: 69, of which 27 were waited for; matrix products, arithmetic and copies ran while one was open for 16% of the time, Pallas kernels for 16%

profile of v3, /device:TPU:11, one launch (start us, length us, event | category | flops | bytes accessed | tf_op | source)
XLA Modules:
  0.0 471.0 jit_solution(1541080461383151719)
XLA Ops:
  4.7 4.3 collective-permute-start
  9.3 2.3 collective-permute-start.2
  14.8 3.5 collective-permute-done
  18.3 1.9 collective-permute-start.3
  20.2 8.4 %collective-permute-done.1 = bf16[3,64,768]{2,1,0:T(8,128)(2,1)S(1)} collective-permute-done((bf16[3,64,768]{2,1,0:T(8,128)(2,1)S(1)}, bf16[3,64,768]{2,1,0:T(8,128)(2,1)S(1)}, u32[]{:S(2)}, u32[]{:S(2)}) %collective-permute-start.1) | collective-permute-done | bytes 294944 | tf_op jit(solution)/shard_map/ppermute | solution.py:197
  28.6 2.9 collective-permute-done.2
  31.5 3.1 collective-permute-done.3
  38.1 3.1 collective-permute-done.6.refs_3_.refs_6_
  42.5 4.4 shard_map.203
  50.1 2.0 collective-permute-done.9.refs_2_.refs_5_
  55.9 3.6 shard_map.204.refs_1_.refs_4_
  59.5 8.2 %collective-permute-done.7.refs_5_.refs_8_ = bf16[2,256,768]{2,1,0:T(8,128)(2,1)} collective-permute-done((bf16[2,256,768]{2,1,0:T(8,128)(2,1)}, bf16[2,256,768]{2,1,0:T(8,128)(2,1)}, u32[]{:S(2)}, u32[]{:S(2)}) %collective-permute-start.7) | collective-permute-done | bytes 786464 | tf_op jit(solution)/shard_map/ppermute | solution.py:221
  71.1 2.4 copy.45
  73.5 8.3 %shard_map.205 = (bf16[256,768]{1,0:T(8,128)(2,1)S(1)}, f32[6,1,512]{2,1,0:T(1,128)S(1)}) custom-call(s32[1024,1]{1,0:T(8,128)S(1)} %copy-done.7, s32[1,256]{1,0:T(1,128)S(1)} %reshape.1153.refs_1_, bf16[256,768]{1,0:T(8,128)(2,1)S(1)} %copy-done.52, bf16[2,256,768]{2,1,0:T(8,128)(2,1)} %get-tuple-element.222.refs_3_.refs_6_, ...), custom_call_target="tpu_custom_call" | custom-call | bytes 28000000 | tf_op jit(solution)/shard_map/pallas_call | solution.py:128
  84.6 5.6 %all-to-all-start = ((bf16[4,192,768]{2,1,0:T(8,128)(2,1)}), bf16[4,192,768]{2,1,0:T(8,128)(2,1)}, u32[]{:S(2)}, u32[]{:S(2)}) async-start(bf16[4,192,768]{2,1,0:T(8,128)(2,1)} %bitcast.246), calls=%async_computation | async-start | bytes 2359296 | tf_op jit(solution)/shard_map/all_to_all | solution.py:724
  91.2 3.3 shard_map.206
  95.3 6.2 %collective-permute-done.15.refs_3_.refs_6_ = bf16[2,256,768]{2,1,0:T(8,128)(2,1)} collective-permute-done((bf16[2,256,768]{2,1,0:T(8,128)(2,1)}, bf16[2,256,768]{2,1,0:T(8,128)(2,1)}, u32[]{:S(2)}, u32[]{:S(2)}) %collective-permute-start.15) | collective-permute-done | bytes 786464 | tf_op jit(solution)/shard_map/ppermute | solution.py:221
  105.0 8.5 %shard_map.207 = (bf16[256,768]{1,0:T(8,128)(2,1)S(1)}, f32[6,1,512]{2,1,0:T(1,128)S(1)}) custom-call(bf16[256,768]{1,0:T(8,128)(2,1)S(1)} %get-tuple-element.236.refs_0_, bf16[2,256,768]{2,1,0:T(8,128)(2,1)} %shard_map.204.refs_1_.refs_4_, bf16[2,256,768]{2,1,0:T(8,128)(2,1)} %collective-permute-done.16.refs_2_.refs_5_, ...), custom_call_target="tpu_custom_call" | custom-call | bytes 28000000 | tf_op jit(solution)/shard_map/pallas_call | solution.py:128
  118.0 2.5 shard_map.208
  123.2 8.5 %collective-permute-done.21.refs_2_ = bf16[256,768]{1,0:T(8,128)(2,1)S(1)} collective-permute-done((bf16[256,768]{1,0:T(8,128)(2,1)S(1)}, bf16[256,768]{1,0:T(8,128)(2,1)S(1)}, u32[]{:S(2)}, u32[]{:S(2)}) %collective-permute-start.21) | collective-permute-done | bytes 393248 | tf_op jit(solution)/shard_map/ppermute | solution.py:733
  134.3 7.2 %shard_map.209 = (bf16[2,256,768]{2,1,0:T(8,128)(2,1)S(1)}, bf16[2,256,768]{2,1,0:T(8,128)(2,1)S(1)}, bf16[2,256,768]{2,1,0:T(8,128)(2,1)S(1)}, bf16[2,256,768]{...) custom-call(f32[24,768]{1,0:T(8,128)S(1)} %get-tuple-element.212.vec, ...), custom_call_target="tpu_custom_call" | custom-call | bytes 28000000 | tf_op jit(solution)/shard_map/pallas_call | solution.py:611
  146.0 1.9 collective-permute-done.24.dn_near_ref
  161.8 2.8 shard_map.210
  167.2 3.3 shard_map.211
  170.6 13.1 %shard_map.212 = (bf16[256,768]{1,0:T(8,128)(2,1)S(1)}, bf16[2,2,256,768]{3,2,1,0:T(8,128)(2,1)S(1)}, bf16[2,2,256,768]{3,2,1,0:T(8,128)(2,1)S(1)}) custom-call(bf16[256,768]{1,0:T(8,128)(2,1)S(1)} %copy-done.55, bf16[256,768]{1,0:T(8,128)(2,1)S(1)} %get-tuple-element.262.refs_1_, bf16[256,768]{1,0:T(8,128)(2,1)S(1)} %copy-done.15, ...), custom_call_target="tpu_custom_call" | custom-call | bytes 45500000 | tf_op jit(solution)/shard_map/pallas_call | solution.py:158
  183.7 9.1 %collective-permute-done.26 = bf16[2,2,8,48,384]{4,3,2,1,0:T(8,128)(2,1)S(1)} collective-permute-done((bf16[2,2,8,48,384]{4,3,2,1,0:T(8,128)(2,1)S(1)}, bf16[2,2,8,48,384]{4,3,2,1,0:T(8,128)(2,1)S(1)}, u32[]{:S(2)}, u32[]{:S(2)}) %collective-permute-start.26) | collective-permute-done | bytes 1179680 | tf_op jit(solution)/shard_map/ppermute | solution.py:272
  195.3 5.5 %shard_map.213 = (f32[256,768]{1,0:T(8,128)S(1)}, bf16[256,768]{1,0:T(8,128)(2,1)S(1)}, bf16[2,3,192,768]{3,2,1,0:T(8,128)(2,1)S(1)}, bf16[2,3,192,768]{3,2,1,0:T(8,128)(2,1)}, f32[16,768]{1,0:T(8,128)S(1)}) custom-call(s32[4]{0:T(128)S(1)} %pad_add_fusion.slot_ref, f32[24,768]{1,0:T(8,128)S(1)} %get-tuple-element.212.vec_ref, ...), custom_call_target="tpu_custom_call" | custom-call | bytes 21000000 | tf_op jit(solution)/shard_map/pallas_call | solution.py:611
  206.3 2.2 fusion.4
  210.0 2.1 dynamic-slice_bitcast_fusion.2
  212.0 2.0 dynamic-slice_bitcast_fusion.3
  214.0 13.7 %shard_map.214 = (bf16[256,768]{1,0:T(8,128)(2,1)S(1)}, bf16[2,2,256,768]{3,2,1,0:T(8,128)(2,1)S(1)}, bf16[2,2,256,768]{3,2,1,0:T(8,128)(2,1)}) custom-call(s32[1024,1]{1,0:T(8,128)S(1)} %copy-done.8, s32[1,256]{1,0:T(1,128)S(1)} %reshape.1153.refs_1_, bf16[256,768]{1,0:T(8,128)(2,1)S(1)} %copy-done.53, bf16[256,768]{1,0:T(8,128)(2,1)S(1)} %copy-done.88, ...), custom_call_target="tpu_custom_call" | custom-call | bytes 45500000 | tf_op jit(solution)/shard_map/pallas_call | solution.py:158
  239.3 4.7 shard_map.215
  244.0 2.0 fusion.3
  246.3 9.4 %collective-permute-done.31 = bf16[3,192,768]{2,1,0:T(8,128)(2,1)S(1)} collective-permute-done((bf16[3,192,768]{2,1,0:T(8,128)(2,1)S(1)}, bf16[3,192,768]{2,1,0:T(8,128)(2,1)S(1)}, u32[]{:S(2)}, u32[]{:S(2)}) %collective-permute-start.31) | collective-permute-done | bytes 884768 | tf_op jit(solution)/shard_map/ppermute | solution.py:263
  255.7 3.3 collective-permute-start.38
  259.0 2.1 collective-permute-start.39
  261.1 1.9 collective-permute-start.40
  267.4 3.0 collective-permute-start.41
  271.0 4.5 collective-permute-done.41
  276.6 3.7 collective-permute-done.37.out_far_ref
  283.6 4.3 all-to-all-start.1
  287.9 2.1 slice_bitcast_fusion.3
  299.3 5.6 %shard_map.216 = (bf16[256,768]{1,0:T(8,128)(2,1)S(1)}, bf16[256,768]{1,0:T(8,128)(2,1)S(1)}, bf16[2,2,192,768]{3,2,1,0:T(8,128)(2,1)S(1)}, bf16[2,2,192,768]{3,2,1,0:T(8,128)(2,1)S(1)}, bf16[4,32,192]{2,1,0:T(8,128)(2,1)S(1)}) custom-call(s32[4]{0:T(128)S(1)} %pad_add_fusion.slot_ref, f32[24,768]{1,0:T(8,128)S(1)} %get-tuple-element.212.vec_ref, ...), custom_call_target="tpu_custom_call" | custom-call | bytes 24500000 | tf_op jit(solution)/shard_map/pallas_call | solution.py:611
  311.4 5.0 %collective-permute-start.45 = (bf16[1,8,48,384]{3,2,1,0:T(8,128)(2,1)S(1)}, bf16[1,8,48,384]{3,2,1,0:T(8,128)(2,1)S(1)}, u32[]{:S(2)}, u32[]{:S(2)}) collective-permute-start(bf16[1,8,48,384]{3,2,1,0:T(8,128)(2,1)S(1)} %maximum_bitcast_fusion), channel_id=1, source_target_pairs={{0,4},{2,6},{4,0},{6,2},{1,5},{3,7},{5,1},{7,3},{8,12},{10,14},{12... | collective-permute-start | bytes 884744 | tf_op jit(solution)/shard_map/ppermute | solution.py:274
  320.9 7.8 %collective-permute-done.45 = bf16[1,8,48,384]{3,2,1,0:T(8,128)(2,1)S(1)} collective-permute-done((bf16[1,8,48,384]{3,2,1,0:T(8,128)(2,1)S(1)}, bf16[1,8,48,384]{3,2,1,0:T(8,128)(2,1)S(1)}, u32[]{:S(2)}, u32[]{:S(2)}) %collective-permute-start.45) | collective-permute-done | bytes 294944 | tf_op jit(solution)/shard_map/ppermute | solution.py:274
  328.8 3.3 collective-permute-done.46
  332.3 2.3 collective-permute-start.49
  340.0 9.0 %collective-permute-done.49 = bf16[2,8,48,384]{3,2,1,0:T(8,128)(2,1)S(1)} collective-permute-done((bf16[2,8,48,384]{3,2,1,0:T(8,128)(2,1)S(1)}, bf16[2,8,48,384]{3,2,1,0:T(8,128)(2,1)S(1)}, u32[]{:S(2)}, u32[]{:S(2)}) %collective-permute-start.49) | collective-permute-done | bytes 589856 | tf_op jit(solution)/shard_map/ppermute | solution.py:274
  349.3 5.8 %collective-permute-done.50 = bf16[72,768]{1,0:T(8,128)(2,1)S(1)} collective-permute-done((bf16[72,768]{1,0:T(8,128)(2,1)S(1)}, bf16[72,768]{1,0:T(8,128)(2,1)S(1)}, u32[]{:S(2)}, u32[]{:S(2)}) %collective-permute-start.50) | collective-permute-done | bytes 110624 | tf_op jit(solution)/shard_map/ppermute | solution.py:274
  359.3 4.5 all-to-all-start.2
  369.5 2.2 collective-permute-start.53
  372.3 8.3 %collective-permute-done.53 = bf16[72,768]{1,0:T(8,128)(2,1)S(1)} collective-permute-done((bf16[72,768]{1,0:T(8,128)(2,1)S(1)}, bf16[72,768]{1,0:T(8,128)(2,1)S(1)}, u32[]{:S(2)}, u32[]{:S(2)}) %collective-permute-start.53) | collective-permute-done | bytes 110624 | tf_op jit(solution)/shard_map/ppermute | solution.py:274
  380.7 6.8 %collective-permute-done.52 = bf16[4,8,48,384]{3,2,1,0:T(8,128)(2,1)S(1)} collective-permute-done((bf16[4,8,48,384]{3,2,1,0:T(8,128)(2,1)S(1)}, bf16[4,8,48,384]{3,2,1,0:T(8,128)(2,1)S(1)}, u32[]{:S(2)}, u32[]{:S(2)}) %collective-permute-start.52) | collective-permute-done | bytes 1179680 | tf_op jit(solution)/shard_map/ppermute | solution.py:272
  393.9 5.2 %all-to-all-start.3 = ((bf16[8,48,768]{2,1,0:T(8,128)(2,1)}), bf16[8,48,768]{2,1,0:T(8,128)(2,1)S(1)}, u32[]{:S(2)}, u32[]{:S(2)}) async-start(bf16[8,48,768]{2,1,0:T(8,128)(2,1)} %broadcast_in_dim.9), calls=%async_computation.3 | async-start | bytes 1179648 | tf_op jit(solution)/shard_map/all_to_all | solution.py:853
  405.2 2.9 reshape.1169
  410.5 1.9 collective-permute-start.61
  412.5 6.9 %collective-permute-start.60 = (bf16[2,64,768]{2,1,0:T(8,128)(2,1)S(1)}, bf16[2,64,768]{2,1,0:T(8,128)(2,1)S(1)}, u32[]{:S(2)}, u32[]{:S(2)}) collective-permute-start(bf16[2,64,768]{2,1,0:T(8,128)(2,1)S(1)} %pad_maximum_fusion.23), channel_id=1, source_target_pairs={{10,0},{2,2},{8,4},{0,6},{14,8},{6,10},{12,12},{4,14},{11,1},{3,3}... | collective-permute-start | bytes 589832 | tf_op jit(solution)/shard_map/ppermute | solution.py:207
  420.2 2.7 collective-permute-start.59
  423.5 3.7 collective-permute-start.57
  428.1 4.5 all-to-all-start.4
  433.2 8.1 %collective-permute-start.58 = (bf16[2,64,768]{2,1,0:T(8,128)(2,1)S(1)}, bf16[2,64,768]{2,1,0:T(8,128)(2,1)S(1)}, u32[]{:S(2)}, u32[]{:S(2)}) collective-permute-start(bf16[2,64,768]{2,1,0:T(8,128)(2,1)S(1)} %pad_maximum_fusion.21), channel_id=1, source_target_pairs={{8,0},{0,2},{10,4},{2,6},{12,8},{4,10},{14,12},{6,14},{9,1},{1,3},... | collective-permute-start | bytes 589832 | tf_op jit(solution)/shard_map/ppermute | solution.py:207
  441.3 9.0 %collective-permute-done.58 = bf16[2,64,768]{2,1,0:T(8,128)(2,1)S(1)} collective-permute-done((bf16[2,64,768]{2,1,0:T(8,128)(2,1)S(1)}, bf16[2,64,768]{2,1,0:T(8,128)(2,1)S(1)}, u32[]{:S(2)}, u32[]{:S(2)}) %collective-permute-start.58) | collective-permute-done | bytes 196640 | tf_op jit(solution)/shard_map/ppermute | solution.py:207
  462.2 4.5 collective-permute-done.63
  468.8 2.0 pad_maximum_fusion
  (513 shorter events, 159.8 us)
Async XLA Ops:
  2.0 34.3 %collective-permute-start.4 = (bf16[608,768]{1,0:T(8,128)(2,1)S(1)}, bf16[608,768]{1,0:T(8,128)(2,1)}, u32[]{:S(2)}, u32[]{:S(2)}) collective-permute-start(bf16[608,768]{1,0:T(8,128)(2,1)S(1)} %pad_maximum_fusion.4.refs_0_.refs_3_), channel_id=1, source_target_pairs={{0,16},{16,0},{1,17},{17,1},{2,18},{18,2},{3,19},{19,3},{4,20},{20... | collective-permute-start | bytes 2801672 | tf_op jit(solution)/shard_map/ppermute | solution.py:657
  2.3 34.0 %collective-permute-start.5 = (bf16[608,768]{1,0:T(8,128)(2,1)S(1)}, bf16[608,768]{1,0:T(8,128)(2,1)}, u32[]{:S(2)}, u32[]{:S(2)}) collective-permute-start(bf16[608,768]{1,0:T(8,128)(2,1)S(1)} %pad_maximum_fusion.4.refs_0_.refs_3_), channel_id=1, source_target_pairs={{0,8},{8,0},{1,9},{9,1},{2,10},{10,2},{3,11},{11,3},{4,12},{12,4},... | collective-permute-start | bytes 2801672 | tf_op jit(solution)/shard_map/ppermute | solution.py:240
  4.7 13.5 %collective-permute-start = (bf16[3,64,768]{2,1,0:T(8,128)(2,1)S(1)}, bf16[3,64,768]{2,1,0:T(8,128)(2,1)S(1)}, u32[]{:S(2)}, u32[]{:S(2)}) collective-permute-start(bf16[3,64,768]{2,1,0:T(8,128)(2,1)S(1)} %pad_maximum_fusion.14), channel_id=1, source_target_pairs={{0,0},{2,10},{4,2},{6,8},{8,4},{10,14},{12,6},{14,12},{1,1},{3,11}... | collective-permute-start | bytes 884744 | tf_op jit(solution)/shard_map/ppermute | solution.py:197
  9.1 19.5 %collective-permute-start.1 = (bf16[3,64,768]{2,1,0:T(8,128)(2,1)S(1)}, bf16[3,64,768]{2,1,0:T(8,128)(2,1)S(1)}, u32[]{:S(2)}, u32[]{:S(2)}) collective-permute-start(bf16[3,64,768]{2,1,0:T(8,128)(2,1)S(1)} %pad_maximum_fusion.15), channel_id=1, source_target_pairs={{0,8},{2,0},{4,10},{6,2},{8,12},{10,4},{12,14},{14,6},{1,9},{3,1},... | collective-permute-start | bytes 884744 | tf_op jit(solution)/shard_map/ppermute | solution.py:197
  9.3 22.2 %collective-permute-start.2 = (bf16[3,64,768]{2,1,0:T(8,128)(2,1)S(1)}, bf16[3,64,768]{2,1,0:T(8,128)(2,1)S(1)}, u32[]{:S(2)}, u32[]{:S(2)}) collective-permute-start(bf16[3,64,768]{2,1,0:T(8,128)(2,1)S(1)} %pad_maximum_fusion.16), channel_id=1, source_target_pairs={{0,2},{2,8},{4,0},{6,10},{8,6},{10,12},{12,4},{14,14},{1,3},{3,9},... | collective-permute-start | bytes 884744 | tf_op jit(solution)/shard_map/ppermute | solution.py:197
  18.3 16.4 %collective-permute-start.3 = (bf16[3,64,768]{2,1,0:T(8,128)(2,1)S(1)}, bf16[3,64,768]{2,1,0:T(8,128)(2,1)S(1)}, u32[]{:S(2)}, u32[]{:S(2)}) collective-permute-start(bf16[3,64,768]{2,1,0:T(8,128)(2,1)S(1)} %pad_maximum_fusion.17), channel_id=1, source_target_pairs={{0,10},{2,2},{4,8},{6,0},{8,14},{10,6},{12,12},{14,4},{1,11},{3,3}... | collective-permute-start | bytes 884744 | tf_op jit(solution)/shard_map/ppermute | solution.py:197
  36.3 15.8 %collective-permute-start.10 = (bf16[5,192,768]{2,1,0:T(8,128)(2,1)S(1)}, bf16[5,192,768]{2,1,0:T(8,128)(2,1)S(1)}, u32[]{:S(2)}, u32[]{:S(2)}) collective-permute-start(bf16[5,192,768]{2,1,0:T(8,128)(2,1)S(1)} %pad_maximum_fusion.2.refs_0_.refs_3_), channel_id=1, source_target_pairs={{0,8},{8,0},{1,9},{9,1},{2,10},{10,2},{3,11},{11,3},{4,12},{12,4},... | collective-permute-start | bytes 4423688 | tf_op jit(solution)/shard_map/ppermute | solution.py:240
  36.8 15.2 %collective-permute-start.9 = (bf16[2,192,768]{2,1,0:T(8,128)(2,1)}, bf16[2,192,768]{2,1,0:T(8,128)(2,1)}, u32[]{:S(2)}, u32[]{:S(2)}) collective-permute-start(bf16[2,192,768]{2,1,0:T(8,128)(2,1)} %slice.241), channel_id=1, source_target_pairs={{0,16},{16,0},{1,17},{17,1},{2,18},{18,2},{3,19},{19,3},{4,20},{20... | collective-permute-start | bytes 1769480 | tf_op jit(solution)/shard_map/ppermute | solution.py:694
  48.4 19.3 %collective-permute-start.7 = (bf16[2,256,768]{2,1,0:T(8,128)(2,1)}, bf16[2,256,768]{2,1,0:T(8,128)(2,1)}, u32[]{:S(2)}, u32[]{:S(2)}) collective-permute-start(bf16[2,256,768]{2,1,0:T(8,128)(2,1)} %get-tuple-element.222.refs_3_.refs_6_), channel_id=1, source_target_pairs={{0,1},{1,0},{2,3},{3,2},{4,5},{5,4},{6,7},{7,6},{8,9},{9,8},{10,11... | collective-permute-start | bytes 2359304 | tf_op jit(solution)/shard_map/ppermute | solution.py:221
  49.7 18.1 %collective-permute-start.8 = (bf16[2,256,768]{2,1,0:T(8,128)(2,1)}, bf16[2,256,768]{2,1,0:T(8,128)(2,1)}, u32[]{:S(2)}, u32[]{:S(2)}) collective-permute-start(bf16[2,256,768]{2,1,0:T(8,128)(2,1)} %get-tuple-element.222.refs_3_.refs_6_), channel_id=1, source_target_pairs={{0,8},{8,0},{1,9},{9,1},{2,10},{10,2},{3,11},{11,3},{4,12},{12,4},... | collective-permute-start | bytes 2359304 | tf_op jit(solution)/shard_map/ppermute | solution.py:240
  52.9 29.6 %collective-permute-start.13 = (bf16[3,192,768]{2,1,0:T(8,128)(2,1)}, bf16[3,192,768]{2,1,0:T(8,128)(2,1)}, u32[]{:S(2)}, u32[]{:S(2)}) collective-permute-start(bf16[3,192,768]{2,1,0:T(8,128)(2,1)} %pad_maximum_fusion.5), channel_id=1, source_target_pairs={{0,16},{16,0},{1,17},{17,1},{2,18},{18,2},{3,19},{19,3},{4,20},{20... | collective-permute-start | bytes 2654216 | tf_op jit(solution)/shard_map/ppermute | solution.py:711
  67.8 5.8 %collective-permute-start.12 = (bf16[2,256,768]{2,1,0:T(8,128)(2,1)}, bf16[2,256,768]{2,1,0:T(8,128)(2,1)}, u32[]{:S(2)}, u32[]{:S(2)}) collective-permute-start(bf16[2,256,768]{2,1,0:T(8,128)(2,1)} %collective-permute-done.7.refs_5_.refs_8_), channel_id=1, source_target_pairs={{0,8},{8,0},{1,9},{9,1},{2,10},{10,2},{3,11},{11,3},{4,12},{12,4},... | collective-permute-start | bytes 2359304 | tf_op jit(solution)/shard_map/ppermute | solution.py:227
  82.6 7.6 %collective-permute-start.14 = (bf16[3,192,768]{2,1,0:T(8,128)(2,1)}, bf16[3,192,768]{2,1,0:T(8,128)(2,1)}, u32[]{:S(2)}, u32[]{:S(2)}) collective-permute-start(bf16[3,192,768]{2,1,0:T(8,128)(2,1)} %collective-permute-done.13.refs_2_), channel_id=1, source_target_pairs={{0,8},{8,0},{1,9},{9,1},{2,10},{10,2},{3,11},{11,3},{4,12},{12,4},... | collective-permute-start | bytes 2654216 | tf_op jit(solution)/shard_map/ppermute | solution.py:240
  82.6 18.9 %collective-permute-start.15 = (bf16[2,256,768]{2,1,0:T(8,128)(2,1)}, bf16[2,256,768]{2,1,0:T(8,128)(2,1)}, u32[]{:S(2)}, u32[]{:S(2)}) collective-permute-start(bf16[2,256,768]{2,1,0:T(8,128)(2,1)} %shard_map.204.refs_1_.refs_4_), channel_id=1, source_target_pairs={{0,1},{1,0},{2,3},{3,2},{4,5},{5,4},{6,7},{7,6},{8,9},{9,8},{10,11... | collective-permute-start | bytes 2359304 | tf_op jit(solution)/shard_map/ppermute | solution.py:221
  83.8 17.7 %collective-permute-start.16 = (bf16[2,256,768]{2,1,0:T(8,128)(2,1)}, bf16[2,256,768]{2,1,0:T(8,128)(2,1)}, u32[]{:S(2)}, u32[]{:S(2)}) collective-permute-start(bf16[2,256,768]{2,1,0:T(8,128)(2,1)} %shard_map.204.refs_1_.refs_4_), channel_id=1, source_target_pairs={{0,8},{8,0},{1,9},{9,1},{2,10},{10,2},{3,11},{11,3},{4,12},{12,4},... | collective-permute-start | bytes 2359304 | tf_op jit(solution)/shard_map/ppermute | solution.py:240
  84.6 31.2 %all-to-all-start = ((bf16[4,192,768]{2,1,0:T(8,128)(2,1)}), bf16[4,192,768]{2,1,0:T(8,128)(2,1)}, u32[]{:S(2)}, u32[]{:S(2)}) async-start(bf16[4,192,768]{2,1,0:T(8,128)(2,1)} %bitcast.246), calls=%async_computation | async-start | bytes 2359296 | tf_op jit(solution)/shard_map/all_to_all | solution.py:724
  102.9 11.4 %collective-permute-start.18 = (bf16[256,768]{1,0:T(8,128)(2,1)S(1)}, bf16[256,768]{1,0:T(8,128)(2,1)S(1)}, u32[]{:S(2)}, u32[]{:S(2)}) collective-permute-start(bf16[256,768]{1,0:T(8,128)(2,1)S(1)} %copy-done.3), channel_id=1, source_target_pairs={{0,16},{16,0},{1,17},{17,1},{2,18},{18,2},{3,19},{19,3},{4,20},{20... | collective-permute-start | bytes 1179656 | tf_op jit(solution)/shard_map/ppermute | solution.py:725
  104.1 11.0 %collective-permute-start.19 = (bf16[256,768]{1,0:T(8,128)(2,1)S(1)}, bf16[256,768]{1,0:T(8,128)(2,1)S(1)}, u32[]{:S(2)}, u32[]{:S(2)}) collective-permute-start(bf16[256,768]{1,0:T(8,128)(2,1)S(1)} %copy-done.3), channel_id=1, source_target_pairs={{0,8},{8,0},{1,9},{9,1},{2,10},{10,2},{3,11},{11,3},{4,12},{12,4},... | collective-permute-start | bytes 1179656 | tf_op jit(solution)/shard_map/ppermute | solution.py:240
  121.4 10.3 %collective-permute-start.21 = (bf16[256,768]{1,0:T(8,128)(2,1)S(1)}, bf16[256,768]{1,0:T(8,128)(2,1)S(1)}, u32[]{:S(2)}, u32[]{:S(2)}) collective-permute-start(bf16[256,768]{1,0:T(8,128)(2,1)S(1)} %get-tuple-element.247.refs_0_), channel_id=1, source_target_pairs={{0,16},{16,0},{1,17},{17,1},{2,18},{18,2},{3,19},{19,3},{4,20},{20... | collective-permute-start | bytes 1179656 | tf_op jit(solution)/shard_map/ppermute | solution.py:733
  122.6 10.3 %collective-permute-start.20 = (bf16[256,768]{1,0:T(8,128)(2,1)S(1)}, bf16[256,768]{1,0:T(8,128)(2,1)S(1)}, u32[]{:S(2)}, u32[]{:S(2)}) collective-permute-start(bf16[256,768]{1,0:T(8,128)(2,1)S(1)} %get-tuple-element.247.refs_0_), channel_id=1, source_target_pairs={{0,8},{8,0},{1,9},{9,1},{2,10},{10,2},{3,11},{11,3},{4,12},{12,4},... | collective-permute-start | bytes 1179656 | tf_op jit(solution)/shard_map/ppermute | solution.py:240
  123.2 9.7 %collective-permute-start.23 = (bf16[256,768]{1,0:T(8,128)(2,1)S(1)}, bf16[256,768]{1,0:T(8,128)(2,1)S(1)}, u32[]{:S(2)}, u32[]{:S(2)}) collective-permute-start(bf16[256,768]{1,0:T(8,128)(2,1)S(1)} %copy-done.57), channel_id=1, source_target_pairs={{0,8},{8,0},{1,9},{9,1},{2,10},{10,2},{3,11},{11,3},{4,12},{12,4},... | collective-permute-start | bytes 1179656 | tf_op jit(solution)/shard_map/ppermute | solution.py:240
  149.8 14.8 %collective-permute-start.25 = (bf16[256,768]{1,0:T(8,128)(2,1)}, bf16[256,768]{1,0:T(8,128)(2,1)}, u32[]{:S(2)}, u32[]{:S(2)}) collective-permute-start(bf16[256,768]{1,0:T(8,128)(2,1)} %fusion.9), channel_id=1, source_target_pairs={{0,16},{16,0},{1,17},{17,1},{2,18},{18,2},{3,19},{19,3},{4,20},{20... | collective-permute-start | bytes 1179656 | tf_op jit(solution)/shard_map/ppermute | solution.py:756
  165.9 26.9 %collective-permute-start.26 = (bf16[2,2,8,48,384]{4,3,2,1,0:T(8,128)(2,1)S(1)}, bf16[2,2,8,48,384]{4,3,2,1,0:T(8,128)(2,1)S(1)}, u32[]{:S(2)}, u32[]{:S(2)}) collective-permute-start(bf16[2,2,8,48,384]{4,3,2,1,0:T(8,128)(2,1)S(1)} %get-tuple-element.411), channel_id=1, source_target_pairs={{0,1},{1,0},{2,3},{3,2},{4,5},{5,4},{6,7},{7,6},{8,9},{9,8},{10,11... | collective-permute-start | bytes 3538952 | tf_op jit(solution)/shard_map/ppermute | solution.py:272
  193.8 9.6 %collective-permute-start.27 = (bf16[2,2,256,768]{3,2,1,0:T(8,128)(2,1)S(1)}, bf16[2,2,256,768]{3,2,1,0:T(8,128)(2,1)S(1)}, u32[]{:S(2)}, u32[]{:S(2)}) collective-permute-start(bf16[2,2,256,768]{3,2,1,0:T(8,128)(2,1)S(1)} %get-tuple-element.278), channel_id=1, source_target_pairs={{0,8},{8,0},{1,9},{9,1},{2,10},{10,2},{3,11},{11,3},{4,12},{12,4},... | collective-permute-start | bytes 4718600 | tf_op jit(solution)/shard_map/ppermute | solution.py:240
  203.4 26.3 %collective-permute-start.30 = (bf16[2,3,192,768]{3,2,1,0:T(8,128)(2,1)}, bf16[2,3,192,768]{3,2,1,0:T(8,128)(2,1)}, u32[]{:S(2)}, u32[]{:S(2)}) collective-permute-start(bf16[2,3,192,768]{3,2,1,0:T(8,128)(2,1)} %get-tuple-element.290), channel_id=1, source_target_pairs={{0,8},{8,0},{1,9},{9,1},{2,10},{10,2},{3,11},{11,3},{4,12},{12,4},... | collective-permute-start | bytes 5308424 | tf_op jit(solution)/shard_map/ppermute | solution.py:240
  205.0 24.6 %collective-permute-start.28 = (bf16[2,256,768]{2,1,0:T(8,128)(2,1)}, bf16[2,256,768]{2,1,0:T(8,128)(2,1)}, u32[]{:S(2)}, u32[]{:S(2)}) collective-permute-start(bf16[2,256,768]{2,1,0:T(8,128)(2,1)} %fusion.2), channel_id=1, source_target_pairs={{1,0},{0,1},{3,2},{2,3},{5,4},{4,5},{7,6},{6,7},{9,8},{8,9},{11,10... | collective-permute-start | bytes 2359304 | tf_op jit(solution)/shard_map/ppermute | solution.py:235
  208.5 21.1 %collective-permute-start.29 = (bf16[2,8,48,384]{3,2,1,0:T(8,128)(2,1)}, bf16[2,8,48,384]{3,2,1,0:T(8,128)(2,1)}, u32[]{:S(2)}, u32[]{:S(2)}) collective-permute-start(bf16[2,8,48,384]{3,2,1,0:T(8,128)(2,1)} %fusion.4), channel_id=1, source_target_pairs={{0,2},{2,0},{4,6},{6,4},{1,3},{3,1},{5,7},{7,5},{8,10},{10,8},{12,... | collective-permute-start | bytes 1769480 | tf_op jit(solution)/shard_map/ppermute | solution.py:274
  229.6 8.1 %collective-permute-start.33 = (bf16[2,2,256,768]{3,2,1,0:T(8,128)(2,1)}, bf16[2,2,256,768]{3,2,1,0:T(8,128)(2,1)}, u32[]{:S(2)}, u32[]{:S(2)}) collective-permute-start(bf16[2,2,256,768]{3,2,1,0:T(8,128)(2,1)} %get-tuple-element.309), channel_id=1, source_target_pairs={{0,8},{8,0},{1,9},{9,1},{2,10},{10,2},{3,11},{11,3},{4,12},{12,4},... | collective-permute-start | bytes 4718600 | tf_op jit(solution)/shard_map/ppermute | solution.py:240
  231.6 14.7 %collective-permute-start.32 = (bf16[8,48,384]{2,1,0:T(8,128)(2,1)S(1)}, bf16[8,48,384]{2,1,0:T(8,128)(2,1)S(1)}, u32[]{:S(2)}, u32[]{:S(2)}) collective-permute-start(bf16[8,48,384]{2,1,0:T(8,128)(2,1)S(1)} %fusion.11), channel_id=1, source_target_pairs={{0,4},{2,6},{4,0},{6,2},{1,5},{3,7},{5,1},{7,3},{8,12},{10,14},{12... | collective-permute-start | bytes 884744 | tf_op jit(solution)/shard_map/ppermute | solution.py:274
  234.9 20.8 %collective-permute-start.31 = (bf16[3,192,768]{2,1,0:T(8,128)(2,1)S(1)}, bf16[3,192,768]{2,1,0:T(8,128)(2,1)S(1)}, u32[]{:S(2)}, u32[]{:S(2)}) collective-permute-start(bf16[3,192,768]{2,1,0:T(8,128)(2,1)S(1)} %fusion), channel_id=1, source_target_pairs={{0,16},{16,0},{1,17},{17,1},{2,18},{18,2},{3,19},{19,3},{4,20},{20... | collective-permute-start | bytes 2654216 | tf_op jit(solution)/shard_map/ppermute | solution.py:263
  237.7 17.9 %collective-permute-start.34 = (bf16[2,256,768]{2,1,0:T(8,128)(2,1)S(1)}, bf16[2,256,768]{2,1,0:T(8,128)(2,1)S(1)}, u32[]{:S(2)}, u32[]{:S(2)}) collective-permute-start(bf16[2,256,768]{2,1,0:T(8,128)(2,1)S(1)} %copy-done.102), channel_id=1, source_target_pairs={{0,8},{8,0},{1,9},{9,1},{2,10},{10,2},{3,11},{11,3},{4,12},{12,4},... | collective-permute-start | bytes 2359304 | tf_op jit(solution)/shard_map/ppermute | solution.py:240
  246.0 30.7 %collective-permute-start.35 = (bf16[2,256,768]{2,1,0:T(8,128)(2,1)S(1)}, bf16[2,256,768]{2,1,0:T(8,128)(2,1)S(1)}, u32[]{:S(2)}, u32[]{:S(2)}) collective-permute-start(bf16[2,256,768]{2,1,0:T(8,128)(2,1)S(1)} %fusion.3), channel_id=1, source_target_pairs={{1,0},{0,1},{3,2},{2,3},{5,4},{4,5},{7,6},{6,7},{9,8},{8,9},{11,10... | collective-permute-start | bytes 2359304 | tf_op jit(solution)/shard_map/ppermute | solution.py:235
  255.7 11.7 %collective-permute-start.38 = (bf16[1,64,768]{2,1,0:T(8,128)(2,1)S(1)}, bf16[1,64,768]{2,1,0:T(8,128)(2,1)S(1)}, u32[]{:S(2)}, u32[]{:S(2)}) collective-permute-start(bf16[1,64,768]{2,1,0:T(8,128)(2,1)S(1)} %get-tuple-element.436), channel_id=1, source_target_pairs={{0,0},{10,2},{2,4},{8,6},{4,8},{14,10},{6,12},{12,14},{1,1},{11,3}... | collective-permute-start | bytes 294920 | tf_op jit(solution)/shard_map/ppermute | solution.py:207
  259.0 11.4 %collective-permute-start.39 = (bf16[1,64,768]{2,1,0:T(8,128)(2,1)S(1)}, bf16[1,64,768]{2,1,0:T(8,128)(2,1)S(1)}, u32[]{:S(2)}, u32[]{:S(2)}) collective-permute-start(bf16[1,64,768]{2,1,0:T(8,128)(2,1)S(1)} %get-tuple-element.435), channel_id=1, source_target_pairs={{8,0},{0,2},{10,4},{2,6},{12,8},{4,10},{14,12},{6,14},{9,1},{1,3},... | collective-permute-start | bytes 294920 | tf_op jit(solution)/shard_map/ppermute | solution.py:207
  261.1 9.6 %collective-permute-start.40 = (bf16[1,64,768]{2,1,0:T(8,128)(2,1)S(1)}, bf16[1,64,768]{2,1,0:T(8,128)(2,1)S(1)}, u32[]{:S(2)}, u32[]{:S(2)}) collective-permute-start(bf16[1,64,768]{2,1,0:T(8,128)(2,1)S(1)} %get-tuple-element.434), channel_id=1, source_target_pairs={{2,0},{8,2},{0,4},{10,6},{6,8},{12,10},{4,12},{14,14},{3,1},{9,3},... | collective-permute-start | bytes 294920 | tf_op jit(solution)/shard_map/ppermute | solution.py:207
  263.0 17.3 %collective-permute-start.36 = (bf16[2,3,192,768]{3,2,1,0:T(8,128)(2,1)S(1)}, bf16[2,3,192,768]{3,2,1,0:T(8,128)(2,1)S(1)}, u32[]{:S(2)}, u32[]{:S(2)}) collective-permute-start(bf16[2,3,192,768]{3,2,1,0:T(8,128)(2,1)S(1)} %get-tuple-element.319), channel_id=1, source_target_pairs={{0,8},{8,0},{1,9},{9,1},{2,10},{10,2},{3,11},{11,3},{4,12},{12,4},... | collective-permute-start | bytes 5308424 | tf_op jit(solution)/shard_map/ppermute | solution.py:240
  267.4 8.2 %collective-permute-start.41 = (bf16[1,64,768]{2,1,0:T(8,128)(2,1)S(1)}, bf16[1,64,768]{2,1,0:T(8,128)(2,1)S(1)}, u32[]{:S(2)}, u32[]{:S(2)}) collective-permute-start(bf16[1,64,768]{2,1,0:T(8,128)(2,1)S(1)} %get-tuple-element.433), channel_id=1, source_target_pairs={{10,0},{2,2},{8,4},{0,6},{14,8},{6,10},{12,12},{4,14},{11,1},{3,3}... | collective-permute-start | bytes 294920 | tf_op jit(solution)/shard_map/ppermute | solution.py:207
  270.4 9.9 %collective-permute-start.37 = (bf16[256,768]{1,0:T(8,128)(2,1)S(1)}, bf16[256,768]{1,0:T(8,128)(2,1)S(1)}, u32[]{:S(2)}, u32[]{:S(2)}) collective-permute-start(bf16[256,768]{1,0:T(8,128)(2,1)S(1)} %fusion.10), channel_id=1, source_target_pairs={{0,16},{16,0},{1,17},{17,1},{2,18},{18,2},{3,19},{19,3},{4,20},{20... | collective-permute-start | bytes 1179656 | tf_op jit(solution)/shard_map/ppermute | solution.py:811
  270.7 38.9 %collective-permute-start.42 = (bf16[2,2,72,768]{3,2,1,0:T(8,128)(2,1)}, bf16[2,2,72,768]{3,2,1,0:T(8,128)(2,1)}, u32[]{:S(2)}, u32[]{:S(2)}) collective-permute-start(bf16[2,2,72,768]{3,2,1,0:T(8,128)(2,1)} %fusion.7), channel_id=1, source_target_pairs={{0,1},{1,0},{2,3},{3,2},{4,5},{5,4},{6,7},{7,6},{8,9},{9,8},{10,11... | collective-permute-start | bytes 1327112 | tf_op jit(solution)/shard_map/ppermute | solution.py:272
  282.5 27.1 %collective-permute-start.43 = (bf16[3,192,768]{2,1,0:T(8,128)(2,1)}, bf16[3,192,768]{2,1,0:T(8,128)(2,1)}, u32[]{:S(2)}, u32[]{:S(2)}) collective-permute-start(bf16[3,192,768]{2,1,0:T(8,128)(2,1)} %fusion.1), channel_id=1, source_target_pairs={{0,16},{16,0},{1,17},{17,1},{2,18},{18,2},{3,19},{19,3},{4,20},{20... | collective-permute-start | bytes 2654216 | tf_op jit(solution)/shard_map/ppermute | solution.py:263
  283.6 24.7 %all-to-all-start.1 = ((bf16[4,48,384]{2,1,0:T(8,128)(2,1)}), bf16[4,48,384]{2,1,0:T(8,128)(2,1)}, u32[]{:S(2)}, u32[]{:S(2)}) async-start(bf16[4,48,384]{2,1,0:T(8,128)(2,1)} %get-tuple-element.449), calls=%async_computation.1 | async-start | bytes 294912 | tf_op jit(solution)/shard_map/all_to_all | solution.py:830
  311.1 20.9 %collective-permute-start.47 = (bf16[2,2,72,768]{3,2,1,0:T(8,128)(2,1)S(1)}, bf16[2,2,72,768]{3,2,1,0:T(8,128)(2,1)S(1)}, u32[]{:S(2)}, u32[]{:S(2)}) collective-permute-start(bf16[2,2,72,768]{3,2,1,0:T(8,128)(2,1)S(1)} %fusion.8), channel_id=1, source_target_pairs={{0,1},{1,0},{2,3},{3,2},{4,5},{5,4},{6,7},{7,6},{8,9},{9,8},{10,11... | collective-permute-start | bytes 1327112 | tf_op jit(solution)/shard_map/ppermute | solution.py:272
  311.4 17.2 %collective-permute-start.45 = (bf16[1,8,48,384]{3,2,1,0:T(8,128)(2,1)S(1)}, bf16[1,8,48,384]{3,2,1,0:T(8,128)(2,1)S(1)}, u32[]{:S(2)}, u32[]{:S(2)}) collective-permute-start(bf16[1,8,48,384]{3,2,1,0:T(8,128)(2,1)S(1)} %maximum_bitcast_fusion), channel_id=1, source_target_pairs={{0,4},{2,6},{4,0},{6,2},{1,5},{3,7},{5,1},{7,3},{8,12},{10,14},{12... | collective-permute-start | bytes 884744 | tf_op jit(solution)/shard_map/ppermute | solution.py:274
  316.5 15.6 %collective-permute-start.44 = (bf16[2,2,192,768]{3,2,1,0:T(8,128)(2,1)S(1)}, bf16[2,2,192,768]{3,2,1,0:T(8,128)(2,1)S(1)}, u32[]{:S(2)}, u32[]{:S(2)}) collective-permute-start(bf16[2,2,192,768]{3,2,1,0:T(8,128)(2,1)S(1)} %copy-done.100), channel_id=1, source_target_pairs={{0,8},{8,0},{1,9},{9,1},{2,10},{10,2},{3,11},{11,3},{4,12},{12,4},... | collective-permute-start | bytes 3538952 | tf_op jit(solution)/shard_map/ppermute | solution.py:240
  320.7 11.4 %collective-permute-start.46 = (bf16[2,72,768]{2,1,0:T(8,128)(2,1)S(1)}, bf16[2,72,768]{2,1,0:T(8,128)(2,1)S(1)}, u32[]{:S(2)}, u32[]{:S(2)}) collective-permute-start(bf16[2,72,768]{2,1,0:T(8,128)(2,1)S(1)} %fusion.12), channel_id=1, source_target_pairs={{0,2},{2,0},{4,6},{6,4},{1,3},{3,1},{5,7},{7,5},{8,10},{10,8},{12,... | collective-permute-start | bytes 663560 | tf_op jit(solution)/shard_map/ppermute | solution.py:274
  332.3 16.7 %collective-permute-start.49 = (bf16[2,8,48,384]{3,2,1,0:T(8,128)(2,1)S(1)}, bf16[2,8,48,384]{3,2,1,0:T(8,128)(2,1)S(1)}, u32[]{:S(2)}, u32[]{:S(2)}) collective-permute-start(bf16[2,8,48,384]{3,2,1,0:T(8,128)(2,1)S(1)} %pad_maximum_fusion.8), channel_id=1, source_target_pairs={{0,2},{2,0},{4,6},{6,4},{1,3},{3,1},{5,7},{7,5},{8,10},{10,8},{12,... | collective-permute-start | bytes 1769480 | tf_op jit(solution)/shard_map/ppermute | solution.py:274
  334.8 20.3 %collective-permute-start.48 = (bf16[2,192,768]{2,1,0:T(8,128)(2,1)S(1)}, bf16[2,192,768]{2,1,0:T(8,128)(2,1)S(1)}, u32[]{:S(2)}, u32[]{:S(2)}) collective-permute-start(bf16[2,192,768]{2,1,0:T(8,128)(2,1)S(1)} %fusion.5), channel_id=1, source_target_pairs={{0,16},{16,0},{1,17},{17,1},{2,18},{18,2},{3,19},{19,3},{4,20},{20... | collective-permute-start | bytes 1769480 | tf_op jit(solution)/shard_map/ppermute | solution.py:263
  338.3 16.8 %collective-permute-start.51 = (bf16[2,72,768]{2,1,0:T(8,128)(2,1)S(1)}, bf16[2,72,768]{2,1,0:T(8,128)(2,1)S(1)}, u32[]{:S(2)}, u32[]{:S(2)}) collective-permute-start(bf16[2,72,768]{2,1,0:T(8,128)(2,1)S(1)} %fusion.13), channel_id=1, source_target_pairs={{0,2},{2,0},{4,6},{6,4},{1,3},{3,1},{5,7},{7,5},{8,10},{10,8},{12,... | collective-permute-start | bytes 663560 | tf_op jit(solution)/shard_map/ppermute | solution.py:274
  339.3 15.8 %collective-permute-start.50 = (bf16[72,768]{1,0:T(8,128)(2,1)S(1)}, bf16[72,768]{1,0:T(8,128)(2,1)S(1)}, u32[]{:S(2)}, u32[]{:S(2)}) collective-permute-start(bf16[72,768]{1,0:T(8,128)(2,1)S(1)} %fusion.14), channel_id=1, source_target_pairs={{0,4},{2,6},{4,0},{6,2},{1,5},{3,7},{5,1},{7,3},{8,12},{10,14},{12... | collective-permute-start | bytes 331784 | tf_op jit(solution)/shard_map/ppermute | solution.py:274
  355.9 32.1 %collective-permute-start.54 = (bf16[72,768]{1,0:T(8,128)(2,1)}, bf16[72,768]{1,0:T(8,128)(2,1)}, u32[]{:S(2)}, u32[]{:S(2)}) collective-permute-start(bf16[72,768]{1,0:T(8,128)(2,1)} %fusion.15), channel_id=1, source_target_pairs={{0,4},{2,6},{4,0},{6,2},{1,5},{3,7},{5,1},{7,3},{8,12},{10,14},{12... | collective-permute-start | bytes 331784 | tf_op jit(solution)/shard_map/ppermute | solution.py:274
  357.0 30.5 %collective-permute-start.52 = (bf16[4,8,48,384]{3,2,1,0:T(8,128)(2,1)S(1)}, bf16[4,8,48,384]{3,2,1,0:T(8,128)(2,1)S(1)}, u32[]{:S(2)}, u32[]{:S(2)}) collective-permute-start(bf16[4,8,48,384]{3,2,1,0:T(8,128)(2,1)S(1)} %pad_maximum_fusion.3), channel_id=1, source_target_pairs={{0,1},{1,0},{2,3},{3,2},{4,5},{5,4},{6,7},{7,6},{8,9},{9,8},{10,11... | collective-permute-start | bytes 3538952 | tf_op jit(solution)/shard_map/ppermute | solution.py:272
  359.3 29.8 %all-to-all-start.2 = ((bf16[8,48,768]{2,1,0:T(8,128)(2,1)}), bf16[8,48,768]{2,1,0:T(8,128)(2,1)S(1)}, u32[]{:S(2)}, u32[]{:S(2)}) async-start(bf16[8,48,768]{2,1,0:T(8,128)(2,1)} %bitcast.114), calls=%async_computation.2 | async-start | bytes 1179648 | tf_op jit(solution)/shard_map/all_to_all | solution.py:847
  369.5 11.2 %collective-permute-start.53 = (bf16[72,768]{1,0:T(8,128)(2,1)S(1)}, bf16[72,768]{1,0:T(8,128)(2,1)S(1)}, u32[]{:S(2)}, u32[]{:S(2)}) collective-permute-start(bf16[72,768]{1,0:T(8,128)(2,1)S(1)} %add_convert_fusion.18), channel_id=1, source_target_pairs={{0,4},{2,6},{4,0},{6,2},{1,5},{3,7},{5,1},{7,3},{8,12},{10,14},{12... | collective-permute-start | bytes 331784 | tf_op jit(solution)/shard_map/ppermute | solution.py:274
  390.9 17.3 %collective-permute-start.56 = (bf16[72,768]{1,0:T(8,128)(2,1)}, bf16[72,768]{1,0:T(8,128)(2,1)}, u32[]{:S(2)}, u32[]{:S(2)}) collective-permute-start(bf16[72,768]{1,0:T(8,128)(2,1)} %add_convert_fusion.17), channel_id=1, source_target_pairs={{0,4},{2,6},{4,0},{6,2},{1,5},{3,7},{5,1},{7,3},{8,12},{10,14},{12... | collective-permute-start | bytes 331784 | tf_op jit(solution)/shard_map/ppermute | solution.py:274
  392.5 16.8 %collective-permute-start.55 = (bf16[144,768]{1,0:T(8,128)(2,1)S(1)}, bf16[144,768]{1,0:T(8,128)(2,1)}, u32[]{:S(2)}, u32[]{:S(2)}) collective-permute-start(bf16[144,768]{1,0:T(8,128)(2,1)S(1)} %pad_maximum_fusion.18), channel_id=1, source_target_pairs={{0,2},{2,0},{4,6},{6,4},{1,3},{3,1},{5,7},{7,5},{8,10},{10,8},{12,... | collective-permute-start | bytes 663560 | tf_op jit(solution)/shard_map/ppermute | solution.py:274
  393.9 16.4 %all-to-all-start.3 = ((bf16[8,48,768]{2,1,0:T(8,128)(2,1)}), bf16[8,48,768]{2,1,0:T(8,128)(2,1)S(1)}, u32[]{:S(2)}, u32[]{:S(2)}) async-start(bf16[8,48,768]{2,1,0:T(8,128)(2,1)} %broadcast_in_dim.9), calls=%async_computation.3 | async-start | bytes 1179648 | tf_op jit(solution)/shard_map/all_to_all | solution.py:853
  410.3 41.2 %collective-permute-start.62 = (bf16[144,768]{1,0:T(8,128)(2,1)S(1)}, bf16[144,768]{1,0:T(8,128)(2,1)}, u32[]{:S(2)}, u32[]{:S(2)}) collective-permute-start(bf16[144,768]{1,0:T(8,128)(2,1)S(1)} %pad_maximum_fusion.19), channel_id=1, source_target_pairs={{0,2},{2,0},{4,6},{6,4},{1,3},{3,1},{5,7},{7,5},{8,10},{10,8},{12,... | collective-permute-start | bytes 663560 | tf_op jit(solution)/shard_map/ppermute | solution.py:274
  410.5 42.8 %collective-permute-start.61 = (bf16[288,768]{1,0:T(8,128)(2,1)S(1)}, bf16[288,768]{1,0:T(8,128)(2,1)}, u32[]{:S(2)}, u32[]{:S(2)}) collective-permute-start(bf16[288,768]{1,0:T(8,128)(2,1)S(1)} %pad_maximum_fusion.9), channel_id=1, source_target_pairs={{0,1},{1,0},{2,3},{3,2},{4,5},{5,4},{6,7},{7,6},{8,9},{9,8},{10,11... | collective-permute-start | bytes 1327112 | tf_op jit(solution)/shard_map/ppermute | solution.py:272
  412.5 37.8 %collective-permute-start.60 = (bf16[2,64,768]{2,1,0:T(8,128)(2,1)S(1)}, bf16[2,64,768]{2,1,0:T(8,128)(2,1)S(1)}, u32[]{:S(2)}, u32[]{:S(2)}) collective-permute-start(bf16[2,64,768]{2,1,0:T(8,128)(2,1)S(1)} %pad_maximum_fusion.23), channel_id=1, source_target_pairs={{10,0},{2,2},{8,4},{0,6},{14,8},{6,10},{12,12},{4,14},{11,1},{3,3}... | collective-permute-start | bytes 589832 | tf_op jit(solution)/shard_map/ppermute | solution.py:207
  420.2 30.1 %collective-permute-start.59 = (bf16[2,64,768]{2,1,0:T(8,128)(2,1)}, bf16[2,64,768]{2,1,0:T(8,128)(2,1)S(1)}, u32[]{:S(2)}, u32[]{:S(2)}) collective-permute-start(bf16[2,64,768]{2,1,0:T(8,128)(2,1)} %pad_maximum_fusion.22), channel_id=1, source_target_pairs={{2,0},{8,2},{0,4},{10,6},{6,8},{12,10},{4,12},{14,14},{3,1},{9,3},... | collective-permute-start | bytes 589832 | tf_op jit(solution)/shard_map/ppermute | solution.py:207
  423.5 9.7 %collective-permute-start.57 = (bf16[2,64,768]{2,1,0:T(8,128)(2,1)}, bf16[2,64,768]{2,1,0:T(8,128)(2,1)S(1)}, u32[]{:S(2)}, u32[]{:S(2)}) collective-permute-start(bf16[2,64,768]{2,1,0:T(8,128)(2,1)} %pad_maximum_fusion.20), channel_id=1, source_target_pairs={{0,0},{10,2},{2,4},{8,6},{4,8},{14,10},{6,12},{12,14},{1,1},{11,3}... | collective-permute-start | bytes 589832 | tf_op jit(solution)/shard_map/ppermute | solution.py:207
  428.1 30.5 %all-to-all-start.4 = ((bf16[32,32,192]{2,1,0:T(8,128)(2,1)}), bf16[32,32,192]{2,1,0:T(8,128)(2,1)}, u32[]{:S(2)}, u32[]{:S(2)}) async-start(bf16[32,32,192]{2,1,0:T(8,128)(2,1)} %bitcast.140), calls=%async_computation.4 | async-start | bytes 1048576 | tf_op jit(solution)/shard_map/all_to_all | solution.py:321
  433.2 17.1 %collective-permute-start.58 = (bf16[2,64,768]{2,1,0:T(8,128)(2,1)S(1)}, bf16[2,64,768]{2,1,0:T(8,128)(2,1)S(1)}, u32[]{:S(2)}, u32[]{:S(2)}) collective-permute-start(bf16[2,64,768]{2,1,0:T(8,128)(2,1)S(1)} %pad_maximum_fusion.21), channel_id=1, source_target_pairs={{8,0},{0,2},{10,4},{2,6},{12,8},{4,10},{14,12},{6,14},{9,1},{1,3},... | collective-permute-start | bytes 589832 | tf_op jit(solution)/shard_map/ppermute | solution.py:207
  454.5 12.2 %collective-permute-start.63 = (bf16[288,768]{1,0:T(8,128)(2,1)}, bf16[288,768]{1,0:T(8,128)(2,1)S(1)}, u32[]{:S(2)}, u32[]{:S(2)}) collective-permute-start(bf16[288,768]{1,0:T(8,128)(2,1)} %pad_maximum_fusion.10), channel_id=1, source_target_pairs={{0,1},{1,0},{2,3},{3,2},{4,5},{5,4},{6,7},{7,6},{8,9},{9,8},{10,11... | collective-permute-start | bytes 1327112 | tf_op jit(solution)/shard_map/ppermute | solution.py:272
  (136 other events, 697.2 us)

commit v4 on v3

--- a/solution.py
+++ b/solution.py
@@ -140,7 +140,7 @@
             jax.ShapeDtypeStruct((width // PAIR, 1, 2 * rows), F32),
         ],
         scratch_shapes=[pltpu.VMEM((keys, 2 * rows), F32)],
-        compiler_params=pltpu.CompilerParams(vmem_limit_bytes=8 * MIB + 4096 * keys),
+        compiler_params=pltpu.CompilerParams(vmem_limit_bytes=60 * MIB),
         cost_estimate=cost(8 * rows * keys / 2**18),
     )(*extra, query, *kv)
 
@@ -164,7 +164,7 @@
         out_specs=[column, blocks, blocks],
         out_shape=[jax.ShapeDtypeStruct((rows, width), BF)]
         + [jax.ShapeDtypeStruct((groups, 2, piece, width), BF)] * 2,
-        compiler_params=pltpu.CompilerParams(vmem_limit_bytes=8 * MIB + 4096 * keys),
+        compiler_params=pltpu.CompilerParams(vmem_limit_bytes=60 * MIB),
         cost_estimate=cost(13 * rows * keys / 2**18),
     )(*extra, query, dout, out, mass, *kv)
 
@@ -196,6 +196,24 @@
         chunk = jnp.stack([lax.dynamic_index_in_dim(c, k, keepdims=False) for c in chunks])
         got.append(lax.ppermute(chunk, ("core", "z"), DEAL[r]))
     return [jnp.concatenate([g[i] for g in got], axis=0) for i in range(len(arrays))]
+
+
+def deal_halves(array):
+    _, rows, width = array.shape
+    parts = array.reshape(2, 2, rows // 2, width)
+    core = lax.axis_index("core")
+    mine = lax.dynamic_index_in_dim(parts, core, 1, keepdims=False)
+    return mine, lax.ppermute(lax.dynamic_index_in_dim(parts, 1 - core, 1, keepdims=False), "core", SWAP)
+
+
+def deal_line(mine, got):
+    core, z = lax.axis_index("core"), lax.axis_index("z")
+    first = core == 0
+    chunks = jnp.where(first, jnp.concatenate([mine, got], axis=0), jnp.concatenate([got, mine], axis=0))
+    chunks = lax.all_to_all(chunks, "z", 0, 0, tiled=True)
+    start = lax.rem(LINE - 2 * lax.rem(z, 2) - core, LINE)
+    mine = lax.dynamic_slice_in_dim(jnp.concatenate([chunks, chunks], axis=0), start, LINE, axis=0)
+    return mine.reshape(-1, mine.shape[-1])
 
 
 def undeal(arrays, kind):
@@ -256,12 +274,16 @@
 
 
 def over_cores(keep, send):
-    return [keep, lax.ppermute(send, "core", SWAP)]
+    return [(keep, ()), (lax.ppermute(send, "core", SWAP), ())]
 
 
 def over_x(terms):
-    got = lax.ppermute(add([term[1] for term in terms]), "fx", SWAP)
-    return [term[0] for term in terms] + [got]
+    got = lax.ppermute(add([array[1] for array, _ in terms]), "fx", SWAP)
+    return [(array, (0,)) for array, _ in terms] + [(got, ())]
+
+
+def part_over_x(terms, first, last):
+    return lax.ppermute(add([array[1, first:last] for array, _ in terms]), "fx", SWAP)
 
 
 HALVES = ("y", "z0", "z1")
@@ -279,47 +301,42 @@
     return lax.axis_index("y") if name == "y" else lax.rem(z, 2) if name == "z0" else lax.div(z, 2)
 
 
-def cut_rows(terms, order):
-    return [term.reshape(2, 2, 2, -1, term.shape[-1]) for term in terms]
+def half_of(term, more=()):
+    array, names = term
+    cut = 1 in names
+    if 0 in names and len(names + more) > 1:
+        array = array.reshape(2, 2, 2, 2, -1, array.shape[-1])
+        cut = True
+    for name in names + more:
+        if name in (0, 1):
+            array = array if name else array[0]
+            continue
+        name, other = name if isinstance(name, tuple) else (name, False)
+        if array.ndim == 3 and not cut:
+            array = array.reshape(2, 2, 2, -1, array.shape[-1])
+        cut = True
+        i = half_index(name)
+        array = lax.dynamic_index_in_dim(array, 1 - i if other else i, 0, keepdims=False)
+    return array
 
 
 def halve(terms, name):
-    i = half_index(name)
-    theirs = add([lax.dynamic_index_in_dim(term, 1 - i, 0, keepdims=False) for term in terms])
+    theirs = add([half_of(term, ((name, True),)) for term in terms])
     got = exchange(theirs, name)
-    return [lax.dynamic_index_in_dim(term, i, 0, keepdims=False) for term in terms] + [got]
+    return [(array, names + (name,)) for array, names in terms] + [(got, (1,))]
+
+
+def both_halves(terms, name):
+    mine = add([half_of(term) for term in terms])
+    got = exchange(mine, name)
+    mine = lax.optimization_barrier(mine)
+    return mine, got
 
 
 def double(part, name):
     other = exchange(part, name)
     first = half_index(name) == 0
-    return jnp.concatenate([jnp.where(first, part, other), jnp.where(first, other, part)], axis=0)
-
-
-def sum_down(terms, order):
-    terms = cut_rows(terms, order)
-    for name in order:
-        terms = halve(terms, name)
-    return add(terms)
-
-
-def send_back(part, order, shape):
-    for name in reversed(order):
-        part = double(part, name)
-    return part.astype(F32).reshape(shape)
-
-
-def over_ctx(terms, order, shape):
-    if lax.axis_size("o") > 1:
-        return lax.psum(add(terms), ("o", "z", "y")).astype(F32).reshape(shape)
-    return send_back(sum_down(terms, order), order, shape)
-
-
-def sum_vectors(cut):
-    n_ctx = lax.axis_size("o") * 2 * LINE
-    cut = jnp.broadcast_to(cut[:, None], (4, n_ctx) + cut.shape[1:]).reshape((4 * n_ctx,) + cut.shape[1:])
-    got = lax.all_to_all(cut, ("fx", "core", "o", "z", "y"), 0, 0, tiled=True)
-    return jnp.sum(got.astype(F32), axis=0)
+    return jnp.where(first, jnp.concatenate([part, other], axis=0), jnp.concatenate([other, part], axis=0))
 
 
 def standard(values):
@@ -393,7 +410,7 @@
         target[j // 2, unit] = block
 
 
-def self_in_kernel(slot_ref, x_ref, *refs):
+def self_in_kernel(ready, slot_ref, x_ref, *refs):
     pieces, (n_ref, query_ref, kv_ref, vec_ref, full_ref, parts_ref, sems) = refs[:4], refs[4:]
     weights, shard = full_ref.shape[0], full_ref.shape[1] // 4
     extra = parts_ref.shape[1]
@@ -405,6 +422,7 @@
         copy.start()
         small.append(copy)
     copies = start_packed(pieces, slot_ref, full_ref, sems)
+    ready()
     z = standard(x_ref[...].astype(F32))[0]
     wait_all(small)
     parts = [parts_ref[lax.bitwise_xor(slot_ref[0], p)].astype(F32)[:, :shard] for p in range(4)]
@@ -421,18 +439,20 @@
     query_ref[...] = (dot(normed, full_ref[0]) + table[BIAS : BIAS + 1]).astype(BF)
 
 
-def cross_in_kernel(slot_ref, vec_ref, enc_ref, *refs):
+def cross_in_kernel(ready, slot_ref, vec_ref, enc_ref, *refs):
     pieces, (kv_ref, full_ref, sems) = refs[:4], refs[4:]
     copies = start_copies(pieces, PAIR_AT, slot_ref, full_ref, sems, 0)
+    ready()
     enc = enc_ref[...]
     wait_all(copies)
     kv_ref[0] = dot(enc, full_ref[0]).astype(BF)
     kv_ref[1] = (dot(enc, full_ref[1]) + vector(vec_ref, BIAS + 4)).astype(BF)
 
 
-def middle_kernel(slot_ref, vec_ref, mixed_ref, x_ref, *refs):
+def middle_kernel(ready, slot_ref, vec_ref, mixed_ref, x_ref, *refs):
     pieces, (res_ref, n_ref, query_ref, full_ref, sems) = refs[:4], refs[4:]
     copies = start_copies(pieces, REST_AT, slot_ref, full_ref, sems, 0)
+    ready()
     wait_all(copies)
     res = x_ref[...].astype(F32) + dot(mixed_ref[...], full_ref[1]) + vector(vec_ref, BIAS + 2)
     res_ref[...] = res
@@ -441,17 +461,20 @@
     query_ref[...] = (dot(normed, full_ref[0]) + vector(vec_ref, BIAS + 3)).astype(BF)
 
 
-def before_feed_kernel(slot_ref, vec_ref, mixed_ref, res_ref, *refs):
+def before_feed_kernel(ready, slot_ref, vec_ref, mixed_ref, res_ref, *refs):
     pieces, (out_ref, n_ref, full_ref, sems) = refs[:4], refs[4:]
-    wait_all(start_copies(pieces, LAST_AT, slot_ref, full_ref, sems, 0))
+    copies = start_copies(pieces, LAST_AT, slot_ref, full_ref, sems, 0)
+    ready()
+    wait_all(copies)
     res = res_ref[...] + dot(mixed_ref[...], full_ref[0]) + vector(vec_ref, BIAS + 5)
     out_ref[...] = res
     n_ref[...] = (standard(res)[0] * vector(vec_ref, GAIN + 2) + vector(vec_ref, BIAS + 8)).astype(BF)
 
 
-def feed_kernel(vec_ref, up_ref, down_ref, *refs):
+def feed_kernel(ready, vec_ref, up_ref, down_ref, *refs):
     normed_refs, cot_refs = refs[:4], refs[4:8]
     dn_keep, dn_send, out_keep, out_send, act_ref, dpre_ref, rows_ref = refs[8:]
+    ready()
     bias = vector(vec_ref, UP)
     total = None
     for j in (1, 3, 0, 2):
@@ -470,32 +493,34 @@
     rows_ref[0:1, :] = total
 
 
-def feed_grad_kernel(act_ref, dpre_ref, *refs):
-    normed_refs, cot_refs, (cut_ref,) = refs[:4], refs[4:8], refs[8:]
-    quarter, half = cut_ref.shape[-2:]
-
-    def put(grad, first):
+def feed_grad_kernel(ready, act_ref, dpre_ref, *refs):
+    normed_refs, cot_refs, (up_ref, down_ref) = refs[:4], refs[4:8], refs[8:]
+    quarter, half = up_ref.shape[-2:]
+    ready()
+
+    def put(grad, cut_ref):
         for p in range(4):
             for q in range(4):
                 rows = grad[(4 * p + q) * quarter : (4 * p + q + 1) * quarter].astype(BF)
-                cut_ref[q, 0, first + p] = rows[:, :half]
-                cut_ref[q, 1, first + p] = rows[:, half:]
+                cut_ref[q, 0, p] = rows[:, :half]
+                cut_ref[q, 1, p] = rows[:, half:]
 
     total = None
     for j in range(4):
         part = t_dot(normed_refs[j][...], dpre_ref[j])
         total = part if total is None else total + part
-    put(total, 0)
+    put(total, up_ref)
     total = None
     for j in range(4):
         part = t_dot(act_ref[j], cot_refs[j][...])
         total = part if total is None else total + part
-    put(total, 4)
-
-
-def after_feed_kernel(slot_ref, vec_ref, dn_ref, dn_near_ref, dn_far_ref, res_ref, cot_ref, *refs):
+    put(total, down_ref)
+
+
+def after_feed_kernel(ready, slot_ref, vec_ref, dn_ref, dn_near_ref, dn_far_ref, res_ref, cot_ref, *refs):
     pieces, (dres_ref, dout_ref, rows_ref, full_ref, sems) = refs[:4], refs[4:]
     copies = start_copies(pieces, LAST_AT, slot_ref, full_ref, sems, 0)
+    ready()
     dn = dn_ref[0].astype(F32) + dn_near_ref[0].astype(F32) + dn_far_ref[...].astype(F32)
     cot = cot_ref[...].astype(F32)
     dvalues, dgain, dshift = norm_back(dn, res_ref[...], vector(vec_ref, GAIN + 2))
@@ -510,9 +535,10 @@
     rows_ref[3:4, :] = column_sum(cot)
 
 
-def middle_back_kernel(slot_ref, vec_ref, dquery_ref, n_ref, res_ref, dres_ref, mixed_ref, cmixed_ref, *refs):
+def middle_back_kernel(ready, slot_ref, vec_ref, dquery_ref, n_ref, res_ref, dres_ref, mixed_ref, cmixed_ref, *refs):
     pieces, (dout_res_ref, dout_ref, keep_ref, send_ref, rows_ref, full_ref, turned_ref, sems) = refs[:4], refs[4:]
     copies = start_copies(pieces, REST_AT, slot_ref, full_ref, sems, 0)
+    ready()
     turned_ref[...] = n_ref[...].T
     dquery = dquery_ref[...]
     put_grad(0, turned_ref, dquery, slot_ref, keep_ref, send_ref)
@@ -540,10 +566,11 @@
     return total.astype(BF)
 
 
-def cross_back_kernel(count, slot_ref, enc_ref, n_ref, dquery_ref, *refs):
+def cross_back_kernel(count, ready, slot_ref, vec_ref, enc_ref, n_ref, dquery_ref, res_ref, out_ref, out_near_ref, out_far_ref, *refs):
     parts, pieces = refs[:count], refs[count : count + 4]
-    denc_ref, keep_ref, send_ref, rows_ref, full_ref, turned_ref, turned_enc_ref, sems = refs[count + 4 :]
+    denc_ref, layer_ref, keep_ref, send_ref, rows_ref, full_ref, turned_ref, turned_enc_ref, sems = refs[count + 4 :]
     copies = start_copies(pieces, PAIR_AT, slot_ref, full_ref, sems, 0)
+    ready()
     turned_ref[...] = n_ref[...].T
     put_grad(2, turned_ref, dquery_ref[...], slot_ref, keep_ref, send_ref)
     dkv = total_of(parts)
@@ -551,21 +578,26 @@
     put_grad(0, turned_enc_ref, dkv[0], slot_ref, keep_ref, send_ref)
     put_grad(1, turned_enc_ref, dkv[1], slot_ref, keep_ref, send_ref)
     rows_ref[0:1, :] = column_sum(dkv[1])
+    out = out_ref[0].astype(F32) + out_near_ref[0].astype(F32) + out_far_ref[...].astype(F32)
+    layer_ref[...] = (res_ref[...] + out + vector(vec_ref, DOWN)).astype(BF)
     wait_all(copies)
     denc_ref[...] = (dot_t(dkv[0], full_ref[0]) + dot_t(dkv[1], full_ref[1])).astype(BF)
 
 
-def self_back_kernel(count, slot_ref, vec_ref, x_ref, n_ref, dquery_ref, dres_ref, up_ref, ffn_ref, mid_ref, enc_ref, res_ref, out_ref, out_near_ref, out_far_ref, *refs):
+def self_back_kernel(count, ready, slot_ref, vec_ref, x_ref, n_ref, dquery_ref, dres_ref, up_ref, ffn_ref, mid_ref, enc_ref, *refs):
     parts, pieces = refs[:count], refs[count : count + 4]
-    dx_ref, layer_ref, keep_ref, send_ref, cut_ref, full_ref, turned_ref, sems = refs[count + 4 :]
+    dx_ref, keep_ref, send_ref, full_ref, turned_ref, sems = refs[count + 4 :]
     copies = start_packed(pieces, slot_ref, full_ref, sems)
+    ready()
     dkv = total_of(parts)
     dquery = dquery_ref[...]
     turned_ref[...] = n_ref[...].T
-    put_grad(0, turned_ref, dkv[0], slot_ref, keep_ref, send_ref)
-    put_grad(1, turned_ref, dkv[1], slot_ref, keep_ref, send_ref)
-    out = out_ref[0].astype(F32) + out_near_ref[0].astype(F32) + out_far_ref[...].astype(F32)
-    layer_ref[...] = (res_ref[...] + out + vector(vec_ref, DOWN)).astype(BF)
+    shard = turned_ref.shape[0] // 4
+    for j in range(4):
+        place = pl.ds(pl.multiple_of(slot_ref[j] * shard, shard), shard)
+        target = send_ref if j % 2 else keep_ref
+        target[j // 2, 0:shard] = dot(turned_ref[place, :], dkv[0]).astype(BF)
+        target[j // 2, shard : 2 * shard] = dot(turned_ref[place, :], dkv[1]).astype(BF)
     wait_all(copies)
     dn = dot_t(dquery, full_ref[0]) + dot_t(dkv[0], full_ref[1]) + dot_t(dkv[1], full_ref[2])
     dvalues, dgain, dshift = norm_back(dn, x_ref[...].astype(F32), vector(vec_ref, GAIN))
@@ -584,18 +616,55 @@
         mid_ref[1:2, :],
         ffn_ref[1:2, :],
     ]
-    shard = dgain.shape[1] // 4
     common = jnp.concatenate(rows + [ffn_ref[3:4, :]], axis=0)
-    pad = jnp.zeros((cut_ref.shape[1] - common.shape[0] - 4, shard), F32)
+    rest = keep_ref.shape[1] - 2 * shard
     for p in range(4):
         up = jnp.where(slot_ref[0] == p, up_ref[0:1, :], 0.0)
-        ups = [up[:, i * shard : (i + 1) * shard] for i in range(4)]
-        cut_ref[p] = jnp.concatenate([common[:, p * shard : (p + 1) * shard]] + ups + [pad], axis=0).astype(BF)
+        parts = [common[i : i + 1, p * shard : (p + 1) * shard] for i in range(common.shape[0])]
+        parts += [up[:, i * shard : (i + 1) * shard] for i in range(4)]
+        parts += [jnp.zeros_like(parts[0])] * (-len(parts) % 4)
+        lines = [jnp.concatenate(parts[i : i + 4], axis=1) for i in range(0, len(parts), 4)]
+        lines.append(jnp.zeros((rest - len(lines), common.shape[1]), F32))
+        lines = jnp.concatenate(lines, axis=0).astype(BF)
+        flip = lax.bitwise_xor(slot_ref[0], p)
+
+        @pl.when(lax.rem(flip, 2) == 0)
+        def _():
+            keep_ref[lax.div(flip, 2), 2 * shard :] = lines
+
+        @pl.when(lax.rem(flip, 2) == 1)
+        def _():
+            send_ref[lax.div(flip, 2), 2 * shard :] = lines
+
+
+def last_kernel(ready, late_ref, middle_ref, own_ref, attn_ref, out_ref, gain_ref, bias_ref, up_ref, down_ref):
+    ready()
+    shard = attn_ref.shape[1]
+
+    def part(ref, i):
+        return ref[i * shard : (i + 1) * shard, :].astype(F32)
+
+    for i, (ref, j) in enumerate(
+        [(late_ref, 2), (own_ref, 0), (own_ref, 1), (middle_ref, 0), (late_ref, 0), (late_ref, 1)]
+    ):
+        attn_ref[i] = part(ref, j)
+    out_ref[0] = part(middle_ref, 1)
+    out_ref[1] = part(middle_ref, 2)
+    sums = own_ref[2 * shard :, :].astype(F32)
+
+    def row(i):
+        return sums[i // 4 : i // 4 + 1, (i % 4) * shard : (i % 4 + 1) * shard]
+
+    gain_ref[...] = jnp.concatenate([row(i) for i in range(3)], axis=0)
+    bias_ref[...] = jnp.concatenate([row(i) for i in range(3, 12)], axis=0)
+    down_ref[...] = row(12)
+    up_ref[...] = jnp.concatenate([row(i) for i in range(13, 17)], axis=1)
 
 
 ROWS_CUT = 32
+ROWS_SUM = 64
 WHOLE = pl.BlockSpec(memory_space=pltpu.VMEM)
-LEFT = pl.BlockSpec(memory_space=pl.ANY)
+LEFT = pl.BlockSpec(memory_space=pltpu.HBM)
 SCALARS = pl.BlockSpec(memory_space=pltpu.SMEM)
 
 
@@ -605,16 +674,36 @@
 
 def dense(kernel, scalars, blocks, pieces, outs, scratch, microseconds, copies=None):
     copies = len(pieces) if copies is None else copies
-    held = sum(math.prod(b.shape) * b.dtype.itemsize for b in blocks)
+    held = 2 * sum(math.prod(b.shape) * b.dtype.itemsize for b in blocks)
     held += sum(math.prod(shape) * jnp.dtype(kind).itemsize for shape, kind in outs)
     held += sum(math.prod(ref.shape) * jnp.dtype(ref.dtype).itemsize for ref in scratch)
+    n_s, n_b, n_p, n_o = len(scalars), len(blocks), len(pieces), len(outs)
+
+    def body(*refs):
+        near, refs = refs[:n_s], refs[n_s:]
+        far, refs = refs[:n_b], refs[n_b:]
+        rest, refs = refs[: n_p + n_o], refs[n_p + n_o :]
+        local, sems, refs = refs[:n_b], refs[n_b], refs[n_b + 1 :]
+        fetches = [pltpu.make_async_copy(far[i], local[i], sems.at[i]) for i in range(n_b)]
+        for fetch in fetches:
+            fetch.start()
+
+        def ready():
+            for fetch in fetches:
+                fetch.wait()
+
+        kernel(ready, *near, *local, *rest, *refs)
+
     return pl.pallas_call(
-        kernel,
-        in_specs=[SCALARS] * len(scalars) + [WHOLE] * len(blocks) + [LEFT] * len(pieces),
-        out_specs=[WHOLE] * len(outs),
+        body,
+        in_specs=[SCALARS] * n_s + [LEFT] * (n_b + n_p),
+        out_specs=[pl.BlockSpec(shape, lambda d=len(shape): (0,) * d) for shape, _ in outs],
         out_shape=[jax.ShapeDtypeStruct(shape, kind) for shape, kind in outs],
-        scratch_shapes=scratch + ([pltpu.SemaphoreType.DMA((copies,))] if pieces else []),
-        compiler_params=pltpu.CompilerParams(vmem_limit_bytes=8 * MIB + held),
+        scratch_shapes=[pltpu.VMEM(b.shape, b.dtype) for b in blocks]
+        + [pltpu.SemaphoreType.DMA((n_b,))]
+        + scratch
+        + ([pltpu.SemaphoreType.DMA((copies,))] if pieces else []),
+        compiler_params=pltpu.CompilerParams(vmem_limit_bytes=60 * MIB),
         cost_estimate=cost(microseconds),
     )(*scalars, *blocks, *pieces)
 
@@ -656,22 +745,22 @@
     qkv_shard = jnp.concatenate([attn_weight[:3].reshape(3 * shard, width), vectors], axis=0)
     qkv_other = lax.ppermute(qkv_shard, "fx", SWAP)
     qkv_near = between_cores(qkv_shard)
-    x_bf, enc_bf, cot = deal([layer_in, encoded, out_cotangent])
-
-    group = o * 2 + y
-    spots = []
-    for step in range(groups):
-        source = lax.rem(group - step + groups, groups)
-        for flip in range(2):
-            c = core if flip == 0 else 1 - core
-            k = 2 * lax.rem(z, 2) + c
-            for r in range(LINE):
-                line = lax.rem(r - k + LINE, LINE)
-                spots.append((((source // 2) * LINE + line) * 2 + lax.rem(source, 2)) * 2 + c)
-    spans = jnp.take(pairing.reshape(-1), jnp.stack(spots), axis=0)
-    key_places = (spans[:, None] * half + jnp.arange(half, dtype=jnp.int32)[None, :]).reshape(-1, 1)
-    query_places = key_places[:rows].reshape(1, -1)
-    places = (key_places, query_places)
+    qkv_near, layer_in, encoded = hold(qkv_near, layer_in, encoded)
+    x_bf, enc_bf = deal([layer_in, encoded])
+
+    def places_of(pairing):
+        group = o * 2 + y
+        spots = []
+        for step in range(groups):
+            source = lax.rem(group - step + groups, groups)
+            for flip in range(2):
+                c = core if flip == 0 else 1 - core
+                k = 2 * lax.rem(z, 2) + c
+                for r in range(LINE):
+                    line = lax.rem(r - k + LINE, LINE)
+                    spots.append((((source // 2) * LINE + line) * 2 + lax.rem(source, 2)) * 2 + c)
+        spans = jnp.take(pairing.reshape(-1), jnp.stack(spots), axis=0)
+        return (spans[:, None] * half + jnp.arange(half, dtype=jnp.int32)[None, :]).reshape(-1, 1)
 
     product = 2 * rows * width * width
     square = (width, width)
@@ -686,10 +775,13 @@
 
     note = ((16, width), F32)
 
+    x_bf, enc_bf, qkv_other, qkv_near, attn_weight, out_weight, up_weight, out_cotangent, pairing = hold(
+        x_bf, enc_bf, qkv_other, qkv_near, attn_weight, out_weight, up_weight, out_cotangent, pairing
+    )
+    pair_shard = attn_weight[4:]
+    key_places = places_of(pairing)
     mid_shard = jnp.concatenate([attn_weight[4:], attn_weight[3:4], out_weight], axis=0)
-    x_bf, enc_bf, cot, qkv_other, qkv_near, mid_shard, pair_shard, rest_shard, up_weight = hold(
-        x_bf, enc_bf, cot, qkv_other, qkv_near, mid_shard, attn_weight[4:], mid_shard[2:], up_weight
-    )
+    rest_shard = jnp.concatenate([attn_weight[3:4], out_weight], axis=0)
     w_qkv = (qkv_shard, qkv_near, qkv_other, between_cores(qkv_other))
     pair_other = lax.ppermute(pair_shard, "fx", SWAP)
     mid_near = between_cores(mid_shard)
@@ -704,32 +796,40 @@
         4,
         copies=16,
     )
-    n1, query, kv, vec = hold(n1, query, kv, vec)
+    n1, query, kv, vec, up_weight, key_places, out_cotangent = hold(
+        n1, query, kv, vec, up_weight, key_places, out_cotangent
+    )
+    places = (key_places, key_places[:rows].reshape(1, -1))
     kv_self = to_others(kv, groups)
     near_self = between_cores(kv)
+    up_cut = up_weight.reshape(shard, 4, width).transpose(1, 0, 2)
+    cot_halves = deal_halves(out_cotangent)
     pair_other, rest_shard, mid_near = hold(pair_other, rest_shard, mid_near)
     rest_other = lax.ppermute(rest_shard, "fx", SWAP)
     w_pair = (mid_shard, mid_near, pair_other, between_cores(pair_other))
     (kv,) = dense(
         cross_in_kernel, [slots], [vec, enc_bf], w_pair, [((2, enc_rows, width), BF)], [weights(2)], 3.5
     )
-    kv_self, near_self, kv = hold(kv_self, near_self, kv)
+    kv_self, near_self, kv, cot_halves, up_cut = hold(kv_self, near_self, kv, cot_halves, up_cut)
+    cot = deal_line(*cot_halves)
     kv_cross = to_others(kv, groups)
     near_cross = between_cores(kv)
     kv_self = [kv_self[0], near_self] + with_cores(kv_self[1:])
     mixed, mass = attention(query, kv_self, places)
-    up_cut = up_weight.reshape(shard, 4, width).transpose(1, 0, 2)
-    mixed, mass, up_cut, rest_other, cot = hold(mixed, mass, up_cut, rest_other, cot)
+    mixed, mass, up_cut, rest_other, kv_cross, near_cross, cot = hold(
+        mixed, mass, up_cut, rest_other, kv_cross, near_cross, cot
+    )
     w_rest = (mid_shard, mid_near, rest_other, between_cores(rest_other))
+    kv_cross = [kv_cross[0], near_cross] + with_cores(kv_cross[1:])
+    r1, n2, cquery = dense(middle_kernel, [slots], [vec, mixed, x_bf], w_rest, [real, act, act], [weights(2)], 3.3)
+    r1, n2, cquery, kv_cross, up_cut = hold(r1, n2, cquery, kv_cross, up_cut)
     up_own = lax.all_to_all(up_cut, ("fx", "core"), 0, 0, tiled=True).reshape(width, width)
     cot_other = lax.ppermute(cot, "fx", SWAP)
     cot_near = between_cores(cot)
-    r1, n2, cquery = dense(middle_kernel, [slots], [vec, mixed, x_bf], w_rest, [real, act, act], [weights(2)], 3.3)
-    r1, n2, cquery, kv_cross, near_cross = hold(r1, n2, cquery, kv_cross, near_cross)
-    kv_cross = [kv_cross[0], near_cross] + with_cores(kv_cross[1:])
     cmixed, cmass = attention(cquery, kv_cross, None)
-    cmixed, cmass, cot_other, cot_near, up_own = hold(cmixed, cmass, cot_other, cot_near, up_own)
+    cmixed, cmass, cot_other, cot_near = hold(cmixed, cmass, cot_other, cot_near)
     r2, n3 = dense(before_feed_kernel, [slots], [vec, cmixed, r1], w_rest, [real, act], [weights(1)], 2.7)
+    r2, n3, cot_other = hold(r2, n3, cot_other)
     n3_other = lax.ppermute(n3, "fx", SWAP)
     cots = (cot, cot_near, cot_other, between_cores(cot_other))
     n3s = (n3, between_cores(n3), n3_other, between_cores(n3_other))
@@ -745,35 +845,36 @@
         8,
     )
 
-    order = ("y", "z0", "z1")
     single = outer == 1
 
     def step(terms, name):
         return halve(terms, name) if single else terms
+
+    def hold_all(*values):
+        flat = hold([[term[0] for term in v] if isinstance(v, list) else v for v in values])[0]
+        return [
+            [(array, term[1]) for array, term in zip(new, old)] if isinstance(old, list) else new
+            for new, old in zip(flat, values)
+        ]
 
     dn_got = between_cores(dn_send)
     dn_keep, dn_got, hidden_act, dpre = hold(dn_keep, dn_got, hidden_act, dpre)
     dn_far = lax.ppermute(add([dn_keep[1], dn_got[1]]), "fx", SWAP)
-    (feed,) = dense(
-        feed_grad_kernel,
-        [],
-        [hidden_act, dpre] + list(n3s) + list(cots),
-        [],
-        [((4, 2, 8, shard // 4, width // 2), BF)],
-        [],
-        6,
-    )
-    dn_far, feed, out_keep, out_send = hold(dn_far, feed, out_keep, out_send)
-    feed = [feed.reshape((2, 2, 2) + feed.shape[2:])]
-    feed = step(feed, "y")
+    cut = ((4, 2, 4, shard // 4, width // 2), BF)
+    up, down = dense(feed_grad_kernel, [], [hidden_act, dpre] + list(n3s) + list(cots), [], [cut, cut], [], 6)
+    dn_far, up, down, out_keep, out_send = hold(dn_far, up, down, out_keep, out_send)
+    up, down = ([(part.reshape((2, 2, 2) + part.shape[2:]), ())] for part in (up, down))
+    up, down = step(up, "y"), step(down, "z0")
+    out_got = between_cores(out_send)
     dr2, doc, ffn_rows = dense(
         after_feed_kernel, [slots], [vec, dn_keep, dn_got, dn_far, r2, cot], w_rest, [real, act, note], [weights(1)], 2.7
     )
 
     dcq, cmine, ctheirs = attention_back(cquery, doc, cmixed, cmass, kv_cross, None)
-    dcq, cmine, ctheirs, feed, dr2, ffn_rows = hold(dcq, cmine, ctheirs, feed, dr2, ffn_rows)
+    dcq, cmine, ctheirs, dr2, ffn_rows, out_keep, out_got, up, down = hold_all(
+        dcq, cmine, ctheirs, dr2, ffn_rows, out_keep, out_got, up, down
+    )
     cgot = between_cores(ctheirs)
-    feed = step(feed, "z0")
     dr1, dos, middle_keep, middle_send, mid_rows = dense(
         middle_back_kernel,
         [slots],
@@ -783,110 +884,125 @@
         [weights(2), turned],
         6,
     )
-    dr1, dos, middle_keep, middle_send, mid_rows, cgot, cmine = hold(
-        dr1, dos, middle_keep, middle_send, mid_rows, cgot, cmine
+    dr1, dos, middle_keep, middle_send, mid_rows, cgot, cmine, up, down, out_keep, out_got = hold_all(
+        dr1, dos, middle_keep, middle_send, mid_rows, cgot, cmine, up, down, out_keep, out_got
     )
     dckv = collect(cmine, cgot, groups)
-    middle_got = between_cores(middle_send)
+    middle = over_cores(middle_keep, middle_send)
+    up, down = step(up, "z0"), step(down, "z1")
+    out_far = lax.ppermute(add([out_keep[1], out_got[1]]), "fx", SWAP)
     dq, mine, theirs = attention_back(query, dos, mixed, mass, kv_self, places)
-    dq, mine, theirs, dckv, feed, middle_keep, middle_got = hold(dq, mine, theirs, dckv, feed, middle_keep, middle_got)
+    dq, mine, theirs, middle, up, down, out_far, dckv_a = hold_all(dq, mine, theirs, middle, up, down, out_far, dckv[-1])
+    dckv = dckv[:-1] + [dckv_a]
     got = between_cores(theirs)
-    middle = over_x([middle_keep, middle_got])
-    feed = step(feed, "z1")
-    mine, got, out_keep, out_send = hold(mine, got, out_keep, out_send)
-    dkv = collect(mine, got, groups)
-    out_got = between_cores(out_send)
-    grad_encoded, late_keep, late_send, enc_rows_sum = dense(
+    middle_a = part_over_x(middle, 0, 1)
+    grad_encoded, layer_out, late_keep, late_send, enc_rows_sum = dense(
         functools.partial(cross_back_kernel, len(dckv)),
         [slots],
-        [enc_bf, n1, dq] + dckv,
+        [vec, enc_bf, n1, dq, r2, out_keep, out_got, out_far] + dckv,
         w_pair,
-        [((enc_rows, width), BF)] + grads(3) + [note],
+        [((enc_rows, width), BF), act] + grads(3) + [note],
         [weights(2), turned, pltpu.VMEM((width, enc_rows), BF)],
         6,
     )
-    grad_encoded, late_keep, late_send, middle, feed, out_keep, out_got = hold(
-        grad_encoded, late_keep, late_send, middle, feed, out_keep, out_got
-    )
-    out_far = lax.ppermute(add([out_keep[1], out_got[1]]), "fx", SWAP)
-    (grad_encoded,) = undeal([grad_encoded], [F32])
-    late_got = between_cores(late_send)
-    middle = cut_rows(middle, order)
-    middle = step(middle, "y")
-    dkv, late_keep, late_got, out_far, feed, grad_encoded = hold(dkv, late_keep, late_got, out_far, feed, grad_encoded)
-    late = over_x([late_keep, late_got])
-    grad_layer, layer_out, keep, send, cut = dense(
+    mine, got, grad_encoded, layer_out, late_keep, late_send, enc_rows_sum, up, down, middle, middle_a = hold_all(
+        mine, got, grad_encoded, layer_out, late_keep, late_send, enc_rows_sum, up, down, middle, middle_a
+    )
+    dkv = collect(mine, got, groups)
+    late = over_cores(late_keep, late_send)
+    late, up, down, middle = hold_all(late, up, down, middle)
+    middle_b = part_over_x(middle, 1, 3)
+    if single:
+        up, down = both_halves(up, "z1"), both_halves(down, "y")
+        dkv_last, up, down, late, middle_b = hold(dkv[-1], up, down, [t[0] for t in late], middle_b)
+        late = [(array, ()) for array in late]
+    else:
+        dkv_last, late, middle_b = hold_all(dkv[-1], late, middle_b)
+    dkv = dkv[:-1] + [dkv_last]
+    middle = [(array, (0,)) for array, _ in middle] + [(jnp.concatenate([middle_a, middle_b], axis=0), ())]
+    late_a = part_over_x(late, 0, 1)
+    if single:
+        up, down = add(up), add(down)
+        up = lax.all_to_all(up, ("fx", "core"), 1, 1, tiled=True)
+    grad_layer, keep, send = dense(
         functools.partial(self_back_kernel, len(dkv)),
         [slots],
-        [vec, x_bf, n1, dq, dr1, up_rows, ffn_rows, mid_rows, enc_rows_sum, r2, out_keep, out_got, out_far] + dkv,
+        [vec, x_bf, n1, dq, dr1, up_rows, ffn_rows, mid_rows, enc_rows_sum] + dkv,
         w_qkv,
-        [act, act] + grads(2) + [((4, ROWS_CUT, shard), BF)],
+        [act] + [((2, 2 * shard + ROWS_SUM, width), BF)] * 2,
         [weights(3), turned],
         7,
         copies=12,
     )
+    grad_layer, keep, send, middle, late, late_a, up, down = hold_all(
+        grad_layer, keep, send, middle, late, late_a, up, down
+    )
+    own = over_cores(keep, send)
+    late_b = part_over_x(late, 1, 3)
     if single:
-        feed = add(feed)
-        feed_up = lax.all_to_all(feed[:4], ("fx", "core"), 0, 0, tiled=True)
-        feed = jnp.concatenate([feed_up, feed[4:]], axis=0)[None]
-    grad_layer, layer_out, keep, send, cut, middle, feed, late = hold(
-        grad_layer, layer_out, keep, send, cut, middle, feed, late
-    )
+        up, down = double(up, "z0"), double(down, "z1")
+        middle = halve(middle, "y")
+        own, up, down, middle, late, late_b = hold_all(own, up, down, middle, late, late_b)
+    late = [(array, (0,)) for array, _ in late] + [(jnp.concatenate([late_a, late_b], axis=0), ())]
     if single:
-        got = between_cores(send)
-        feed = double(feed, "z1")
-        middle = halve(middle, "z0")
-        late = halve(cut_rows(late, order), "y")
-        keep, got, feed, middle, late, grad_layer, layer_out = hold(keep, got, feed, middle, late, grad_layer, layer_out)
-        own = over_x([keep, got])
-        feed = double(feed, "z0")
-        middle = halve(middle, "z1")
-        late = halve(late, "z0")
-        own, feed, middle, late, grad_layer, layer_out = hold(own, feed, middle, late, grad_layer, layer_out)
-        own = add(own).reshape(2 * LINE, -1, width)
-        own = lax.all_to_all(own, ("z", "y"), 0, 0, tiled=True)
-        feed = double(feed, "y")
-        middle = double(add(middle), "z1")
-        late = halve(late, "z1")
-        own, feed, middle, late, grad_layer, layer_out = hold(own, feed, middle, late, grad_layer, layer_out)
+        own = add([half_of(term) for term in own])
+        own = jnp.where(fx == 0, own, own[::-1]).reshape(4 * LINE, -1, width)
+        own = lax.all_to_all(own, ("fx", "z", "y"), 0, 0, tiled=True)
+        up, down = double(up, "y"), double(down, "z0")
+        late, middle = halve(late, "y"), halve(middle, "z0")
+        late, middle, up, down, grad_layer = hold_all(late, middle, up, down, grad_layer)
+        late, middle = halve(late, "z0"), both_halves(middle, "z1")
+        late, middle = hold_all(late, [(part, ()) for part in middle])
+        middle = [part for part, _ in middle]
+        late, middle = both_halves(late, "z1"), double(add(middle), "z0")
+        own, late, middle = hold(own, late, middle)
         own = jnp.sum(own.astype(F32), axis=0, keepdims=True).astype(BF)
         own = lax.all_to_all(jnp.broadcast_to(own, (2 * LINE,) + own.shape[1:]), ("z", "y"), 0, 0, tiled=True)
-        middle = double(middle, "z0")
-        late = double(add(late), "z1")
-        own, middle, late, grad_layer, layer_out, cut = hold(own, middle, late, grad_layer, layer_out, cut)
-        total = sum_vectors(cut)
-        middle = double(middle, "y")
-        late = double(late, "z0")
-        layer_out, grad_layer = undeal([layer_out, grad_layer], [BF, F32])
-        middle, late = hold(middle, late)
-        late = double(late, "y").astype(F32).reshape(3, shard, width)
-        middle = middle.astype(F32).reshape(3, shard, width)
-        own = own.astype(F32).reshape(2, shard, width)
-        feed = feed.astype(F32).reshape(2, 2, 2, 8, shard // 4, width // 2)
+        late, middle = double(add(late), "z0"), double(middle, "y")
+        late, middle, grad_layer, grad_encoded, layer_out = hold(late, middle, grad_layer, grad_encoded, layer_out)
+        late = double(late, "y")
+        grad_encoded, layer_out, grad_layer = undeal([grad_encoded, layer_out, grad_layer], [F32, BF, F32])
+        grad_attn, grad_out, *total = dense(
+            last_kernel,
+            [],
+            [part.reshape(-1, width) for part in (late, middle, own)],
+            [],
+            [((6, shard, width), F32), ((2, shard, width), F32), ((3, shard), F32), ((9, shard), F32)]
+            + [((1, blocks * shard), F32), ((1, shard), F32)],
+            [],
+            3,
+        )
+        up, down = (part.astype(F32).reshape(2, 2, 2, 4, shard // 4, width // 2) for part in (up, down))
     else:
-        own = over_ctx(over_x(over_cores(keep, send)), (), (2, shard, width))
-        total = sum_vectors(cut)
-        layer_out, grad_layer = undeal([layer_out, grad_layer], [BF, F32])
-        feed = lax.psum(feed[0], ("o", "z", "y"))
-        feed_up = feed[:, :, :, :4].transpose(3, 0, 1, 2, 4, 5)
-        feed_up = lax.all_to_all(feed_up, ("fx", "core"), 0, 0, tiled=True).transpose(1, 2, 3, 0, 4, 5)
-        feed = jnp.concatenate([feed_up, feed[:, :, :, 4:]], axis=3).astype(F32)
-        middle = over_ctx([t.reshape(3, shard, width) for t in middle], order, (3, shard, width))
-        late = over_ctx(late, order, (3, shard, width))
-    g_up = feed[:, :, :, :4].transpose(0, 1, 4, 3, 2, 5).reshape(shard, hidden)
-    g_down = feed[:, :, :, 4:].transpose(3, 0, 1, 4, 2, 5).reshape(hidden // 4, width)
+        (grad_layer,) = undeal([grad_layer], [F32])
+        (grad_encoded,), (layer_out,) = undeal([grad_encoded], [F32]), undeal([layer_out], [BF])
+
+        def over_ctx(terms, n):
+            total = add([array[0] if 0 in names else array for array, names in terms])
+            return lax.psum(total, ("o", "z", "y")).astype(F32).reshape(n, -1, width)
+
+        own, middle, late = over_ctx(over_x(own), 1)[0], over_ctx(middle, 3), over_ctx(late, 3)
+        up, down = (lax.psum(part[0][0], ("o", "z", "y")).astype(F32) for part in (up, down))
+        up = lax.all_to_all(up.astype(BF), ("fx", "core"), 3, 3, tiled=True).astype(F32)
+        total = own[2 * shard : 2 * shard + 5].reshape(-1, shard)
+        total = [total[:3], total[3:12], total[13 : 13 + blocks].reshape(1, -1), total[12:13]]
+        own = own[: 2 * shard].reshape(2, shard, width)
+        grad_attn = jnp.concatenate([late[2:], own, middle[:1], late[:2]], axis=0)
+        grad_out = middle[1:]
+    g_up = up.transpose(0, 1, 4, 3, 2, 5).reshape(shard, hidden)
+    g_down = down.transpose(3, 0, 1, 4, 2, 5).reshape(hidden // 4, width)
     return (
         layer_out,
         grad_layer,
         grad_encoded,
-        jnp.concatenate([late[2:], own, middle[:1], late[:2]], axis=0),
-        middle[1:],
+        grad_attn,
+        grad_out,
         g_up,
         g_down,
-        total[:3],
-        total[3:12],
-        total[13 : 13 + blocks].reshape(-1),
-        total[12],
+        total[0],
+        total[1],
+        total[2].reshape(-1),
+        total[3].reshape(-1),
     )
 
 

time: 479 us -> 448 us (0.935)
  the two profiles are of different devices: /device:TPU:11 before, /device:TPU:9 now
where the time goes in v4:
time: 448 us; the launch traced here: 440 us
  waiting for transfers between devices  129 us (29%)
  Pallas kernels  112 us (25%)
  starting transfers between devices  104 us (23%)
  other arithmetic  56.2 us (13%)
  local copies, waits for them, and re-layouts  36.1 us (8%)
    pallas_call x11, Pallas kernels, dense(): pl.pallas_call(body, in_specs=[SCALARS] * n_s + [LEFT] * (n_b + n_p), out...  67.7 us
    ppermute x13, waiting for transfers between devices, exchange(): return lax.ppermute(array, 'z', [(i, i ^ flip) for i in range(LINE)])  48.3 us
    convert_element_type x23, other arithmetic, add(): return total.astype(BF)  26.9 us
    pallas_call x2, Pallas kernels, attention_back(): pl.pallas_call(functools.partial(backward_kernel, masked, len(kv)), grid=...  26.6 us
    ppermute x4, waiting for transfers between devices, undeal(): got.append(lax.ppermute(chunk, ('core', 'z'), [(b, a) for a, b in DEAL[r]]))  22.2 us
    ppermute x13, starting transfers between devices, exchange(): return lax.ppermute(array, 'z', [(i, i ^ flip) for i in range(LINE)])  19.1 us
    pallas_call x2, Pallas kernels, attention(): pl.pallas_call(functools.partial(forward_kernel, masked, len(kv)), grid=(...  17.9 us
    select_n x8, other arithmetic, double(): jnp.where(first, jnp.concatenate([part, other], axis=0), jnp.concatenate(...  15.2 us
  transfers between devices with their start and end apart: 69, of which 23 were waited for; matrix products, arithmetic and copies ran while one was open for 17% of the time, Pallas kernels for 22%

profile of v4, /device:TPU:9, one launch (start us, length us, event | category | flops | bytes accessed | tf_op | source)
XLA Modules:
  0.0 440.2 jit_solution(3531391959707318159)
XLA Ops:
  4.9 4.2 collective-permute-start.1
  9.3 2.5 collective-permute-start.3
  11.8 4.0 collective-permute-start.4
  16.3 5.6 %collective-permute-done.2 = bf16[2,64,768]{2,1,0:T(8,128)(2,1)S(1)} collective-permute-done((bf16[2,64,768]{2,1,0:T(8,128)(2,1)S(1)}, bf16[2,64,768]{2,1,0:T(8,128)(2,1)S(1)}, u32[]{:S(2)}, u32[]{:S(2)}) %collective-permute-start.2) | collective-permute-done | bytes 196640 | tf_op jit(solution)/shard_map/ppermute | solution.py:197
  21.9 2.5 collective-permute-done.3
  24.4 2.1 collective-permute-done.4
  33.5 5.1 %shard_map.203 = (bf16[256,768]{1,0:T(8,128)(2,1)}, bf16[256,768]{1,0:T(8,128)(2,1)}, bf16[2,256,768]{2,1,0:T(8,128)(2,1)}, f32[24,768]{1,0:T(8,128)}) custom-call(s32[4]{0:T(128)} %pad_add_fusion.refs_0_, bf16[256,768]{1,0:T(8,128)(2,1)} %pad_maximum_fusion.4.refs_1_.refs_3_.refs_2_, bf16[608,768]{1,0:T(8,128)(2,1)} %copy-done.4, ...), custom_call_target="tpu_custom_call" | custom-call | bytes 14000000 | tf_op jit(solution)/shard_map/pallas_call | solution.py:697
  40.6 2.1 pad_maximum_fusion.2
  42.7 3.0 collective-permute-done.9.refs_5_.refs_14_
  49.3 2.4 copy.50
  52.5 4.2 shard_map.204.refs_1_.refs_4_
  61.3 5.8 %all-to-all-start = ((bf16[4,64,768]{2,1,0:T(8,128)(2,1)}), bf16[4,64,768]{2,1,0:T(8,128)(2,1)S(1)}, u32[]{:S(2)}, u32[]{:S(2)}) async-start(bf16[4,64,768]{2,1,0:T(8,128)(2,1)} %maximum_select_fusion.8), calls=%async_computation | async-start | bytes 786432 | tf_op jit(solution)/shard_map/all_to_all | solution.py:213
  68.7 6.7 %all-to-all-done = bf16[4,64,768]{2,1,0:T(8,128)(2,1)S(1)} async-done(((bf16[4,64,768]{2,1,0:T(8,128)(2,1)}), bf16[4,64,768]{2,1,0:T(8,128)(2,1)S(1)}, u32[]{:S(2)}, u32[]{:S(2)}) %all-to-all-start) | async-done | bytes 393248 | tf_op jit(solution)/shard_map/all_to_all | solution.py:213
  76.6 9.2 %shard_map.205 = (bf16[256,768]{1,0:T(8,128)(2,1)}, f32[6,1,512]{2,1,0:T(1,128)}) custom-call(s32[1024,1]{1,0:T(8,128)} %copy.37.refs_0_, s32[1,256]{1,0:T(1,128)} %slice_bitcast_fusion.20.refs_1_, bf16[256,768]{1,0:T(8,128)(2,1)} %get-tuple-element.259.refs_2_, bf16[2,256,768]{2,1,0:T(8,128)(2,1)} %get-tuple-element.268.refs_3_.refs_6_, ...), custom_call_target="tpu_custom_call" | custom-call | bytes 28000000 | tf_op jit(solution)/shard_map/pallas_call | solution.py:128
  85.8 2.1 collective-permute-start.17
  91.4 4.7 %shard_map.206 = (f32[256,768]{1,0:T(8,128)}, bf16[256,768]{1,0:T(8,128)(2,1)}, bf16[256,768]{1,0:T(8,128)(2,1)}) custom-call(s32[4]{0:T(128)} %pad_add_fusion.refs_0_, f32[24,768]{1,0:T(8,128)} %get-tuple-element.256.refs_1_.refs_0_, bf16[256,768]{1,0:T(8,128)(2,1)} %get-tuple-element.278.refs_2_.refs_6_.refs_4_, ...), custom_call_target="tpu_custom_call" | custom-call | bytes 11550000 | tf_op jit(solution)/shard_map/pallas_call | solution.py:697
  96.1 4.0 all-to-all-start.1
  100.1 8.7 %shard_map.207 = (bf16[256,768]{1,0:T(8,128)(2,1)}, f32[6,1,512]{2,1,0:T(1,128)}) custom-call(bf16[256,768]{1,0:T(8,128)(2,1)} %get-tuple-element.287.refs_0_, bf16[2,256,768]{2,1,0:T(8,128)(2,1)} %shard_map.204.refs_1_.refs_4_, bf16[2,256,768]{2,1,0:T(8,128)(2,1)} %collective-permute-done.16.refs_2_.refs_5_, bf16[2,256,768]{2,1,0:T(8,128)(2,1)} %copy-done.18, ...), custom_call_target="tpu_custom_call" | custom-call | bytes 28000000 | tf_op jit(solution)/shard_map/pallas_call | solution.py:128
  108.9 3.8 shard_map.208
  114.8 8.9 %collective-permute-done.22.refs_5_.refs_4_ = bf16[256,768]{1,0:T(8,128)(2,1)S(1)} collective-permute-done((bf16[256,768]{1,0:T(8,128)(2,1)}, bf16[256,768]{1,0:T(8,128)(2,1)S(1)}, u32[]{:S(2)}, u32[]{:S(2)}) %collective-permute-start.22) | collective-permute-done | bytes 393248 | tf_op jit(solution)/shard_map/ppermute | solution.py:833
  127.0 9.8 %shard_map.209 = (bf16[2,256,768]{2,1,0:T(8,128)(2,1)}, bf16[2,256,768]{2,1,0:T(8,128)(2,1)}, bf16[2,256,768]{2,1,0:T(8,128)(2,1)}, bf16[2,256,768]{2,1,0:T(8,12...) custom-call(f32[24,768]{1,0:T(8,128)} %get-tuple-element.256.refs_1_.refs_0_, ...), custom_call_target="tpu_custom_call" | custom-call | bytes 28000000 | tf_op jit(solution)/shard_map/pallas_call | solution.py:697
  137.3 2.1 collective-permute-done.25.refs_3_
  142.2 6.9 %shard_map.210 = (bf16[4,2,4,48,384]{4,3,2,1,0:T(8,128)(2,1)}, bf16[4,2,4,48,384]{4,3,2,1,0:T(8,128)(2,1)}) custom-call(bf16[4,256,768]{2,1,0:T(8,128)(2,1)} %get-tuple-element.310.refs_0_, bf16[4,256,768]{2,1,0:T(8,128)(2,1)} %get-tuple-element.311.refs_1_, bf16[256,768]{1,0:T(8,128)(2,1)} %get-tuple-element.301.refs_3_.refs_2_, ...), custom_call_target="tpu_custom_call" | custom-call | bytes 21000000 | tf_op jit(solution)/shard_map/pallas_call | solution.py:697
  149.1 2.0 collective-permute-done.26.refs_4_
  153.5 2.3 collective-permute-start.29
  156.2 4.8 %shard_map.211 = (f32[256,768]{1,0:T(8,128)}, bf16[256,768]{1,0:T(8,128)(2,1)}, f32[16,768]{1,0:T(8,128)}) custom-call(s32[4]{0:T(128)} %pad_add_fusion.refs_0_, f32[24,768]{1,0:T(8,128)} %get-tuple-element.256.refs_1_.refs_0_, bf16[2,256,768]{2,1,0:T(8,128)(2,1)} %get-tuple-element.308.refs_2_, bf16[2,256,768]{2,1,0:T(8,128)(2,1)} %copy-done.25, ...), custom_call_target="tpu_custom_call" | custom-call | bytes 9450000 | tf_op jit(solution)/shard_map/pallas_call | solution.py:697
  160.9 13.2 %shard_map.212 = (bf16[256,768]{1,0:T(8,128)(2,1)}, bf16[2,2,256,768]{3,2,1,0:T(8,128)(2,1)}, bf16[2,2,256,768]{3,2,1,0:T(8,128)(2,1)}) custom-call(bf16[256,768]{1,0:T(8,128)(2,1)} %get-tuple-element.287.refs_0_, bf16[256,768]{1,0:T(8,128)(2,1)} %get-tuple-element.318.refs_1_, bf16[256,768]{1,0:T(8,128)(2,1)} %get-tuple-element.296.refs_2_.refs_7_, ...), custom_call_target="tpu_custom_call" | custom-call | bytes 45500000 | tf_op jit(solution)/shard_map/pallas_call | solution.py:158
  176.2 7.1 %shard_map.213 = (f32[256,768]{1,0:T(8,128)}, bf16[256,768]{1,0:T(8,128)(2,1)}, bf16[2,3,192,768]{3,2,1,0:T(8,128)(2,1)}, bf16[2,3,192,768]{3,2,1,0:T(8,128)(2,1)}, f32[16,768]{1,0:T(8,128)}) custom-call(s32[4]{0:T(128)} %pad_add_fusion.refs_0_, f32[24,768]{1,0:T(8,128)} %get-tuple-element.256.refs_1_.refs_0_, bf16[256,768]{1,0:T(8,128)(2,1)} %get-tuple-element.329.refs_2_, ...), custom_call_target="tpu_custom_call" | custom-call | bytes 21000000 | tf_op jit(solution)/shard_map/pallas_call | solution.py:697
  184.6 2.3 fusion
  189.7 1.8 fusion.8
  191.5 1.7 fusion.9
  194.7 13.4 %shard_map.214 = (bf16[256,768]{1,0:T(8,128)(2,1)}, bf16[2,2,256,768]{3,2,1,0:T(8,128)(2,1)}, bf16[2,2,256,768]{3,2,1,0:T(8,128)(2,1)}) custom-call(s32[1024,1]{1,0:T(8,128)} %copy.37.refs_0_, s32[1,256]{1,0:T(1,128)} %slice_bitcast_fusion.20.refs_1_, bf16[256,768]{1,0:T(8,128)(2,1)} %get-tuple-element.259.refs_2_, ...), custom_call_target="tpu_custom_call" | custom-call | bytes 45500000 | tf_op jit(solution)/shard_map/pallas_call | solution.py:158
  208.1 1.6 collective-permute-start.36
  209.9 8.3 %shard_map.215 = (bf16[256,768]{1,0:T(8,128)(2,1)}, bf16[256,768]{1,0:T(8,128)(2,1)}, bf16[2,3,192,768]{3,2,1,0:T(8,128)(2,1)}, bf16[2,3,192,768]{3,2,1,0:T(8,128)(2,1)}, f32[16,768]{1,0:T(8,128)}) custom-call(s32[4]{0:T(128)} %pad_add_fusion.refs_0_, f32[24,768]{1,0:T(8,128)} %get-tuple-element.256.refs_1_.refs_0_, ...), custom_call_target="tpu_custom_call" | custom-call | bytes 21000000 | tf_op jit(solution)/shard_map/pallas_call | solution.py:697
  221.2 1.8 collective-permute-done.39
  228.2 11.9 %collective-permute-done.38.refs_12_ = bf16[2,256,768]{2,1,0:T(8,128)(2,1)S(1)} collective-permute-done((bf16[2,256,768]{2,1,0:T(8,128)(2,1)S(1)}, bf16[2,256,768]{2,1,0:T(8,128)(2,1)S(1)}, u32[]{:S(2)}, u32[]{:S(2)}) %collective-permute-start.38) | collective-permute-done | bytes 786464 | tf_op jit(solution)/shard_map/ppermute | solution.py:253
  240.2 6.3 %collective-permute-done.41 = bf16[2,4,48,384]{3,2,1,0:T(8,128)(2,1)S(1)} collective-permute-done((bf16[2,4,48,384]{3,2,1,0:T(8,128)(2,1)S(1)}, bf16[2,4,48,384]{3,2,1,0:T(8,128)(2,1)S(1)}, u32[]{:S(2)}, u32[]{:S(2)}) %collective-permute-start.41) | collective-permute-done | bytes 294944 | tf_op jit(solution)/shard_map/ppermute | solution.py:294
  248.8 5.0 %all-to-all-start.2 = ((bf16[2,4,48,384]{3,2,0,1:T(8,128)(2,1)}), bf16[2,4,48,384]{3,2,0,1:T(8,128)(2,1)}, u32[]{:S(2)}, u32[]{:S(2)}) async-start(bf16[2,4,48,384]{3,2,0,1:T(8,128)(2,1)} %add_convert_fusion.10), calls=%async_computation.2 | async-start | bytes 589824 | tf_op jit(solution)/shard_map/all_to_all | solution.py:926
  253.8 1.8 fusion.22
  257.0 2.1 pad_maximum_fusion.3
  259.2 9.0 %shard_map.216 = (bf16[256,768]{1,0:T(8,128)(2,1)}, bf16[2,448,768]{2,1,0:T(8,128)(2,1)}, bf16[2,448,768]{2,1,0:T(8,128)(2,1)}) custom-call(s32[4]{0:T(128)} %pad_add_fusion.refs_0_, f32[24,768]{1,0:T(8,128)} %get-tuple-element.256.refs_1_.refs_0_, bf16[256,768]{1,0:T(8,128)(2,1)} %pad_maximum_fusion.4.refs_1_.refs_3_.refs_2_, ...), custom_call_target="tpu_custom_call" | custom-call | bytes 24500000 | tf_op jit(solution)/shard_map/pallas_call | solution.py:697
  268.2 1.7 add_convert_fusion.9
  270.6 2.2 fusion.3
  276.5 10.2 %collective-permute-done.46 = bf16[2,4,48,384]{3,2,1,0:T(8,128)(2,1)} collective-permute-done((bf16[2,4,48,384]{3,2,1,0:T(8,128)(2,1)}, bf16[2,4,48,384]{3,2,1,0:T(8,128)(2,1)}, u32[]{:S(2)}, u32[]{:S(2)}) %collective-permute-start.46) | collective-permute-done | bytes 294944 | tf_op jit(solution)/shard_map/ppermute | solution.py:296
  286.7 2.2 maximum_select_fusion.5
  289.0 2.1 maximum_select_fusion.4
  291.1 1.7 add_convert_fusion
  294.2 6.7 %all-to-all-start.3 = ((bf16[16,56,768]{2,1,0:T(8,128)(2,1)}), bf16[16,56,768]{2,1,0:T(8,128)(2,1)}, u32[]{:S(2)}, u32[]{:S(2)}) async-start(bf16[16,56,768]{2,1,0:T(8,128)(2,1)} %bitcast.215), calls=%async_computation.3 | async-start | bytes 2752512 | tf_op jit(solution)/shard_map/all_to_all | solution.py:950
  311.7 23.8 %collective-permute-done.52 = bf16[4,4,48,384]{3,2,1,0:T(8,128)(2,1)} collective-permute-done((bf16[4,4,48,384]{3,2,1,0:T(8,128)(2,1)}, bf16[4,4,48,384]{3,2,1,0:T(8,128)(2,1)}, u32[]{:S(2)}, u32[]{:S(2)}) %collective-permute-start.52) | collective-permute-done | bytes 589856 | tf_op jit(solution)/shard_map/ppermute | solution.py:296
  335.5 2.5 maximum_select_fusion.1
  338.0 2.5 maximum_select_fusion
  341.9 3.1 collective-permute-start.54
  347.7 6.6 %collective-permute-done.54 = bf16[2,72,768]{2,1,0:T(8,128)(2,1)S(1)} collective-permute-done((bf16[2,72,768]{2,1,0:T(8,128)(2,1)S(1)}, bf16[2,72,768]{2,1,0:T(8,128)(2,1)S(1)}, u32[]{:S(2)}, u32[]{:S(2)}) %collective-permute-start.54) | collective-permute-done | bytes 221216 | tf_op jit(solution)/shard_map/ppermute | solution.py:296
  358.4 3.1 collective-permute-start.55
  362.3 7.7 %collective-permute-done.55 = bf16[2,72,768]{2,1,0:T(8,128)(2,1)S(1)} collective-permute-done((bf16[2,72,768]{2,1,0:T(8,128)(2,1)S(1)}, bf16[2,72,768]{2,1,0:T(8,128)(2,1)S(1)}, u32[]{:S(2)}, u32[]{:S(2)}) %collective-permute-start.55) | collective-permute-done | bytes 221216 | tf_op jit(solution)/shard_map/ppermute | solution.py:296
  370.7 2.4 collective-permute-start.57
  374.6 2.9 reshape.1338
  382.8 4.6 %all-to-all-start.4 = ((bf16[8,56,768]{2,1,0:T(8,128)(2,1)}), bf16[8,56,768]{2,1,0:T(8,128)(2,1)S(1)}, u32[]{:S(2)}, u32[]{:S(2)}) async-start(bf16[8,56,768]{2,1,0:T(8,128)(2,1)} %broadcast_in_dim.4), calls=%async_computation.4 | async-start | bytes 1376256 | tf_op jit(solution)/shard_map/all_to_all | solution.py:960
  388.8 2.5 maximum_select_fusion.2
  392.7 5.2 %collective-permute-start.59 = (bf16[3,64,768]{2,1,0:T(8,128)(2,1)S(1)}, bf16[3,64,768]{2,1,0:T(8,128)(2,1)S(1)}, u32[]{:S(2)}, u32[]{:S(2)}) collective-permute-start(bf16[3,64,768]{2,1,0:T(8,128)(2,1)S(1)} %pad_maximum_fusion.6), channel_id=1, source_target_pairs={{0,0},{10,2},{2,4},{8,6},{4,8},{14,10},{6,12},{12,14},{1,1},{11,3}... | collective-permute-start | bytes 884744 | tf_op jit(solution)/shard_map/ppermute | solution.py:225
  397.9 1.9 collective-permute-start.62
  401.1 6.4 %collective-permute-start.61 = (bf16[3,64,768]{2,1,0:T(8,128)(2,1)S(1)}, bf16[3,64,768]{2,1,0:T(8,128)(2,1)S(1)}, u32[]{:S(2)}, u32[]{:S(2)}) collective-permute-start(bf16[3,64,768]{2,1,0:T(8,128)(2,1)S(1)} %pad_maximum_fusion.8), channel_id=1, source_target_pairs={{2,0},{8,2},{0,4},{10,6},{6,8},{12,10},{4,12},{14,14},{3,1},{9,3},... | collective-permute-start | bytes 884744 | tf_op jit(solution)/shard_map/ppermute | solution.py:225
  407.6 22.2 %collective-permute-done.60 = bf16[3,64,768]{2,1,0:T(8,128)(2,1)S(1)} collective-permute-done((bf16[3,64,768]{2,1,0:T(8,128)(2,1)S(1)}, bf16[3,64,768]{2,1,0:T(8,128)(2,1)S(1)}, u32[]{:S(2)}, u32[]{:S(2)}) %collective-permute-start.60) | collective-permute-done | bytes 294944 | tf_op jit(solution)/shard_map/ppermute | solution.py:225
  434.7 4.0 shard_map.217
  (328 shorter events, 102.7 us)
Async XLA Ops:
  2.7 25.4 %collective-permute-start.5 = (bf16[608,768]{1,0:T(8,128)(2,1)S(1)}, bf16[608,768]{1,0:T(8,128)(2,1)}, u32[]{:S(2)}, u32[]{:S(2)}) collective-permute-start(bf16[608,768]{1,0:T(8,128)(2,1)S(1)} %pad_maximum_fusion.1.refs_2_.refs_13_), channel_id=1, source_target_pairs={{0,16},{16,0},{1,17},{17,1},{2,18},{18,2},{3,19},{19,3},{4,20},{20... | collective-permute-start | bytes 2801672 | tf_op jit(solution)/shard_map/ppermute | solution.py:746
  4.9 11.3 %collective-permute-start.1 = (bf16[2,64,768]{2,1,0:T(8,128)(2,1)S(1)}, bf16[2,64,768]{2,1,0:T(8,128)(2,1)S(1)}, u32[]{:S(2)}, u32[]{:S(2)}) collective-permute-start(bf16[2,64,768]{2,1,0:T(8,128)(2,1)S(1)} %pad_maximum_fusion.10), channel_id=1, source_target_pairs={{0,0},{2,10},{4,2},{6,8},{8,4},{10,14},{12,6},{14,12},{1,1},{3,11}... | collective-permute-start | bytes 589832 | tf_op jit(solution)/shard_map/ppermute | solution.py:197
  9.2 12.7 %collective-permute-start.2 = (bf16[2,64,768]{2,1,0:T(8,128)(2,1)S(1)}, bf16[2,64,768]{2,1,0:T(8,128)(2,1)S(1)}, u32[]{:S(2)}, u32[]{:S(2)}) collective-permute-start(bf16[2,64,768]{2,1,0:T(8,128)(2,1)S(1)} %pad_maximum_fusion.11), channel_id=1, source_target_pairs={{0,8},{2,0},{4,10},{6,2},{8,12},{10,4},{12,14},{14,6},{1,9},{3,1},... | collective-permute-start | bytes 589832 | tf_op jit(solution)/shard_map/ppermute | solution.py:197
  9.3 15.1 %collective-permute-start.3 = (bf16[2,64,768]{2,1,0:T(8,128)(2,1)S(1)}, bf16[2,64,768]{2,1,0:T(8,128)(2,1)S(1)}, u32[]{:S(2)}, u32[]{:S(2)}) collective-permute-start(bf16[2,64,768]{2,1,0:T(8,128)(2,1)S(1)} %pad_maximum_fusion.12), channel_id=1, source_target_pairs={{0,2},{2,8},{4,0},{6,10},{8,6},{10,12},{12,4},{14,14},{1,3},{3,9},... | collective-permute-start | bytes 589832 | tf_op jit(solution)/shard_map/ppermute | solution.py:197
  11.8 14.7 %collective-permute-start.4 = (bf16[2,64,768]{2,1,0:T(8,128)(2,1)S(1)}, bf16[2,64,768]{2,1,0:T(8,128)(2,1)S(1)}, u32[]{:S(2)}, u32[]{:S(2)}) collective-permute-start(bf16[2,64,768]{2,1,0:T(8,128)(2,1)S(1)} %pad_maximum_fusion.13), channel_id=1, source_target_pairs={{0,10},{2,2},{4,8},{6,0},{8,14},{10,6},{12,12},{14,4},{1,11},{3,3}... | collective-permute-start | bytes 589832 | tf_op jit(solution)/shard_map/ppermute | solution.py:197
  29.0 16.7 %collective-permute-start.10 = (bf16[5,192,768]{2,1,0:T(8,128)(2,1)S(1)}, bf16[5,192,768]{2,1,0:T(8,128)(2,1)S(1)}, u32[]{:S(2)}, u32[]{:S(2)}) collective-permute-start(bf16[5,192,768]{2,1,0:T(8,128)(2,1)S(1)} %pad_maximum_fusion.refs_3_.refs_4_.refs_7_.refs_8_.refs_12_), channel_id=1, source_target_pairs={{0,8},{8,0},{1,9},{9,1},{2,10},{10,2},{3,11},{11,3},{4,12},{12,4},... | collective-permute-start | bytes 4423688 | tf_op jit(solution)/shard_map/ppermute | solution.py:258
  30.3 15.3 %collective-permute-start.9 = (bf16[2,192,768]{2,1,0:T(8,128)(2,1)}, bf16[2,192,768]{2,1,0:T(8,128)(2,1)}, u32[]{:S(2)}, u32[]{:S(2)}) collective-permute-start(bf16[2,192,768]{2,1,0:T(8,128)(2,1)} %copy-done.23), channel_id=1, source_target_pairs={{0,16},{16,0},{1,17},{17,1},{2,18},{18,2},{3,19},{19,3},{4,20},{20... | collective-permute-start | bytes 1769480 | tf_op jit(solution)/shard_map/ppermute | solution.py:786
  38.6 19.1 %collective-permute-start.7 = (bf16[2,256,768]{2,1,0:T(8,128)(2,1)}, bf16[2,256,768]{2,1,0:T(8,128)(2,1)}, u32[]{:S(2)}, u32[]{:S(2)}) collective-permute-start(bf16[2,256,768]{2,1,0:T(8,128)(2,1)} %get-tuple-element.268.refs_3_.refs_6_), channel_id=1, source_target_pairs={{0,1},{1,0},{2,3},{3,2},{4,5},{5,4},{6,7},{7,6},{8,9},{9,8},{10,11... | collective-permute-start | bytes 2359304 | tf_op jit(solution)/shard_map/ppermute | solution.py:239
  40.0 17.8 %collective-permute-start.8 = (bf16[2,256,768]{2,1,0:T(8,128)(2,1)}, bf16[2,256,768]{2,1,0:T(8,128)(2,1)}, u32[]{:S(2)}, u32[]{:S(2)}) collective-permute-start(bf16[2,256,768]{2,1,0:T(8,128)(2,1)} %get-tuple-element.268.refs_3_.refs_6_), channel_id=1, source_target_pairs={{0,8},{8,0},{1,9},{9,1},{2,10},{10,2},{3,11},{11,3},{4,12},{12,4},... | collective-permute-start | bytes 2359304 | tf_op jit(solution)/shard_map/ppermute | solution.py:258
  45.7 6.0 %collective-permute-start.11 = (bf16[2,192,768]{2,1,0:T(8,128)(2,1)}, bf16[2,192,768]{2,1,0:T(8,128)(2,1)S(1)}, u32[]{:S(2)}, u32[]{:S(2)}) collective-permute-start(bf16[2,192,768]{2,1,0:T(8,128)(2,1)} %collective-permute-done.9.refs_5_.refs_14_), channel_id=1, source_target_pairs={{0,8},{8,0},{1,9},{9,1},{2,10},{10,2},{3,11},{11,3},{4,12},{12,4},... | collective-permute-start | bytes 1769480 | tf_op jit(solution)/shard_map/ppermute | solution.py:258
  47.5 9.2 %collective-permute-start.12 = (bf16[2,64,768]{2,1,0:T(8,128)(2,1)S(1)}, bf16[2,64,768]{2,1,0:T(8,128)(2,1)S(1)}, u32[]{:S(2)}, u32[]{:S(2)}) collective-permute-start(bf16[2,64,768]{2,1,0:T(8,128)(2,1)S(1)} %get-tuple-element.487), channel_id=1, source_target_pairs={{0,8},{8,0},{1,9},{9,1},{2,10},{10,2},{3,11},{11,3},{4,12},{12,4},... | collective-permute-start | bytes 589832 | tf_op jit(solution)/shard_map/ppermute | solution.py:206
  48.1 37.7 %collective-permute-start.14 = (bf16[3,192,768]{2,1,0:T(8,128)(2,1)}, bf16[3,192,768]{2,1,0:T(8,128)(2,1)S(1)}, u32[]{:S(2)}, u32[]{:S(2)}) collective-permute-start(bf16[3,192,768]{2,1,0:T(8,128)(2,1)} %pad_maximum_fusion.2), channel_id=1, source_target_pairs={{0,16},{16,0},{1,17},{17,1},{2,18},{18,2},{3,19},{19,3},{4,20},{20... | collective-permute-start | bytes 2654216 | tf_op jit(solution)/shard_map/ppermute | solution.py:808
  57.8 28.0 %collective-permute-start.15 = (bf16[2,256,768]{2,1,0:T(8,128)(2,1)}, bf16[2,256,768]{2,1,0:T(8,128)(2,1)S(1)}, u32[]{:S(2)}, u32[]{:S(2)}) collective-permute-start(bf16[2,256,768]{2,1,0:T(8,128)(2,1)} %shard_map.204.refs_1_.refs_4_), channel_id=1, source_target_pairs={{0,1},{1,0},{2,3},{3,2},{4,5},{5,4},{6,7},{7,6},{8,9},{9,8},{10,11... | collective-permute-start | bytes 2359304 | tf_op jit(solution)/shard_map/ppermute | solution.py:239
  59.0 26.8 %collective-permute-start.16 = (bf16[2,256,768]{2,1,0:T(8,128)(2,1)}, bf16[2,256,768]{2,1,0:T(8,128)(2,1)}, u32[]{:S(2)}, u32[]{:S(2)}) collective-permute-start(bf16[2,256,768]{2,1,0:T(8,128)(2,1)} %shard_map.204.refs_1_.refs_4_), channel_id=1, source_target_pairs={{0,8},{8,0},{1,9},{9,1},{2,10},{10,2},{3,11},{11,3},{4,12},{12,4},... | collective-permute-start | bytes 2359304 | tf_op jit(solution)/shard_map/ppermute | solution.py:258
  60.5 15.1 %collective-permute-start.13 = (bf16[2,256,768]{2,1,0:T(8,128)(2,1)}, bf16[2,256,768]{2,1,0:T(8,128)(2,1)S(1)}, u32[]{:S(2)}, u32[]{:S(2)}) collective-permute-start(bf16[2,256,768]{2,1,0:T(8,128)(2,1)} %collective-permute-done.7.refs_5_.refs_8_), channel_id=1, source_target_pairs={{0,8},{8,0},{1,9},{9,1},{2,10},{10,2},{3,11},{11,3},{4,12},{12,4},... | collective-permute-start | bytes 2359304 | tf_op jit(solution)/shard_map/ppermute | solution.py:245
  61.3 14.2 %all-to-all-start = ((bf16[4,64,768]{2,1,0:T(8,128)(2,1)}), bf16[4,64,768]{2,1,0:T(8,128)(2,1)S(1)}, u32[]{:S(2)}, u32[]{:S(2)}) async-start(bf16[4,64,768]{2,1,0:T(8,128)(2,1)} %maximum_select_fusion.8), calls=%async_computation | async-start | bytes 786432 | tf_op jit(solution)/shard_map/all_to_all | solution.py:213
  85.8 4.6 %collective-permute-start.17 = (bf16[3,192,768]{2,1,0:T(8,128)(2,1)S(1)}, bf16[3,192,768]{2,1,0:T(8,128)(2,1)S(1)}, u32[]{:S(2)}, u32[]{:S(2)}) collective-permute-start(bf16[3,192,768]{2,1,0:T(8,128)(2,1)S(1)} %collective-permute-done.14.refs_6_.refs_9_.refs_10_), channel_id=1, source_target_pairs={{0,8},{8,0},{1,9},{9,1},{2,10},{10,2},{3,11},{11,3},{4,12},{12,4},... | collective-permute-start | bytes 2654216 | tf_op jit(solution)/shard_map/ppermute | solution.py:258
  87.9 8.2 %collective-permute-start.18 = (bf16[2,256,768]{2,1,0:T(8,128)(2,1)S(1)}, bf16[2,256,768]{2,1,0:T(8,128)(2,1)}, u32[]{:S(2)}, u32[]{:S(2)}) collective-permute-start(bf16[2,256,768]{2,1,0:T(8,128)(2,1)S(1)} %collective-permute-done.15.refs_3_.refs_6_), channel_id=1, source_target_pairs={{0,8},{8,0},{1,9},{9,1},{2,10},{10,2},{3,11},{11,3},{4,12},{12,4},... | collective-permute-start | bytes 2359304 | tf_op jit(solution)/shard_map/ppermute | solution.py:245
  88.0 20.9 %collective-permute-start.19 = (bf16[256,768]{1,0:T(8,128)(2,1)S(1)}, bf16[256,768]{1,0:T(8,128)(2,1)S(1)}, u32[]{:S(2)}, u32[]{:S(2)}) collective-permute-start(bf16[256,768]{1,0:T(8,128)(2,1)S(1)} %bitcast.210), channel_id=1, source_target_pairs={{0,16},{16,0},{1,17},{17,1},{2,18},{18,2},{3,19},{19,3},{4,20},{20... | collective-permute-start | bytes 1179656 | tf_op jit(solution)/shard_map/ppermute | solution.py:827
  89.2 19.7 %collective-permute-start.20 = (bf16[256,768]{1,0:T(8,128)(2,1)S(1)}, bf16[256,768]{1,0:T(8,128)(2,1)}, u32[]{:S(2)}, u32[]{:S(2)}) collective-permute-start(bf16[256,768]{1,0:T(8,128)(2,1)S(1)} %bitcast.211), channel_id=1, source_target_pairs={{0,8},{8,0},{1,9},{9,1},{2,10},{10,2},{3,11},{11,3},{4,12},{12,4},... | collective-permute-start | bytes 1179656 | tf_op jit(solution)/shard_map/ppermute | solution.py:258
  96.1 29.8 %all-to-all-start.1 = ((bf16[4,192,768]{2,1,0:T(8,128)(2,1)}), bf16[4,192,768]{2,1,0:T(8,128)(2,1)S(1)}, u32[]{:S(2)}, u32[]{:S(2)}) async-start(bf16[4,192,768]{2,1,0:T(8,128)(2,1)} %bitcast.206), calls=%async_computation.1 | async-start | bytes 2359296 | tf_op jit(solution)/shard_map/all_to_all | solution.py:826
  112.7 11.0 %collective-permute-start.22 = (bf16[256,768]{1,0:T(8,128)(2,1)}, bf16[256,768]{1,0:T(8,128)(2,1)S(1)}, u32[]{:S(2)}, u32[]{:S(2)}) collective-permute-start(bf16[256,768]{1,0:T(8,128)(2,1)} %get-tuple-element.301.refs_3_.refs_2_), channel_id=1, source_target_pairs={{0,16},{16,0},{1,17},{17,1},{2,18},{18,2},{3,19},{19,3},{4,20},{20... | collective-permute-start | bytes 1179656 | tf_op jit(solution)/shard_map/ppermute | solution.py:833
  114.2 10.4 %collective-permute-start.21 = (bf16[256,768]{1,0:T(8,128)(2,1)}, bf16[256,768]{1,0:T(8,128)(2,1)S(1)}, u32[]{:S(2)}, u32[]{:S(2)}) collective-permute-start(bf16[256,768]{1,0:T(8,128)(2,1)} %get-tuple-element.301.refs_3_.refs_2_), channel_id=1, source_target_pairs={{0,8},{8,0},{1,9},{9,1},{2,10},{10,2},{3,11},{11,3},{4,12},{12,4},... | collective-permute-start | bytes 1179656 | tf_op jit(solution)/shard_map/ppermute | solution.py:258
  114.8 9.7 %collective-permute-start.24 = (bf16[256,768]{1,0:T(8,128)(2,1)S(1)}, bf16[256,768]{1,0:T(8,128)(2,1)S(1)}, u32[]{:S(2)}, u32[]{:S(2)}) collective-permute-start(bf16[256,768]{1,0:T(8,128)(2,1)S(1)} %collective-permute-done.19.refs_9_.refs_8_), channel_id=1, source_target_pairs={{0,8},{8,0},{1,9},{9,1},{2,10},{10,2},{3,11},{11,3},{4,12},{12,4},... | collective-permute-start | bytes 1179656 | tf_op jit(solution)/shard_map/ppermute | solution.py:258
  140.7 10.4 %collective-permute-start.26 = (bf16[256,768]{1,0:T(8,128)(2,1)S(1)}, bf16[256,768]{1,0:T(8,128)(2,1)S(1)}, u32[]{:S(2)}, u32[]{:S(2)}) collective-permute-start(bf16[256,768]{1,0:T(8,128)(2,1)S(1)} %fusion.18), channel_id=1, source_target_pairs={{0,16},{16,0},{1,17},{17,1},{2,18},{18,2},{3,19},{19,3},{4,20},{20... | collective-permute-start | bytes 1179656 | tf_op jit(solution)/shard_map/ppermute | solution.py:862
  151.1 23.1 %collective-permute-start.27 = (bf16[2,256,768]{2,1,0:T(8,128)(2,1)}, bf16[2,256,768]{2,1,0:T(8,128)(2,1)S(1)}, u32[]{:S(2)}, u32[]{:S(2)}) collective-permute-start(bf16[2,256,768]{2,1,0:T(8,128)(2,1)} %get-tuple-element.326), channel_id=1, source_target_pairs={{0,8},{8,0},{1,9},{9,1},{2,10},{10,2},{3,11},{11,3},{4,12},{12,4},... | collective-permute-start | bytes 2359304 | tf_op jit(solution)/shard_map/ppermute | solution.py:258
  153.5 20.7 %collective-permute-start.29 = (bf16[2,2,4,48,384]{4,3,2,1,0:T(8,128)(2,1)S(1)}, bf16[2,2,4,48,384]{4,3,2,1,0:T(8,128)(2,1)S(1)}, u32[]{:S(2)}, u32[]{:S(2)}) collective-permute-start(bf16[2,2,4,48,384]{4,3,2,1,0:T(8,128)(2,1)S(1)} %dynamic-slice_bitcast_fusion), channel_id=1, source_target_pairs={{0,2},{2,0},{4,6},{6,4},{1,3},{3,1},{5,7},{7,5},{8,10},{10,8},{12,... | collective-permute-start | bytes 1769480 | tf_op jit(solution)/shard_map/ppermute | solution.py:296
  155.9 18.4 %collective-permute-start.28 = (bf16[2,2,4,48,384]{4,3,1,2,0:T(8,128)(2,1)S(1)}, bf16[2,2,4,48,384]{4,3,1,2,0:T(8,128)(2,1)S(1)}, u32[]{:S(2)}, u32[]{:S(2)}) collective-permute-start(bf16[2,2,4,48,384]{4,3,1,2,0:T(8,128)(2,1)S(1)} %copy_bitcast_fusion), channel_id=1, source_target_pairs={{0,1},{1,0},{2,3},{3,2},{4,5},{5,4},{6,7},{7,6},{8,9},{9,8},{10,11... | collective-permute-start | bytes 1769480 | tf_op jit(solution)/shard_map/ppermute | solution.py:294
  175.4 7.9 %collective-permute-start.30 = (bf16[2,2,256,768]{3,2,1,0:T(8,128)(2,1)}, bf16[2,2,256,768]{3,2,1,0:T(8,128)(2,1)S(1)}, u32[]{:S(2)}, u32[]{:S(2)}) collective-permute-start(bf16[2,2,256,768]{3,2,1,0:T(8,128)(2,1)} %get-tuple-element.337), channel_id=1, source_target_pairs={{0,8},{8,0},{1,9},{9,1},{2,10},{10,2},{3,11},{11,3},{4,12},{12,4},... | collective-permute-start | bytes 4718600 | tf_op jit(solution)/shard_map/ppermute | solution.py:258
  184.5 23.6 %collective-permute-start.31 = (bf16[2,3,192,768]{3,2,1,0:T(8,128)(2,1)}, bf16[2,3,192,768]{3,2,1,0:T(8,128)(2,1)S(1)}, u32[]{:S(2)}, u32[]{:S(2)}) collective-permute-start(bf16[2,3,192,768]{3,2,1,0:T(8,128)(2,1)} %get-tuple-element.351), channel_id=1, source_target_pairs={{0,8},{8,0},{1,9},{9,1},{2,10},{10,2},{3,11},{11,3},{4,12},{12,4},... | collective-permute-start | bytes 5308424 | tf_op jit(solution)/shard_map/ppermute | solution.py:277
  187.0 21.1 %collective-permute-start.35 = (bf16[2,256,768]{2,1,0:T(8,128)(2,1)}, bf16[2,256,768]{2,1,0:T(8,128)(2,1)}, u32[]{:S(2)}, u32[]{:S(2)}) collective-permute-start(bf16[2,256,768]{2,1,0:T(8,128)(2,1)} %fusion), channel_id=1, source_target_pairs={{1,0},{0,1},{3,2},{2,3},{5,4},{4,5},{7,6},{6,7},{9,8},{8,9},{11,10... | collective-permute-start | bytes 2359304 | tf_op jit(solution)/shard_map/ppermute | solution.py:253
  188.3 19.8 %collective-permute-start.34 = (bf16[256,768]{1,0:T(8,128)(2,1)S(1)}, bf16[256,768]{1,0:T(8,128)(2,1)}, u32[]{:S(2)}, u32[]{:S(2)}) collective-permute-start(bf16[256,768]{1,0:T(8,128)(2,1)S(1)} %fusion.19), channel_id=1, source_target_pairs={{0,16},{16,0},{1,17},{17,1},{2,18},{18,2},{3,19},{19,3},{4,20},{20... | collective-permute-start | bytes 1179656 | tf_op jit(solution)/shard_map/ppermute | solution.py:893
  191.5 16.6 %collective-permute-start.33 = (bf16[2,4,48,384]{3,2,1,0:T(8,128)(2,1)}, bf16[2,4,48,384]{3,2,1,0:T(8,128)(2,1)}, u32[]{:S(2)}, u32[]{:S(2)}) collective-permute-start(bf16[2,4,48,384]{3,2,1,0:T(8,128)(2,1)} %fusion.8), channel_id=1, source_target_pairs={{0,4},{2,6},{4,0},{6,2},{1,5},{3,7},{5,1},{7,3},{8,12},{10,14},{12... | collective-permute-start | bytes 884744 | tf_op jit(solution)/shard_map/ppermute | solution.py:296
  193.2 14.8 %collective-permute-start.32 = (bf16[2,4,48,384]{3,2,0,1:T(8,128)(2,1)}, bf16[2,4,48,384]{3,2,0,1:T(8,128)(2,1)}, u32[]{:S(2)}, u32[]{:S(2)}) collective-permute-start(bf16[2,4,48,384]{3,2,0,1:T(8,128)(2,1)} %fusion.9), channel_id=1, source_target_pairs={{0,2},{2,0},{4,6},{6,4},{1,3},{3,1},{5,7},{7,5},{8,10},{10,8},{12,... | collective-permute-start | bytes 884744 | tf_op jit(solution)/shard_map/ppermute | solution.py:296
  208.1 10.4 %collective-permute-start.36 = (bf16[2,2,256,768]{3,2,1,0:T(8,128)(2,1)}, bf16[2,2,256,768]{3,2,1,0:T(8,128)(2,1)}, u32[]{:S(2)}, u32[]{:S(2)}) collective-permute-start(bf16[2,2,256,768]{3,2,1,0:T(8,128)(2,1)} %get-tuple-element.366), channel_id=1, source_target_pairs={{0,8},{8,0},{1,9},{9,1},{2,10},{10,2},{3,11},{11,3},{4,12},{12,4},... | collective-permute-start | bytes 4718600 | tf_op jit(solution)/shard_map/ppermute | solution.py:258
  209.8 8.8 %collective-permute-start.37 = (bf16[1,192,768]{2,1,0:T(8,128)(2,1)S(1)}, bf16[1,192,768]{2,1,0:T(8,128)(2,1)}, u32[]{:S(2)}, u32[]{:S(2)}) collective-permute-start(bf16[1,192,768]{2,1,0:T(8,128)(2,1)S(1)} %fusion.21), channel_id=1, source_target_pairs={{0,16},{16,0},{1,17},{17,1},{2,18},{18,2},{3,19},{19,3},{4,20},{20... | collective-permute-start | bytes 884744 | tf_op jit(solution)/shard_map/ppermute | solution.py:286
  220.9 19.2 %collective-permute-start.38 = (bf16[2,256,768]{2,1,0:T(8,128)(2,1)S(1)}, bf16[2,256,768]{2,1,0:T(8,128)(2,1)S(1)}, u32[]{:S(2)}, u32[]{:S(2)}) collective-permute-start(bf16[2,256,768]{2,1,0:T(8,128)(2,1)S(1)} %fusion.1), channel_id=1, source_target_pairs={{1,0},{0,1},{3,2},{2,3},{5,4},{4,5},{7,6},{6,7},{9,8},{8,9},{11,10... | collective-permute-start | bytes 2359304 | tf_op jit(solution)/shard_map/ppermute | solution.py:253
  223.2 23.3 %collective-permute-start.42 = (bf16[2,192,768]{2,1,0:T(8,128)(2,1)S(1)}, bf16[2,192,768]{2,1,0:T(8,128)(2,1)S(1)}, u32[]{:S(2)}, u32[]{:S(2)}) collective-permute-start(bf16[2,192,768]{2,1,0:T(8,128)(2,1)S(1)} %fusion.2), channel_id=1, source_target_pairs={{0,16},{16,0},{1,17},{17,1},{2,18},{18,2},{3,19},{19,3},{4,20},{20... | collective-permute-start | bytes 1769480 | tf_op jit(solution)/shard_map/ppermute | solution.py:286
  225.9 20.6 %collective-permute-start.41 = (bf16[2,4,48,384]{3,2,1,0:T(8,128)(2,1)S(1)}, bf16[2,4,48,384]{3,2,1,0:T(8,128)(2,1)S(1)}, u32[]{:S(2)}, u32[]{:S(2)}) collective-permute-start(bf16[2,4,48,384]{3,2,1,0:T(8,128)(2,1)S(1)} %fusion.5), channel_id=1, source_target_pairs={{0,1},{1,0},{2,3},{3,2},{4,5},{5,4},{6,7},{7,6},{8,9},{9,8},{10,11... | collective-permute-start | bytes 884744 | tf_op jit(solution)/shard_map/ppermute | solution.py:294
  227.3 19.2 %collective-permute-start.40 = (bf16[2,4,48,384]{3,2,0,1:T(8,128)(2,1)S(1)}, bf16[2,4,48,384]{3,2,0,1:T(8,128)(2,1)S(1)}, u32[]{:S(2)}, u32[]{:S(2)}) collective-permute-start(bf16[2,4,48,384]{3,2,0,1:T(8,128)(2,1)S(1)} %fusion.7), channel_id=1, source_target_pairs={{0,4},{2,6},{4,0},{6,2},{1,5},{3,7},{5,1},{7,3},{8,12},{10,14},{12... | collective-permute-start | bytes 884744 | tf_op jit(solution)/shard_map/ppermute | solution.py:296
  248.8 21.2 %all-to-all-start.2 = ((bf16[2,4,48,384]{3,2,0,1:T(8,128)(2,1)}), bf16[2,4,48,384]{3,2,0,1:T(8,128)(2,1)}, u32[]{:S(2)}, u32[]{:S(2)}) async-start(bf16[2,4,48,384]{3,2,0,1:T(8,128)(2,1)} %add_convert_fusion.10), calls=%async_computation.2 | async-start | bytes 589824 | tf_op jit(solution)/shard_map/all_to_all | solution.py:926
  255.6 14.3 %collective-permute-start.43 = (bf16[1,192,768]{2,1,0:T(8,128)(2,1)}, bf16[1,192,768]{2,1,0:T(8,128)(2,1)}, u32[]{:S(2)}, u32[]{:S(2)}) collective-permute-start(bf16[1,192,768]{2,1,0:T(8,128)(2,1)} %fusion.22), channel_id=1, source_target_pairs={{0,16},{16,0},{1,17},{17,1},{2,18},{18,2},{3,19},{19,3},{4,20},{20... | collective-permute-start | bytes 884744 | tf_op jit(solution)/shard_map/ppermute | solution.py:286
  269.9 21.2 %collective-permute-start.44 = (bf16[2,448,768]{2,1,0:T(8,128)(2,1)}, bf16[2,448,768]{2,1,0:T(8,128)(2,1)}, u32[]{:S(2)}, u32[]{:S(2)}) collective-permute-start(bf16[2,448,768]{2,1,0:T(8,128)(2,1)} %get-tuple-element.418), channel_id=1, source_target_pairs={{0,8},{8,0},{1,9},{9,1},{2,10},{10,2},{3,11},{11,3},{4,12},{12,4},... | collective-permute-start | bytes 4128776 | tf_op jit(solution)/shard_map/ppermute | solution.py:277
  272.8 18.3 %collective-permute-start.48 = (bf16[2,192,768]{2,1,0:T(8,128)(2,1)}, bf16[2,192,768]{2,1,0:T(8,128)(2,1)}, u32[]{:S(2)}, u32[]{:S(2)}) collective-permute-start(bf16[2,192,768]{2,1,0:T(8,128)(2,1)} %fusion.3), channel_id=1, source_target_pairs={{0,16},{16,0},{1,17},{17,1},{2,18},{18,2},{3,19},{19,3},{4,20},{20... | collective-permute-start | bytes 1769480 | tf_op jit(solution)/shard_map/ppermute | solution.py:286
  272.9 13.8 %collective-permute-start.46 = (bf16[2,4,48,384]{3,2,1,0:T(8,128)(2,1)}, bf16[2,4,48,384]{3,2,1,0:T(8,128)(2,1)}, u32[]{:S(2)}, u32[]{:S(2)}) collective-permute-start(bf16[2,4,48,384]{3,2,1,0:T(8,128)(2,1)} %add_convert_fusion.9), channel_id=1, source_target_pairs={{0,4},{2,6},{4,0},{6,2},{1,5},{3,7},{5,1},{7,3},{8,12},{10,14},{12... | collective-permute-start | bytes 884744 | tf_op jit(solution)/shard_map/ppermute | solution.py:296
  274.9 16.2 %collective-permute-start.47 = (bf16[2,2,72,768]{3,2,1,0:T(8,128)(2,1)}, bf16[2,2,72,768]{3,2,1,0:T(8,128)(2,1)}, u32[]{:S(2)}, u32[]{:S(2)}) collective-permute-start(bf16[2,2,72,768]{3,2,1,0:T(8,128)(2,1)} %fusion.10), channel_id=1, source_target_pairs={{0,1},{1,0},{2,3},{3,2},{4,5},{5,4},{6,7},{7,6},{8,9},{9,8},{10,11... | collective-permute-start | bytes 1327112 | tf_op jit(solution)/shard_map/ppermute | solution.py:294
  275.1 13.9 %collective-permute-start.45 = (bf16[2,4,48,384]{3,2,0,1:T(8,128)(2,1)}, bf16[2,4,48,384]{3,2,0,1:T(8,128)(2,1)}, u32[]{:S(2)}, u32[]{:S(2)}) collective-permute-start(bf16[2,4,48,384]{3,2,0,1:T(8,128)(2,1)} %all-to-all-done.2), channel_id=1, source_target_pairs={{0,2},{2,0},{4,6},{6,4},{1,3},{3,1},{5,7},{7,5},{8,10},{10,8},{12,... | collective-permute-start | bytes 884744 | tf_op jit(solution)/shard_map/ppermute | solution.py:296
  294.2 75.8 %all-to-all-start.3 = ((bf16[16,56,768]{2,1,0:T(8,128)(2,1)}), bf16[16,56,768]{2,1,0:T(8,128)(2,1)}, u32[]{:S(2)}, u32[]{:S(2)}) async-start(bf16[16,56,768]{2,1,0:T(8,128)(2,1)} %bitcast.215), calls=%async_computation.3 | async-start | bytes 2752512 | tf_op jit(solution)/shard_map/all_to_all | solution.py:950
  300.9 34.6 %collective-permute-start.52 = (bf16[4,4,48,384]{3,2,1,0:T(8,128)(2,1)}, bf16[4,4,48,384]{3,2,1,0:T(8,128)(2,1)}, u32[]{:S(2)}, u32[]{:S(2)}) collective-permute-start(bf16[4,4,48,384]{3,2,1,0:T(8,128)(2,1)} %maximum_select_fusion.5), channel_id=1, source_target_pairs={{0,2},{2,0},{4,6},{6,4},{1,3},{3,1},{5,7},{7,5},{8,10},{10,8},{12,... | collective-permute-start | bytes 1769480 | tf_op jit(solution)/shard_map/ppermute | solution.py:296
  301.1 37.0 %collective-permute-start.51 = (bf16[4,4,48,384]{3,2,0,1:T(8,128)(2,1)}, bf16[4,4,48,384]{3,2,0,1:T(8,128)(2,1)}, u32[]{:S(2)}, u32[]{:S(2)}) collective-permute-start(bf16[4,4,48,384]{3,2,0,1:T(8,128)(2,1)} %maximum_select_fusion.4), channel_id=1, source_target_pairs={{0,1},{1,0},{2,3},{3,2},{4,5},{5,4},{6,7},{7,6},{8,9},{9,8},{10,11... | collective-permute-start | bytes 1769480 | tf_op jit(solution)/shard_map/ppermute | solution.py:294
  307.9 32.6 %collective-permute-start.49 = (bf16[2,2,72,768]{3,2,1,0:T(8,128)(2,1)}, bf16[2,2,72,768]{3,2,1,0:T(8,128)(2,1)}, u32[]{:S(2)}, u32[]{:S(2)}) collective-permute-start(bf16[2,2,72,768]{3,2,1,0:T(8,128)(2,1)} %fusion.11), channel_id=1, source_target_pairs={{0,1},{1,0},{2,3},{3,2},{4,5},{5,4},{6,7},{7,6},{8,9},{9,8},{10,11... | collective-permute-start | bytes 1327112 | tf_op jit(solution)/shard_map/ppermute | solution.py:294
  310.4 30.1 %collective-permute-start.50 = (bf16[2,72,768]{2,1,0:T(8,128)(2,1)S(1)}, bf16[2,72,768]{2,1,0:T(8,128)(2,1)S(1)}, u32[]{:S(2)}, u32[]{:S(2)}) collective-permute-start(bf16[2,72,768]{2,1,0:T(8,128)(2,1)S(1)} %fusion.17), channel_id=1, source_target_pairs={{0,2},{2,0},{4,6},{6,4},{1,3},{3,1},{5,7},{7,5},{8,10},{10,8},{12,... | collective-permute-start | bytes 663560 | tf_op jit(solution)/shard_map/ppermute | solution.py:296
  341.9 12.4 %collective-permute-start.54 = (bf16[2,72,768]{2,1,0:T(8,128)(2,1)S(1)}, bf16[2,72,768]{2,1,0:T(8,128)(2,1)S(1)}, u32[]{:S(2)}, u32[]{:S(2)}) collective-permute-start(bf16[2,72,768]{2,1,0:T(8,128)(2,1)S(1)} %fusion.15), channel_id=1, source_target_pairs={{0,4},{2,6},{4,0},{6,2},{1,5},{3,7},{5,1},{7,3},{8,12},{10,14},{12... | collective-permute-start | bytes 663560 | tf_op jit(solution)/shard_map/ppermute | solution.py:296
  347.4 6.9 %collective-permute-start.53 = (bf16[2,72,768]{2,1,0:T(8,128)(2,1)S(1)}, bf16[2,72,768]{2,1,0:T(8,128)(2,1)S(1)}, u32[]{:S(2)}, u32[]{:S(2)}) collective-permute-start(bf16[2,72,768]{2,1,0:T(8,128)(2,1)S(1)} %fusion.16), channel_id=1, source_target_pairs={{0,2},{2,0},{4,6},{6,4},{1,3},{3,1},{5,7},{7,5},{8,10},{10,8},{12,... | collective-permute-start | bytes 663560 | tf_op jit(solution)/shard_map/ppermute | solution.py:296
  354.3 7.1 %collective-permute-start.56 = (bf16[2,72,768]{2,1,0:T(8,128)(2,1)S(1)}, bf16[2,72,768]{2,1,0:T(8,128)(2,1)S(1)}, u32[]{:S(2)}, u32[]{:S(2)}) collective-permute-start(bf16[2,72,768]{2,1,0:T(8,128)(2,1)S(1)} %add_convert_fusion.14), channel_id=1, source_target_pairs={{0,2},{2,0},{4,6},{6,4},{1,3},{3,1},{5,7},{7,5},{8,10},{10,8},{12,... | collective-permute-start | bytes 663560 | tf_op jit(solution)/shard_map/ppermute | solution.py:296
  358.4 11.6 %collective-permute-start.55 = (bf16[2,72,768]{2,1,0:T(8,128)(2,1)S(1)}, bf16[2,72,768]{2,1,0:T(8,128)(2,1)S(1)}, u32[]{:S(2)}, u32[]{:S(2)}) collective-permute-start(bf16[2,72,768]{2,1,0:T(8,128)(2,1)S(1)} %fusion.13), channel_id=1, source_target_pairs={{0,4},{2,6},{4,0},{6,2},{1,5},{3,7},{5,1},{7,3},{8,12},{10,14},{12... | collective-permute-start | bytes 663560 | tf_op jit(solution)/shard_map/ppermute | solution.py:296
  370.0 18.8 %collective-permute-start.58 = (bf16[4,72,768]{2,1,0:T(8,128)(2,1)}, bf16[4,72,768]{2,1,0:T(8,128)(2,1)}, u32[]{:S(2)}, u32[]{:S(2)}) collective-permute-start(bf16[4,72,768]{2,1,0:T(8,128)(2,1)} %maximum_select_fusion.6), channel_id=1, source_target_pairs={{0,1},{1,0},{2,3},{3,2},{4,5},{5,4},{6,7},{7,6},{8,9},{9,8},{10,11... | collective-permute-start | bytes 1327112 | tf_op jit(solution)/shard_map/ppermute | solution.py:294
  370.7 16.6 %collective-permute-start.57 = (bf16[2,72,768]{2,1,0:T(8,128)(2,1)}, bf16[2,72,768]{2,1,0:T(8,128)(2,1)}, u32[]{:S(2)}, u32[]{:S(2)}) collective-permute-start(bf16[2,72,768]{2,1,0:T(8,128)(2,1)} %add_convert_fusion.13), channel_id=1, source_target_pairs={{0,2},{2,0},{4,6},{6,4},{1,3},{3,1},{5,7},{7,5},{8,10},{10,8},{12,... | collective-permute-start | bytes 663560 | tf_op jit(solution)/shard_map/ppermute | solution.py:296
  382.8 51.1 %all-to-all-start.4 = ((bf16[8,56,768]{2,1,0:T(8,128)(2,1)}), bf16[8,56,768]{2,1,0:T(8,128)(2,1)S(1)}, u32[]{:S(2)}, u32[]{:S(2)}) async-start(bf16[8,56,768]{2,1,0:T(8,128)(2,1)} %broadcast_in_dim.4), calls=%async_computation.4 | async-start | bytes 1376256 | tf_op jit(solution)/shard_map/all_to_all | solution.py:960
  391.3 41.4 %collective-permute-start.63 = (bf16[4,72,768]{2,1,0:T(8,128)(2,1)S(1)}, bf16[4,72,768]{2,1,0:T(8,128)(2,1)S(1)}, u32[]{:S(2)}, u32[]{:S(2)}) collective-permute-start(bf16[4,72,768]{2,1,0:T(8,128)(2,1)S(1)} %maximum_select_fusion.7), channel_id=1, source_target_pairs={{0,1},{1,0},{2,3},{3,2},{4,5},{5,4},{6,7},{7,6},{8,9},{9,8},{10,11... | collective-permute-start | bytes 1327112 | tf_op jit(solution)/shard_map/ppermute | solution.py:294
  392.7 14.9 %collective-permute-start.59 = (bf16[3,64,768]{2,1,0:T(8,128)(2,1)S(1)}, bf16[3,64,768]{2,1,0:T(8,128)(2,1)S(1)}, u32[]{:S(2)}, u32[]{:S(2)}) collective-permute-start(bf16[3,64,768]{2,1,0:T(8,128)(2,1)S(1)} %pad_maximum_fusion.6), channel_id=1, source_target_pairs={{0,0},{10,2},{2,4},{8,6},{4,8},{14,10},{6,12},{12,14},{1,1},{11,3}... | collective-permute-start | bytes 884744 | tf_op jit(solution)/shard_map/ppermute | solution.py:225
  397.9 31.9 %collective-permute-start.62 = (bf16[3,64,768]{2,1,0:T(8,128)(2,1)S(1)}, bf16[3,64,768]{2,1,0:T(8,128)(2,1)S(1)}, u32[]{:S(2)}, u32[]{:S(2)}) collective-permute-start(bf16[3,64,768]{2,1,0:T(8,128)(2,1)S(1)} %pad_maximum_fusion.9), channel_id=1, source_target_pairs={{10,0},{2,2},{8,4},{0,6},{14,8},{6,10},{12,12},{4,14},{11,1},{3,3}... | collective-permute-start | bytes 884744 | tf_op jit(solution)/shard_map/ppermute | solution.py:225
  399.9 29.9 %collective-permute-start.60 = (bf16[3,64,768]{2,1,0:T(8,128)(2,1)S(1)}, bf16[3,64,768]{2,1,0:T(8,128)(2,1)S(1)}, u32[]{:S(2)}, u32[]{:S(2)}) collective-permute-start(bf16[3,64,768]{2,1,0:T(8,128)(2,1)S(1)} %pad_maximum_fusion.7), channel_id=1, source_target_pairs={{8,0},{0,2},{10,4},{2,6},{12,8},{4,10},{14,12},{6,14},{9,1},{1,3},... | collective-permute-start | bytes 884744 | tf_op jit(solution)/shard_map/ppermute | solution.py:225
  401.1 28.7 %collective-permute-start.61 = (bf16[3,64,768]{2,1,0:T(8,128)(2,1)S(1)}, bf16[3,64,768]{2,1,0:T(8,128)(2,1)S(1)}, u32[]{:S(2)}, u32[]{:S(2)}) collective-permute-start(bf16[3,64,768]{2,1,0:T(8,128)(2,1)S(1)} %pad_maximum_fusion.8), channel_id=1, source_target_pairs={{2,0},{8,2},{0,4},{10,6},{6,8},{12,10},{4,12},{14,14},{3,1},{9,3},... | collective-permute-start | bytes 884744 | tf_op jit(solution)/shard_map/ppermute | solution.py:225
  (66 other events, 328.7 us)

commit v5 on v4

--- a/solution.py
+++ b/solution.py
@@ -198,6 +198,31 @@
     return [jnp.concatenate([g[i] for g in got], axis=0) for i in range(len(arrays))]
 
 
+def undeal_line(arrays):
+    core, z = lax.axis_index("core"), lax.axis_index("z")
+    chunks = jnp.stack([array.reshape(LINE, -1, array.shape[-1]) for array in arrays], axis=1)
+    start = lax.rem(2 * lax.rem(z, 2) + core, LINE)
+    chunks = lax.dynamic_slice_in_dim(jnp.concatenate([chunks, chunks], axis=0), start, LINE, axis=0)
+    return lax.all_to_all(chunks, "z", 0, 0, tiled=True)
+
+
+def undeal_cores(chunks):
+    core = lax.axis_index("core")
+    chunks = chunks.reshape((2, 2) + chunks.shape[1:])
+    mine = lax.dynamic_index_in_dim(chunks, core, 0, keepdims=False)
+    return mine, lax.ppermute(lax.dynamic_index_in_dim(chunks, 1 - core, 0, keepdims=False), "core", SWAP)
+
+
+def undealt(halves, kinds):
+    first = lax.axis_index("core") == 0
+    outs = []
+    for i, kind in enumerate(kinds):
+        mine, got = (half[:, i].astype(kind) for half in halves)
+        both = jnp.where(first, jnp.stack([mine, got], axis=1), jnp.stack([got, mine], axis=1))
+        outs.append(both.reshape(2, -1, both.shape[-1]))
+    return outs
+
+
 def deal_halves(array):
     _, rows, width = array.shape
     parts = array.reshape(2, 2, rows // 2, width)
@@ -207,10 +232,13 @@
 
 
 def deal_line(mine, got):
+    first = lax.axis_index("core") == 0
+    chunks = jnp.where(first, jnp.concatenate([mine, got], axis=0), jnp.concatenate([got, mine], axis=0))
+    return lax.all_to_all(chunks, "z", 0, 0, tiled=True)
+
+
+def deal_order(chunks):
     core, z = lax.axis_index("core"), lax.axis_index("z")
-    first = core == 0
-    chunks = jnp.where(first, jnp.concatenate([mine, got], axis=0), jnp.concatenate([got, mine], axis=0))
-    chunks = lax.all_to_all(chunks, "z", 0, 0, tiled=True)
     start = lax.rem(LINE - 2 * lax.rem(z, 2) - core, LINE)
     mine = lax.dynamic_slice_in_dim(jnp.concatenate([chunks, chunks], axis=0), start, LINE, axis=0)
     return mine.reshape(-1, mine.shape[-1])
@@ -286,6 +314,12 @@
     return lax.ppermute(add([array[1, first:last] for array, _ in terms]), "fx", SWAP)
 
 
+def pick(array, *path):
+    for axis, index in path:
+        array = lax.dynamic_index_in_dim(array, index, axis, keepdims=False)
+    return array
+
+
 HALVES = ("y", "z0", "z1")
 
 
@@ -304,12 +338,15 @@
 def half_of(term, more=()):
     array, names = term
     cut = 1 in names
-    if 0 in names and len(names + more) > 1:
+    if 0 in names and 1 not in names and len(names + more) > 1:
         array = array.reshape(2, 2, 2, 2, -1, array.shape[-1])
         cut = True
     for name in names + more:
         if name in (0, 1):
             array = array if name else array[0]
+            continue
+        if name[0] == "at":
+            array = pick(array, name[1:])
             continue
         name, other = name if isinstance(name, tuple) else (name, False)
         if array.ndim == 3 and not cut:
@@ -819,6 +856,7 @@
     mixed, mass, up_cut, rest_other, kv_cross, near_cross, cot = hold(
         mixed, mass, up_cut, rest_other, kv_cross, near_cross, cot
     )
+    cot = deal_order(cot)
     w_rest = (mid_shard, mid_near, rest_other, between_cores(rest_other))
     kv_cross = [kv_cross[0], near_cross] + with_cores(kv_cross[1:])
     r1, n2, cquery = dense(middle_kernel, [slots], [vec, mixed, x_bf], w_rest, [real, act, act], [weights(2)], 3.3)
@@ -895,7 +933,6 @@
     dq, mine, theirs, middle, up, down, out_far, dckv_a = hold_all(dq, mine, theirs, middle, up, down, out_far, dckv[-1])
     dckv = dckv[:-1] + [dckv_a]
     got = between_cores(theirs)
-    middle_a = part_over_x(middle, 0, 1)
     grad_encoded, layer_out, late_keep, late_send, enc_rows_sum = dense(
         functools.partial(cross_back_kernel, len(dckv)),
         [slots],
@@ -905,25 +942,28 @@
         [weights(2), turned, pltpu.VMEM((width, enc_rows), BF)],
         6,
     )
-    mine, got, grad_encoded, layer_out, late_keep, late_send, enc_rows_sum, up, down, middle, middle_a = hold_all(
-        mine, got, grad_encoded, layer_out, late_keep, late_send, enc_rows_sum, up, down, middle, middle_a
+    mine, got, grad_encoded, layer_out, late_keep, late_send, enc_rows_sum, up, down, middle = hold_all(
+        mine, got, grad_encoded, layer_out, late_keep, late_send, enc_rows_sum, up, down, middle
     )
     dkv = collect(mine, got, groups)
     late = over_cores(late_keep, late_send)
-    late, up, down, middle = hold_all(late, up, down, middle)
-    middle_b = part_over_x(middle, 1, 3)
+    late = over_x(late)
     if single:
+        at = {name: half_index(name) for name in HALVES}
+        middle = [array.reshape(2, 2, 2, 2, -1, width) for array, _ in middle]
+        middle_z0 = exchange(add([pick(array, (1, 1 - at["z0"])) for array in middle]), "z0")
         up, down = both_halves(up, "z1"), both_halves(down, "y")
-        dkv_last, up, down, late, middle_b = hold(dkv[-1], up, down, [t[0] for t in late], middle_b)
-        late = [(array, ()) for array in late]
+        dkv_last, up, down, late, middle, middle_z0 = hold_all(
+            dkv[-1], [(part, ()) for part in up], [(part, ()) for part in down], late, [(part, ()) for part in middle], middle_z0
+        )
+        home = undeal_line([grad_encoded, layer_out])
+        middle = [(array, (1, ("at", 1, at["z0"]))) for array, _ in middle] + [(middle_z0, (1,))]
+        middle_x = lax.ppermute(add([half_of(term)[1] for term in middle]), "fx", SWAP)
+        late = halve(late, "y")
     else:
-        dkv_last, late, middle_b = hold_all(dkv[-1], late, middle_b)
+        middle = over_x(middle)
+        dkv_last, late, middle = hold_all(dkv[-1], late, middle)
     dkv = dkv[:-1] + [dkv_last]
-    middle = [(array, (0,)) for array, _ in middle] + [(jnp.concatenate([middle_a, middle_b], axis=0), ())]
-    late_a = part_over_x(late, 0, 1)
-    if single:
-        up, down = add(up), add(down)
-        up = lax.all_to_all(up, ("fx", "core"), 1, 1, tiled=True)
     grad_layer, keep, send = dense(
         functools.partial(self_back_kernel, len(dkv)),
         [slots],
@@ -934,34 +974,38 @@
         7,
         copies=12,
     )
-    grad_layer, keep, send, middle, late, late_a, up, down = hold_all(
-        grad_layer, keep, send, middle, late, late_a, up, down
-    )
-    own = over_cores(keep, send)
-    late_b = part_over_x(late, 1, 3)
     if single:
-        up, down = double(up, "z0"), double(down, "z1")
-        middle = halve(middle, "y")
-        own, up, down, middle, late, late_b = hold_all(own, up, down, middle, late, late_b)
-    late = [(array, (0,)) for array, _ in late] + [(jnp.concatenate([late_a, late_b], axis=0), ())]
-    if single:
-        own = add([half_of(term) for term in own])
-        own = jnp.where(fx == 0, own, own[::-1]).reshape(4 * LINE, -1, width)
-        own = lax.all_to_all(own, ("fx", "z", "y"), 0, 0, tiled=True)
+        grad_layer, keep, send, late, up, down, middle_x, home = hold_all(
+            grad_layer, keep, send, late, up, down, middle_x, home
+        )
+        up, down = (add([part for part, _ in parts]) for parts in (up, down))
+        up = lax.all_to_all(up, ("fx", "core"), 1, 1, tiled=True)
+        own = over_cores(keep, send)
+        middle = [(array, names + (0,)) for array, names in middle] + [(middle_x, (1,))]
+        home = undeal_cores(home)
+        down, late, middle = double(down, "z1"), halve(late, "z0"), halve(middle, "y")
+        own, up, late, middle, home, down, grad_layer = hold_all(
+            own, up, late, middle, [(p, ()) for p in home], down, grad_layer
+        )
+        own = over_x(own)
+        last = undeal_line([grad_layer])
+        up = double(up, "z0")
+        late, middle = both_halves(late, "z1"), both_halves(middle, "z1")
+        own, late, middle, home, up, down, last = hold_all(
+            own, [(p, ()) for p in late], [(p, ()) for p in middle], home, up, down, last
+        )
+        grad_encoded, layer_out = undealt([p for p, _ in home], [F32, BF])
+        last = undeal_cores(last)
+        late, middle = (add([part for part, _ in parts]) for parts in (late, middle))
+        own = add([array[0] if 0 in names else array for array, names in own]).reshape(2 * LINE, -1, width)
+        own = lax.all_to_all(own, ("z", "y"), 0, 0, tiled=True)
+        late, middle = double(late, "z0"), double(middle, "y")
         up, down = double(up, "y"), double(down, "z0")
-        late, middle = halve(late, "y"), halve(middle, "z0")
-        late, middle, up, down, grad_layer = hold_all(late, middle, up, down, grad_layer)
-        late, middle = halve(late, "z0"), both_halves(middle, "z1")
-        late, middle = hold_all(late, [(part, ()) for part in middle])
-        middle = [part for part, _ in middle]
-        late, middle = both_halves(late, "z1"), double(add(middle), "z0")
-        own, late, middle = hold(own, late, middle)
+        own, late, middle, up, down, last = hold(own, late, middle, up, down, last)
         own = jnp.sum(own.astype(F32), axis=0, keepdims=True).astype(BF)
         own = lax.all_to_all(jnp.broadcast_to(own, (2 * LINE,) + own.shape[1:]), ("z", "y"), 0, 0, tiled=True)
-        late, middle = double(add(late), "z0"), double(middle, "y")
-        late, middle, grad_layer, grad_encoded, layer_out = hold(late, middle, grad_layer, grad_encoded, layer_out)
-        late = double(late, "y")
-        grad_encoded, layer_out, grad_layer = undeal([grad_encoded, layer_out, grad_layer], [F32, BF, F32])
+        late, middle = double(late, "y"), double(middle, "z0")
+        (grad_layer,) = undealt(last, [F32])
         grad_attn, grad_out, *total = dense(
             last_kernel,
             [],
@@ -974,6 +1018,7 @@
         )
         up, down = (part.astype(F32).reshape(2, 2, 2, 4, shard // 4, width // 2) for part in (up, down))
     else:
+        own = over_cores(keep, send)
         (grad_layer,) = undeal([grad_layer], [F32])
         (grad_encoded,), (layer_out,) = undeal([grad_encoded], [F32]), undeal([layer_out], [BF])
 

time: 448 us -> 424 us (0.946)
  the two profiles are of different devices: /device:TPU:9 before, /device:TPU:0 now
where the time goes in v5:
time: 424 us; the launch traced here: 416 us
  Pallas kernels  112 us (26%)
  waiting for transfers between devices  110 us (26%)
  starting transfers between devices  90.5 us (21%)
  other arithmetic  65.9 us (16%)
  local copies, waits for them, and re-layouts  34.8 us (8%)
    pallas_call x11, Pallas kernels, dense(): pl.pallas_call(body, in_specs=[SCALARS] * n_s + [LEFT] * (n_b + n_p), out...  67.8 us
    ppermute x13, waiting for transfers between devices, exchange(): return lax.ppermute(array, 'z', [(i, i ^ flip) for i in range(LINE)])  62.6 us
    convert_element_type x22, other arithmetic, add(): return total.astype(BF)  36.7 us
    pallas_call x2, Pallas kernels, attention_back(): pl.pallas_call(functools.partial(backward_kernel, masked, len(kv)), grid=...  26.4 us
    pallas_call x2, Pallas kernels, attention(): pl.pallas_call(functools.partial(forward_kernel, masked, len(kv)), grid=(...  18 us
    ppermute x13, starting transfers between devices, exchange(): return lax.ppermute(array, 'z', [(i, i ^ flip) for i in range(LINE)])  17.4 us
    select_n x8, other arithmetic, double(): jnp.where(first, jnp.concatenate([part, other], axis=0), jnp.concatenate(...  13.2 us
    unnamed x111, local copies, waits for them, and re-layouts  11.7 us
  transfers between devices with their start and end apart: 68, of which 21 were waited for; matrix products, arithmetic and copies ran while one was open for 21% of the time, Pallas kernels for 24%

profile of v5, /device:TPU:0, one launch (start us, length us, event | category | flops | bytes accessed | tf_op | source)
XLA Modules:
  0.0 416.0 jit_solution(217543932691268564)
XLA Ops:
  2.5 2.6 collective-permute-start.5
  5.9 4.9 %collective-permute-start.2 = (bf16[2,64,768]{2,1,0:T(8,128)(2,1)S(1)}, bf16[2,64,768]{2,1,0:T(8,128)(2,1)S(1)}, u32[]{:S(2)}, u32[]{:S(2)}) collective-permute-start(bf16[2,64,768]{2,1,0:T(8,128)(2,1)S(1)} %pad_maximum_fusion.6), channel_id=1, source_target_pairs={{0,8},{2,0},{4,10},{6,2},{8,12},{10,4},{12,14},{14,6},{1,9},{3,1},... | collective-permute-start | bytes 589832 | tf_op jit(solution)/shard_map/ppermute | solution.py:197
  10.8 1.9 collective-permute-start.3
  12.8 3.4 collective-permute-start.4
  16.3 11.0 %collective-permute-done.3 = bf16[2,64,768]{2,1,0:T(8,128)(2,1)S(1)} collective-permute-done((bf16[2,64,768]{2,1,0:T(8,128)(2,1)S(1)}, bf16[2,64,768]{2,1,0:T(8,128)(2,1)S(1)}, u32[]{:S(2)}, u32[]{:S(2)}) %collective-permute-start.3) | collective-permute-done | bytes 196640 | tf_op jit(solution)/shard_map/ppermute | solution.py:197
  36.2 5.1 %shard_map.203 = (bf16[256,768]{1,0:T(8,128)(2,1)}, bf16[256,768]{1,0:T(8,128)(2,1)}, bf16[2,256,768]{2,1,0:T(8,128)(2,1)}, f32[24,768]{1,0:T(8,128)}) custom-call(s32[4]{0:T(128)} %pad_add_fusion.refs_0_, bf16[256,768]{1,0:T(8,128)(2,1)} %pad_maximum_fusion.3.refs_1_.refs_3_.refs_2_, bf16[608,768]{1,0:T(8,128)(2,1)} %copy-done.4, ...), custom_call_target="tpu_custom_call" | custom-call | bytes 14000000 | tf_op jit(solution)/shard_map/pallas_call | solution.py:734
  42.8 2.1 pad_maximum_fusion.2
  44.9 3.8 collective-permute-done.9.refs_5_.refs_14_
  48.7 2.2 dynamic-slice_bitcast_fusion.5
  52.5 2.4 copy.58
  55.7 4.3 %shard_map.204.refs_1_.refs_4_ = bf16[2,256,768]{2,1,0:T(8,128)(2,1)} custom-call(s32[4]{0:T(128)} %pad_add_fusion.refs_0_, f32[24,768]{1,0:T(8,128)} %get-tuple-element.247.refs_1_.refs_0_, bf16[256,768]{1,0:T(8,128)(2,1)} %pad_maximum_fusion.4.refs_2_, bf16[5,192,768]{2,1,0:T(8,128)(2,1)} %copy-done, bf16[5,192,768]{2,1,0:T(8,128)(2,1)} %copy-done.1, ...), custom_call_target="tpu_custom_call" | custom-call | bytes 12250000 | tf_op jit(solution)/shard_map/pallas_call | solution.py:734
  64.8 4.5 %all-to-all-start = ((bf16[4,64,768]{2,1,0:T(8,128)(2,1)}), bf16[4,64,768]{2,1,0:T(8,128)(2,1)S(1)}, u32[]{:S(2)}, u32[]{:S(2)}) async-start(bf16[4,64,768]{2,1,0:T(8,128)(2,1)} %maximum_select_fusion.10), calls=%async_computation | async-start | bytes 786432 | tf_op jit(solution)/shard_map/all_to_all | solution.py:237
  71.8 9.2 %shard_map.205 = (bf16[256,768]{1,0:T(8,128)(2,1)}, f32[6,1,512]{2,1,0:T(1,128)}) custom-call(s32[1024,1]{1,0:T(8,128)} %copy.41.refs_0_, s32[1,256]{1,0:T(1,128)} %slice_bitcast_fusion.8.refs_1_, bf16[256,768]{1,0:T(8,128)(2,1)} %get-tuple-element.250.refs_2_, bf16[2,256,768]{2,1,0:T(8,128)(2,1)} %get-tuple-element.259.refs_3_.refs_6_, ...), custom_call_target="tpu_custom_call" | custom-call | bytes 28000000 | tf_op jit(solution)/shard_map/pallas_call | solution.py:128
  87.0 4.7 %shard_map.206 = (f32[256,768]{1,0:T(8,128)}, bf16[256,768]{1,0:T(8,128)(2,1)}, bf16[256,768]{1,0:T(8,128)(2,1)}) custom-call(s32[4]{0:T(128)} %pad_add_fusion.refs_0_, f32[24,768]{1,0:T(8,128)} %get-tuple-element.247.refs_1_.refs_0_, bf16[256,768]{1,0:T(8,128)(2,1)} %get-tuple-element.269.refs_2_.refs_6_.refs_4_, ...), custom_call_target="tpu_custom_call" | custom-call | bytes 11550000 | tf_op jit(solution)/shard_map/pallas_call | solution.py:734
  91.7 3.7 all-to-all-start.1
  95.4 8.8 %shard_map.207 = (bf16[256,768]{1,0:T(8,128)(2,1)}, f32[6,1,512]{2,1,0:T(1,128)}) custom-call(bf16[256,768]{1,0:T(8,128)(2,1)} %get-tuple-element.278.refs_0_, bf16[2,256,768]{2,1,0:T(8,128)(2,1)} %shard_map.204.refs_1_.refs_4_, bf16[2,256,768]{2,1,0:T(8,128)(2,1)} %collective-permute-done.16.refs_2_.refs_5_, bf16[2,256,768]{2,1,0:T(8,128)(2,1)} %copy-done.14, ...), custom_call_target="tpu_custom_call" | custom-call | bytes 28000000 | tf_op jit(solution)/shard_map/pallas_call | solution.py:128
  104.2 3.9 shard_map.208
  108.1 2.1 collective-permute-start.22
  110.7 9.2 %collective-permute-done.22.refs_5_.refs_4_ = bf16[256,768]{1,0:T(8,128)(2,1)S(1)} collective-permute-done((bf16[256,768]{1,0:T(8,128)(2,1)}, bf16[256,768]{1,0:T(8,128)(2,1)S(1)}, u32[]{:S(2)}, u32[]{:S(2)}) %collective-permute-start.22) | collective-permute-done | bytes 393248 | tf_op jit(solution)/shard_map/ppermute | solution.py:871
  122.7 9.7 %shard_map.209 = (bf16[2,256,768]{2,1,0:T(8,128)(2,1)}, bf16[2,256,768]{2,1,0:T(8,128)(2,1)}, bf16[2,256,768]{2,1,0:T(8,128)(2,1)}, bf16[2,256,768]{2,1,0:T(8,12...) custom-call(f32[24,768]{1,0:T(8,128)} %get-tuple-element.247.refs_1_.refs_0_, ...), custom_call_target="tpu_custom_call" | custom-call | bytes 28000000 | tf_op jit(solution)/shard_map/pallas_call | solution.py:734
  132.7 2.4 collective-permute-done.25.refs_3_
  138.1 6.9 %shard_map.210 = (bf16[4,2,4,48,384]{4,3,2,1,0:T(8,128)(2,1)}, bf16[4,2,4,48,384]{4,3,2,1,0:T(8,128)(2,1)}) custom-call(bf16[4,256,768]{2,1,0:T(8,128)(2,1)} %get-tuple-element.301.refs_0_, bf16[4,256,768]{2,1,0:T(8,128)(2,1)} %get-tuple-element.302.refs_1_, bf16[256,768]{1,0:T(8,128)(2,1)} %get-tuple-element.292.refs_3_.refs_2_, ...), custom_call_target="tpu_custom_call" | custom-call | bytes 21000000 | tf_op jit(solution)/shard_map/pallas_call | solution.py:734
  145.1 2.5 collective-permute-done.26.refs_4_
  152.6 4.8 %shard_map.211 = (f32[256,768]{1,0:T(8,128)}, bf16[256,768]{1,0:T(8,128)(2,1)}, f32[16,768]{1,0:T(8,128)}) custom-call(s32[4]{0:T(128)} %pad_add_fusion.refs_0_, f32[24,768]{1,0:T(8,128)} %get-tuple-element.247.refs_1_.refs_0_, bf16[2,256,768]{2,1,0:T(8,128)(2,1)} %get-tuple-element.299.refs_2_, bf16[2,256,768]{2,1,0:T(8,128)(2,1)} %copy-done.22, ...), custom_call_target="tpu_custom_call" | custom-call | bytes 9450000 | tf_op jit(solution)/shard_map/pallas_call | solution.py:734
  157.3 13.0 %shard_map.212 = (bf16[256,768]{1,0:T(8,128)(2,1)}, bf16[2,2,256,768]{3,2,1,0:T(8,128)(2,1)}, bf16[2,2,256,768]{3,2,1,0:T(8,128)(2,1)}) custom-call(bf16[256,768]{1,0:T(8,128)(2,1)} %get-tuple-element.278.refs_0_, bf16[256,768]{1,0:T(8,128)(2,1)} %get-tuple-element.309.refs_1_, bf16[256,768]{1,0:T(8,128)(2,1)} %get-tuple-element.287.refs_2_.refs_7_, ...), custom_call_target="tpu_custom_call" | custom-call | bytes 45500000 | tf_op jit(solution)/shard_map/pallas_call | solution.py:158
  171.5 7.3 %shard_map.213 = (f32[256,768]{1,0:T(8,128)}, bf16[256,768]{1,0:T(8,128)(2,1)}, bf16[2,3,192,768]{3,2,1,0:T(8,128)(2,1)}, bf16[2,3,192,768]{3,2,1,0:T(8,128)(2,1)}, f32[16,768]{1,0:T(8,128)}) custom-call(s32[4]{0:T(128)} %pad_add_fusion.refs_0_, f32[24,768]{1,0:T(8,128)} %get-tuple-element.247.refs_1_.refs_0_, bf16[256,768]{1,0:T(8,128)(2,1)} %get-tuple-element.320.refs_2_, ...), custom_call_target="tpu_custom_call" | custom-call | bytes 21000000 | tf_op jit(solution)/shard_map/pallas_call | solution.py:734
  179.0 2.3 fusion.4
  185.7 2.4 collective-permute-start.33
  189.8 13.3 %shard_map.214 = (bf16[256,768]{1,0:T(8,128)(2,1)}, bf16[2,2,256,768]{3,2,1,0:T(8,128)(2,1)}, bf16[2,2,256,768]{3,2,1,0:T(8,128)(2,1)}) custom-call(s32[1024,1]{1,0:T(8,128)} %copy.41.refs_0_, s32[1,256]{1,0:T(1,128)} %slice_bitcast_fusion.8.refs_1_, bf16[256,768]{1,0:T(8,128)(2,1)} %get-tuple-element.250.refs_2_, ...), custom_call_target="tpu_custom_call" | custom-call | bytes 45500000 | tf_op jit(solution)/shard_map/pallas_call | solution.py:158
  204.9 8.3 %shard_map.215 = (bf16[256,768]{1,0:T(8,128)(2,1)}, bf16[256,768]{1,0:T(8,128)(2,1)}, bf16[2,3,192,768]{3,2,1,0:T(8,128)(2,1)}, bf16[2,3,192,768]{3,2,1,0:T(8,128)(2,1)}, f32[16,768]{1,0:T(8,128)}) custom-call(s32[4]{0:T(128)} %pad_add_fusion.refs_0_, f32[24,768]{1,0:T(8,128)} %get-tuple-element.247.refs_1_.refs_0_, ...), custom_call_target="tpu_custom_call" | custom-call | bytes 21000000 | tf_op jit(solution)/shard_map/pallas_call | solution.py:734
  214.8 2.4 fusion.2
  218.0 2.2 fusion.5
  224.2 4.4 %all-to-all-start.2 = ((bf16[4,2,64,768]{3,2,1,0:T(8,128)(2,1)}), bf16[4,2,64,768]{3,2,1,0:T(8,128)(2,1)}, u32[]{:S(2)}, u32[]{:S(2)}) async-start(bf16[4,2,64,768]{3,2,1,0:T(8,128)(2,1)} %fusion.7), calls=%async_computation.2 | async-start | bytes 1572864 | tf_op jit(solution)/shard_map/all_to_all | solution.py:206
  228.7 2.0 fusion.11
  231.5 2.0 fusion.13
  233.4 2.9 collective-permute-start.38
  236.3 9.9 %collective-permute-done.39 = bf16[2,4,48,384]{3,2,1,0:T(8,128)(2,1)} collective-permute-done((bf16[2,4,48,384]{3,2,1,0:T(8,128)(2,1)}, bf16[2,4,48,384]{3,2,1,0:T(8,128)(2,1)}, u32[]{:S(2)}, u32[]{:S(2)}) %collective-permute-start.39) | collective-permute-done | bytes 294944 | tf_op jit(solution)/shard_map/ppermute | solution.py:328
  246.2 15.1 %collective-permute-done.38 = bf16[2,4,48,384]{3,2,0,1:T(8,128)(2,1)} collective-permute-done((bf16[2,4,48,384]{3,2,0,1:T(8,128)(2,1)}, bf16[2,4,48,384]{3,2,0,1:T(8,128)(2,1)}, u32[]{:S(2)}, u32[]{:S(2)}) %collective-permute-start.38) | collective-permute-done | bytes 294944 | tf_op jit(solution)/shard_map/ppermute | solution.py:330
  261.3 2.2 fusion.3
  265.2 1.9 fusion.16
  268.0 8.9 %shard_map.216 = (bf16[256,768]{1,0:T(8,128)(2,1)}, bf16[2,448,768]{2,1,0:T(8,128)(2,1)}, bf16[2,448,768]{2,1,0:T(8,128)(2,1)}) custom-call(s32[4]{0:T(128)} %pad_add_fusion.refs_0_, f32[24,768]{1,0:T(8,128)} %get-tuple-element.247.refs_1_.refs_0_, bf16[256,768]{1,0:T(8,128)(2,1)} %pad_maximum_fusion.3.refs_1_.refs_3_.refs_2_, ...), custom_call_target="tpu_custom_call" | custom-call | bytes 24500000 | tf_op jit(solution)/shard_map/pallas_call | solution.py:734
  280.6 2.0 fusion.21
  285.3 2.3 collective-permute-start.46
  287.7 2.0 dynamic-slice_bitcast_fusion.1
  291.6 4.1 all-to-all-start.3
  296.4 2.2 maximum_select_fusion.6
  299.7 2.4 all-to-all-done.3
  304.0 2.3 fusion.9
  307.6 4.1 all-to-all-start.4
  311.7 2.2 fusion.18
  313.9 2.9 collective-permute-start.52
  319.7 19.1 %collective-permute-done.52 = bf16[2,72,768]{2,1,0:T(8,128)(2,1)} collective-permute-done((bf16[2,72,768]{2,1,0:T(8,128)(2,1)}, bf16[2,72,768]{2,1,0:T(8,128)(2,1)}, u32[]{:S(2)}, u32[]{:S(2)}) %collective-permute-start.52) | collective-permute-done | bytes 221216 | tf_op jit(solution)/shard_map/ppermute | solution.py:330
  338.8 3.6 collective-permute-done.51
  343.4 2.6 fusion
  346.1 3.9 all-to-all-start.5
  351.1 2.1 collective-permute-start.55
  357.2 15.3 %collective-permute-done.54 = bf16[2,72,768]{2,1,0:T(8,128)(2,1)S(1)} collective-permute-done((bf16[2,72,768]{2,1,0:T(8,128)(2,1)S(1)}, bf16[2,72,768]{2,1,0:T(8,128)(2,1)S(1)}, u32[]{:S(2)}, u32[]{:S(2)}) %collective-permute-start.54) | collective-permute-done | bytes 221216 | tf_op jit(solution)/shard_map/ppermute | solution.py:330
  378.3 4.5 %all-to-all-start.6 = ((bf16[8,56,768]{2,1,0:T(8,128)(2,1)}), bf16[8,56,768]{2,1,0:T(8,128)(2,1)}, u32[]{:S(2)}, u32[]{:S(2)}) async-start(bf16[8,56,768]{2,1,0:T(8,128)(2,1)} %broadcast_in_dim.4), calls=%async_computation.6 | async-start | bytes 1376256 | tf_op jit(solution)/shard_map/all_to_all | solution.py:1006
  385.6 2.0 collective-permute-start.60
  390.5 2.9 reshape.1277
  398.1 7.0 %collective-permute-done.60 = bf16[4,72,768]{2,1,0:T(8,128)(2,1)} collective-permute-done((bf16[4,72,768]{2,1,0:T(8,128)(2,1)}, bf16[4,72,768]{2,1,0:T(8,128)(2,1)}, u32[]{:S(2)}, u32[]{:S(2)}) %collective-permute-start.60) | collective-permute-done | bytes 442400 | tf_op jit(solution)/shard_map/ppermute | solution.py:330
  405.1 2.6 maximum_select_fusion.3
  407.7 2.5 maximum_select_fusion.2
  410.2 4.0 shard_map.217
  (294 shorter events, 98.8 us)
Async XLA Ops:
  2.5 26.5 %collective-permute-start.5 = (bf16[608,768]{1,0:T(8,128)(2,1)S(1)}, bf16[608,768]{1,0:T(8,128)(2,1)}, u32[]{:S(2)}, u32[]{:S(2)}) collective-permute-start(bf16[608,768]{1,0:T(8,128)(2,1)S(1)} %pad_maximum_fusion.1.refs_2_.refs_13_), channel_id=1, source_target_pairs={{0,16},{16,0},{1,17},{17,1},{2,18},{18,2},{3,19},{19,3},{4,20},{20... | collective-permute-start | bytes 2801672 | tf_op jit(solution)/shard_map/ppermute | solution.py:783
  5.2 11.0 %collective-permute-start.1 = (bf16[2,64,768]{2,1,0:T(8,128)(2,1)S(1)}, bf16[2,64,768]{2,1,0:T(8,128)(2,1)S(1)}, u32[]{:S(2)}, u32[]{:S(2)}) collective-permute-start(bf16[2,64,768]{2,1,0:T(8,128)(2,1)S(1)} %pad_maximum_fusion.5), channel_id=1, source_target_pairs={{0,0},{2,10},{4,2},{6,8},{8,4},{10,14},{12,6},{14,12},{1,1},{3,11}... | collective-permute-start | bytes 589832 | tf_op jit(solution)/shard_map/ppermute | solution.py:197
  5.9 10.4 %collective-permute-start.2 = (bf16[2,64,768]{2,1,0:T(8,128)(2,1)S(1)}, bf16[2,64,768]{2,1,0:T(8,128)(2,1)S(1)}, u32[]{:S(2)}, u32[]{:S(2)}) collective-permute-start(bf16[2,64,768]{2,1,0:T(8,128)(2,1)S(1)} %pad_maximum_fusion.6), channel_id=1, source_target_pairs={{0,8},{2,0},{4,10},{6,2},{8,12},{10,4},{12,14},{14,6},{1,9},{3,1},... | collective-permute-start | bytes 589832 | tf_op jit(solution)/shard_map/ppermute | solution.py:197
  10.8 16.5 %collective-permute-start.3 = (bf16[2,64,768]{2,1,0:T(8,128)(2,1)S(1)}, bf16[2,64,768]{2,1,0:T(8,128)(2,1)S(1)}, u32[]{:S(2)}, u32[]{:S(2)}) collective-permute-start(bf16[2,64,768]{2,1,0:T(8,128)(2,1)S(1)} %pad_maximum_fusion.7), channel_id=1, source_target_pairs={{0,2},{2,8},{4,0},{6,10},{8,6},{10,12},{12,4},{14,14},{1,3},{3,9},... | collective-permute-start | bytes 589832 | tf_op jit(solution)/shard_map/ppermute | solution.py:197
  12.8 14.5 %collective-permute-start.4 = (bf16[2,64,768]{2,1,0:T(8,128)(2,1)S(1)}, bf16[2,64,768]{2,1,0:T(8,128)(2,1)S(1)}, u32[]{:S(2)}, u32[]{:S(2)}) collective-permute-start(bf16[2,64,768]{2,1,0:T(8,128)(2,1)S(1)} %pad_maximum_fusion.8), channel_id=1, source_target_pairs={{0,10},{2,2},{4,8},{6,0},{8,14},{10,6},{12,12},{14,4},{1,11},{3,3}... | collective-permute-start | bytes 589832 | tf_op jit(solution)/shard_map/ppermute | solution.py:197
  29.8 18.9 %collective-permute-start.10 = (bf16[5,192,768]{2,1,0:T(8,128)(2,1)S(1)}, bf16[5,192,768]{2,1,0:T(8,128)(2,1)S(1)}, u32[]{:S(2)}, u32[]{:S(2)}) collective-permute-start(bf16[5,192,768]{2,1,0:T(8,128)(2,1)S(1)} %pad_maximum_fusion.refs_3_.refs_4_.refs_7_.refs_8_.refs_12_), channel_id=1, source_target_pairs={{0,8},{8,0},{1,9},{9,1},{2,10},{10,2},{3,11},{11,3},{4,12},{12,4},... | collective-permute-start | bytes 4423688 | tf_op jit(solution)/shard_map/ppermute | solution.py:286
  31.7 4.4 %collective-permute-start.6 = (bf16[608,768]{1,0:T(8,128)(2,1)}, bf16[608,768]{1,0:T(8,128)(2,1)}, u32[]{:S(2)}, u32[]{:S(2)}) collective-permute-start(bf16[608,768]{1,0:T(8,128)(2,1)} %collective-permute-done.5.refs_4_.refs_15_), channel_id=1, source_target_pairs={{0,8},{8,0},{1,9},{9,1},{2,10},{10,2},{3,11},{11,3},{4,12},{12,4},... | collective-permute-start | bytes 2801672 | tf_op jit(solution)/shard_map/ppermute | solution.py:286
  32.6 16.1 %collective-permute-start.9 = (bf16[2,192,768]{2,1,0:T(8,128)(2,1)}, bf16[2,192,768]{2,1,0:T(8,128)(2,1)}, u32[]{:S(2)}, u32[]{:S(2)}) collective-permute-start(bf16[2,192,768]{2,1,0:T(8,128)(2,1)} %copy-done.20), channel_id=1, source_target_pairs={{0,16},{16,0},{1,17},{17,1},{2,18},{18,2},{3,19},{19,3},{4,20},{20... | collective-permute-start | bytes 1769480 | tf_op jit(solution)/shard_map/ppermute | solution.py:823
  41.3 20.0 %collective-permute-start.7 = (bf16[2,256,768]{2,1,0:T(8,128)(2,1)}, bf16[2,256,768]{2,1,0:T(8,128)(2,1)}, u32[]{:S(2)}, u32[]{:S(2)}) collective-permute-start(bf16[2,256,768]{2,1,0:T(8,128)(2,1)} %get-tuple-element.259.refs_3_.refs_6_), channel_id=1, source_target_pairs={{0,1},{1,0},{2,3},{3,2},{4,5},{5,4},{6,7},{7,6},{8,9},{9,8},{10,11... | collective-permute-start | bytes 2359304 | tf_op jit(solution)/shard_map/ppermute | solution.py:267
  42.8 18.4 %collective-permute-start.8 = (bf16[2,256,768]{2,1,0:T(8,128)(2,1)}, bf16[2,256,768]{2,1,0:T(8,128)(2,1)}, u32[]{:S(2)}, u32[]{:S(2)}) collective-permute-start(bf16[2,256,768]{2,1,0:T(8,128)(2,1)} %get-tuple-element.259.refs_3_.refs_6_), channel_id=1, source_target_pairs={{0,8},{8,0},{1,9},{9,1},{2,10},{10,2},{3,11},{11,3},{4,12},{12,4},... | collective-permute-start | bytes 2359304 | tf_op jit(solution)/shard_map/ppermute | solution.py:286
  48.7 6.1 %collective-permute-start.11 = (bf16[2,192,768]{2,1,0:T(8,128)(2,1)}, bf16[2,192,768]{2,1,0:T(8,128)(2,1)S(1)}, u32[]{:S(2)}, u32[]{:S(2)}) collective-permute-start(bf16[2,192,768]{2,1,0:T(8,128)(2,1)} %collective-permute-done.9.refs_5_.refs_14_), channel_id=1, source_target_pairs={{0,8},{8,0},{1,9},{9,1},{2,10},{10,2},{3,11},{11,3},{4,12},{12,4},... | collective-permute-start | bytes 1769480 | tf_op jit(solution)/shard_map/ppermute | solution.py:286
  50.9 9.0 %collective-permute-start.12 = (bf16[2,64,768]{2,1,0:T(8,128)(2,1)S(1)}, bf16[2,64,768]{2,1,0:T(8,128)(2,1)S(1)}, u32[]{:S(2)}, u32[]{:S(2)}) collective-permute-start(bf16[2,64,768]{2,1,0:T(8,128)(2,1)S(1)} %get-tuple-element.465), channel_id=1, source_target_pairs={{0,8},{8,0},{1,9},{9,1},{2,10},{10,2},{3,11},{11,3},{4,12},{12,4},... | collective-permute-start | bytes 589832 | tf_op jit(solution)/shard_map/ppermute | solution.py:231
  51.0 30.0 %collective-permute-start.14 = (bf16[3,192,768]{2,1,0:T(8,128)(2,1)}, bf16[3,192,768]{2,1,0:T(8,128)(2,1)S(1)}, u32[]{:S(2)}, u32[]{:S(2)}) collective-permute-start(bf16[3,192,768]{2,1,0:T(8,128)(2,1)} %pad_maximum_fusion.2), channel_id=1, source_target_pairs={{0,16},{16,0},{1,17},{17,1},{2,18},{18,2},{3,19},{19,3},{4,20},{20... | collective-permute-start | bytes 2654216 | tf_op jit(solution)/shard_map/ppermute | solution.py:845
  61.2 9.7 %collective-permute-start.13 = (bf16[2,256,768]{2,1,0:T(8,128)(2,1)}, bf16[2,256,768]{2,1,0:T(8,128)(2,1)S(1)}, u32[]{:S(2)}, u32[]{:S(2)}) collective-permute-start(bf16[2,256,768]{2,1,0:T(8,128)(2,1)} %collective-permute-done.7.refs_5_.refs_8_), channel_id=1, source_target_pairs={{0,8},{8,0},{1,9},{9,1},{2,10},{10,2},{3,11},{11,3},{4,12},{12,4},... | collective-permute-start | bytes 2359304 | tf_op jit(solution)/shard_map/ppermute | solution.py:273
  61.2 20.3 %collective-permute-start.15 = (bf16[2,256,768]{2,1,0:T(8,128)(2,1)}, bf16[2,256,768]{2,1,0:T(8,128)(2,1)S(1)}, u32[]{:S(2)}, u32[]{:S(2)}) collective-permute-start(bf16[2,256,768]{2,1,0:T(8,128)(2,1)} %shard_map.204.refs_1_.refs_4_), channel_id=1, source_target_pairs={{0,1},{1,0},{2,3},{3,2},{4,5},{5,4},{6,7},{7,6},{8,9},{9,8},{10,11... | collective-permute-start | bytes 2359304 | tf_op jit(solution)/shard_map/ppermute | solution.py:267
  62.8 18.7 %collective-permute-start.16 = (bf16[2,256,768]{2,1,0:T(8,128)(2,1)}, bf16[2,256,768]{2,1,0:T(8,128)(2,1)}, u32[]{:S(2)}, u32[]{:S(2)}) collective-permute-start(bf16[2,256,768]{2,1,0:T(8,128)(2,1)} %shard_map.204.refs_1_.refs_4_), channel_id=1, source_target_pairs={{0,8},{8,0},{1,9},{9,1},{2,10},{10,2},{3,11},{11,3},{4,12},{12,4},... | collective-permute-start | bytes 2359304 | tf_op jit(solution)/shard_map/ppermute | solution.py:286
  64.8 16.7 %all-to-all-start = ((bf16[4,64,768]{2,1,0:T(8,128)(2,1)}), bf16[4,64,768]{2,1,0:T(8,128)(2,1)S(1)}, u32[]{:S(2)}, u32[]{:S(2)}) async-start(bf16[4,64,768]{2,1,0:T(8,128)(2,1)} %maximum_select_fusion.10), calls=%async_computation | async-start | bytes 786432 | tf_op jit(solution)/shard_map/all_to_all | solution.py:237
  82.4 9.3 %collective-permute-start.18 = (bf16[2,256,768]{2,1,0:T(8,128)(2,1)}, bf16[2,256,768]{2,1,0:T(8,128)(2,1)S(1)}, u32[]{:S(2)}, u32[]{:S(2)}) collective-permute-start(bf16[2,256,768]{2,1,0:T(8,128)(2,1)} %copy-done.14), channel_id=1, source_target_pairs={{0,8},{8,0},{1,9},{9,1},{2,10},{10,2},{3,11},{11,3},{4,12},{12,4},... | collective-permute-start | bytes 2359304 | tf_op jit(solution)/shard_map/ppermute | solution.py:273
  83.1 21.1 %collective-permute-start.19 = (bf16[256,768]{1,0:T(8,128)(2,1)S(1)}, bf16[256,768]{1,0:T(8,128)(2,1)}, u32[]{:S(2)}, u32[]{:S(2)}) collective-permute-start(bf16[256,768]{1,0:T(8,128)(2,1)S(1)} %bitcast.203), channel_id=1, source_target_pairs={{0,16},{16,0},{1,17},{17,1},{2,18},{18,2},{3,19},{19,3},{4,20},{20... | collective-permute-start | bytes 1179656 | tf_op jit(solution)/shard_map/ppermute | solution.py:865
  84.6 19.6 %collective-permute-start.20 = (bf16[256,768]{1,0:T(8,128)(2,1)S(1)}, bf16[256,768]{1,0:T(8,128)(2,1)}, u32[]{:S(2)}, u32[]{:S(2)}) collective-permute-start(bf16[256,768]{1,0:T(8,128)(2,1)S(1)} %bitcast.204), channel_id=1, source_target_pairs={{0,8},{8,0},{1,9},{9,1},{2,10},{10,2},{3,11},{11,3},{4,12},{12,4},... | collective-permute-start | bytes 1179656 | tf_op jit(solution)/shard_map/ppermute | solution.py:286
  91.7 29.9 %all-to-all-start.1 = ((bf16[4,192,768]{2,1,0:T(8,128)(2,1)}), bf16[4,192,768]{2,1,0:T(8,128)(2,1)S(1)}, u32[]{:S(2)}, u32[]{:S(2)}) async-start(bf16[4,192,768]{2,1,0:T(8,128)(2,1)} %bitcast.201), calls=%async_computation.1 | async-start | bytes 2359296 | tf_op jit(solution)/shard_map/all_to_all | solution.py:864
  108.1 11.8 %collective-permute-start.22 = (bf16[256,768]{1,0:T(8,128)(2,1)}, bf16[256,768]{1,0:T(8,128)(2,1)S(1)}, u32[]{:S(2)}, u32[]{:S(2)}) collective-permute-start(bf16[256,768]{1,0:T(8,128)(2,1)} %get-tuple-element.292.refs_3_.refs_2_), channel_id=1, source_target_pairs={{0,16},{16,0},{1,17},{17,1},{2,18},{18,2},{3,19},{19,3},{4,20},{20... | collective-permute-start | bytes 1179656 | tf_op jit(solution)/shard_map/ppermute | solution.py:871
  110.1 9.7 %collective-permute-start.21 = (bf16[256,768]{1,0:T(8,128)(2,1)}, bf16[256,768]{1,0:T(8,128)(2,1)S(1)}, u32[]{:S(2)}, u32[]{:S(2)}) collective-permute-start(bf16[256,768]{1,0:T(8,128)(2,1)} %get-tuple-element.292.refs_3_.refs_2_), channel_id=1, source_target_pairs={{0,8},{8,0},{1,9},{9,1},{2,10},{10,2},{3,11},{11,3},{4,12},{12,4},... | collective-permute-start | bytes 1179656 | tf_op jit(solution)/shard_map/ppermute | solution.py:286
  110.1 9.7 %collective-permute-start.24 = (bf16[256,768]{1,0:T(8,128)(2,1)}, bf16[256,768]{1,0:T(8,128)(2,1)S(1)}, u32[]{:S(2)}, u32[]{:S(2)}) collective-permute-start(bf16[256,768]{1,0:T(8,128)(2,1)} %collective-permute-done.19.refs_9_.refs_8_), channel_id=1, source_target_pairs={{0,8},{8,0},{1,9},{9,1},{2,10},{10,2},{3,11},{11,3},{4,12},{12,4},... | collective-permute-start | bytes 1179656 | tf_op jit(solution)/shard_map/ppermute | solution.py:286
  136.4 11.2 %collective-permute-start.26 = (bf16[256,768]{1,0:T(8,128)(2,1)S(1)}, bf16[256,768]{1,0:T(8,128)(2,1)S(1)}, u32[]{:S(2)}, u32[]{:S(2)}) collective-permute-start(bf16[256,768]{1,0:T(8,128)(2,1)S(1)} %fusion.23), channel_id=1, source_target_pairs={{0,16},{16,0},{1,17},{17,1},{2,18},{18,2},{3,19},{19,3},{4,20},{20... | collective-permute-start | bytes 1179656 | tf_op jit(solution)/shard_map/ppermute | solution.py:900
  147.6 22.8 %collective-permute-start.27 = (bf16[2,256,768]{2,1,0:T(8,128)(2,1)}, bf16[2,256,768]{2,1,0:T(8,128)(2,1)S(1)}, u32[]{:S(2)}, u32[]{:S(2)}) collective-permute-start(bf16[2,256,768]{2,1,0:T(8,128)(2,1)} %get-tuple-element.317), channel_id=1, source_target_pairs={{0,8},{8,0},{1,9},{9,1},{2,10},{10,2},{3,11},{11,3},{4,12},{12,4},... | collective-permute-start | bytes 2359304 | tf_op jit(solution)/shard_map/ppermute | solution.py:286
  149.5 20.9 %collective-permute-start.29 = (bf16[2,2,4,48,384]{4,3,2,1,0:T(8,128)(2,1)S(1)}, bf16[2,2,4,48,384]{4,3,2,1,0:T(8,128)(2,1)S(1)}, u32[]{:S(2)}, u32[]{:S(2)}) collective-permute-start(bf16[2,2,4,48,384]{4,3,2,1,0:T(8,128)(2,1)S(1)} %dynamic-slice_bitcast_fusion), channel_id=1, source_target_pairs={{0,2},{2,0},{4,6},{6,4},{1,3},{3,1},{5,7},{7,5},{8,10},{10,8},{12,... | collective-permute-start | bytes 1769480 | tf_op jit(solution)/shard_map/ppermute | solution.py:330
  152.1 18.3 %collective-permute-start.28 = (bf16[2,2,4,48,384]{4,3,1,2,0:T(8,128)(2,1)}, bf16[2,2,4,48,384]{4,3,1,2,0:T(8,128)(2,1)S(1)}, u32[]{:S(2)}, u32[]{:S(2)}) collective-permute-start(bf16[2,2,4,48,384]{4,3,1,2,0:T(8,128)(2,1)} %copy_bitcast_fusion), channel_id=1, source_target_pairs={{0,1},{1,0},{2,3},{3,2},{4,5},{5,4},{6,7},{7,6},{8,9},{9,8},{10,11... | collective-permute-start | bytes 1769480 | tf_op jit(solution)/shard_map/ppermute | solution.py:328
  171.2 7.5 %collective-permute-start.30 = (bf16[2,2,256,768]{3,2,1,0:T(8,128)(2,1)}, bf16[2,2,256,768]{3,2,1,0:T(8,128)(2,1)}, u32[]{:S(2)}, u32[]{:S(2)}) collective-permute-start(bf16[2,2,256,768]{3,2,1,0:T(8,128)(2,1)} %get-tuple-element.328), channel_id=1, source_target_pairs={{0,8},{8,0},{1,9},{9,1},{2,10},{10,2},{3,11},{11,3},{4,12},{12,4},... | collective-permute-start | bytes 4718600 | tf_op jit(solution)/shard_map/ppermute | solution.py:286
  178.8 25.1 %collective-permute-start.31 = (bf16[2,3,192,768]{3,2,1,0:T(8,128)(2,1)}, bf16[2,3,192,768]{3,2,1,0:T(8,128)(2,1)}, u32[]{:S(2)}, u32[]{:S(2)}) collective-permute-start(bf16[2,3,192,768]{3,2,1,0:T(8,128)(2,1)} %get-tuple-element.342), channel_id=1, source_target_pairs={{0,8},{8,0},{1,9},{9,1},{2,10},{10,2},{3,11},{11,3},{4,12},{12,4},... | collective-permute-start | bytes 5308424 | tf_op jit(solution)/shard_map/ppermute | solution.py:305
  181.2 22.6 %collective-permute-start.35 = (bf16[2,256,768]{2,1,0:T(8,128)(2,1)}, bf16[2,256,768]{2,1,0:T(8,128)(2,1)S(1)}, u32[]{:S(2)}, u32[]{:S(2)}) collective-permute-start(bf16[2,256,768]{2,1,0:T(8,128)(2,1)} %fusion.4), channel_id=1, source_target_pairs={{1,0},{0,1},{3,2},{2,3},{5,4},{4,5},{7,6},{6,7},{9,8},{8,9},{11,10... | collective-permute-start | bytes 2359304 | tf_op jit(solution)/shard_map/ppermute | solution.py:281
  182.9 20.9 %collective-permute-start.34 = (bf16[256,768]{1,0:T(8,128)(2,1)S(1)}, bf16[256,768]{1,0:T(8,128)(2,1)S(1)}, u32[]{:S(2)}, u32[]{:S(2)}) collective-permute-start(bf16[256,768]{1,0:T(8,128)(2,1)S(1)} %fusion.24), channel_id=1, source_target_pairs={{0,16},{16,0},{1,17},{17,1},{2,18},{18,2},{3,19},{19,3},{4,20},{20... | collective-permute-start | bytes 1179656 | tf_op jit(solution)/shard_map/ppermute | solution.py:931
  185.7 17.4 %collective-permute-start.33 = (bf16[2,4,48,384]{3,2,1,0:T(8,128)(2,1)S(1)}, bf16[2,4,48,384]{3,2,1,0:T(8,128)(2,1)S(1)}, u32[]{:S(2)}, u32[]{:S(2)}) collective-permute-start(bf16[2,4,48,384]{3,2,1,0:T(8,128)(2,1)S(1)} %fusion.14), channel_id=1, source_target_pairs={{0,4},{2,6},{4,0},{6,2},{1,5},{3,7},{5,1},{7,3},{8,12},{10,14},{12... | collective-permute-start | bytes 884744 | tf_op jit(solution)/shard_map/ppermute | solution.py:330
  189.1 14.7 %collective-permute-start.32 = (bf16[2,4,48,384]{3,2,0,1:T(8,128)(2,1)S(1)}, bf16[2,4,48,384]{3,2,0,1:T(8,128)(2,1)S(1)}, u32[]{:S(2)}, u32[]{:S(2)}) collective-permute-start(bf16[2,4,48,384]{3,2,0,1:T(8,128)(2,1)S(1)} %fusion.15), channel_id=1, source_target_pairs={{0,2},{2,0},{4,6},{6,4},{1,3},{3,1},{5,7},{7,5},{8,10},{10,8},{12,... | collective-permute-start | bytes 884744 | tf_op jit(solution)/shard_map/ppermute | solution.py:330
  204.9 8.3 %collective-permute-start.36 = (bf16[2,2,256,768]{3,2,1,0:T(8,128)(2,1)}, bf16[2,2,256,768]{3,2,1,0:T(8,128)(2,1)S(1)}, u32[]{:S(2)}, u32[]{:S(2)}) collective-permute-start(bf16[2,2,256,768]{3,2,1,0:T(8,128)(2,1)} %get-tuple-element.357), channel_id=1, source_target_pairs={{0,8},{8,0},{1,9},{9,1},{2,10},{10,2},{3,11},{11,3},{4,12},{12,4},... | collective-permute-start | bytes 4718600 | tf_op jit(solution)/shard_map/ppermute | solution.py:286
  214.4 7.1 %collective-permute-start.40 = (bf16[2,3,192,768]{3,2,1,0:T(8,128)(2,1)}, bf16[2,3,192,768]{3,2,1,0:T(8,128)(2,1)S(1)}, u32[]{:S(2)}, u32[]{:S(2)}) collective-permute-start(bf16[2,3,192,768]{3,2,1,0:T(8,128)(2,1)} %get-tuple-element.383), channel_id=1, source_target_pairs={{0,8},{8,0},{1,9},{9,1},{2,10},{10,2},{3,11},{11,3},{4,12},{12,4},... | collective-permute-start | bytes 5308424 | tf_op jit(solution)/shard_map/ppermute | solution.py:305
  217.2 44.0 %collective-permute-start.42 = (bf16[2,2,2,72,768]{4,3,2,1,0:T(8,128)(2,1)}, bf16[2,2,2,72,768]{4,3,2,1,0:T(8,128)(2,1)}, u32[]{:S(2)}, u32[]{:S(2)}) collective-permute-start(bf16[2,2,2,72,768]{4,3,2,1,0:T(8,128)(2,1)} %fusion.2), channel_id=1, source_target_pairs={{0,2},{2,0},{4,6},{6,4},{1,3},{3,1},{5,7},{7,5},{8,10},{10,8},{12,... | collective-permute-start | bytes 2654216 | tf_op jit(solution)/shard_map/ppermute | solution.py:330
  220.3 41.0 %collective-permute-start.37 = (bf16[2,256,768]{2,1,0:T(8,128)(2,1)}, bf16[2,256,768]{2,1,0:T(8,128)(2,1)}, u32[]{:S(2)}, u32[]{:S(2)}) collective-permute-start(bf16[2,256,768]{2,1,0:T(8,128)(2,1)} %fusion.5), channel_id=1, source_target_pairs={{1,0},{0,1},{3,2},{2,3},{5,4},{4,5},{7,6},{6,7},{9,8},{8,9},{11,10... | collective-permute-start | bytes 2359304 | tf_op jit(solution)/shard_map/ppermute | solution.py:281
  222.6 38.7 %collective-permute-start.41 = (bf16[3,192,768]{2,1,0:T(8,128)(2,1)}, bf16[3,192,768]{2,1,0:T(8,128)(2,1)}, u32[]{:S(2)}, u32[]{:S(2)}) collective-permute-start(bf16[3,192,768]{2,1,0:T(8,128)(2,1)} %fusion.1), channel_id=1, source_target_pairs={{0,16},{16,0},{1,17},{17,1},{2,18},{18,2},{3,19},{19,3},{4,20},{20... | collective-permute-start | bytes 2654216 | tf_op jit(solution)/shard_map/ppermute | solution.py:309
  224.2 52.7 %all-to-all-start.2 = ((bf16[4,2,64,768]{3,2,1,0:T(8,128)(2,1)}), bf16[4,2,64,768]{3,2,1,0:T(8,128)(2,1)}, u32[]{:S(2)}, u32[]{:S(2)}) async-start(bf16[4,2,64,768]{3,2,1,0:T(8,128)(2,1)} %fusion.7), calls=%async_computation.2 | async-start | bytes 1572864 | tf_op jit(solution)/shard_map/all_to_all | solution.py:206
  230.6 15.6 %collective-permute-start.39 = (bf16[2,4,48,384]{3,2,1,0:T(8,128)(2,1)}, bf16[2,4,48,384]{3,2,1,0:T(8,128)(2,1)}, u32[]{:S(2)}, u32[]{:S(2)}) collective-permute-start(bf16[2,4,48,384]{3,2,1,0:T(8,128)(2,1)} %fusion.11), channel_id=1, source_target_pairs={{0,1},{1,0},{2,3},{3,2},{4,5},{5,4},{6,7},{7,6},{8,9},{9,8},{10,11... | collective-permute-start | bytes 884744 | tf_op jit(solution)/shard_map/ppermute | solution.py:328
  233.4 27.8 %collective-permute-start.38 = (bf16[2,4,48,384]{3,2,0,1:T(8,128)(2,1)}, bf16[2,4,48,384]{3,2,0,1:T(8,128)(2,1)}, u32[]{:S(2)}, u32[]{:S(2)}) collective-permute-start(bf16[2,4,48,384]{3,2,0,1:T(8,128)(2,1)} %fusion.13), channel_id=1, source_target_pairs={{0,4},{2,6},{4,0},{6,2},{1,5},{3,7},{5,1},{7,3},{8,12},{10,14},{12... | collective-permute-start | bytes 884744 | tf_op jit(solution)/shard_map/ppermute | solution.py:330
  263.5 13.4 %collective-permute-start.44 = (bf16[2,2,72,768]{3,2,1,0:T(8,128)(2,1)}, bf16[2,2,72,768]{3,2,1,0:T(8,128)(2,1)}, u32[]{:S(2)}, u32[]{:S(2)}) collective-permute-start(bf16[2,2,72,768]{3,2,1,0:T(8,128)(2,1)} %fusion.3), channel_id=1, source_target_pairs={{0,16},{16,0},{1,17},{17,1},{2,18},{18,2},{3,19},{19,3},{4,20},{20... | collective-permute-start | bytes 1327112 | tf_op jit(solution)/shard_map/ppermute | solution.py:961
  267.2 10.5 %collective-permute-start.43 = (bf16[2,2,72,768]{3,2,1,0:T(8,128)(2,1)}, bf16[2,2,72,768]{3,2,1,0:T(8,128)(2,1)}, u32[]{:S(2)}, u32[]{:S(2)}) collective-permute-start(bf16[2,2,72,768]{3,2,1,0:T(8,128)(2,1)} %fusion.16), channel_id=1, source_target_pairs={{0,1},{1,0},{2,3},{3,2},{4,5},{5,4},{6,7},{7,6},{8,9},{9,8},{10,11... | collective-permute-start | bytes 1327112 | tf_op jit(solution)/shard_map/ppermute | solution.py:328
  277.7 24.4 %collective-permute-start.45 = (bf16[2,448,768]{2,1,0:T(8,128)(2,1)}, bf16[2,448,768]{2,1,0:T(8,128)(2,1)}, u32[]{:S(2)}, u32[]{:S(2)}) collective-permute-start(bf16[2,448,768]{2,1,0:T(8,128)(2,1)} %get-tuple-element.403), channel_id=1, source_target_pairs={{0,8},{8,0},{1,9},{9,1},{2,10},{10,2},{3,11},{11,3},{4,12},{12,4},... | collective-permute-start | bytes 4128776 | tf_op jit(solution)/shard_map/ppermute | solution.py:305
  280.6 15.9 %collective-permute-start.49 = (bf16[2,4,48,384]{3,2,1,0:T(8,128)(2,1)}, bf16[2,4,48,384]{3,2,1,0:T(8,128)(2,1)}, u32[]{:S(2)}, u32[]{:S(2)}) collective-permute-start(bf16[2,4,48,384]{3,2,1,0:T(8,128)(2,1)} %add_convert_fusion.8), channel_id=1, source_target_pairs={{0,4},{2,6},{4,0},{6,2},{1,5},{3,7},{5,1},{7,3},{8,12},{10,14},{12... | collective-permute-start | bytes 884744 | tf_op jit(solution)/shard_map/ppermute | solution.py:330
  282.5 16.1 %collective-permute-start.47 = (bf16[2,72,768]{2,1,0:T(8,128)(2,1)}, bf16[2,72,768]{2,1,0:T(8,128)(2,1)}, u32[]{:S(2)}, u32[]{:S(2)}) collective-permute-start(bf16[2,72,768]{2,1,0:T(8,128)(2,1)} %fusion.21), channel_id=1, source_target_pairs={{0,1},{1,0},{2,3},{3,2},{4,5},{5,4},{6,7},{7,6},{8,9},{9,8},{10,11... | collective-permute-start | bytes 663560 | tf_op jit(solution)/shard_map/ppermute | solution.py:328
  285.3 14.4 %collective-permute-start.46 = (bf16[2,72,768]{2,1,0:T(8,128)(2,1)}, bf16[2,72,768]{2,1,0:T(8,128)(2,1)}, u32[]{:S(2)}, u32[]{:S(2)}) collective-permute-start(bf16[2,72,768]{2,1,0:T(8,128)(2,1)} %fusion.22), channel_id=1, source_target_pairs={{0,2},{2,0},{4,6},{6,4},{1,3},{3,1},{5,7},{7,5},{8,10},{10,8},{12,... | collective-permute-start | bytes 663560 | tf_op jit(solution)/shard_map/ppermute | solution.py:330
  289.7 12.4 %collective-permute-start.48 = (bf16[2,2,64,768]{3,2,1,0:T(8,128)(2,1)}, bf16[2,2,64,768]{3,2,1,0:T(8,128)(2,1)}, u32[]{:S(2)}, u32[]{:S(2)}) collective-permute-start(bf16[2,2,64,768]{3,2,1,0:T(8,128)(2,1)} %get-tuple-element.457), channel_id=1, source_target_pairs={{0,8},{8,0},{1,9},{9,1},{2,10},{10,2},{3,11},{11,3},{4,12},{12,4},... | collective-permute-start | bytes 1179656 | tf_op jit(solution)/shard_map/ppermute | solution.py:213
  291.6 10.5 %all-to-all-start.3 = ((bf16[2,4,48,384]{3,2,0,1:T(8,128)(2,1)}), bf16[2,4,48,384]{3,2,0,1:T(8,128)(2,1)}, u32[]{:S(2)}, u32[]{:S(2)}) async-start(bf16[2,4,48,384]{3,2,0,1:T(8,128)(2,1)} %add_convert_fusion.9), calls=%async_computation.3 | async-start | bytes 589824 | tf_op jit(solution)/shard_map/all_to_all | solution.py:982
  302.1 16.3 %collective-permute-start.53 = (bf16[2,4,48,384]{3,2,0,1:T(8,128)(2,1)}, bf16[2,4,48,384]{3,2,0,1:T(8,128)(2,1)}, u32[]{:S(2)}, u32[]{:S(2)}) collective-permute-start(bf16[2,4,48,384]{3,2,0,1:T(8,128)(2,1)} %all-to-all-done.3), channel_id=1, source_target_pairs={{0,2},{2,0},{4,6},{6,4},{1,3},{3,1},{5,7},{7,5},{8,10},{10,8},{12,... | collective-permute-start | bytes 884744 | tf_op jit(solution)/shard_map/ppermute | solution.py:330
  306.3 36.1 %collective-permute-start.50 = (bf16[448,768]{1,0:T(8,128)(2,1)}, bf16[448,768]{1,0:T(8,128)(2,1)}, u32[]{:S(2)}, u32[]{:S(2)}) collective-permute-start(bf16[448,768]{1,0:T(8,128)(2,1)} %fusion.9), channel_id=1, source_target_pairs={{0,16},{16,0},{1,17},{17,1},{2,18},{18,2},{3,19},{19,3},{4,20},{20... | collective-permute-start | bytes 2064392 | tf_op jit(solution)/shard_map/ppermute | solution.py:309
  307.6 34.8 %all-to-all-start.4 = ((bf16[4,1,64,768]{3,2,1,0:T(8,128)(2,1)}), bf16[4,1,64,768]{3,2,1,0:T(8,128)(2,1)}, u32[]{:S(2)}, u32[]{:S(2)}) async-start(bf16[4,1,64,768]{3,2,1,0:T(8,128)(2,1)} %fusion.25), calls=%async_computation.4 | async-start | bytes 786432 | tf_op jit(solution)/shard_map/all_to_all | solution.py:206
  313.9 24.9 %collective-permute-start.52 = (bf16[2,72,768]{2,1,0:T(8,128)(2,1)}, bf16[2,72,768]{2,1,0:T(8,128)(2,1)}, u32[]{:S(2)}, u32[]{:S(2)}) collective-permute-start(bf16[2,72,768]{2,1,0:T(8,128)(2,1)} %fusion.18), channel_id=1, source_target_pairs={{0,4},{2,6},{4,0},{6,2},{1,5},{3,7},{5,1},{7,3},{8,12},{10,14},{12... | collective-permute-start | bytes 663560 | tf_op jit(solution)/shard_map/ppermute | solution.py:330
  318.3 24.1 %collective-permute-start.51 = (bf16[2,72,768]{2,1,0:T(8,128)(2,1)S(1)}, bf16[2,72,768]{2,1,0:T(8,128)(2,1)S(1)}, u32[]{:S(2)}, u32[]{:S(2)}) collective-permute-start(bf16[2,72,768]{2,1,0:T(8,128)(2,1)S(1)} %fusion.20), channel_id=1, source_target_pairs={{0,4},{2,6},{4,0},{6,2},{1,5},{3,7},{5,1},{7,3},{8,12},{10,14},{12... | collective-permute-start | bytes 663560 | tf_op jit(solution)/shard_map/ppermute | solution.py:330
  342.4 31.8 %collective-permute-start.57 = (bf16[4,4,48,384]{3,2,1,0:T(8,128)(2,1)S(1)}, bf16[4,4,48,384]{3,2,1,0:T(8,128)(2,1)}, u32[]{:S(2)}, u32[]{:S(2)}) collective-permute-start(bf16[4,4,48,384]{3,2,1,0:T(8,128)(2,1)S(1)} %copy-done.16), channel_id=1, source_target_pairs={{0,2},{2,0},{4,6},{6,4},{1,3},{3,1},{5,7},{7,5},{8,10},{10,8},{12,... | collective-permute-start | bytes 1769480 | tf_op jit(solution)/shard_map/ppermute | solution.py:330
  342.5 33.2 %collective-permute-start.56 = (bf16[4,4,48,384]{3,2,0,1:T(8,128)(2,1)S(1)}, bf16[4,4,48,384]{3,2,0,1:T(8,128)(2,1)}, u32[]{:S(2)}, u32[]{:S(2)}) collective-permute-start(bf16[4,4,48,384]{3,2,0,1:T(8,128)(2,1)S(1)} %maximum_select_fusion.7), channel_id=1, source_target_pairs={{0,1},{1,0},{2,3},{3,2},{4,5},{5,4},{6,7},{7,6},{8,9},{9,8},{10,11... | collective-permute-start | bytes 1769480 | tf_op jit(solution)/shard_map/ppermute | solution.py:328
  346.1 31.2 %all-to-all-start.5 = ((bf16[8,56,768]{2,1,0:T(8,128)(2,1)}), bf16[8,56,768]{2,1,0:T(8,128)(2,1)S(1)}, u32[]{:S(2)}, u32[]{:S(2)}) async-start(bf16[8,56,768]{2,1,0:T(8,128)(2,1)} %bitcast.109), calls=%async_computation.5 | async-start | bytes 1376256 | tf_op jit(solution)/shard_map/all_to_all | solution.py:1001
  351.1 22.3 %collective-permute-start.55 = (bf16[2,72,768]{2,1,0:T(8,128)(2,1)S(1)}, bf16[2,72,768]{2,1,0:T(8,128)(2,1)S(1)}, u32[]{:S(2)}, u32[]{:S(2)}) collective-permute-start(bf16[2,72,768]{2,1,0:T(8,128)(2,1)S(1)} %add_convert_fusion.10), channel_id=1, source_target_pairs={{0,1},{1,0},{2,3},{3,2},{4,5},{5,4},{6,7},{7,6},{8,9},{9,8},{10,11... | collective-permute-start | bytes 663560 | tf_op jit(solution)/shard_map/ppermute | solution.py:328
  353.2 19.4 %collective-permute-start.54 = (bf16[2,72,768]{2,1,0:T(8,128)(2,1)S(1)}, bf16[2,72,768]{2,1,0:T(8,128)(2,1)S(1)}, u32[]{:S(2)}, u32[]{:S(2)}) collective-permute-start(bf16[2,72,768]{2,1,0:T(8,128)(2,1)S(1)} %add_convert_fusion.11), channel_id=1, source_target_pairs={{0,2},{2,0},{4,6},{6,4},{1,3},{3,1},{5,7},{7,5},{8,10},{10,8},{12,... | collective-permute-start | bytes 663560 | tf_op jit(solution)/shard_map/ppermute | solution.py:330
  356.5 20.7 %collective-permute-start.58 = (bf16[2,1,64,768]{3,2,1,0:T(8,128)(2,1)S(1)}, bf16[2,1,64,768]{3,2,1,0:T(8,128)(2,1)}, u32[]{:S(2)}, u32[]{:S(2)}) collective-permute-start(bf16[2,1,64,768]{3,2,1,0:T(8,128)(2,1)S(1)} %get-tuple-element.463), channel_id=1, source_target_pairs={{0,8},{8,0},{1,9},{9,1},{2,10},{10,2},{3,11},{11,3},{4,12},{12,4},... | collective-permute-start | bytes 589832 | tf_op jit(solution)/shard_map/ppermute | solution.py:213
  378.3 32.0 %all-to-all-start.6 = ((bf16[8,56,768]{2,1,0:T(8,128)(2,1)}), bf16[8,56,768]{2,1,0:T(8,128)(2,1)}, u32[]{:S(2)}, u32[]{:S(2)}) async-start(bf16[8,56,768]{2,1,0:T(8,128)(2,1)} %broadcast_in_dim.4), calls=%async_computation.6 | async-start | bytes 1376256 | tf_op jit(solution)/shard_map/all_to_all | solution.py:1006
  385.6 19.5 %collective-permute-start.60 = (bf16[4,72,768]{2,1,0:T(8,128)(2,1)}, bf16[4,72,768]{2,1,0:T(8,128)(2,1)}, u32[]{:S(2)}, u32[]{:S(2)}) collective-permute-start(bf16[4,72,768]{2,1,0:T(8,128)(2,1)} %maximum_select_fusion.9), channel_id=1, source_target_pairs={{0,2},{2,0},{4,6},{6,4},{1,3},{3,1},{5,7},{7,5},{8,10},{10,8},{12,... | collective-permute-start | bytes 1327112 | tf_op jit(solution)/shard_map/ppermute | solution.py:330
  387.5 20.2 %collective-permute-start.59 = (bf16[4,72,768]{2,1,0:T(8,128)(2,1)}, bf16[4,72,768]{2,1,0:T(8,128)(2,1)}, u32[]{:S(2)}, u32[]{:S(2)}) collective-permute-start(bf16[4,72,768]{2,1,0:T(8,128)(2,1)} %maximum_select_fusion.8), channel_id=1, source_target_pairs={{0,1},{1,0},{2,3},{3,2},{4,5},{5,4},{6,7},{7,6},{8,9},{9,8},{10,11... | collective-permute-start | bytes 1327112 | tf_op jit(solution)/shard_map/ppermute | solution.py:328
  (60 other events, 289.0 us)
